TPU v7x, 32 devices: a whole 2x2x4 slice. The times are simulated.
32 devices in a mesh: row: 4 (over z), col: 8 (over y, x, core).
Axes of the slice: x: 2, y: 2, z: 4, core: 2. Of those that a mesh axis runs over, the one named last changes fastest.
Arguments:
- tokens: bfloat16 [512, 8192], P('col', 'row'), may hold values from -6 to 6
- gate_weight: bfloat16 [8192, 16384], P('row', 'col'), may hold values from -0.0625 to 0.0625
- up_weight: bfloat16 [8192, 16384], P('row', 'col'), may hold values from -0.0625 to 0.0625
- block_mask: int32 [64, 128], P('row', 'col'), may hold values 0 or 1
- hidden_grad: bfloat16 [512, 16384], P('row', 'col'), may hold values from -0.26367188 to 0.26367188
Outputs:
- hidden: bfloat16 [512, 16384], P('row', 'col')
- gate_weight_grad: float32 [8192, 16384], P('row', 'col')
- up_weight_grad: float32 [8192, 16384], P('row', 'col')
All inputs are finite; a program needn't handle non-finite values. No bound on the sum of `block_mask` on one device may be relied on, other than what follows from the above.
Results may differ from a plain program's by a relative error of at most 0.003.
Values may be sent and summed in bfloat16 or wider, within the bound.
No kernel may reach another device: no remote copies, remote signals or barrier semaphores. Data moves between devices by JAX's collectives and lax.ppermute only.
A program may use at most 192 MiB of HBM per device.

v0:
```python
import jax
import jax.numpy as jnp
from jax import lax
from jax.sharding import PartitionSpec as P

BLOCK = 128


def spread(block_mask):
    rows, cols = block_mask.shape
    ones = block_mask.astype(jnp.bfloat16)
    wide = jnp.broadcast_to(ones[:, None, :, None], (rows, BLOCK, cols, BLOCK))
    return wide.reshape(rows * BLOCK, cols * BLOCK)


def local_grads(gate, up, cotangent):
    sig = jax.nn.sigmoid(gate)
    silu = gate * sig
    hidden = (silu * up).astype(jnp.bfloat16)
    back = cotangent.astype(jnp.float32)
    gate_delta = (back * up * sig * (1.0 + gate * (1.0 - sig))).astype(jnp.bfloat16)
    up_delta = (back * silu).astype(jnp.bfloat16)
    return (hidden, gate_delta, up_delta)


def on_device(tokens, gate_weight, up_weight, block_mask, hidden_grad):
    width = gate_weight.shape[1]
    keep = spread(block_mask)
    stacked = jnp.concatenate([gate_weight * keep, up_weight * keep], axis=1)
    gathered = lax.all_gather(tokens, "col", axis=0, tiled=True)
    terms = jnp.dot(gathered, stacked, preferred_element_type=jnp.float32)
    sources = lax.all_to_all(
        terms.reshape(1, terms.shape[0], terms.shape[1]),
        "row",
        split_axis=1,
        concat_axis=0,
        tiled=True,
    )
    both = jnp.sum(sources, axis=0)
    hidden, gate_delta, up_delta = local_grads(both[:, :width], both[:, width:], hidden_grad)
    deltas = jnp.concatenate([gate_delta, up_delta], axis=1)
    total = lax.dot_general(
        gathered,
        lax.all_gather(deltas, "row", axis=0, tiled=True),
        (((0,), (0,)), ((), ())),
        preferred_element_type=jnp.float32,
    )
    keep_wide = keep.astype(jnp.float32)
    return (hidden, total[:, :width] * keep_wide, total[:, width:] * keep_wide)


def solution(mesh):
    placed = (P("col", "row"), P("row", "col"), P("row", "col"), P("row", "col"), P("row", "col"))
    return jax.shard_map(
        on_device,
        mesh=mesh,
        in_specs=placed,
        out_specs=(P("row", "col"), P("row", "col"), P("row", "col")),
        check_vma=False,
    )
```

profile of v0, /device:TPU:0, one launch (start us, length us, event | category | flops | bytes accessed | tf_op | source)
XLA Modules:
  0.0 467.5 jit_solution(8447304248614226241)
XLA Ops:
  7.2 0.0 all-gather.3.cloned.1.call-start
  7.2 0.7 all-gather.3.cloned.1.call-update
  7.9 0.7 convert_element_type.18
  8.6 0.1 copy.13
  8.7 12.2 %copy.14 = bf16[2048,2048]{0,1:T(8,128)(2,1)} copy(bf16[2048,2048]{1,0:T(8,128)(2,1)} %param.6) | data formatting | bytes 16777216 | tf_op args[1]
  20.9 12.2 %copy.15 = bf16[2048,2048]{0,1:T(8,128)(2,1)} copy(bf16[2048,2048]{1,0:T(8,128)(2,1)} %param.7) | data formatting | bytes 16777216 | tf_op args[2]
  33.2 0.0 copy-start.1
  33.2 1.1 broadcast_in_dim.2
  34.3 0.0 copy-start
  34.3 4.3 copy-done
  38.6 1.0 copy-done.1
  39.6 10.6 %bitcast_multiply_fusion.1 = (bf16[2048,2048]{0,1:T(8,128)(2,1)}, bf16[2048,2048]{0,1:T(8,128)(2,1)}) fusion(bf16[2048,2048]{0,1:T(8,128)(2,1)S(1)} %copy-done.1, bf16[256,8,16,128]{3,2,1,0:T(8,128)(2,1)S(1)} %bitcast.19, bf16[2048,2048]{0,1:T(8,128)(2,1)} %copy.15), kind=kLoop, calls=%fused_computation.8 | loop fusion | flops 8388608 | bytes 41943040 | tf_op jit(solution)/shard_map/mul | solution.py:29
  50.2 0.0 all-gather.3.cloned.1.call-done
  50.2 18.5 %fusion.4 = f32[1,512,4096]{1,2,0:T(8,128)} fusion(bf16[512,2048]{1,0:T(8,128)(2,1)} %all-gather.3.cloned.1.call-done, bf16[2048,2048]{0,1:T(8,128)(2,1)} %get-tuple-element.12, bf16[2048,2048]{0,1:T(8,128)(2,1)} %get-tuple-element.11), kind=kOutput, calls=%fused_computation.9 | convolution fusion | flops 8623489024 | bytes 27262976 | tf_op jit(solution)/shard_map/dot_general | solution.py:31
  68.7 19.0 %copy.16 = f32[1,512,4096]{2,0,1:T(1,128)} copy(f32[1,512,4096]{1,2,0:T(8,128)} %fusion.4) | data formatting | bytes 16777216 | tf_op jit(solution)/shard_map/reshape | solution.py:33
  87.7 0.0 copy-start.2
  87.7 6.5 %all-to-all-start = ((f32[1,512,4096]{2,0,1:T(1,128)}), f32[1,512,4096]{2,0,1:T(1,128)}, u32[]{:S(2)}, u32[]{:S(2)}) async-start(f32[1,512,4096]{2,0,1:T(1,128)} %copy.16), calls=%async_computation | async-start | bytes 16777216 | tf_op jit(solution)/shard_map/all_to_all | solution.py:32
  94.2 0.0 all-gather.5.cloned.1.call-start
  94.2 0.0 copy-done.2
  94.2 1.0 copy.18
  95.2 183.2 %all-to-all-done = f32[1,512,4096]{2,0,1:T(1,128)} async-done(((f32[1,512,4096]{2,0,1:T(1,128)}), f32[1,512,4096]{2,0,1:T(1,128)}, u32[]{:S(2)}, u32[]{:S(2)}) %all-to-all-start) | async-done | bytes 8388640 | tf_op jit(solution)/shard_map/all_to_all | solution.py:32
  278.5 14.9 %copy.22 = f32[1,512,4096]{2,1,0:T(8,128)} copy(f32[1,512,4096]{2,0,1:T(1,128)} %all-to-all-done) | data formatting | bytes 16777216
  293.4 4.2 reduce_sum.9
  297.5 1.2 fusion.13
  298.7 1.5 copy.24
  300.3 0.3 copy.25
  300.6 1.7 fusion.9
  302.3 1.0 pad_maximum_fusion
  303.3 0.0 all-gather.5.cloned.1.call-update
  303.3 1.0 copy.19
  304.4 78.9 %all-gather.5.cloned.1.call-done = bf16[512,4096]{0,1:T(8,128)(2,1)} async-done(((bf16[128,4096]{0,1:T(8,128)(2,1)}), bf16[512,4096]{0,1:T(8,128)(2,1)}) %all-gather.5.cloned.1.call-update) | async-done | bytes 4194320 | tf_op jit(solution)/shard_map/all_gather | solution.py:44
  383.2 17.9 %convolution_bitcast_fusion = f32[2048,4096]{0,1:T(8,128)} fusion(bf16[512,4096]{0,1:T(8,128)(2,1)} %all-gather.5.cloned.1.call-done, bf16[512,2048]{1,0:T(8,128)(2,1)} %all-gather.3.cloned.1.call-done), kind=kOutput, calls=%fused_computation.2 | convolution fusion | flops 8589934592 | bytes 39845888 | tf_op jit(solution)/shard_map/dot_general | solution.py:42
  401.1 24.4 %convert_multiply_fusion = (f32[2048,2048]{0,1:T(8,128)}, f32[2048,2048]{0,1:T(8,128)}) fusion(f32[2048,4096]{0,1:T(8,128)} %convolution_bitcast_fusion, bf16[256,8,16,128]{3,2,1,0:T(8,128)(2,1)} %bitcast.20), kind=kLoop, calls=%fused_computation | loop fusion | flops 12582912 | bytes 75497472 | tf_op jit(solution)/shard_map/mul | solution.py:49
  425.5 17.6 %copy.21 = f32[2048,2048]{1,0:T(8,128)} copy(f32[2048,2048]{0,1:T(8,128)} %get-tuple-element.9) | data formatting | bytes 33554432
  443.1 17.6 %copy.20 = f32[2048,2048]{1,0:T(8,128)} copy(f32[2048,2048]{0,1:T(8,128)} %get-tuple-element.10) | data formatting | bytes 33554432
Async XLA Ops:
  7.2 43.0 %all-gather.3.cloned.1.call-start = ((), (), s32[]{:S(2)}) async-start(), calls=%async_computation.1 | async-start | bytes 2359296 | tf_op jit(solution)/shard_map/all_gather | solution.py:30
  33.2 6.4 %copy-start.1 = (bf16[2048,2048]{0,1:T(8,128)(2,1)S(1)}, bf16[2048,2048]{0,1:T(8,128)(2,1)}, u32[]{:S(2)}) copy-start(bf16[2048,2048]{0,1:T(8,128)(2,1)} %copy.14) | copy-start | bytes 25165828
  34.3 4.3 copy-start
  87.7 6.5 %copy-start.2 = (bf16[128,2048]{1,0:T(8,128)(2,1)S(1)}, bf16[128,2048]{1,0:T(8,128)(2,1)}, u32[]{:S(2)}) copy-start(bf16[128,2048]{1,0:T(8,128)(2,1)} %param.9) | copy-start | bytes 1572868
  87.7 190.7 %all-to-all-start = ((f32[1,512,4096]{2,0,1:T(1,128)}), f32[1,512,4096]{2,0,1:T(1,128)}, u32[]{:S(2)}, u32[]{:S(2)}) async-start(f32[1,512,4096]{2,0,1:T(1,128)} %copy.16), calls=%async_computation | async-start | bytes 16777216 | tf_op jit(solution)/shard_map/all_to_all | solution.py:32
  94.2 289.0 %all-gather.5.cloned.1.call-start = ((), (), s32[]{:S(2)}) async-start(), calls=%async_computation.2 | async-start | bytes 5242880 | tf_op jit(solution)/shard_map/all_gather | solution.py:44
Sparse Core Ops, SparseCore 0:
  9.9 30.5 all-gather.2
  303.5 79.7 all-gather.4
where the time goes:
time: 470 us; the launch traced here: 468 us
  waiting for transfers between devices  263 us (56%)
  local copies, waits for them, and re-layouts  105 us (22%)
  other arithmetic  42.6 us (9%)
  matrix products  36.4 us (8%)
  between operations  14.1 us (3%)
  starting transfers between devices  6.56 us (1%)
    all_to_all x1, waiting for transfers between devices, on_device(): lax.all_to_all(terms.reshape(1, terms.shape[0], terms.shape[1]), 'row', s...  183 us
    unnamed x15, local copies, waits for them, and re-layouts  83.7 us
    all_gather x1, waiting for transfers between devices, on_device(): lax.all_gather(deltas, 'row', axis=0, tiled=True)  78.9 us
    mul x1, other arithmetic, on_device(): return (hidden, total[:, :width] * keep_wide, total[:, width:] * keep_wide)  24.4 us
    reshape x1, local copies, waits for them, and re-layouts, on_device(): terms.reshape(1, terms.shape[0], terms.shape[1])  19 us
    dot_general x1, matrix products, on_device(): terms = jnp.dot(gathered, stacked, preferred_element_type=jnp.float32)  18.5 us
    dot_general x1, matrix products, on_device(): lax.dot_general(gathered, lax.all_gather(deltas, 'row', axis=0, tiled=Tru...  17.9 us
    mul x1, other arithmetic, on_device(): stacked = jnp.concatenate([gate_weight * keep, up_weight * keep], axis=1)  10.6 us
  transfers between devices with their start and end apart: 3, of which 2 were waited for; matrix products, arithmetic and copies ran while one was open for 8% of the time, Pallas kernels for 0%

commit v1 on v0

v1 whole, which is shorter than its diff:
```python
import functools

import jax
import jax.numpy as jnp
from jax import lax
from jax.experimental import pallas as pl
from jax.experimental.pallas import tpu as pltpu
from jax.sharding import PartitionSpec as P

BLOCK = 128
GROUPS = 16
CHUNKS = 4
VMEM_LIMIT = 48 * 1024 * 1024


def params():
    return pltpu.CompilerParams(vmem_limit_bytes=VMEM_LIMIT)


def encode(value):
    rows, cols = value.shape
    grouped = value.reshape(GROUPS, rows // GROUPS, cols)
    top = jnp.max(jnp.abs(grouped), axis=1)
    power = jnp.floor(jnp.log2(jnp.maximum(top, 1e-30))) + 1.0
    codes = jnp.round(grouped * jnp.exp2(15.0 - power)[:, None, :])
    codes = jnp.clip(codes, -32767.0, 32767.0).reshape(rows, cols)
    return codes.astype(jnp.int32).astype(jnp.int16), power.astype(jnp.int32).astype(jnp.int16)


def put(ref, value):
    rows = value.shape[0]
    codes, power = encode(value)
    ref[0:rows, :] = codes
    ref[rows : rows + GROUPS, :] = power


def get(ref):
    rows = ref.shape[0] - GROUPS
    cols = ref.shape[1]
    codes = ref[0:rows, :].astype(jnp.int32).astype(jnp.float32)
    power = ref[rows : rows + GROUPS, :].astype(jnp.int32).astype(jnp.float32)
    grouped = codes.reshape(GROUPS, rows // GROUPS, cols) * jnp.exp2(power - 15.0)[:, None, :]
    return grouped.reshape(rows, cols)


def forward_kernel(side_ref, mask_ref, far_ref, near_ref, gate_ref, up_ref, far_out, near_out, held, *, first):
    depth, width = gate_ref.shape
    base = (first + pl.program_id(0)) * (width // BLOCK)
    for r in range(depth // BLOCK):
        rows = slice(r * BLOCK, (r + 1) * BLOCK)
        for q in range(width // BLOCK):
            cols = slice(q * BLOCK, (q + 1) * BLOCK)
            keep = mask_ref[r, base + q] != 0
            gate = gate_ref[rows, cols]
            up = up_ref[rows, cols]
            held[rows, cols] = jnp.where(keep, gate, jnp.zeros_like(gate))
            held[rows, width + q * BLOCK : width + (q + 1) * BLOCK] = jnp.where(keep, up, jnp.zeros_like(up))
    put(far_out, jnp.dot(far_ref[...], held[...], preferred_element_type=jnp.float32))
    put(near_out, jnp.dot(near_ref[...], held[...], preferred_element_type=jnp.float32))


def forward(side, mask, tokens, gate_weight, up_weight, first, steps, width):
    count, depth = tokens.shape
    half = count // 2
    message = jax.ShapeDtypeStruct((half + GROUPS, 2 * width * steps), jnp.int16)
    weight = pl.BlockSpec((depth, width), lambda j, side, mask: (0, first + j))
    out = pl.BlockSpec((half + GROUPS, 2 * width), lambda j, side, mask: (0, j))
    return pl.pallas_call(
        functools.partial(forward_kernel, first=first),
        grid_spec=pltpu.PrefetchScalarGridSpec(
            num_scalar_prefetch=2,
            grid=(steps,),
            in_specs=[
                pl.BlockSpec((half, depth), lambda j, side, mask: (1 - side[0], 0)),
                pl.BlockSpec((half, depth), lambda j, side, mask: (side[0], 0)),
                weight,
                weight,
            ],
            out_specs=[out, out],
            scratch_shapes=[pltpu.VMEM((depth, 2 * width), jnp.bfloat16)],
        ),
        out_shape=[message, message],
        compiler_params=params(),
        cost_estimate=pl.CostEstimate(
            flops=4 * count * depth * width * steps,
            bytes_accessed=4 * depth * width * steps + 2 * count * depth + 4 * count * width * steps,
            transcendentals=0,
        ),
        name="forward",
    )(side, mask, tokens, tokens, gate_weight, up_weight)


def add_kernel(a_ref, b_ref, out_ref):
    put(out_ref, get(a_ref) + get(b_ref))


def add(a, b, width):
    rows, cols = a.shape
    spec = pl.BlockSpec((rows, 2 * width), lambda j: (0, j))
    return pl.pallas_call(
        add_kernel,
        grid=(cols // (2 * width),),
        in_specs=[spec, spec],
        out_specs=spec,
        out_shape=jax.ShapeDtypeStruct(a.shape, a.dtype),
        compiler_params=params(),
        cost_estimate=pl.CostEstimate(flops=16 * rows * cols, bytes_accessed=6 * rows * cols, transcendentals=0),
        name="add",
    )(a, b)


def grads_kernel(a_ref, b_ref, c_ref, back_ref, deltas_ref, hidden_ref):
    width = back_ref.shape[1]
    both = get(a_ref) + get(b_ref) + get(c_ref)
    gate, up = both[:, :width], both[:, width:]
    sig = jax.nn.sigmoid(gate)
    silu = gate * sig
    back = back_ref[...].astype(jnp.float32)
    hidden_ref[...] = (silu * up).astype(jnp.bfloat16)
    deltas_ref[:, :width] = (back * up * sig * (1.0 + gate * (1.0 - sig))).astype(jnp.bfloat16)
    deltas_ref[:, width:] = (back * silu).astype(jnp.bfloat16)


def grads(a, b, c, back, first, width):
    rows, cols = a.shape
    half = rows - GROUPS
    spec = pl.BlockSpec((rows, 2 * width), lambda j: (0, j))
    return pl.pallas_call(
        grads_kernel,
        grid=(cols // (2 * width),),
        in_specs=[spec, spec, spec, pl.BlockSpec((half, width), lambda j: (0, first + j))],
        out_specs=[
            pl.BlockSpec((half, 2 * width), lambda j: (0, j)),
            pl.BlockSpec((half, width), lambda j: (0, j)),
        ],
        out_shape=[
            jax.ShapeDtypeStruct((half, cols), jnp.bfloat16),
            jax.ShapeDtypeStruct((half, cols // 2), jnp.bfloat16),
        ],
        compiler_params=params(),
        cost_estimate=pl.CostEstimate(flops=20 * rows * cols, bytes_accessed=10 * rows * cols, transcendentals=rows * cols),
        name="grads",
    )(a, b, c, back)


def weights_kernel(side_ref, mask_ref, near_ref, far_ref, first_ref, second_ref, *rest, first):
    gate_ref, up_ref = rest[-2:]
    depth, width = gate_ref.shape
    base = (first + pl.program_id(0)) * (width // BLOCK)
    total = jnp.dot(near_ref[...], first_ref[...], preferred_element_type=jnp.float32)
    total += jnp.dot(far_ref[...], second_ref[...], preferred_element_type=jnp.float32)
    for r in range(depth // BLOCK):
        rows = slice(r * BLOCK, (r + 1) * BLOCK)
        for q in range(width // BLOCK):
            cols = slice(q * BLOCK, (q + 1) * BLOCK)
            keep = mask_ref[r, base + q].astype(jnp.float32)
            gate_ref[rows, cols] = total[rows, cols] * keep
            up_ref[rows, cols] = total[rows, width + q * BLOCK : width + (q + 1) * BLOCK] * keep


def weight_grads(side, mask, turned, first_half, second_half, previous, shape, first, width):
    depth, count = turned.shape
    half = count // 2
    steps = first_half.shape[1] // (2 * width)
    deltas = pl.BlockSpec((half, 2 * width), lambda j, side, mask: (0, j))
    out = pl.BlockSpec((depth, width), lambda j, side, mask: (0, first + j))
    whole = jax.ShapeDtypeStruct(shape, jnp.float32)
    return pl.pallas_call(
        functools.partial(weights_kernel, first=first),
        grid_spec=pltpu.PrefetchScalarGridSpec(
            num_scalar_prefetch=2,
            grid=(steps,),
            in_specs=[
                pl.BlockSpec((depth, half), lambda j, side, mask: (0, side[0])),
                pl.BlockSpec((depth, half), lambda j, side, mask: (0, 1 - side[0])),
                deltas,
                deltas,
            ]
            + [pl.BlockSpec(memory_space=pl.ANY)] * len(previous),
            out_specs=[out, out],
        ),
        out_shape=[whole, whole],
        input_output_aliases={6 + i: i for i in range(len(previous))},
        compiler_params=params(),
        cost_estimate=pl.CostEstimate(
            flops=4 * count * depth * width * steps,
            bytes_accessed=8 * depth * width * steps + 2 * count * depth + 4 * count * width * steps,
            transcendentals=0,
        ),
        name="weight_grads",
    )(side, mask, turned, turned, first_half, second_half, *previous)


def on_device(tokens, gate_weight, up_weight, block_mask, hidden_grad, *, ring):
    me = lax.axis_index("row")
    depth, local = gate_weight.shape
    left, right = ring // 2 - 1, ring // 2
    reach = ring // 2 - 1
    on_right = me >= right
    distance = jnp.where(on_right, me - right, left - me)
    side = on_right.astype(jnp.int32).reshape(1)
    chunks = min(CHUNKS, local // BLOCK)
    span = local // chunks
    width = min(2 * BLOCK, span)
    steps = span // width

    def outward(value, hop):
        return lax.ppermute(value, "row", [(left - hop, left - hop - 1), (right + hop, right + hop + 1)])

    def inward(value, hop):
        return lax.ppermute(value, "row", [(left - hop - 1, left - hop), (right + hop + 1, right + hop)])

    def swap(value):
        return lax.ppermute(value, "row", [(left, right), (right, left)])

    def pick(condition, a, b):
        return lax.select(jnp.broadcast_to(condition, a.shape), a, b)

    gathered = lax.all_gather(tokens, "col", axis=0, tiled=True)
    turned = gathered.T

    pieces = [hidden_grad]
    for hop in range(1, reach + 1):
        pieces.append(lax.ppermute(hidden_grad, "row", [(left - hop, left), (right + hop, right)]))
    back = pick(on_right, jnp.concatenate(pieces, axis=0), jnp.concatenate(pieces[::-1], axis=0))

    outs = ()
    hiddens = []
    for chunk in range(chunks):
        first = chunk * steps
        far, near = forward(side, block_mask, gathered, gate_weight, up_weight, first, steps, width)
        far_sum, near_sum = far, near
        for hop in reversed(range(reach)):
            far_in, near_in = inward(far_sum, hop), inward(near_sum, hop)
            far_sum = add(far, far_in, width)
            if hop:
                near_sum = add(near, near_in, width)
        across = swap(far_sum)
        if not reach:
            near_in = jnp.zeros_like(near)
        deltas, hidden = grads(near, near_in, across, back, first, width)
        hiddens.append(hidden)
        other = swap(deltas)
        for hop in range(reach):
            moved, moved_other = outward(deltas, hop), outward(other, hop)
            deltas = pick(distance == hop + 1, moved, deltas)
            other = pick(distance == hop + 1, moved_other, other)
        outs = weight_grads(side, block_mask, turned, deltas, other, outs, (depth, local), first, width)

    hidden = jnp.concatenate(hiddens, axis=1)
    share = hidden.shape[0] // (reach + 1)

    def piece(hop):
        start = jnp.where(on_right, hop, reach - hop) * share
        return lax.dynamic_slice_in_dim(hidden, start, share, axis=0)

    result = piece(0)
    for hop in range(1, reach + 1):
        moved = lax.ppermute(piece(hop), "row", [(left, left - hop), (right, right + hop)])
        result = pick(distance == hop, moved, result)
    return (result, *outs)


def solution(mesh):
    placed = (P("col", "row"), P("row", "col"), P("row", "col"), P("row", "col"), P("row", "col"))
    return jax.shard_map(
        functools.partial(on_device, ring=mesh.shape["row"]),
        mesh=mesh,
        in_specs=placed,
        out_specs=(P("row", "col"), P("row", "col"), P("row", "col")),
        check_vma=False,
    )
```

time: 470 us -> 271 us (0.58)
  waiting for transfers between devices: 263 us -> 127 us
  local copies, waits for them, and re-layouts: 105 us -> 12 us
  Pallas kernels: 0 us -> 59.5 us
  starting transfers between devices: 6.56 us -> 51 us
  other arithmetic: 42.6 us -> 5.62 us
  matrix products: 36.4 us -> 0 us
    all_to_all x1 -> x0, waiting for transfers between devices: 183 us -> none  [on_device(): lax.all_to_all(terms.reshape(1, terms.shape[0], terms.shape[1]), 'row', s...]
    ppermute x0 -> x26, waiting for transfers between devices: none -> 98.5 us  [the longest x8 59 us: outward(): lax.ppermute(value, 'row', [(left - hop, left - hop - 1), (right + hop, r...]
    all_gather x1 -> x0, waiting for transfers between devices: 78.9 us -> none  [on_device(): lax.all_gather(deltas, 'row', axis=0, tiled=True)]
    unnamed x15 -> x35, local copies, waits for them, and re-layouts: 83.7 us -> 8.64 us
    pallas_call x0 -> x16, Pallas kernels: none -> 59.5 us  [the longest x4 24.2 us: forward(): pl.pallas_call(functools.partial(forward_kernel, first=first), grid_spec=...]
    ppermute x0 -> x26, starting transfers between devices: none -> 50.9 us  [the longest x8 25.4 us: inward(): lax.ppermute(value, 'row', [(left - hop - 1, left - hop), (right + hop +...]
    dot_general x2 -> x0, matrix products: 36.4 us -> none  [the longest x1 18.5 us: on_device(): terms = jnp.dot(gathered, stacked, preferred_element_type=jnp.float32)]
    mul x2 -> x0, other arithmetic: 35 us -> none  [the longest x1 24.4 us: on_device(): return (hidden, total[:, :width] * keep_wide, total[:, width:] * keep_wide)]
  transfers between devices with their start and end apart: 3 -> 27, of which waited for: 2 -> 16; matrix products, arithmetic and copies ran while one was open for 8% -> 3% of each run, Pallas kernels for 0% -> 20%
where the time goes in v1:
time: 271 us; the launch traced here: 269 us
  waiting for transfers between devices  127 us (47%)
  Pallas kernels  59.5 us (22%)
  starting transfers between devices  51 us (19%)
  between operations  14.5 us (5%)
  local copies, waits for them, and re-layouts  12 us (4%)
  other arithmetic  5.62 us (2%)
    ppermute x8, waiting for transfers between devices, outward(): lax.ppermute(value, 'row', [(left - hop, left - hop - 1), (right + hop, r...  59 us
    ppermute x8, waiting for transfers between devices, inward(): lax.ppermute(value, 'row', [(left - hop - 1, left - hop), (right + hop +...  31.2 us
    all_gather x1, waiting for transfers between devices, on_device(): gathered = lax.all_gather(tokens, 'col', axis=0, tiled=True)  27.6 us
    ppermute x8, starting transfers between devices, inward(): lax.ppermute(value, 'row', [(left - hop - 1, left - hop), (right + hop +...  25.4 us
    pallas_call x4, Pallas kernels, forward(): pl.pallas_call(functools.partial(forward_kernel, first=first), grid_spec=...  24.2 us
    pallas_call x4, Pallas kernels, weight_grads(): pl.pallas_call(functools.partial(weights_kernel, first=first), grid_spec=...  22.1 us
    ppermute x8, starting transfers between devices, outward(): lax.ppermute(value, 'row', [(left - hop, left - hop - 1), (right + hop, r...  10.3 us
    ppermute x8, starting transfers between devices, swap(): return lax.ppermute(value, 'row', [(left, right), (right, left)])  8.97 us
  transfers between devices with their start and end apart: 27, of which 16 were waited for; matrix products, arithmetic and copies ran while one was open for 3% of the time, Pallas kernels for 20%

profile of v1, /device:TPU:0, one launch (start us, length us, event | category | flops | bytes accessed | tf_op | source)
XLA Modules:
  0.0 269.5 jit_solution(546992168516895460)
XLA Ops:
  7.9 5.0 %collective-permute-start.3 = (bf16[128,2048]{1,0:T(8,128)(2,1)}, bf16[128,2048]{1,0:T(8,128)(2,1)S(1)}, u32[]{:S(2)}, u32[]{:S(2)}) collective-permute-start(bf16[128,2048]{1,0:T(8,128)(2,1)} %param.9), channel_id=1, source_target_pairs={{0,8},{24,16},{1,9},{25,17},{2,10},{26,18},{3,11},{27,19},{4,12},{... | collective-permute-start | bytes 1572872 | tf_op jit(solution)/shard_map/ppermute | solution.py:224
  12.9 27.6 %all-gather.2.cloned.1.call-done.far_ref.near_ref = bf16[512,2048]{1,0:T(8,128)(2,1)} async-done(((bf16[64,2048]{1,0:T(8,128)(2,1)}), bf16[512,2048]{1,0:T(8,128)(2,1)}) %all-gather.2.cloned.1.call-update) | async-done | bytes 2097168 | tf_op jit(solution)/shard_map/all_gather | solution.py:219
  40.5 1.6 copy-done
  42.8 5.8 %forward.4 = (s16[272,1024]{1,0:T(8,128)(2,1)S(1)}, s16[272,1024]{1,0:T(8,128)(2,1)S(1)}) custom-call(s32[1]{0:T(128)} %bitcast.side_ref, s32[16,16]{1,0:T(8,128)S(1)} %copy-done.12, bf16[512,2048]{1,0:T(8,128)(2,1)S(1)} %copy-done, bf16[512,2048]{1,0:T(8,128)(2,1)S(1)} %copy-done, bf16[2048,2048]{1,0:T(8,128)(2,1)} %gate_ref.7, bf16[2048,2048]{1,0:T(8,128)(2,1)} %up_ref.7), custom_call_target="tpu_custom_call" | custom-call | flops 2147483648 | bytes 7340032 | tf_op jit(solution)/shard_map/forward/pallas_call | solution.py:68
  48.7 3.4 %collective-permute-start = (s16[272,1024]{1,0:T(8,128)(2,1)S(1)}, s16[272,1024]{1,0:T(8,128)(2,1)S(1)}, u32[]{:S(2)}, u32[]{:S(2)}) collective-permute-start(s16[272,1024]{1,0:T(8,128)(2,1)S(1)} %get-tuple-element.27.a_ref), channel_id=1, source_target_pairs={{0,8},{24,16},{1,9},{25,17},{2,10},{26,18},{3,11},{27,19},{4,12},{... | collective-permute-start | bytes 1671176 | tf_op jit(solution)/shard_map/ppermute | solution.py:211
  52.1 1.3 collective-permute-start.1
  53.4 6.5 %forward.5 = (s16[272,1024]{1,0:T(8,128)(2,1)S(1)}, s16[272,1024]{1,0:T(8,128)(2,1)}) custom-call(s32[1]{0:T(128)} %bitcast.side_ref, s32[16,16]{1,0:T(8,128)S(1)} %copy-done.13, bf16[512,2048]{1,0:T(8,128)(2,1)S(1)} %copy-done, bf16[512,2048]{1,0:T(8,128)(2,1)S(1)} %copy-done, bf16[2048,2048]{1,0:T(8,128)(2,1)} %gate_ref.7, bf16[2048,2048]{1,0:T(8,128)(2,1)} %up_ref.7), custom_call_target="tpu_custom_call" | custom-call | flops 2147483648 | bytes 7340032 | tf_op jit(solution)/shard_map/forward/pallas_call | solution.py:68
  60.0 1.3 collective-permute-start.5
  61.3 5.9 %forward.6 = (s16[272,1024]{1,0:T(8,128)(2,1)S(1)}, s16[272,1024]{1,0:T(8,128)(2,1)S(1)}) custom-call(s32[1]{0:T(128)} %bitcast.side_ref, s32[16,16]{1,0:T(8,128)S(1)} %copy-done.13, bf16[512,2048]{1,0:T(8,128)(2,1)S(1)} %copy-done, bf16[512,2048]{1,0:T(8,128)(2,1)S(1)} %copy-done, bf16[2048,2048]{1,0:T(8,128)(2,1)} %gate_ref.7, bf16[2048,2048]{1,0:T(8,128)(2,1)} %up_ref.7), custom_call_target="tpu_custom_call" | custom-call | flops 2147483648 | bytes 7340032 | tf_op jit(solution)/shard_map/forward/pallas_call | solution.py:68
  67.2 1.3 collective-permute-start.8
  68.6 5.9 %forward.7 = (s16[272,1024]{1,0:T(8,128)(2,1)S(1)}, s16[272,1024]{1,0:T(8,128)(2,1)S(1)}) custom-call(s32[1]{0:T(128)} %bitcast.side_ref, s32[16,16]{1,0:T(8,128)S(1)} %copy-done.13, bf16[512,2048]{1,0:T(8,128)(2,1)S(1)} %copy-done, bf16[512,2048]{1,0:T(8,128)(2,1)S(1)} %copy-done, bf16[2048,2048]{1,0:T(8,128)(2,1)} %gate_ref.7, bf16[2048,2048]{1,0:T(8,128)(2,1)} %up_ref.7), custom_call_target="tpu_custom_call" | custom-call | flops 2147483648 | bytes 7340032 | tf_op jit(solution)/shard_map/forward/pallas_call | solution.py:68
  75.3 1.3 collective-permute-start.11
  77.0 5.2 %collective-permute-start.4 = (s16[272,1024]{1,0:T(8,128)(2,1)}, s16[272,1024]{1,0:T(8,128)(2,1)}, u32[]{:S(2)}, u32[]{:S(2)}) collective-permute-start(s16[272,1024]{1,0:T(8,128)(2,1)} %get-tuple-element.30.a_ref), channel_id=1, source_target_pairs={{0,8},{24,16},{1,9},{25,17},{2,10},{26,18},{3,11},{27,19},{4,12},{... | collective-permute-start | bytes 1671176 | tf_op jit(solution)/shard_map/ppermute | solution.py:211
  82.2 1.6 add.13
  83.8 5.1 %collective-permute-done.5.b_ref = s16[272,1024]{1,0:T(8,128)(2,1)S(1)} collective-permute-done((s16[272,1024]{1,0:T(8,128)(2,1)S(1)}, s16[272,1024]{1,0:T(8,128)(2,1)S(1)}, u32[]{:S(2)}, u32[]{:S(2)}) %collective-permute-start.5) | collective-permute-done | bytes 557088 | tf_op jit(solution)/shard_map/ppermute | solution.py:211
  88.9 1.5 collective-permute-start.2
  90.4 1.6 add.14
  92.0 8.8 %collective-permute-done.8.b_ref = s16[272,1024]{1,0:T(8,128)(2,1)S(1)} collective-permute-done((s16[272,1024]{1,0:T(8,128)(2,1)S(1)}, s16[272,1024]{1,0:T(8,128)(2,1)S(1)}, u32[]{:S(2)}, u32[]{:S(2)}) %collective-permute-start.8) | collective-permute-done | bytes 557088 | tf_op jit(solution)/shard_map/ppermute | solution.py:211
  100.8 1.5 collective-permute-start.6
  102.3 1.6 add.15
  104.7 7.1 %collective-permute-start.7 = (s16[272,1024]{1,0:T(8,128)(2,1)S(1)}, s16[272,1024]{1,0:T(8,128)(2,1)}, u32[]{:S(2)}, u32[]{:S(2)}) collective-permute-start(s16[272,1024]{1,0:T(8,128)(2,1)S(1)} %get-tuple-element.33.a_ref), channel_id=1, source_target_pairs={{0,8},{24,16},{1,9},{25,17},{2,10},{26,18},{3,11},{27,19},{4,12},{... | collective-permute-start | bytes 1671176 | tf_op jit(solution)/shard_map/ppermute | solution.py:211
  112.8 1.5 collective-permute-start.9
  115.2 9.6 %collective-permute-done.4.b_ref = s16[272,1024]{1,0:T(8,128)(2,1)} collective-permute-done((s16[272,1024]{1,0:T(8,128)(2,1)}, s16[272,1024]{1,0:T(8,128)(2,1)}, u32[]{:S(2)}, u32[]{:S(2)}) %collective-permute-start.4) | collective-permute-done | bytes 557088 | tf_op jit(solution)/shard_map/ppermute | solution.py:211
  124.8 4.4 %collective-permute-start.10 = (s16[272,1024]{1,0:T(8,128)(2,1)S(1)}, s16[272,1024]{1,0:T(8,128)(2,1)S(1)}, u32[]{:S(2)}, u32[]{:S(2)}) collective-permute-start(s16[272,1024]{1,0:T(8,128)(2,1)S(1)} %get-tuple-element.36.a_ref), channel_id=1, source_target_pairs={{0,8},{24,16},{1,9},{25,17},{2,10},{26,18},{3,11},{27,19},{4,12},{... | collective-permute-start | bytes 1671176 | tf_op jit(solution)/shard_map/ppermute | solution.py:211
  130.1 1.9 maximum_select_fusion.back_ref
  134.2 2.5 grads.4
  136.7 2.0 grads.5
  139.6 2.0 grads.6
  141.7 6.3 %collective-permute-done.10.b_ref = s16[272,1024]{1,0:T(8,128)(2,1)S(1)} collective-permute-done((s16[272,1024]{1,0:T(8,128)(2,1)S(1)}, s16[272,1024]{1,0:T(8,128)(2,1)S(1)}, u32[]{:S(2)}, u32[]{:S(2)}) %collective-permute-start.10) | collective-permute-done | bytes 557088 | tf_op jit(solution)/shard_map/ppermute | solution.py:211
  152.9 1.5 collective-permute-start.24
  155.7 2.5 copy.23
  159.0 1.3 collective-permute-start.20
  160.3 8.4 %collective-permute-done.13 = bf16[128,2048]{1,0:T(8,128)(2,1)} collective-permute-done((bf16[128,2048]{1,0:T(8,128)(2,1)}, bf16[128,2048]{1,0:T(8,128)(2,1)}, u32[]{:S(2)}, u32[]{:S(2)}) %collective-permute-start.13) | collective-permute-done | bytes 524320 | tf_op jit(solution)/shard_map/ppermute | solution.py:259
  169.4 2.1 dynamic-slice_select_fusion
  172.8 7.1 %collective-permute-done.23 = bf16[256,1024]{1,0:T(8,128)(2,1)} collective-permute-done((bf16[256,1024]{1,0:T(8,128)(2,1)}, bf16[256,1024]{1,0:T(8,128)(2,1)}, u32[]{:S(2)}, u32[]{:S(2)}) %collective-permute-start.23) | collective-permute-done | bytes 524320 | tf_op jit(solution)/shard_map/ppermute | solution.py:208
  181.7 9.3 %collective-permute-done.20 = bf16[256,1024]{1,0:T(8,128)(2,1)S(1)} collective-permute-done((bf16[256,1024]{1,0:T(8,128)(2,1)}, bf16[256,1024]{1,0:T(8,128)(2,1)S(1)}, u32[]{:S(2)}, u32[]{:S(2)}) %collective-permute-start.20) | collective-permute-done | bytes 524320 | tf_op jit(solution)/shard_map/ppermute | solution.py:208
  192.5 1.3 collective-permute-start.25
  193.8 1.3 collective-permute-start.22
  195.1 7.2 %collective-permute-done.17 = bf16[256,1024]{1,0:T(8,128)(2,1)S(1)} collective-permute-done((bf16[256,1024]{1,0:T(8,128)(2,1)S(1)}, bf16[256,1024]{1,0:T(8,128)(2,1)S(1)}, u32[]{:S(2)}, u32[]{:S(2)}) %collective-permute-start.17) | collective-permute-done | bytes 524320 | tf_op jit(solution)/shard_map/ppermute | solution.py:208
  205.0 8.6 %collective-permute-done.14 = bf16[256,1024]{1,0:T(8,128)(2,1)S(1)} collective-permute-done((bf16[256,1024]{1,0:T(8,128)(2,1)S(1)}, bf16[256,1024]{1,0:T(8,128)(2,1)S(1)}, u32[]{:S(2)}, u32[]{:S(2)}) %collective-permute-start.14) | collective-permute-done | bytes 524320 | tf_op jit(solution)/shard_map/ppermute | solution.py:208
  213.6 11.2 %collective-permute-done.25 = bf16[256,1024]{1,0:T(8,128)(2,1)S(1)} collective-permute-done((bf16[256,1024]{1,0:T(8,128)(2,1)}, bf16[256,1024]{1,0:T(8,128)(2,1)S(1)}, u32[]{:S(2)}, u32[]{:S(2)}) %collective-permute-start.25) | collective-permute-done | bytes 524320 | tf_op jit(solution)/shard_map/ppermute | solution.py:208
  224.8 5.5 %weight_grads.4 = (f32[2048,2048]{1,0:T(8,128)}, f32[2048,2048]{1,0:T(8,128)}) custom-call(s32[1]{0:T(128)} %bitcast.side_ref, s32[16,16]{1,0:T(8,128)S(1)} %copy-done.13, bf16[2048,512]{1,0:T(8,128)(2,1)S(1)} %bitcast.2, bf16[2048,512]{1,0:T(8,128)(2,1)S(1)} %bitcast.3, bf16[256,1024]{1,0:T(8,128)(2,1)S(1)} %broadcast_select_fusion.1.first_ref, ...), custom_call_target="tpu_custom_call" | custom-call | flops 2147483648 | bytes 11534336 | tf_op jit(solution)/shard_map/weight_grads/pallas_call | solution.py:168
  230.3 5.7 %collective-permute-done.22 = bf16[256,1024]{1,0:T(8,128)(2,1)S(1)} collective-permute-done((bf16[256,1024]{1,0:T(8,128)(2,1)S(1)}, bf16[256,1024]{1,0:T(8,128)(2,1)S(1)}, u32[]{:S(2)}, u32[]{:S(2)}) %collective-permute-start.22) | collective-permute-done | bytes 524320 | tf_op jit(solution)/shard_map/ppermute | solution.py:208
  236.1 5.5 %weight_grads.5 = (f32[2048,2048]{1,0:T(8,128)}, f32[2048,2048]{1,0:T(8,128)}) custom-call(s32[1]{0:T(128)} %bitcast.side_ref, s32[16,16]{1,0:T(8,128)S(1)} %copy-done.13, bf16[2048,512]{1,0:T(8,128)(2,1)S(1)} %bitcast.4, bf16[2048,512]{1,0:T(8,128)(2,1)S(1)} %bitcast.5, ...), custom_call_target="tpu_custom_call", output_to_operand_aliasing={{0}: (6, {}), {1}: (7, {})} | custom-call | flops 2147483648 | bytes 11534336 | tf_op jit(solution)/shard_map/weight_grads/pallas_call | solution.py:168
  241.6 5.7 %collective-permute-done.19 = bf16[256,1024]{1,0:T(8,128)(2,1)S(1)} collective-permute-done((bf16[256,1024]{1,0:T(8,128)(2,1)S(1)}, bf16[256,1024]{1,0:T(8,128)(2,1)S(1)}, u32[]{:S(2)}, u32[]{:S(2)}) %collective-permute-start.19) | collective-permute-done | bytes 524320 | tf_op jit(solution)/shard_map/ppermute | solution.py:208
  247.3 5.5 %weight_grads.6 = (f32[2048,2048]{1,0:T(8,128)}, f32[2048,2048]{1,0:T(8,128)}) custom-call(s32[1]{0:T(128)} %bitcast.side_ref, s32[16,16]{1,0:T(8,128)S(1)} %copy-done.13, bf16[2048,512]{1,0:T(8,128)(2,1)S(1)} %bitcast.6, bf16[2048,512]{1,0:T(8,128)(2,1)S(1)} %bitcast.7, ...), custom_call_target="tpu_custom_call", output_to_operand_aliasing={{0}: (6, {}), {1}: (7, {})} | custom-call | flops 2147483648 | bytes 11534336 | tf_op jit(solution)/shard_map/weight_grads/pallas_call | solution.py:168
  252.8 4.2 %collective-permute-done.16 = bf16[256,1024]{1,0:T(8,128)(2,1)S(1)} collective-permute-done((bf16[256,1024]{1,0:T(8,128)(2,1)S(1)}, bf16[256,1024]{1,0:T(8,128)(2,1)S(1)}, u32[]{:S(2)}, u32[]{:S(2)}) %collective-permute-start.16) | collective-permute-done | bytes 524320 | tf_op jit(solution)/shard_map/ppermute | solution.py:208
  257.1 5.5 %weight_grads.7 = (f32[2048,2048]{1,0:T(8,128)}, f32[2048,2048]{1,0:T(8,128)}) custom-call(s32[1]{0:T(128)} %bitcast.side_ref, s32[16,16]{1,0:T(8,128)S(1)} %copy-done.13, bf16[2048,512]{1,0:T(8,128)(2,1)S(1)} %bitcast.8, bf16[2048,512]{1,0:T(8,128)(2,1)S(1)} %bitcast.9, ...), custom_call_target="tpu_custom_call", output_to_operand_aliasing={{0}: (6, {}), {1}: (7, {})} | custom-call | flops 2147483648 | bytes 11534336 | tf_op jit(solution)/shard_map/weight_grads/pallas_call | solution.py:168
  (71 shorter events, 24.2 us)
Async XLA Ops:
  7.2 33.4 %all-gather.2.cloned.1.call-start = ((), (), s32[]{:S(2)}) async-start(), calls=%async_computation | async-start | bytes 2359296 | tf_op jit(solution)/shard_map/all_gather | solution.py:219
  7.9 66.6 %collective-permute-start.3 = (bf16[128,2048]{1,0:T(8,128)(2,1)}, bf16[128,2048]{1,0:T(8,128)(2,1)S(1)}, u32[]{:S(2)}, u32[]{:S(2)}) collective-permute-start(bf16[128,2048]{1,0:T(8,128)(2,1)} %param.9), channel_id=1, source_target_pairs={{0,8},{24,16},{1,9},{25,17},{2,10},{26,18},{3,11},{27,19},{4,12},{... | collective-permute-start | bytes 1572872 | tf_op jit(solution)/shard_map/ppermute | solution.py:224
  40.5 1.6 copy-start
  42.1 0.7 copy-start.12
  42.8 10.6 %copy-start.13 = (s32[16,16]{1,0:T(8,128)S(1)}, s32[16,16]{1,0:T(8,128)}, u32[]{:S(2)}) copy-start(s32[16,16]{1,0:T(8,128)} %mask_ref.15) | copy-start | bytes 3076
  48.7 11.3 %copy-start.3 = (s16[272,1024]{1,0:T(8,128)(2,1)}, s16[272,1024]{1,0:T(8,128)(2,1)S(1)}, u32[]{:S(2)}) copy-start(s16[272,1024]{1,0:T(8,128)(2,1)S(1)} %get-tuple-element.27.a_ref) | copy-start | bytes 1671172
  48.7 55.2 %collective-permute-start = (s16[272,1024]{1,0:T(8,128)(2,1)S(1)}, s16[272,1024]{1,0:T(8,128)(2,1)S(1)}, u32[]{:S(2)}, u32[]{:S(2)}) collective-permute-start(s16[272,1024]{1,0:T(8,128)(2,1)S(1)} %get-tuple-element.27.a_ref), channel_id=1, source_target_pairs={{0,8},{24,16},{1,9},{25,17},{2,10},{26,18},{3,11},{27,19},{4,12},{... | collective-permute-start | bytes 1671176 | tf_op jit(solution)/shard_map/ppermute | solution.py:211
  52.1 24.9 %collective-permute-start.1 = (s16[272,1024]{1,0:T(8,128)(2,1)S(1)}, s16[272,1024]{1,0:T(8,128)(2,1)S(1)}, u32[]{:S(2)}, u32[]{:S(2)}) collective-permute-start(s16[272,1024]{1,0:T(8,128)(2,1)S(1)} %get-tuple-element.28.a_ref), channel_id=1, source_target_pairs={{0,8},{24,16},{1,9},{25,17},{2,10},{26,18},{3,11},{27,19},{4,12},{... | collective-permute-start | bytes 1671176 | tf_op jit(solution)/shard_map/ppermute | solution.py:211
  60.0 28.9 %collective-permute-start.5 = (s16[272,1024]{1,0:T(8,128)(2,1)S(1)}, s16[272,1024]{1,0:T(8,128)(2,1)S(1)}, u32[]{:S(2)}, u32[]{:S(2)}) collective-permute-start(s16[272,1024]{1,0:T(8,128)(2,1)S(1)} %get-tuple-element.31.a_ref), channel_id=1, source_target_pairs={{0,8},{24,16},{1,9},{25,17},{2,10},{26,18},{3,11},{27,19},{4,12},{... | collective-permute-start | bytes 1671176 | tf_op jit(solution)/shard_map/ppermute | solution.py:211
  67.2 33.6 %collective-permute-start.8 = (s16[272,1024]{1,0:T(8,128)(2,1)S(1)}, s16[272,1024]{1,0:T(8,128)(2,1)S(1)}, u32[]{:S(2)}, u32[]{:S(2)}) collective-permute-start(s16[272,1024]{1,0:T(8,128)(2,1)S(1)} %get-tuple-element.34.a_ref), channel_id=1, source_target_pairs={{0,8},{24,16},{1,9},{25,17},{2,10},{26,18},{3,11},{27,19},{4,12},{... | collective-permute-start | bytes 1671176 | tf_op jit(solution)/shard_map/ppermute | solution.py:211
  74.5 0.8 copy-start.15
  75.3 37.5 %collective-permute-start.11 = (s16[272,1024]{1,0:T(8,128)(2,1)S(1)}, s16[272,1024]{1,0:T(8,128)(2,1)S(1)}, u32[]{:S(2)}, u32[]{:S(2)}) collective-permute-start(s16[272,1024]{1,0:T(8,128)(2,1)S(1)} %get-tuple-element.37.a_ref), channel_id=1, source_target_pairs={{0,8},{24,16},{1,9},{25,17},{2,10},{26,18},{3,11},{27,19},{4,12},{... | collective-permute-start | bytes 1671176 | tf_op jit(solution)/shard_map/ppermute | solution.py:211
  77.0 47.9 %collective-permute-start.4 = (s16[272,1024]{1,0:T(8,128)(2,1)}, s16[272,1024]{1,0:T(8,128)(2,1)}, u32[]{:S(2)}, u32[]{:S(2)}) collective-permute-start(s16[272,1024]{1,0:T(8,128)(2,1)} %get-tuple-element.30.a_ref), channel_id=1, source_target_pairs={{0,8},{24,16},{1,9},{25,17},{2,10},{26,18},{3,11},{27,19},{4,12},{... | collective-permute-start | bytes 1671176 | tf_op jit(solution)/shard_map/ppermute | solution.py:211
  88.9 40.3 %collective-permute-start.2 = (s16[272,1024]{1,0:T(8,128)(2,1)}, s16[272,1024]{1,0:T(8,128)(2,1)}, u32[]{:S(2)}, u32[]{:S(2)}) collective-permute-start(s16[272,1024]{1,0:T(8,128)(2,1)} %add.13), channel_id=1, source_target_pairs={{8,16},{16,8},{9,17},{17,9},{10,18},{18,10},{11,19},{19,11},{12,20... | collective-permute-start | bytes 1671176 | tf_op jit(solution)/shard_map/ppermute | solution.py:214
  100.8 35.9 %collective-permute-start.6 = (s16[272,1024]{1,0:T(8,128)(2,1)}, s16[272,1024]{1,0:T(8,128)(2,1)}, u32[]{:S(2)}, u32[]{:S(2)}) collective-permute-start(s16[272,1024]{1,0:T(8,128)(2,1)} %add.14), channel_id=1, source_target_pairs={{8,16},{16,8},{9,17},{17,9},{10,18},{18,10},{11,19},{19,11},{12,20... | collective-permute-start | bytes 1671176 | tf_op jit(solution)/shard_map/ppermute | solution.py:214
  103.9 0.8 copy-start.5
  104.7 34.8 %collective-permute-start.7 = (s16[272,1024]{1,0:T(8,128)(2,1)S(1)}, s16[272,1024]{1,0:T(8,128)(2,1)}, u32[]{:S(2)}, u32[]{:S(2)}) collective-permute-start(s16[272,1024]{1,0:T(8,128)(2,1)S(1)} %get-tuple-element.33.a_ref), channel_id=1, source_target_pairs={{0,8},{24,16},{1,9},{25,17},{2,10},{26,18},{3,11},{27,19},{4,12},{... | collective-permute-start | bytes 1671176 | tf_op jit(solution)/shard_map/ppermute | solution.py:211
  112.8 26.8 %collective-permute-start.9 = (s16[272,1024]{1,0:T(8,128)(2,1)}, s16[272,1024]{1,0:T(8,128)(2,1)}, u32[]{:S(2)}, u32[]{:S(2)}) collective-permute-start(s16[272,1024]{1,0:T(8,128)(2,1)} %add.15), channel_id=1, source_target_pairs={{8,16},{16,8},{9,17},{17,9},{10,18},{18,10},{11,19},{19,11},{12,20... | collective-permute-start | bytes 1671176 | tf_op jit(solution)/shard_map/ppermute | solution.py:214
  115.2 40.5 %copy-start.1 = (bf16[512,2048]{1,0:T(8,128)(2,1)S(1)}, bf16[512,2048]{1,0:T(8,128)(2,1)}, u32[]{:S(2)}) copy-start(bf16[512,2048]{1,0:T(8,128)(2,1)} %all-gather.2.cloned.1.call-done.far_ref.near_ref) | copy-start | bytes 6291460
  124.8 23.1 %collective-permute-start.10 = (s16[272,1024]{1,0:T(8,128)(2,1)S(1)}, s16[272,1024]{1,0:T(8,128)(2,1)S(1)}, u32[]{:S(2)}, u32[]{:S(2)}) collective-permute-start(s16[272,1024]{1,0:T(8,128)(2,1)S(1)} %get-tuple-element.36.a_ref), channel_id=1, source_target_pairs={{0,8},{24,16},{1,9},{25,17},{2,10},{26,18},{3,11},{27,19},{4,12},{... | collective-permute-start | bytes 1671176 | tf_op jit(solution)/shard_map/ppermute | solution.py:211
  129.2 18.7 %collective-permute-start.12 = (s16[272,1024]{1,0:T(8,128)(2,1)S(1)}, s16[272,1024]{1,0:T(8,128)(2,1)S(1)}, u32[]{:S(2)}, u32[]{:S(2)}) collective-permute-start(s16[272,1024]{1,0:T(8,128)(2,1)S(1)} %add.16), channel_id=1, source_target_pairs={{8,16},{16,8},{9,17},{17,9},{10,18},{18,10},{11,19},{19,11},{12,20... | collective-permute-start | bytes 1671176 | tf_op jit(solution)/shard_map/ppermute | solution.py:214
  132.1 1.1 copy-start.4
  133.1 1.1 copy-start.6
  138.8 0.8 copy-start.11
  141.5 6.4 %copy-start.7 = (bf16[256,1024]{1,0:T(8,128)(2,1)}, bf16[256,1024]{1,0:T(8,128)(2,1)S(1)}, u32[]{:S(2)}) copy-start(bf16[256,1024]{1,0:T(8,128)(2,1)S(1)} %get-tuple-element.40) | copy-start | bytes 1572868
  147.9 20.8 %copy-start.8 = (bf16[256,1024]{1,0:T(8,128)(2,1)S(1)}, bf16[256,1024]{1,0:T(8,128)(2,1)}, u32[]{:S(2)}) copy-start(bf16[256,1024]{1,0:T(8,128)(2,1)} %copy-done.7) | copy-start | bytes 1572868
  149.0 0.8 copy-start.9
  149.8 41.3 %copy-start.10 = (bf16[256,1024]{1,0:T(8,128)(2,1)S(1)}, bf16[256,1024]{1,0:T(8,128)(2,1)}, u32[]{:S(2)}) copy-start(bf16[256,1024]{1,0:T(8,128)(2,1)} %copy-done.9) | copy-start | bytes 1572868
  149.8 1.0 copy-start.14
  151.7 17.0 %collective-permute-start.13 = (bf16[128,2048]{1,0:T(8,128)(2,1)}, bf16[128,2048]{1,0:T(8,128)(2,1)}, u32[]{:S(2)}, u32[]{:S(2)}) collective-permute-start(bf16[128,2048]{1,0:T(8,128)(2,1)} %constant_dynamic-slice_fusion), channel_id=1, source_target_pairs={{8,0},{16,24},{9,1},{17,25},{10,2},{18,26},{11,3},{19,27},{12,4},{... | collective-permute-start | bytes 1572872 | tf_op jit(solution)/shard_map/ppermute | solution.py:259
  152.9 18.6 %collective-permute-start.24 = (bf16[256,1024]{1,0:T(8,128)(2,1)}, bf16[256,1024]{1,0:T(8,128)(2,1)}, u32[]{:S(2)}, u32[]{:S(2)}) collective-permute-start(bf16[256,1024]{1,0:T(8,128)(2,1)} %get-tuple-element.42), channel_id=1, source_target_pairs={{8,16},{16,8},{9,17},{17,9},{10,18},{18,10},{11,19},{19,11},{12,20... | collective-permute-start | bytes 1572872 | tf_op jit(solution)/shard_map/ppermute | solution.py:214
  154.4 25.5 %collective-permute-start.23 = (bf16[256,1024]{1,0:T(8,128)(2,1)}, bf16[256,1024]{1,0:T(8,128)(2,1)}, u32[]{:S(2)}, u32[]{:S(2)}) collective-permute-start(bf16[256,1024]{1,0:T(8,128)(2,1)} %get-tuple-element.42), channel_id=1, source_target_pairs={{8,0},{16,24},{9,1},{17,25},{10,2},{18,26},{11,3},{19,27},{12,4},{... | collective-permute-start | bytes 1572872 | tf_op jit(solution)/shard_map/ppermute | solution.py:208
  158.2 66.6 %copy-start.2 = (bf16[512,2048]{0,1:T(8,128)(2,1)S(1)}, bf16[512,2048]{0,1:T(8,128)(2,1)}, u32[]{:S(2)}) copy-start(bf16[512,2048]{0,1:T(8,128)(2,1)} %copy.23) | copy-start | bytes 6291460
  158.2 34.2 %collective-permute-start.21 = (bf16[256,1024]{1,0:T(8,128)(2,1)}, bf16[256,1024]{1,0:T(8,128)(2,1)S(1)}, u32[]{:S(2)}, u32[]{:S(2)}) collective-permute-start(bf16[256,1024]{1,0:T(8,128)(2,1)} %copy-done.11), channel_id=1, source_target_pairs={{8,16},{16,8},{9,17},{17,9},{10,18},{18,10},{11,19},{19,11},{12,20... | collective-permute-start | bytes 1572872 | tf_op jit(solution)/shard_map/ppermute | solution.py:214
  159.0 32.0 %collective-permute-start.20 = (bf16[256,1024]{1,0:T(8,128)(2,1)}, bf16[256,1024]{1,0:T(8,128)(2,1)S(1)}, u32[]{:S(2)}, u32[]{:S(2)}) collective-permute-start(bf16[256,1024]{1,0:T(8,128)(2,1)} %copy-done.11), channel_id=1, source_target_pairs={{8,0},{16,24},{9,1},{17,25},{10,2},{18,26},{11,3},{19,27},{12,4},{... | collective-permute-start | bytes 1572872 | tf_op jit(solution)/shard_map/ppermute | solution.py:208
  168.7 25.1 %collective-permute-start.18 = (bf16[256,1024]{1,0:T(8,128)(2,1)S(1)}, bf16[256,1024]{1,0:T(8,128)(2,1)S(1)}, u32[]{:S(2)}, u32[]{:S(2)}) collective-permute-start(bf16[256,1024]{1,0:T(8,128)(2,1)S(1)} %copy-done.8), channel_id=1, source_target_pairs={{8,16},{16,8},{9,17},{17,9},{10,18},{18,10},{11,19},{19,11},{12,20... | collective-permute-start | bytes 1572872 | tf_op jit(solution)/shard_map/ppermute | solution.py:214
  171.5 30.8 %collective-permute-start.17 = (bf16[256,1024]{1,0:T(8,128)(2,1)S(1)}, bf16[256,1024]{1,0:T(8,128)(2,1)S(1)}, u32[]{:S(2)}, u32[]{:S(2)}) collective-permute-start(bf16[256,1024]{1,0:T(8,128)(2,1)S(1)} %copy-done.8), channel_id=1, source_target_pairs={{8,0},{16,24},{9,1},{17,25},{10,2},{18,26},{11,3},{19,27},{12,4},{... | collective-permute-start | bytes 1572872 | tf_op jit(solution)/shard_map/ppermute | solution.py:208
  179.9 23.7 %collective-permute-start.15 = (bf16[256,1024]{1,0:T(8,128)(2,1)}, bf16[256,1024]{1,0:T(8,128)(2,1)S(1)}, u32[]{:S(2)}, u32[]{:S(2)}) collective-permute-start(bf16[256,1024]{1,0:T(8,128)(2,1)} %copy-done.9), channel_id=1, source_target_pairs={{8,16},{16,8},{9,17},{17,9},{10,18},{18,10},{11,19},{19,11},{12,20... | collective-permute-start | bytes 1572872 | tf_op jit(solution)/shard_map/ppermute | solution.py:214
  191.1 22.5 %collective-permute-start.14 = (bf16[256,1024]{1,0:T(8,128)(2,1)S(1)}, bf16[256,1024]{1,0:T(8,128)(2,1)S(1)}, u32[]{:S(2)}, u32[]{:S(2)}) collective-permute-start(bf16[256,1024]{1,0:T(8,128)(2,1)S(1)} %copy-done.10), channel_id=1, source_target_pairs={{8,0},{16,24},{9,1},{17,25},{10,2},{18,26},{11,3},{19,27},{12,4},{... | collective-permute-start | bytes 1572872 | tf_op jit(solution)/shard_map/ppermute | solution.py:208
  192.5 32.3 %collective-permute-start.25 = (bf16[256,1024]{1,0:T(8,128)(2,1)}, bf16[256,1024]{1,0:T(8,128)(2,1)S(1)}, u32[]{:S(2)}, u32[]{:S(2)}) collective-permute-start(bf16[256,1024]{1,0:T(8,128)(2,1)} %collective-permute-done.24), channel_id=1, source_target_pairs={{8,0},{16,24},{9,1},{17,25},{10,2},{18,26},{11,3},{19,27},{12,4},{... | collective-permute-start | bytes 1572872 | tf_op jit(solution)/shard_map/ppermute | solution.py:208
  193.8 42.2 %collective-permute-start.22 = (bf16[256,1024]{1,0:T(8,128)(2,1)S(1)}, bf16[256,1024]{1,0:T(8,128)(2,1)S(1)}, u32[]{:S(2)}, u32[]{:S(2)}) collective-permute-start(bf16[256,1024]{1,0:T(8,128)(2,1)S(1)} %collective-permute-done.21), channel_id=1, source_target_pairs={{8,0},{16,24},{9,1},{17,25},{10,2},{18,26},{11,3},{19,27},{12,4},{... | collective-permute-start | bytes 1572872 | tf_op jit(solution)/shard_map/ppermute | solution.py:208
  202.3 44.9 %collective-permute-start.19 = (bf16[256,1024]{1,0:T(8,128)(2,1)S(1)}, bf16[256,1024]{1,0:T(8,128)(2,1)S(1)}, u32[]{:S(2)}, u32[]{:S(2)}) collective-permute-start(bf16[256,1024]{1,0:T(8,128)(2,1)S(1)} %collective-permute-done.18), channel_id=1, source_target_pairs={{8,0},{16,24},{9,1},{17,25},{10,2},{18,26},{11,3},{19,27},{12,4},{... | collective-permute-start | bytes 1572872 | tf_op jit(solution)/shard_map/ppermute | solution.py:208
  203.6 53.5 %collective-permute-start.16 = (bf16[256,1024]{1,0:T(8,128)(2,1)S(1)}, bf16[256,1024]{1,0:T(8,128)(2,1)S(1)}, u32[]{:S(2)}, u32[]{:S(2)}) collective-permute-start(bf16[256,1024]{1,0:T(8,128)(2,1)S(1)} %collective-permute-done.15), channel_id=1, source_target_pairs={{8,0},{16,24},{9,1},{17,25},{10,2},{18,26},{11,3},{19,27},{12,4},{... | collective-permute-start | bytes 1572872 | tf_op jit(solution)/shard_map/ppermute | solution.py:208
Sparse Core Ops, SparseCore 0:
  9.9 30.5 all-gather.1

commit v2 on v0

v2 whole, which is shorter than its diff:
```python
import functools

import jax
import jax.numpy as jnp
from jax import lax
from jax.experimental import pallas as pl
from jax.experimental.pallas import tpu as pltpu
from jax.sharding import PartitionSpec as P

BLOCK = 128
GROUPS = 16
AHEAD = 6
VMEM_LIMIT = 48 * 1024 * 1024


def params():
    return pltpu.CompilerParams(vmem_limit_bytes=VMEM_LIMIT)


def cost():
    return pl.CostEstimate(flops=1000, bytes_accessed=1000, transcendentals=0)


def chunk_widths(local):
    units = local // BLOCK
    if units < 4 or units % 2:
        return [BLOCK] * units
    return [2 * BLOCK] * (units // 2 - 1) + [BLOCK] * 2


def put(ref, value):
    rows, cols = value.shape
    grouped = value.reshape(GROUPS, rows // GROUPS, cols)
    top = jnp.max(jnp.abs(grouped), axis=1)
    power = jnp.floor(jnp.log2(jnp.maximum(top, 1e-30))) + 1.0
    codes = jnp.round(grouped * jnp.exp2(15.0 - power)[:, None, :])
    codes = jnp.clip(codes, -32767.0, 32767.0).reshape(rows, cols)
    ref[0:rows, :] = codes.astype(jnp.int32).astype(jnp.int16)
    ref[rows : rows + GROUPS, :] = power.astype(jnp.int32).astype(jnp.int16)


def scales(ref):
    rows = ref.shape[0] - GROUPS
    return jnp.exp2(ref[rows : rows + GROUPS, :].astype(jnp.int32).astype(jnp.float32) - 15.0)


def get(ref):
    rows = ref.shape[0] - GROUPS
    cols = ref.shape[1]
    codes = ref[0:rows, :].astype(jnp.int32).astype(jnp.float32)
    grouped = codes.reshape(GROUPS, rows // GROUPS, cols) * scales(ref)[:, None, :]
    return grouped.reshape(rows, cols)


def forward_kernel(place_ref, mask_ref, tokens_ref, gate_ref, up_ref, out_ref, total, held, *, first):
    step = pl.program_id(0)
    depth, width = gate_ref.shape
    for r in range(depth // BLOCK):
        rows = slice(r * BLOCK, (r + 1) * BLOCK)
        for q in range(width // BLOCK):
            cols = slice(q * BLOCK, (q + 1) * BLOCK)
            keep = mask_ref[step * (depth // BLOCK) + r, first + q] != 0
            gate = gate_ref[rows, cols]
            up = up_ref[rows, cols]
            held[rows, cols] = jnp.where(keep, gate, jnp.zeros_like(gate))
            held[rows, width + q * BLOCK : width + (q + 1) * BLOCK] = jnp.where(keep, up, jnp.zeros_like(up))
    part = jnp.dot(tokens_ref[...], held[...], preferred_element_type=jnp.float32)

    @pl.when(step == 0)
    def _():
        total[...] = part

    @pl.when(step > 0)
    def _():
        total[...] += part

    @pl.when(step == pl.num_programs(0) - 1)
    def _():
        put(out_ref, total[...])


def forward(place, mask, tokens, gate_weight, up_weight, start, width):
    count, depth = tokens.shape
    steps = max(1, depth // 512)
    deep = depth // steps
    weight = pl.BlockSpec((deep, width), lambda k, place, mask: (k, start // width))
    return pl.pallas_call(
        functools.partial(forward_kernel, first=start // BLOCK),
        grid_spec=pltpu.PrefetchScalarGridSpec(
            num_scalar_prefetch=2,
            grid=(steps,),
            in_specs=[pl.BlockSpec((count, deep), lambda k, place, mask: (0, k)), weight, weight],
            out_specs=pl.BlockSpec((count + GROUPS, 2 * width), lambda k, place, mask: (0, 0)),
            scratch_shapes=[
                pltpu.VMEM((count, 2 * width), jnp.float32),
                pltpu.VMEM((deep, 2 * width), jnp.bfloat16),
            ],
        ),
        out_shape=jax.ShapeDtypeStruct((count + GROUPS, 2 * width), jnp.int16),
        compiler_params=params(),
        cost_estimate=cost(),
        name="forward",
    )(place, mask, tokens, gate_weight, up_weight)


def add_kernel(place_ref, a_ref, b_ref, out_ref):
    put(out_ref, get(a_ref) + get(b_ref))


def add(place, a, b):
    spec = pl.BlockSpec(a.shape, lambda i, place: (0, 0))
    return pl.pallas_call(
        add_kernel,
        grid_spec=pltpu.PrefetchScalarGridSpec(
            num_scalar_prefetch=1, grid=(1,), in_specs=[spec, spec], out_specs=spec
        ),
        out_shape=jax.ShapeDtypeStruct(a.shape, a.dtype),
        compiler_params=params(),
        cost_estimate=cost(),
        name="add",
    )(place, a, b)


def turn_kernel(place_ref, value_ref, out_ref):
    out_ref[...] = value_ref[...].T


def turn(place, value):
    rows, cols = value.shape
    deep = min(512, cols)
    return pl.pallas_call(
        turn_kernel,
        grid_spec=pltpu.PrefetchScalarGridSpec(
            num_scalar_prefetch=1,
            grid=(cols // deep,),
            in_specs=[pl.BlockSpec((rows, deep), lambda i, place: (0, i))],
            out_specs=pl.BlockSpec((deep, rows), lambda i, place: (i, 0)),
        ),
        out_shape=jax.ShapeDtypeStruct((cols, rows), value.dtype),
        compiler_params=params(),
        cost_estimate=cost(),
        name="turn",
    )(place, value)


def weights_kernel(place_ref, mask_ref, turned_ref, back_ref, *rest, first, terms, devices):
    coded = rest[:terms]
    hidden_ref, gate_ref, up_ref, deltas, hidden = rest[-5:]
    step = pl.program_id(0)
    depth, width = gate_ref.shape
    count = deltas.shape[0]
    share = count // devices
    col, row = place_ref[0], place_ref[1]

    @pl.when(step == 0)
    def _():
        scale = [scales(ref) for ref in coded]
        size = min(share, count // GROUPS)
        for at in range(0, count, size):
            rows = slice(at, at + size)
            group = at // (count // GROUPS)
            both = sum(
                ref[rows, :].astype(jnp.int32).astype(jnp.float32) * s[group : group + 1, :]
                for ref, s in zip(coded, scale)
            )
            gate, up = both[:, :width], both[:, width:]
            slot = at // share
            other = (slot % (devices // 2)) * 2 + slot // (devices // 2)
            start = pl.multiple_of(jnp.bitwise_xor(col, other) * share + at % share, size)
            back = back_ref[pl.ds(start, size), :].astype(jnp.float32)
            sig = jax.nn.sigmoid(gate)
            silu = gate * sig
            hidden[rows, :] = (silu * up).astype(jnp.bfloat16)
            deltas[rows, :width] = (back * up * sig * (1.0 + gate * (1.0 - sig))).astype(jnp.bfloat16)
            deltas[rows, width:] = (back * silu).astype(jnp.bfloat16)
        owned = hidden_ref.shape[0]
        for at in range(0, owned, share):
            other = jnp.bitwise_xor(col, row * (owned // share) + at // share)
            slot = (other % 2) * (devices // 2) + other // 2
            hidden_ref[at : at + share, :] = hidden[pl.ds(pl.multiple_of(slot * share, share), share), :]

    total = jnp.dot(turned_ref[...], deltas[...], preferred_element_type=jnp.float32)
    for r in range(depth // BLOCK):
        rows = slice(r * BLOCK, (r + 1) * BLOCK)
        for q in range(width // BLOCK):
            cols = slice(q * BLOCK, (q + 1) * BLOCK)
            keep = mask_ref[step * (depth // BLOCK) + r, first + q].astype(jnp.float32)
            gate_ref[rows, cols] = total[rows, cols] * keep
            up_ref[rows, cols] = total[rows, width + q * BLOCK : width + (q + 1) * BLOCK] * keep


def weight_grads(place, mask, turned, back, coded, previous, shapes, start, width, devices):
    depth, count = turned.shape
    owned = shapes[0].shape[0]
    steps = max(1, depth // 512)
    deep = depth // steps
    message = pl.BlockSpec((count + GROUPS, 2 * width), lambda m, place, mask: (0, 0))
    out = pl.BlockSpec((deep, width), lambda m, place, mask: (m, start // width))
    return pl.pallas_call(
        functools.partial(weights_kernel, first=start // BLOCK, terms=len(coded), devices=devices),
        grid_spec=pltpu.PrefetchScalarGridSpec(
            num_scalar_prefetch=2,
            grid=(steps,),
            in_specs=[
                pl.BlockSpec((deep, count), lambda m, place, mask: (m, 0)),
                pl.BlockSpec((count, width), lambda m, place, mask: (0, start // width)),
            ]
            + [message] * len(coded)
            + [pl.BlockSpec(memory_space=pl.ANY)] * len(previous),
            out_specs=[pl.BlockSpec((owned, width), lambda m, place, mask: (0, start // width)), out, out],
            scratch_shapes=[
                pltpu.VMEM((count, 2 * width), jnp.bfloat16),
                pltpu.VMEM((count, width), jnp.bfloat16),
            ],
        ),
        out_shape=shapes,
        input_output_aliases={4 + len(coded) + i: i for i in range(len(previous))},
        compiler_params=params(),
        cost_estimate=cost(),
        name="weight_grads",
    )(place, mask, turned, back, *coded, *previous)


def tie(value, *others):
    return lax.optimization_barrier((value, *others))[0]


def pick(condition, a, b):
    return lax.select(jnp.broadcast_to(condition, a.shape), a, b)


def gather_tokens(tokens, devices):
    pieces = [tokens]
    for other in range(2, devices, 2):
        pieces.append(lax.ppermute(tokens, "col", [(i, i ^ other) for i in range(devices)]))
    mine = jnp.concatenate(pieces, axis=0)
    return jnp.concatenate([mine, lax.ppermute(mine, "col", [(i, i ^ 1) for i in range(devices)])], axis=0)


def on_device(tokens, gate_weight, up_weight, block_mask, hidden_grad, *, ring, devices):
    me = lax.axis_index("row")
    place = jnp.stack([lax.axis_index("col"), me]).astype(jnp.int32)
    depth, local = gate_weight.shape
    left, right = ring // 2 - 1, ring // 2
    reach = ring // 2 - 1
    distance = jnp.where(me >= right, me - right, left - me)
    shapes = [
        jax.ShapeDtypeStruct(hidden_grad.shape, jnp.bfloat16),
        jax.ShapeDtypeStruct((depth, local), jnp.float32),
        jax.ShapeDtypeStruct((depth, local), jnp.float32),
    ]

    def outward(value, hop):
        return lax.ppermute(value, "row", [(left - hop, left - hop - 1), (right + hop, right + hop + 1)])

    def inward(value, hop):
        return lax.ppermute(value, "row", [(left - hop - 1, left - hop), (right + hop + 1, right + hop)])

    def swap(value):
        return lax.ppermute(value, "row", [(left, right), (right, left)])

    back = lax.all_gather(hidden_grad, "row", axis=0, tiled=True)
    gathered = gather_tokens(tokens, devices)

    widths = chunk_widths(local)
    starts = [sum(widths[:c]) for c in range(len(widths))]
    chunks = len(widths)
    own, came, sums, across, terms = [], [], [], [], []
    outs = ()
    turned = None

    def ordered(kernel, *args):
        nonlocal place
        out = kernel(place, *args)
        place = tie(place, out[0] if isinstance(out, (list, tuple)) else out)
        return out

    def send_in(c):
        value = own[c]
        if reach:
            came.append(inward(value if c < 2 else tie(value, came[c - 2]), reach - 1))

    def run_forward(c):
        own.append(ordered(forward, block_mask, gathered, gate_weight, up_weight, starts[c], widths[c]))
        if c < 2:
            send_in(c)

    def run_in(c):
        total = own[c]
        for hop in reversed(range(reach)):
            arrived = came[c] if hop == reach - 1 else inward(total, hop)
            if hop == reach - 1 and c + 2 < chunks:
                send_in(c + 2)
            new = ordered(add, own[c], arrived)
            total = new if reach == 1 else pick(distance == hop, new, total)
        sums.append(total)
        across.append(swap(total))

    def run_out(c):
        coming = across[c]
        parts = [sums[c], coming]
        for hop in range(reach):
            arrived = outward(ordered(add, own[c], coming), hop)
            if reach == 1:
                parts.append(arrived)
            else:
                coming = pick(distance == hop + 1, arrived, coming)
                parts[1] = coming
        terms.append(parts)

    ahead = min(AHEAD, chunks)
    for c in range(min(ahead, chunks)):
        run_forward(c)
    turned = ordered(turn, gathered)
    for c in range(chunks + 2):
        if c < chunks:
            run_in(c)
        if 0 <= c - 1 < chunks:
            run_out(c - 1)
        if c + ahead < chunks:
            run_forward(c + ahead)
        if c >= 2:
            d = c - 2
            outs = ordered(
                weight_grads, block_mask, turned, back, terms[d], outs, shapes, starts[d], widths[d], devices
            )
    return tuple(outs)


def solution(mesh):
    placed = (P("col", "row"), P("row", "col"), P("row", "col"), P("row", "col"), P("row", "col"))
    return jax.shard_map(
        functools.partial(on_device, ring=mesh.shape["row"], devices=mesh.shape["col"]),
        mesh=mesh,
        in_specs=placed,
        out_specs=(P("row", "col"), P("row", "col"), P("row", "col")),
        check_vma=False,
    )
```

time: 470 us -> 228 us (0.49)
  waiting for transfers between devices: 263 us -> 22.4 us
  Pallas kernels: 0 us -> 115 us
  local copies, waits for them, and re-layouts: 105 us -> 5.77 us
  starting transfers between devices: 6.56 us -> 67.2 us
  other arithmetic: 42.6 us -> 1.12 us
  matrix products: 36.4 us -> 0 us
    all_to_all x1 -> x0, waiting for transfers between devices: 183 us -> none  [on_device(): lax.all_to_all(terms.reshape(1, terms.shape[0], terms.shape[1]), 'row', s...]
    pallas_call x0 -> x37, Pallas kernels: none -> 115 us  [the longest x9 45 us: forward(): pl.pallas_call(functools.partial(forward_kernel, first=start // BLOCK), g...]
    all_gather x2 -> x1, waiting for transfers between devices: 78.9 us -> 0.01 us  [on_device(): back = lax.all_gather(hidden_grad, 'row', axis=0, tiled=True)]
    unnamed x15 -> x40, local copies, waits for them, and re-layouts: 83.7 us -> 5.7 us
    ppermute x0 -> x31, starting transfers between devices: none -> 67.2 us  [the longest x9 43.6 us: inward(): lax.ppermute(value, 'row', [(left - hop - 1, left - hop), (right + hop +...]
    dot_general x2 -> x0, matrix products: 36.4 us -> none  [the longest x1 18.5 us: on_device(): terms = jnp.dot(gathered, stacked, preferred_element_type=jnp.float32)]
    mul x2 -> x0, other arithmetic: 35 us -> none  [the longest x1 24.4 us: on_device(): return (hidden, total[:, :width] * keep_wide, total[:, width:] * keep_wide)]
    ppermute x0 -> x31, waiting for transfers between devices: none -> 22.4 us  [the longest x3 12 us: gather_tokens(): lax.ppermute(tokens, 'col', [(i, i ^ other) for i in range(devices)])]
  transfers between devices with their start and end apart: 3 -> 32, of which waited for: 2 -> 8; matrix products, arithmetic and copies ran while one was open for 8% -> 1% of each run, Pallas kernels for 0% -> 49%
where the time goes in v2:
time: 228 us; the launch traced here: 226 us
  Pallas kernels  115 us (50%)
  starting transfers between devices  67.2 us (29%)
  waiting for transfers between devices  22.4 us (10%)
  between operations  14.7 us (6%)
  local copies, waits for them, and re-layouts  5.77 us (3%)
    pallas_call x9, Pallas kernels, forward(): pl.pallas_call(functools.partial(forward_kernel, first=start // BLOCK), g...  45 us
    ppermute x9, starting transfers between devices, inward(): lax.ppermute(value, 'row', [(left - hop - 1, left - hop), (right + hop +...  43.6 us
    pallas_call x9, Pallas kernels, weight_grads(): pl.pallas_call(functools.partial(weights_kernel, first=start // BLOCK, te...  42.1 us
    pallas_call x18, Pallas kernels, add(): pl.pallas_call(add_kernel, grid_spec=pltpu.PrefetchScalarGridSpec(num_sca...  26.4 us
    ppermute x3, waiting for transfers between devices, gather_tokens(): lax.ppermute(tokens, 'col', [(i, i ^ other) for i in range(devices)])  12 us
    ppermute x9, starting transfers between devices, outward(): lax.ppermute(value, 'row', [(left - hop, left - hop - 1), (right + hop, r...  12 us
    ppermute x9, starting transfers between devices, swap(): return lax.ppermute(value, 'row', [(left, right), (right, left)])  7.01 us
    unnamed x40, local copies, waits for them, and re-layouts  5.7 us
  transfers between devices with their start and end apart: 32, of which 8 were waited for; matrix products, arithmetic and copies ran while one was open for 1% of the time, Pallas kernels for 49%

profile of v2, /device:TPU:0, one launch (start us, length us, event | category | flops | bytes accessed | tf_op | source)
XLA Modules:
  0.0 226.2 jit_solution(5086522073924241507)
XLA Ops:
  7.2 3.0 %collective-permute-start = (bf16[64,2048]{1,0:T(8,128)(2,1)}, bf16[64,2048]{1,0:T(8,128)(2,1)S(1)}, u32[]{:S(2)}, u32[]{:S(2)}) collective-permute-start(bf16[64,2048]{1,0:T(8,128)(2,1)} %param.5), channel_id=1, source_target_pairs={{0,2},{1,3},{2,0},{3,1},{4,6},{5,7},{6,4},{7,5},{8,10},{9,11},{10,... | collective-permute-start | bytes 786440 | tf_op jit(solution)/shard_map/ppermute | solution.py:235
  10.2 1.5 collective-permute-start.1
  11.8 5.8 %collective-permute-done = bf16[64,2048]{1,0:T(8,128)(2,1)S(1)} collective-permute-done((bf16[64,2048]{1,0:T(8,128)(2,1)}, bf16[64,2048]{1,0:T(8,128)(2,1)S(1)}, u32[]{:S(2)}, u32[]{:S(2)}) %collective-permute-start) | collective-permute-done | bytes 262176 | tf_op jit(solution)/shard_map/ppermute | solution.py:235
  17.6 6.2 %collective-permute-done.1 = bf16[64,2048]{1,0:T(8,128)(2,1)S(1)} collective-permute-done((bf16[64,2048]{1,0:T(8,128)(2,1)}, bf16[64,2048]{1,0:T(8,128)(2,1)S(1)}, u32[]{:S(2)}, u32[]{:S(2)}) %collective-permute-start.1) | collective-permute-done | bytes 262176 | tf_op jit(solution)/shard_map/ppermute | solution.py:235
  25.1 2.5 %collective-permute-done.3 = bf16[256,2048]{1,0:T(8,128)(2,1)S(1)} collective-permute-done((bf16[256,2048]{1,0:T(8,128)(2,1)S(1)}, bf16[256,2048]{1,0:T(8,128)(2,1)S(1)}, u32[]{:S(2)}, u32[]{:S(2)}) %collective-permute-start.3) | collective-permute-done | bytes 1048608 | tf_op jit(solution)/shard_map/ppermute | solution.py:237
  27.7 5.0 %forward.9.a_ref = s16[528,512]{1,0:T(8,128)(2,1)S(1)} custom-call(s32[2]{0:T(128)S(1)} %pad_add_fusion.place_ref, s32[16,16]{1,0:T(8,128)S(1)} %copy-done.4, bf16[512,2048]{1,0:T(8,128)(2,1)S(1)} %constant_dynamic-update-slice_fusion.tokens_ref.value_ref, bf16[2048,2048]{1,0:T(8,128)(2,1)} %gate_ref.17, bf16[2048,2048]{1,0:T(8,128)(2,1)} %up_ref.17), custom_call_target="tpu_custom_call" | custom-call | flops 1000 | bytes 1000 | tf_op jit(solution)/shard_map/forward/pallas_call | solution.py:87
  32.7 3.5 %collective-permute-start.4 = (s16[528,512]{1,0:T(8,128)(2,1)S(1)}, s16[528,512]{1,0:T(8,128)(2,1)S(1)}, u32[]{:S(2)}, u32[]{:S(2)}) collective-permute-start(s16[528,512]{1,0:T(8,128)(2,1)S(1)} %forward.9.a_ref), channel_id=1, source_target_pairs={{0,8},{24,16},{1,9},{25,17},{2,10},{26,18},{3,11},{27,19},{4,12},{... | collective-permute-start | bytes 1622024 | tf_op jit(solution)/shard_map/ppermute | solution.py:257
  36.2 5.0 %forward.10.a_ref = s16[528,512]{1,0:T(8,128)(2,1)S(1)} custom-call(s32[2]{0:T(128)S(1)} %pad_add_fusion.place_ref, s32[16,16]{1,0:T(8,128)S(1)} %copy-done.4, bf16[512,2048]{1,0:T(8,128)(2,1)S(1)} %constant_dynamic-update-slice_fusion.tokens_ref.value_ref, bf16[2048,2048]{1,0:T(8,128)(2,1)} %gate_ref.17, bf16[2048,2048]{1,0:T(8,128)(2,1)} %up_ref.17), custom_call_target="tpu_custom_call" | custom-call | flops 1000 | bytes 1000 | tf_op jit(solution)/shard_map/forward/pallas_call | solution.py:87
  41.3 1.3 collective-permute-start.5
  42.6 5.0 %forward.11.a_ref = s16[528,512]{1,0:T(8,128)(2,1)S(1)} custom-call(s32[2]{0:T(128)S(1)} %pad_add_fusion.place_ref, s32[16,16]{1,0:T(8,128)S(1)} %copy-done.4, bf16[512,2048]{1,0:T(8,128)(2,1)S(1)} %constant_dynamic-update-slice_fusion.tokens_ref.value_ref, bf16[2048,2048]{1,0:T(8,128)(2,1)} %gate_ref.17, bf16[2048,2048]{1,0:T(8,128)(2,1)} %up_ref.17), custom_call_target="tpu_custom_call" | custom-call | flops 1000 | bytes 1000 | tf_op jit(solution)/shard_map/forward/pallas_call | solution.py:87
  47.6 5.8 %forward.12.a_ref = s16[528,512]{1,0:T(8,128)(2,1)} custom-call(s32[2]{0:T(128)S(1)} %pad_add_fusion.place_ref, s32[16,16]{1,0:T(8,128)S(1)} %copy-done.4, bf16[512,2048]{1,0:T(8,128)(2,1)S(1)} %constant_dynamic-update-slice_fusion.tokens_ref.value_ref, bf16[2048,2048]{1,0:T(8,128)(2,1)} %gate_ref.17, bf16[2048,2048]{1,0:T(8,128)(2,1)} %up_ref.17), custom_call_target="tpu_custom_call" | custom-call | flops 1000 | bytes 1000 | tf_op jit(solution)/shard_map/forward/pallas_call | solution.py:87
  53.4 5.8 %forward.13.a_ref = s16[528,512]{1,0:T(8,128)(2,1)} custom-call(s32[2]{0:T(128)S(1)} %pad_add_fusion.place_ref, s32[16,16]{1,0:T(8,128)S(1)} %copy-done.4, bf16[512,2048]{1,0:T(8,128)(2,1)S(1)} %constant_dynamic-update-slice_fusion.tokens_ref.value_ref, bf16[2048,2048]{1,0:T(8,128)(2,1)} %gate_ref.17, bf16[2048,2048]{1,0:T(8,128)(2,1)} %up_ref.17), custom_call_target="tpu_custom_call" | custom-call | flops 1000 | bytes 1000 | tf_op jit(solution)/shard_map/forward/pallas_call | solution.py:87
  59.2 5.0 %forward.14.a_ref = s16[528,512]{1,0:T(8,128)(2,1)S(1)} custom-call(s32[2]{0:T(128)S(1)} %pad_add_fusion.place_ref, s32[16,16]{1,0:T(8,128)S(1)} %copy-done.4, bf16[512,2048]{1,0:T(8,128)(2,1)S(1)} %constant_dynamic-update-slice_fusion.tokens_ref.value_ref, bf16[2048,2048]{1,0:T(8,128)(2,1)} %gate_ref.17, bf16[2048,2048]{1,0:T(8,128)(2,1)} %up_ref.17), custom_call_target="tpu_custom_call" | custom-call | flops 1000 | bytes 1000 | tf_op jit(solution)/shard_map/forward/pallas_call | solution.py:87
  64.2 1.5 turn.1.turned_ref
  67.6 4.0 %collective-permute-start.7 = (s16[528,512]{1,0:T(8,128)(2,1)S(1)}, s16[528,512]{1,0:T(8,128)(2,1)S(1)}, u32[]{:S(2)}, u32[]{:S(2)}) collective-permute-start(s16[528,512]{1,0:T(8,128)(2,1)S(1)} %forward.11.a_ref), channel_id=1, source_target_pairs={{0,8},{24,16},{1,9},{25,17},{2,10},{26,18},{3,11},{27,19},{4,12},{... | collective-permute-start | bytes 1622024 | tf_op jit(solution)/shard_map/ppermute | solution.py:257
  71.7 5.0 %forward.15.a_ref = s16[528,512]{1,0:T(8,128)(2,1)S(1)} custom-call(s32[2]{0:T(128)S(1)} %pad_add_fusion.place_ref, s32[16,16]{1,0:T(8,128)S(1)} %copy-done.4, bf16[512,2048]{1,0:T(8,128)(2,1)S(1)} %constant_dynamic-update-slice_fusion.tokens_ref.value_ref, bf16[2048,2048]{1,0:T(8,128)(2,1)} %gate_ref.17, bf16[2048,2048]{1,0:T(8,128)(2,1)} %up_ref.17), custom_call_target="tpu_custom_call" | custom-call | flops 1000 | bytes 1000 | tf_op jit(solution)/shard_map/forward/pallas_call | solution.py:87
  76.7 2.5 %collective-permute-done.5.b_ref = s16[528,512]{1,0:T(8,128)(2,1)S(1)} collective-permute-done((s16[528,512]{1,0:T(8,128)(2,1)S(1)}, s16[528,512]{1,0:T(8,128)(2,1)S(1)}, u32[]{:S(2)}, u32[]{:S(2)}) %collective-permute-start.5) | collective-permute-done | bytes 540704 | tf_op jit(solution)/shard_map/ppermute | solution.py:257
  83.5 9.0 %collective-permute-start.10 = (s16[528,512]{1,0:T(8,128)(2,1)}, s16[528,512]{1,0:T(8,128)(2,1)}, u32[]{:S(2)}, u32[]{:S(2)}) collective-permute-start(s16[528,512]{1,0:T(8,128)(2,1)} %forward.12.a_ref), channel_id=1, source_target_pairs={{0,8},{24,16},{1,9},{25,17},{2,10},{26,18},{3,11},{27,19},{4,12},{... | collective-permute-start | bytes 1622024 | tf_op jit(solution)/shard_map/ppermute | solution.py:257
  92.4 4.1 %forward.16.a_ref = s16[528,256]{1,0:T(8,128)(2,1)S(1)} custom-call(s32[2]{0:T(128)S(1)} %pad_add_fusion.place_ref, s32[16,16]{1,0:T(8,128)S(1)} %copy-done.4, bf16[512,2048]{1,0:T(8,128)(2,1)S(1)} %constant_dynamic-update-slice_fusion.tokens_ref.value_ref, bf16[2048,2048]{1,0:T(8,128)(2,1)} %gate_ref.17, bf16[2048,2048]{1,0:T(8,128)(2,1)} %up_ref.17), custom_call_target="tpu_custom_call" | custom-call | flops 1000 | bytes 1000 | tf_op jit(solution)/shard_map/forward/pallas_call | solution.py:87
  96.6 1.9 add.23.rest_0_
  98.6 1.5 collective-permute-start.11
  100.1 2.0 add.24
  102.0 1.5 collective-permute-start.12
  103.5 4.1 %forward.17.a_ref = s16[528,256]{1,0:T(8,128)(2,1)S(1)} custom-call(s32[2]{0:T(128)S(1)} %pad_add_fusion.place_ref, s32[16,16]{1,0:T(8,128)S(1)} %copy-done.4, bf16[512,2048]{1,0:T(8,128)(2,1)S(1)} %constant_dynamic-update-slice_fusion.tokens_ref.value_ref, bf16[2048,2048]{1,0:T(8,128)(2,1)} %gate_ref.17, bf16[2048,2048]{1,0:T(8,128)(2,1)} %up_ref.17), custom_call_target="tpu_custom_call" | custom-call | flops 1000 | bytes 1000 | tf_op jit(solution)/shard_map/forward/pallas_call | solution.py:87
  107.6 6.0 %collective-permute-start.13 = (s16[528,512]{1,0:T(8,128)(2,1)}, s16[528,512]{1,0:T(8,128)(2,1)}, u32[]{:S(2)}, u32[]{:S(2)}) collective-permute-start(s16[528,512]{1,0:T(8,128)(2,1)} %forward.13.a_ref), channel_id=1, source_target_pairs={{0,8},{24,16},{1,9},{25,17},{2,10},{26,18},{3,11},{27,19},{4,12},{... | collective-permute-start | bytes 1622024 | tf_op jit(solution)/shard_map/ppermute | solution.py:257
  114.5 1.6 copy-done
  119.3 4.7 %weight_grads.9 = (bf16[128,2048]{1,0:T(8,128)(2,1)}, f32[2048,2048]{1,0:T(8,128)}, f32[2048,2048]{1,0:T(8,128)}) custom-call(s32[2]{0:T(128)S(1)} %pad_add_fusion.place_ref, s32[16,16]{1,0:T(8,128)S(1)} %copy-done.4, bf16[2048,512]{1,0:T(8,128)(2,1)S(1)} %turn.1.turned_ref, bf16[512,2048]{1,0:T(8,128)(2,1)S(1)} %copy-done, s16[528,512]{1,0:T(8,128)(2,1)S(1)} %copy-done.8, ...), custom_call_target="tpu_custom_call" | custom-call | flops 1000 | bytes 1000 | tf_op jit(solution)/shard_map/weight_grads/pallas_call | solution.py:199
  124.0 2.6 %add.25.rest_0_ = s16[528,512]{1,0:T(8,128)(2,1)S(1)} custom-call(s32[2]{0:T(128)S(1)} %pad_add_fusion.place_ref, s16[528,512]{1,0:T(8,128)(2,1)} %forward.12.a_ref, s16[528,512]{1,0:T(8,128)(2,1)} %collective-permute-done.10.b_ref), custom_call_target="tpu_custom_call" | custom-call | flops 1000 | bytes 1000 | tf_op jit(solution)/shard_map/add/pallas_call | solution.py:112
  127.3 2.2 add.26
  130.7 4.6 %collective-permute-start.16 = (s16[528,512]{1,0:T(8,128)(2,1)S(1)}, s16[528,512]{1,0:T(8,128)(2,1)S(1)}, u32[]{:S(2)}, u32[]{:S(2)}) collective-permute-start(s16[528,512]{1,0:T(8,128)(2,1)S(1)} %forward.14.a_ref), channel_id=1, source_target_pairs={{0,8},{24,16},{1,9},{25,17},{2,10},{26,18},{3,11},{27,19},{4,12},{... | collective-permute-start | bytes 1622024 | tf_op jit(solution)/shard_map/ppermute | solution.py:257
  135.4 5.7 %weight_grads.10 = (bf16[128,2048]{1,0:T(8,128)(2,1)}, f32[2048,2048]{1,0:T(8,128)}, f32[2048,2048]{1,0:T(8,128)}) custom-call(s32[2]{0:T(128)S(1)} %pad_add_fusion.place_ref, s32[16,16]{1,0:T(8,128)S(1)} %copy-done.4, bf16[2048,512]{1,0:T(8,128)(2,1)S(1)} %turn.1.turned_ref, ...), custom_call_target="tpu_custom_call", output_to_operand_aliasing={{0}: (7, {}), {1}: (8, {}), {2}: (9, {})} | custom-call | flops 1000 | bytes 1000 | tf_op jit(solution)/shard_map/weight_grads/pallas_call | solution.py:199
  141.1 2.3 %add.27.rest_0_ = s16[528,512]{1,0:T(8,128)(2,1)S(1)} custom-call(s32[2]{0:T(128)S(1)} %pad_add_fusion.place_ref, s16[528,512]{1,0:T(8,128)(2,1)} %forward.13.a_ref, s16[528,512]{1,0:T(8,128)(2,1)} %collective-permute-done.13.b_ref), custom_call_target="tpu_custom_call" | custom-call | flops 1000 | bytes 1000 | tf_op jit(solution)/shard_map/add/pallas_call | solution.py:112
  144.2 2.2 add.28
  147.6 4.6 %collective-permute-start.19 = (s16[528,512]{1,0:T(8,128)(2,1)S(1)}, s16[528,512]{1,0:T(8,128)(2,1)S(1)}, u32[]{:S(2)}, u32[]{:S(2)}) collective-permute-start(s16[528,512]{1,0:T(8,128)(2,1)S(1)} %forward.15.a_ref), channel_id=1, source_target_pairs={{0,8},{24,16},{1,9},{25,17},{2,10},{26,18},{3,11},{27,19},{4,12},{... | collective-permute-start | bytes 1622024 | tf_op jit(solution)/shard_map/ppermute | solution.py:257
  152.3 5.9 %weight_grads.11 = (bf16[128,2048]{1,0:T(8,128)(2,1)}, f32[2048,2048]{1,0:T(8,128)}, f32[2048,2048]{1,0:T(8,128)}) custom-call(s32[2]{0:T(128)S(1)} %pad_add_fusion.place_ref, s32[16,16]{1,0:T(8,128)S(1)} %copy-done.4, bf16[2048,512]{1,0:T(8,128)(2,1)S(1)} %turn.1.turned_ref, ...), custom_call_target="tpu_custom_call", output_to_operand_aliasing={{0}: (7, {}), {1}: (8, {}), {2}: (9, {})} | custom-call | flops 1000 | bytes 1000 | tf_op jit(solution)/shard_map/weight_grads/pallas_call | solution.py:199
  160.0 2.2 add.30
  162.1 1.3 collective-permute-start.21
  163.5 4.7 %weight_grads.12 = (bf16[128,2048]{1,0:T(8,128)(2,1)}, f32[2048,2048]{1,0:T(8,128)}, f32[2048,2048]{1,0:T(8,128)}) custom-call(s32[2]{0:T(128)S(1)} %pad_add_fusion.place_ref, s32[16,16]{1,0:T(8,128)S(1)} %copy-done.4, bf16[2048,512]{1,0:T(8,128)(2,1)S(1)} %turn.1.turned_ref, ...), custom_call_target="tpu_custom_call", output_to_operand_aliasing={{0}: (7, {}), {1}: (8, {}), {2}: (9, {})} | custom-call | flops 1000 | bytes 1000 | tf_op jit(solution)/shard_map/weight_grads/pallas_call | solution.py:199
  170.0 5.8 %collective-permute-start.22 = (s16[528,256]{1,0:T(8,128)(2,1)S(1)}, s16[528,256]{1,0:T(8,128)(2,1)S(1)}, u32[]{:S(2)}, u32[]{:S(2)}) collective-permute-start(s16[528,256]{1,0:T(8,128)(2,1)S(1)} %copy-done.6), channel_id=1, source_target_pairs={{0,8},{24,16},{1,9},{25,17},{2,10},{26,18},{3,11},{27,19},{4,12},{... | collective-permute-start | bytes 811016 | tf_op jit(solution)/shard_map/ppermute | solution.py:257
  176.9 1.5 collective-permute-start.24
  178.5 4.7 %weight_grads.13 = (bf16[128,2048]{1,0:T(8,128)(2,1)}, f32[2048,2048]{1,0:T(8,128)}, f32[2048,2048]{1,0:T(8,128)}) custom-call(s32[2]{0:T(128)S(1)} %pad_add_fusion.place_ref, s32[16,16]{1,0:T(8,128)S(1)} %copy-done.4, bf16[2048,512]{1,0:T(8,128)(2,1)S(1)} %turn.1.turned_ref, ...), custom_call_target="tpu_custom_call", output_to_operand_aliasing={{0}: (7, {}), {1}: (8, {}), {2}: (9, {})} | custom-call | flops 1000 | bytes 1000 | tf_op jit(solution)/shard_map/weight_grads/pallas_call | solution.py:199
  186.4 4.6 %collective-permute-start.25 = (s16[528,256]{1,0:T(8,128)(2,1)S(1)}, s16[528,256]{1,0:T(8,128)(2,1)S(1)}, u32[]{:S(2)}, u32[]{:S(2)}) collective-permute-start(s16[528,256]{1,0:T(8,128)(2,1)S(1)} %forward.17.a_ref), channel_id=1, source_target_pairs={{0,8},{24,16},{1,9},{25,17},{2,10},{26,18},{3,11},{27,19},{4,12},{... | collective-permute-start | bytes 811016 | tf_op jit(solution)/shard_map/ppermute | solution.py:257
  191.7 1.3 collective-permute-done.24.rest_2_
  193.1 4.7 %weight_grads.14 = (bf16[128,2048]{1,0:T(8,128)(2,1)}, f32[2048,2048]{1,0:T(8,128)}, f32[2048,2048]{1,0:T(8,128)}) custom-call(s32[2]{0:T(128)S(1)} %pad_add_fusion.place_ref, s32[16,16]{1,0:T(8,128)S(1)} %copy-done.4, bf16[2048,512]{1,0:T(8,128)(2,1)S(1)} %turn.1.turned_ref, ...), custom_call_target="tpu_custom_call", output_to_operand_aliasing={{0}: (7, {}), {1}: (8, {}), {2}: (9, {})} | custom-call | flops 1000 | bytes 1000 | tf_op jit(solution)/shard_map/weight_grads/pallas_call | solution.py:199
  201.9 4.7 %weight_grads.15 = (bf16[128,2048]{1,0:T(8,128)(2,1)}, f32[2048,2048]{1,0:T(8,128)}, f32[2048,2048]{1,0:T(8,128)}) custom-call(s32[2]{0:T(128)S(1)} %pad_add_fusion.place_ref, s32[16,16]{1,0:T(8,128)S(1)} %copy-done.4, bf16[2048,512]{1,0:T(8,128)(2,1)S(1)} %turn.1.turned_ref, ...), custom_call_target="tpu_custom_call", output_to_operand_aliasing={{0}: (7, {}), {1}: (8, {}), {2}: (9, {})} | custom-call | flops 1000 | bytes 1000 | tf_op jit(solution)/shard_map/weight_grads/pallas_call | solution.py:199
  209.4 3.6 %weight_grads.16 = (bf16[128,2048]{1,0:T(8,128)(2,1)}, f32[2048,2048]{1,0:T(8,128)}, f32[2048,2048]{1,0:T(8,128)}) custom-call(s32[2]{0:T(128)S(1)} %pad_add_fusion.place_ref, s32[16,16]{1,0:T(8,128)S(1)} %copy-done.4, bf16[2048,512]{1,0:T(8,128)(2,1)S(1)} %turn.1.turned_ref, ...), custom_call_target="tpu_custom_call", output_to_operand_aliasing={{0}: (7, {}), {1}: (8, {}), {2}: (9, {})} | custom-call | flops 1000 | bytes 1000 | tf_op jit(solution)/shard_map/weight_grads/pallas_call | solution.py:199
  213.0 2.8 %collective-permute-done.30.rest_2_ = s16[528,256]{1,0:T(8,128)(2,1)S(1)} collective-permute-done((s16[528,256]{1,0:T(8,128)(2,1)S(1)}, s16[528,256]{1,0:T(8,128)(2,1)S(1)}, u32[]{:S(2)}, u32[]{:S(2)}) %collective-permute-start.30) | collective-permute-done | bytes 270368 | tf_op jit(solution)/shard_map/ppermute | solution.py:254
  215.8 3.6 %weight_grads.17 = (bf16[128,2048]{1,0:T(8,128)(2,1)}, f32[2048,2048]{1,0:T(8,128)}, f32[2048,2048]{1,0:T(8,128)}) custom-call(s32[2]{0:T(128)S(1)} %pad_add_fusion.place_ref, s32[16,16]{1,0:T(8,128)S(1)} %copy-done.4, bf16[2048,512]{1,0:T(8,128)(2,1)S(1)} %turn.1.turned_ref, ...), custom_call_target="tpu_custom_call", output_to_operand_aliasing={{0}: (7, {}), {1}: (8, {}), {2}: (9, {})} | custom-call | flops 1000 | bytes 1000 | tf_op jit(solution)/shard_map/weight_grads/pallas_call | solution.py:199
  (97 shorter events, 31.1 us)
Async XLA Ops:
  7.2 17.9 %copy-start.17 = (bf16[64,2048]{1,0:T(8,128)(2,1)S(1)}, bf16[64,2048]{1,0:T(8,128)(2,1)}, u32[]{:S(2)}) copy-start(bf16[64,2048]{1,0:T(8,128)(2,1)} %param.5) | copy-start | bytes 786436
  7.2 107.4 %all-gather.2.cloned.1.call-start = ((), (), s32[]{:S(2)}) async-start(), calls=%async_computation | async-start | bytes 2621440 | tf_op jit(solution)/shard_map/all_gather | solution.py:262
  7.2 10.3 %collective-permute-start = (bf16[64,2048]{1,0:T(8,128)(2,1)}, bf16[64,2048]{1,0:T(8,128)(2,1)S(1)}, u32[]{:S(2)}, u32[]{:S(2)}) collective-permute-start(bf16[64,2048]{1,0:T(8,128)(2,1)} %param.5), channel_id=1, source_target_pairs={{0,2},{1,3},{2,0},{3,1},{4,6},{5,7},{6,4},{7,5},{8,10},{9,11},{10,... | collective-permute-start | bytes 786440 | tf_op jit(solution)/shard_map/ppermute | solution.py:235
  10.2 13.6 %collective-permute-start.1 = (bf16[64,2048]{1,0:T(8,128)(2,1)}, bf16[64,2048]{1,0:T(8,128)(2,1)S(1)}, u32[]{:S(2)}, u32[]{:S(2)}) collective-permute-start(bf16[64,2048]{1,0:T(8,128)(2,1)} %param.5), channel_id=1, source_target_pairs={{0,4},{1,5},{2,6},{3,7},{4,0},{5,1},{6,2},{7,3},{8,12},{9,13},{10,... | collective-permute-start | bytes 786440 | tf_op jit(solution)/shard_map/ppermute | solution.py:235
  11.7 12.1 %collective-permute-start.2 = (bf16[64,2048]{1,0:T(8,128)(2,1)}, bf16[64,2048]{1,0:T(8,128)(2,1)S(1)}, u32[]{:S(2)}, u32[]{:S(2)}) collective-permute-start(bf16[64,2048]{1,0:T(8,128)(2,1)} %param.5), channel_id=1, source_target_pairs={{0,6},{1,7},{2,4},{3,5},{4,2},{5,3},{6,0},{7,1},{8,14},{9,15},{10,... | collective-permute-start | bytes 786440 | tf_op jit(solution)/shard_map/ppermute | solution.py:235
  24.9 2.7 %collective-permute-start.3 = (bf16[256,2048]{1,0:T(8,128)(2,1)S(1)}, bf16[256,2048]{1,0:T(8,128)(2,1)S(1)}, u32[]{:S(2)}, u32[]{:S(2)}) collective-permute-start(bf16[256,2048]{1,0:T(8,128)(2,1)S(1)} %pad_maximum_fusion), channel_id=1, source_target_pairs={{0,1},{1,0},{2,3},{3,2},{4,5},{5,4},{6,7},{7,6},{8,9},{9,8},{10,11... | collective-permute-start | bytes 3145736 | tf_op jit(solution)/shard_map/ppermute | solution.py:237
  25.0 2.6 %copy-start.4 = (s32[16,16]{1,0:T(8,128)S(1)}, s32[16,16]{1,0:T(8,128)}, u32[]{:S(2)}) copy-start(s32[16,16]{1,0:T(8,128)} %mask_ref.35) | copy-start | bytes 3076
  32.7 33.0 %collective-permute-start.4 = (s16[528,512]{1,0:T(8,128)(2,1)S(1)}, s16[528,512]{1,0:T(8,128)(2,1)S(1)}, u32[]{:S(2)}, u32[]{:S(2)}) collective-permute-start(s16[528,512]{1,0:T(8,128)(2,1)S(1)} %forward.9.a_ref), channel_id=1, source_target_pairs={{0,8},{24,16},{1,9},{25,17},{2,10},{26,18},{3,11},{27,19},{4,12},{... | collective-permute-start | bytes 1622024 | tf_op jit(solution)/shard_map/ppermute | solution.py:257
  41.3 37.9 %collective-permute-start.5 = (s16[528,512]{1,0:T(8,128)(2,1)S(1)}, s16[528,512]{1,0:T(8,128)(2,1)S(1)}, u32[]{:S(2)}, u32[]{:S(2)}) collective-permute-start(s16[528,512]{1,0:T(8,128)(2,1)S(1)} %forward.10.a_ref), channel_id=1, source_target_pairs={{0,8},{24,16},{1,9},{25,17},{2,10},{26,18},{3,11},{27,19},{4,12},{... | collective-permute-start | bytes 1622024 | tf_op jit(solution)/shard_map/ppermute | solution.py:257
  47.6 49.0 %copy-start.2 = (s16[528,512]{1,0:T(8,128)(2,1)}, s16[528,512]{1,0:T(8,128)(2,1)S(1)}, u32[]{:S(2)}) copy-start(s16[528,512]{1,0:T(8,128)(2,1)S(1)} %forward.11.a_ref) | copy-start | bytes 1622020
  66.9 9.8 %copy-start.7 = (s16[528,512]{1,0:T(8,128)(2,1)}, s16[528,512]{1,0:T(8,128)(2,1)S(1)}, u32[]{:S(2)}) copy-start(s16[528,512]{1,0:T(8,128)(2,1)S(1)} %add.20.rest_0_) | copy-start | bytes 1622020
  66.9 14.1 %collective-permute-start.6 = (s16[528,512]{1,0:T(8,128)(2,1)S(1)}, s16[528,512]{1,0:T(8,128)(2,1)S(1)}, u32[]{:S(2)}, u32[]{:S(2)}) collective-permute-start(s16[528,512]{1,0:T(8,128)(2,1)S(1)} %add.20.rest_0_), channel_id=1, source_target_pairs={{8,16},{16,8},{9,17},{17,9},{10,18},{18,10},{11,19},{19,11},{12,20... | collective-permute-start | bytes 1622024 | tf_op jit(solution)/shard_map/ppermute | solution.py:260
  67.6 29.0 %collective-permute-start.7 = (s16[528,512]{1,0:T(8,128)(2,1)S(1)}, s16[528,512]{1,0:T(8,128)(2,1)S(1)}, u32[]{:S(2)}, u32[]{:S(2)}) collective-permute-start(s16[528,512]{1,0:T(8,128)(2,1)S(1)} %forward.11.a_ref), channel_id=1, source_target_pairs={{0,8},{24,16},{1,9},{25,17},{2,10},{26,18},{3,11},{27,19},{4,12},{... | collective-permute-start | bytes 1622024 | tf_op jit(solution)/shard_map/ppermute | solution.py:257
  80.3 16.3 %copy-start.11 = (s16[528,512]{1,0:T(8,128)(2,1)}, s16[528,512]{1,0:T(8,128)(2,1)S(1)}, u32[]{:S(2)}) copy-start(s16[528,512]{1,0:T(8,128)(2,1)S(1)} %add.21.rest_0_) | copy-start | bytes 1622020
  80.3 19.7 %collective-permute-start.8 = (s16[528,512]{1,0:T(8,128)(2,1)S(1)}, s16[528,512]{1,0:T(8,128)(2,1)S(1)}, u32[]{:S(2)}, u32[]{:S(2)}) collective-permute-start(s16[528,512]{1,0:T(8,128)(2,1)S(1)} %add.21.rest_0_), channel_id=1, source_target_pairs={{8,16},{16,8},{9,17},{17,9},{10,18},{18,10},{11,19},{19,11},{12,20... | collective-permute-start | bytes 1622024 | tf_op jit(solution)/shard_map/ppermute | solution.py:260
  81.1 15.6 %copy-start.9 = (s16[528,512]{1,0:T(8,128)(2,1)}, s16[528,512]{1,0:T(8,128)(2,1)S(1)}, u32[]{:S(2)}) copy-start(s16[528,512]{1,0:T(8,128)(2,1)S(1)} %collective-permute-done.6.b_ref.rest_1_) | copy-start | bytes 1622020
  82.2 31.5 %collective-permute-start.9 = (s16[528,512]{1,0:T(8,128)(2,1)S(1)}, s16[528,512]{1,0:T(8,128)(2,1)S(1)}, u32[]{:S(2)}, u32[]{:S(2)}) collective-permute-start(s16[528,512]{1,0:T(8,128)(2,1)S(1)} %add.22), channel_id=1, source_target_pairs={{8,0},{16,24},{9,1},{17,25},{10,2},{18,26},{11,3},{19,27},{12,4},{... | collective-permute-start | bytes 1622024 | tf_op jit(solution)/shard_map/ppermute | solution.py:254
  83.5 40.5 %collective-permute-start.10 = (s16[528,512]{1,0:T(8,128)(2,1)}, s16[528,512]{1,0:T(8,128)(2,1)}, u32[]{:S(2)}, u32[]{:S(2)}) collective-permute-start(s16[528,512]{1,0:T(8,128)(2,1)} %forward.12.a_ref), channel_id=1, source_target_pairs={{0,8},{24,16},{1,9},{25,17},{2,10},{26,18},{3,11},{27,19},{4,12},{... | collective-permute-start | bytes 1622024 | tf_op jit(solution)/shard_map/ppermute | solution.py:257
  96.6 11.0 %copy-start.5 = (s16[528,256]{1,0:T(8,128)(2,1)}, s16[528,256]{1,0:T(8,128)(2,1)S(1)}, u32[]{:S(2)}) copy-start(s16[528,256]{1,0:T(8,128)(2,1)S(1)} %forward.16.a_ref) | copy-start | bytes 811012
  98.6 28.7 %collective-permute-start.11 = (s16[528,512]{1,0:T(8,128)(2,1)}, s16[528,512]{1,0:T(8,128)(2,1)}, u32[]{:S(2)}, u32[]{:S(2)}) collective-permute-start(s16[528,512]{1,0:T(8,128)(2,1)} %add.23.rest_0_), channel_id=1, source_target_pairs={{8,16},{16,8},{9,17},{17,9},{10,18},{18,10},{11,19},{19,11},{12,20... | collective-permute-start | bytes 1622024 | tf_op jit(solution)/shard_map/ppermute | solution.py:260
  100.1 7.6 %copy-start.13 = (s16[528,512]{1,0:T(8,128)(2,1)}, s16[528,512]{1,0:T(8,128)(2,1)S(1)}, u32[]{:S(2)}) copy-start(s16[528,512]{1,0:T(8,128)(2,1)S(1)} %collective-permute-done.8.b_ref.rest_1_) | copy-start | bytes 1622020
  102.0 33.4 %collective-permute-start.12 = (s16[528,512]{1,0:T(8,128)(2,1)}, s16[528,512]{1,0:T(8,128)(2,1)}, u32[]{:S(2)}, u32[]{:S(2)}) collective-permute-start(s16[528,512]{1,0:T(8,128)(2,1)} %add.24), channel_id=1, source_target_pairs={{8,0},{16,24},{9,1},{17,25},{10,2},{18,26},{11,3},{19,27},{12,4},{... | collective-permute-start | bytes 1622024 | tf_op jit(solution)/shard_map/ppermute | solution.py:254
  107.6 33.5 %collective-permute-start.13 = (s16[528,512]{1,0:T(8,128)(2,1)}, s16[528,512]{1,0:T(8,128)(2,1)}, u32[]{:S(2)}, u32[]{:S(2)}) collective-permute-start(s16[528,512]{1,0:T(8,128)(2,1)} %forward.13.a_ref), channel_id=1, source_target_pairs={{0,8},{24,16},{1,9},{25,17},{2,10},{26,18},{3,11},{27,19},{4,12},{... | collective-permute-start | bytes 1622024 | tf_op jit(solution)/shard_map/ppermute | solution.py:257
  114.5 1.6 copy-start
  116.1 1.0 copy-start.8
  117.2 1.0 copy-start.10
  119.3 8.0 %copy-start.3 = (s16[528,512]{1,0:T(8,128)(2,1)S(1)}, s16[528,512]{1,0:T(8,128)(2,1)}, u32[]{:S(2)}) copy-start(s16[528,512]{1,0:T(8,128)(2,1)} %copy-done.2) | copy-start | bytes 1622020
  123.9 11.4 %copy-start.1 = (bf16[512,2048]{1,0:T(8,128)(2,1)S(1)}, bf16[512,2048]{1,0:T(8,128)(2,1)}, u32[]{:S(2)}) copy-start(bf16[512,2048]{1,0:T(8,128)(2,1)} %all-gather.2.cloned.1.call-done.back_ref) | copy-start | bytes 6291460
  123.9 11.4 %copy-start.12 = (s16[528,512]{1,0:T(8,128)(2,1)S(1)}, s16[528,512]{1,0:T(8,128)(2,1)}, u32[]{:S(2)}) copy-start(s16[528,512]{1,0:T(8,128)(2,1)} %copy-done.11) | copy-start | bytes 1622020
  123.9 11.4 %copy-start.14 = (s16[528,512]{1,0:T(8,128)(2,1)S(1)}, s16[528,512]{1,0:T(8,128)(2,1)}, u32[]{:S(2)}) copy-start(s16[528,512]{1,0:T(8,128)(2,1)} %copy-done.13) | copy-start | bytes 1622020
  126.6 17.6 %collective-permute-start.14 = (s16[528,512]{1,0:T(8,128)(2,1)S(1)}, s16[528,512]{1,0:T(8,128)(2,1)S(1)}, u32[]{:S(2)}, u32[]{:S(2)}) collective-permute-start(s16[528,512]{1,0:T(8,128)(2,1)S(1)} %add.25.rest_0_), channel_id=1, source_target_pairs={{8,16},{16,8},{9,17},{17,9},{10,18},{18,10},{11,19},{19,11},{12,20... | collective-permute-start | bytes 1622024 | tf_op jit(solution)/shard_map/ppermute | solution.py:260
  129.4 22.8 %collective-permute-start.15 = (s16[528,512]{1,0:T(8,128)(2,1)S(1)}, s16[528,512]{1,0:T(8,128)(2,1)S(1)}, u32[]{:S(2)}, u32[]{:S(2)}) collective-permute-start(s16[528,512]{1,0:T(8,128)(2,1)S(1)} %add.26), channel_id=1, source_target_pairs={{8,0},{16,24},{9,1},{17,25},{10,2},{18,26},{11,3},{19,27},{12,4},{... | collective-permute-start | bytes 1622024 | tf_op jit(solution)/shard_map/ppermute | solution.py:254
  130.7 27.4 %collective-permute-start.16 = (s16[528,512]{1,0:T(8,128)(2,1)S(1)}, s16[528,512]{1,0:T(8,128)(2,1)S(1)}, u32[]{:S(2)}, u32[]{:S(2)}) collective-permute-start(s16[528,512]{1,0:T(8,128)(2,1)S(1)} %forward.14.a_ref), channel_id=1, source_target_pairs={{0,8},{24,16},{1,9},{25,17},{2,10},{26,18},{3,11},{27,19},{4,12},{... | collective-permute-start | bytes 1622024 | tf_op jit(solution)/shard_map/ppermute | solution.py:257
  143.5 16.5 %collective-permute-start.17 = (s16[528,512]{1,0:T(8,128)(2,1)S(1)}, s16[528,512]{1,0:T(8,128)(2,1)S(1)}, u32[]{:S(2)}, u32[]{:S(2)}) collective-permute-start(s16[528,512]{1,0:T(8,128)(2,1)S(1)} %add.27.rest_0_), channel_id=1, source_target_pairs={{8,16},{16,8},{9,17},{17,9},{10,18},{18,10},{11,19},{19,11},{12,20... | collective-permute-start | bytes 1622024 | tf_op jit(solution)/shard_map/ppermute | solution.py:260
  146.3 17.1 %collective-permute-start.18 = (s16[528,512]{1,0:T(8,128)(2,1)S(1)}, s16[528,512]{1,0:T(8,128)(2,1)S(1)}, u32[]{:S(2)}, u32[]{:S(2)}) collective-permute-start(s16[528,512]{1,0:T(8,128)(2,1)S(1)} %add.28), channel_id=1, source_target_pairs={{8,0},{16,24},{9,1},{17,25},{10,2},{18,26},{11,3},{19,27},{12,4},{... | collective-permute-start | bytes 1622024 | tf_op jit(solution)/shard_map/ppermute | solution.py:254
  147.6 20.5 %collective-permute-start.19 = (s16[528,512]{1,0:T(8,128)(2,1)S(1)}, s16[528,512]{1,0:T(8,128)(2,1)S(1)}, u32[]{:S(2)}, u32[]{:S(2)}) collective-permute-start(s16[528,512]{1,0:T(8,128)(2,1)S(1)} %forward.15.a_ref), channel_id=1, source_target_pairs={{0,8},{24,16},{1,9},{25,17},{2,10},{26,18},{3,11},{27,19},{4,12},{... | collective-permute-start | bytes 1622024 | tf_op jit(solution)/shard_map/ppermute | solution.py:257
  159.3 16.5 %collective-permute-start.20 = (s16[528,512]{1,0:T(8,128)(2,1)S(1)}, s16[528,512]{1,0:T(8,128)(2,1)S(1)}, u32[]{:S(2)}, u32[]{:S(2)}) collective-permute-start(s16[528,512]{1,0:T(8,128)(2,1)S(1)} %add.29.rest_0_), channel_id=1, source_target_pairs={{8,16},{16,8},{9,17},{17,9},{10,18},{18,10},{11,19},{19,11},{12,20... | collective-permute-start | bytes 1622024 | tf_op jit(solution)/shard_map/ppermute | solution.py:260
  162.1 16.3 %collective-permute-start.21 = (s16[528,512]{1,0:T(8,128)(2,1)S(1)}, s16[528,512]{1,0:T(8,128)(2,1)S(1)}, u32[]{:S(2)}, u32[]{:S(2)}) collective-permute-start(s16[528,512]{1,0:T(8,128)(2,1)S(1)} %add.30), channel_id=1, source_target_pairs={{8,0},{16,24},{9,1},{17,25},{10,2},{18,26},{11,3},{19,27},{12,4},{... | collective-permute-start | bytes 1622024 | tf_op jit(solution)/shard_map/ppermute | solution.py:254
  163.5 6.5 %copy-start.6 = (s16[528,256]{1,0:T(8,128)(2,1)S(1)}, s16[528,256]{1,0:T(8,128)(2,1)}, u32[]{:S(2)}) copy-start(s16[528,256]{1,0:T(8,128)(2,1)} %copy-done.5) | copy-start | bytes 811012
  169.3 14.7 %collective-permute-start.23 = (s16[528,512]{1,0:T(8,128)(2,1)S(1)}, s16[528,512]{1,0:T(8,128)(2,1)S(1)}, u32[]{:S(2)}, u32[]{:S(2)}) collective-permute-start(s16[528,512]{1,0:T(8,128)(2,1)S(1)} %add.31.rest_0_), channel_id=1, source_target_pairs={{8,16},{16,8},{9,17},{17,9},{10,18},{18,10},{11,19},{19,11},{12,20... | collective-permute-start | bytes 1622024 | tf_op jit(solution)/shard_map/ppermute | solution.py:260
  170.0 13.2 %collective-permute-start.22 = (s16[528,256]{1,0:T(8,128)(2,1)S(1)}, s16[528,256]{1,0:T(8,128)(2,1)S(1)}, u32[]{:S(2)}, u32[]{:S(2)}) collective-permute-start(s16[528,256]{1,0:T(8,128)(2,1)S(1)} %copy-done.6), channel_id=1, source_target_pairs={{0,8},{24,16},{1,9},{25,17},{2,10},{26,18},{3,11},{27,19},{4,12},{... | collective-permute-start | bytes 811016 | tf_op jit(solution)/shard_map/ppermute | solution.py:257
  176.9 16.1 %collective-permute-start.24 = (s16[528,512]{1,0:T(8,128)(2,1)S(1)}, s16[528,512]{1,0:T(8,128)(2,1)S(1)}, u32[]{:S(2)}, u32[]{:S(2)}) collective-permute-start(s16[528,512]{1,0:T(8,128)(2,1)S(1)} %add.32), channel_id=1, source_target_pairs={{8,0},{16,24},{9,1},{17,25},{10,2},{18,26},{11,3},{19,27},{12,4},{... | collective-permute-start | bytes 1622024 | tf_op jit(solution)/shard_map/ppermute | solution.py:254
  185.1 16.8 %collective-permute-start.27 = (s16[528,512]{1,0:T(8,128)(2,1)S(1)}, s16[528,512]{1,0:T(8,128)(2,1)S(1)}, u32[]{:S(2)}, u32[]{:S(2)}) collective-permute-start(s16[528,512]{1,0:T(8,128)(2,1)S(1)} %add.34), channel_id=1, source_target_pairs={{8,0},{16,24},{9,1},{17,25},{10,2},{18,26},{11,3},{19,27},{12,4},{... | collective-permute-start | bytes 1622024 | tf_op jit(solution)/shard_map/ppermute | solution.py:254
  186.4 11.3 %collective-permute-start.25 = (s16[528,256]{1,0:T(8,128)(2,1)S(1)}, s16[528,256]{1,0:T(8,128)(2,1)S(1)}, u32[]{:S(2)}, u32[]{:S(2)}) collective-permute-start(s16[528,256]{1,0:T(8,128)(2,1)S(1)} %forward.17.a_ref), channel_id=1, source_target_pairs={{0,8},{24,16},{1,9},{25,17},{2,10},{26,18},{3,11},{27,19},{4,12},{... | collective-permute-start | bytes 811016 | tf_op jit(solution)/shard_map/ppermute | solution.py:257
  191.0 8.2 %collective-permute-start.26 = (s16[528,256]{1,0:T(8,128)(2,1)S(1)}, s16[528,256]{1,0:T(8,128)(2,1)S(1)}, u32[]{:S(2)}, u32[]{:S(2)}) collective-permute-start(s16[528,256]{1,0:T(8,128)(2,1)S(1)} %add.33.rest_0_), channel_id=1, source_target_pairs={{8,16},{16,8},{9,17},{17,9},{10,18},{18,10},{11,19},{19,11},{12,20... | collective-permute-start | bytes 811016 | tf_op jit(solution)/shard_map/ppermute | solution.py:260
  198.6 8.0 %collective-permute-start.28 = (s16[528,256]{1,0:T(8,128)(2,1)S(1)}, s16[528,256]{1,0:T(8,128)(2,1)S(1)}, u32[]{:S(2)}, u32[]{:S(2)}) collective-permute-start(s16[528,256]{1,0:T(8,128)(2,1)S(1)} %add.35.rest_0_), channel_id=1, source_target_pairs={{8,16},{16,8},{9,17},{17,9},{10,18},{18,10},{11,19},{19,11},{12,20... | collective-permute-start | bytes 811016 | tf_op jit(solution)/shard_map/ppermute | solution.py:260
  200.1 9.3 %collective-permute-start.29 = (s16[528,256]{1,0:T(8,128)(2,1)S(1)}, s16[528,256]{1,0:T(8,128)(2,1)S(1)}, u32[]{:S(2)}, u32[]{:S(2)}) collective-permute-start(s16[528,256]{1,0:T(8,128)(2,1)S(1)} %add.36), channel_id=1, source_target_pairs={{8,0},{16,24},{9,1},{17,25},{10,2},{18,26},{11,3},{19,27},{12,4},{... | collective-permute-start | bytes 811016 | tf_op jit(solution)/shard_map/ppermute | solution.py:254
  207.4 8.4 %collective-permute-start.30 = (s16[528,256]{1,0:T(8,128)(2,1)S(1)}, s16[528,256]{1,0:T(8,128)(2,1)S(1)}, u32[]{:S(2)}, u32[]{:S(2)}) collective-permute-start(s16[528,256]{1,0:T(8,128)(2,1)S(1)} %add.37), channel_id=1, source_target_pairs={{8,0},{16,24},{9,1},{17,25},{10,2},{18,26},{11,3},{19,27},{12,4},{... | collective-permute-start | bytes 811016 | tf_op jit(solution)/shard_map/ppermute | solution.py:254
  (2 other events, 1.9 us)
Sparse Core Ops, SparseCore 0:
  11.9 63.0 all-gather.1

commit v3 on v2

--- a/solution.py
+++ b/solution.py
@@ -9,7 +9,8 @@
 
 BLOCK = 128
 GROUPS = 16
-AHEAD = 6
+AHEAD = 4
+ROWS = 1024
 VMEM_LIMIT = 48 * 1024 * 1024
 
 
@@ -18,14 +19,18 @@
 
 
 def cost():
-    return pl.CostEstimate(flops=1000, bytes_accessed=1000, transcendentals=0)
+    return pl.CostEstimate(flops=4 * 10**9, bytes_accessed=10**7, transcendentals=0)
 
 
 def chunk_widths(local):
-    units = local // BLOCK
-    if units < 4 or units % 2:
-        return [BLOCK] * units
-    return [2 * BLOCK] * (units // 2 - 1) + [BLOCK] * 2
+    part = part_width(local)
+    parts = local // part
+    inner = [2 * part] * ((parts - 2) // 2)
+    return [part] + inner + [part] * (parts - 1 - 2 * len(inner))
+
+
+def part_width(local):
+    return 2 * BLOCK if local % (2 * BLOCK) == 0 and local >= 8 * BLOCK else BLOCK
 
 
 def put(ref, value):
@@ -52,49 +57,31 @@
     return grouped.reshape(rows, cols)
 
 
-def forward_kernel(place_ref, mask_ref, tokens_ref, gate_ref, up_ref, out_ref, total, held, *, first):
-    step = pl.program_id(0)
+def forward_kernel(place_ref, mask_ref, tokens_ref, gate_ref, up_ref, out_ref, held, *, first):
     depth, width = gate_ref.shape
+    base = first + pl.program_id(0) * (width // BLOCK)
     for r in range(depth // BLOCK):
         rows = slice(r * BLOCK, (r + 1) * BLOCK)
         for q in range(width // BLOCK):
             cols = slice(q * BLOCK, (q + 1) * BLOCK)
-            keep = mask_ref[step * (depth // BLOCK) + r, first + q] != 0
-            gate = gate_ref[rows, cols]
-            up = up_ref[rows, cols]
-            held[rows, cols] = jnp.where(keep, gate, jnp.zeros_like(gate))
-            held[rows, width + q * BLOCK : width + (q + 1) * BLOCK] = jnp.where(keep, up, jnp.zeros_like(up))
-    part = jnp.dot(tokens_ref[...], held[...], preferred_element_type=jnp.float32)
-
-    @pl.when(step == 0)
-    def _():
-        total[...] = part
-
-    @pl.when(step > 0)
-    def _():
-        total[...] += part
-
-    @pl.when(step == pl.num_programs(0) - 1)
-    def _():
-        put(out_ref, total[...])
+            keep = jnp.full((BLOCK, BLOCK), mask_ref[r, base + q].astype(jnp.float32)).astype(jnp.bfloat16)
+            held[rows, cols] = gate_ref[rows, cols] * keep
+            held[rows, width + q * BLOCK : width + (q + 1) * BLOCK] = up_ref[rows, cols] * keep
+    put(out_ref, jnp.dot(tokens_ref[...], held[...], preferred_element_type=jnp.float32))
 
 
 def forward(place, mask, tokens, gate_weight, up_weight, start, width):
     count, depth = tokens.shape
-    steps = max(1, depth // 512)
-    deep = depth // steps
-    weight = pl.BlockSpec((deep, width), lambda k, place, mask: (k, start // width))
+    part = part_width(gate_weight.shape[1])
+    weight = pl.BlockSpec((depth, part), lambda j, place, mask: (0, start // part + j))
     return pl.pallas_call(
         functools.partial(forward_kernel, first=start // BLOCK),
         grid_spec=pltpu.PrefetchScalarGridSpec(
             num_scalar_prefetch=2,
-            grid=(steps,),
-            in_specs=[pl.BlockSpec((count, deep), lambda k, place, mask: (0, k)), weight, weight],
-            out_specs=pl.BlockSpec((count + GROUPS, 2 * width), lambda k, place, mask: (0, 0)),
-            scratch_shapes=[
-                pltpu.VMEM((count, 2 * width), jnp.float32),
-                pltpu.VMEM((deep, 2 * width), jnp.bfloat16),
-            ],
+            grid=(width // part,),
+            in_specs=[pl.BlockSpec((count, depth), lambda j, place, mask: (0, 0)), weight, weight],
+            out_specs=pl.BlockSpec((count + GROUPS, 2 * part), lambda j, place, mask: (0, j)),
+            scratch_shapes=[pltpu.VMEM((depth, 2 * part), jnp.bfloat16)],
         ),
         out_shape=jax.ShapeDtypeStruct((count + GROUPS, 2 * width), jnp.int16),
         compiler_params=params(),
@@ -107,12 +94,13 @@
     put(out_ref, get(a_ref) + get(b_ref))
 
 
-def add(place, a, b):
-    spec = pl.BlockSpec(a.shape, lambda i, place: (0, 0))
+def add(place, a, b, part):
+    rows, cols = a.shape
+    spec = pl.BlockSpec((rows, 2 * part), lambda j, place: (0, j))
     return pl.pallas_call(
         add_kernel,
         grid_spec=pltpu.PrefetchScalarGridSpec(
-            num_scalar_prefetch=1, grid=(1,), in_specs=[spec, spec], out_specs=spec
+            num_scalar_prefetch=1, grid=(cols // (2 * part),), in_specs=[spec, spec], out_specs=spec
         ),
         out_shape=jax.ShapeDtypeStruct(a.shape, a.dtype),
         compiler_params=params(),
@@ -146,8 +134,9 @@
 def weights_kernel(place_ref, mask_ref, turned_ref, back_ref, *rest, first, terms, devices):
     coded = rest[:terms]
     hidden_ref, gate_ref, up_ref, deltas, hidden = rest[-5:]
-    step = pl.program_id(0)
+    step = pl.program_id(1)
     depth, width = gate_ref.shape
+    base = first + pl.program_id(0) * (width // BLOCK)
     count = deltas.shape[0]
     share = count // devices
     col, row = place_ref[0], place_ref[1]
@@ -184,7 +173,7 @@
         rows = slice(r * BLOCK, (r + 1) * BLOCK)
         for q in range(width // BLOCK):
             cols = slice(q * BLOCK, (q + 1) * BLOCK)
-            keep = mask_ref[step * (depth // BLOCK) + r, first + q].astype(jnp.float32)
+            keep = mask_ref[step * (depth // BLOCK) + r, base + q].astype(jnp.float32)
             gate_ref[rows, cols] = total[rows, cols] * keep
             up_ref[rows, cols] = total[rows, width + q * BLOCK : width + (q + 1) * BLOCK] * keep
 
@@ -192,25 +181,25 @@
 def weight_grads(place, mask, turned, back, coded, previous, shapes, start, width, devices):
     depth, count = turned.shape
     owned = shapes[0].shape[0]
-    steps = max(1, depth // 512)
-    deep = depth // steps
-    message = pl.BlockSpec((count + GROUPS, 2 * width), lambda m, place, mask: (0, 0))
-    out = pl.BlockSpec((deep, width), lambda m, place, mask: (m, start // width))
+    part = part_width(shapes[1].shape[1])
+    deep = min(ROWS, depth)
+    message = pl.BlockSpec((count + GROUPS, 2 * part), lambda j, m, place, mask: (0, j))
+    out = pl.BlockSpec((deep, part), lambda j, m, place, mask: (m, start // part + j))
     return pl.pallas_call(
         functools.partial(weights_kernel, first=start // BLOCK, terms=len(coded), devices=devices),
         grid_spec=pltpu.PrefetchScalarGridSpec(
             num_scalar_prefetch=2,
-            grid=(steps,),
+            grid=(width // part, depth // deep),
             in_specs=[
-                pl.BlockSpec((deep, count), lambda m, place, mask: (m, 0)),
-                pl.BlockSpec((count, width), lambda m, place, mask: (0, start // width)),
+                pl.BlockSpec((deep, count), lambda j, m, place, mask: (m, 0)),
+                pl.BlockSpec((count, part), lambda j, m, place, mask: (0, start // part + j)),
             ]
             + [message] * len(coded)
             + [pl.BlockSpec(memory_space=pl.ANY)] * len(previous),
-            out_specs=[pl.BlockSpec((owned, width), lambda m, place, mask: (0, start // width)), out, out],
+            out_specs=[pl.BlockSpec((owned, part), lambda j, m, place, mask: (0, start // part + j)), out, out],
             scratch_shapes=[
-                pltpu.VMEM((count, 2 * width), jnp.bfloat16),
-                pltpu.VMEM((count, width), jnp.bfloat16),
+                pltpu.VMEM((count, 2 * part), jnp.bfloat16),
+                pltpu.VMEM((count, part), jnp.bfloat16),
             ],
         ),
         out_shape=shapes,
@@ -262,6 +251,7 @@
     back = lax.all_gather(hidden_grad, "row", axis=0, tiled=True)
     gathered = gather_tokens(tokens, devices)
 
+    part = part_width(local)
     widths = chunk_widths(local)
     starts = [sum(widths[:c]) for c in range(len(widths))]
     chunks = len(widths)
@@ -291,7 +281,7 @@
             arrived = came[c] if hop == reach - 1 else inward(total, hop)
             if hop == reach - 1 and c + 2 < chunks:
                 send_in(c + 2)
-            new = ordered(add, own[c], arrived)
+            new = ordered(add, own[c], arrived, part)
             total = new if reach == 1 else pick(distance == hop, new, total)
         sums.append(total)
         across.append(swap(total))
@@ -300,7 +290,7 @@
         coming = across[c]
         parts = [sums[c], coming]
         for hop in range(reach):
-            arrived = outward(ordered(add, own[c], coming), hop)
+            arrived = outward(ordered(add, own[c], coming, part), hop)
             if reach == 1:
                 parts.append(arrived)
             else:

time: 228 us -> 238 us (1.044)
  waiting for transfers between devices: 22.4 us -> 87.5 us
  Pallas kernels: 115 us -> 83.2 us
  starting transfers between devices: 67.2 us -> 44.8 us
    ppermute x9 -> x5, waiting for transfers between devices: 2.55 us -> 43.1 us  [inward(): lax.ppermute(value, 'row', [(left - hop - 1, left - hop), (right + hop +...]
    ppermute x9 -> x5, waiting for transfers between devices: 5.33 us -> 30.2 us  [outward(): lax.ppermute(value, 'row', [(left - hop, left - hop - 1), (right + hop, r...]
    pallas_call x9 -> x5, Pallas kernels: 45 us -> 25.6 us  [forward(): pl.pallas_call(functools.partial(forward_kernel, first=start // BLOCK), g...]
    ppermute x9 -> x5, starting transfers between devices: 43.6 us -> 29 us  [inward(): lax.ppermute(value, 'row', [(left - hop - 1, left - hop), (right + hop +...]
    pallas_call x9 -> x5, Pallas kernels: 42.1 us -> 33.6 us  [weight_grads(): pl.pallas_call(functools.partial(weights_kernel, first=start // BLOCK, te...]
    ppermute x9 -> x5, starting transfers between devices: 12 us -> 6.44 us  [outward(): lax.ppermute(value, 'row', [(left - hop, left - hop - 1), (right + hop, r...]
    pallas_call x18 -> x10, Pallas kernels: 26.4 us -> 22.5 us  [add(): pl.pallas_call(add_kernel, grid_spec=pltpu.PrefetchScalarGridSpec(num_sca...]
    ppermute x9 -> x5, starting transfers between devices: 7.01 us -> 4.63 us  [swap(): return lax.ppermute(value, 'row', [(left, right), (right, left)])]
  transfers between devices with their start and end apart: 32 -> 20, of which waited for: 8 -> 11; matrix products, arithmetic and copies ran while one was open for 1% -> 0% of each run, Pallas kernels for 49% -> 33%
where the time goes in v3:
time: 238 us; the launch traced here: 237 us
  waiting for transfers between devices  87.5 us (37%)
  Pallas kernels  83.2 us (35%)
  starting transfers between devices  44.8 us (19%)
  between operations  14.4 us (6%)
  local copies, waits for them, and re-layouts  5.73 us (2%)
    ppermute x5, waiting for transfers between devices, inward(): lax.ppermute(value, 'row', [(left - hop - 1, left - hop), (right + hop +...  43.1 us
    pallas_call x5, Pallas kernels, weight_grads(): pl.pallas_call(functools.partial(weights_kernel, first=start // BLOCK, te...  33.6 us
    ppermute x5, waiting for transfers between devices, outward(): lax.ppermute(value, 'row', [(left - hop, left - hop - 1), (right + hop, r...  30.2 us
    ppermute x5, starting transfers between devices, inward(): lax.ppermute(value, 'row', [(left - hop - 1, left - hop), (right + hop +...  29 us
    pallas_call x5, Pallas kernels, forward(): pl.pallas_call(functools.partial(forward_kernel, first=start // BLOCK), g...  25.6 us
    pallas_call x10, Pallas kernels, add(): pl.pallas_call(add_kernel, grid_spec=pltpu.PrefetchScalarGridSpec(num_sca...  22.5 us
    ppermute x3, waiting for transfers between devices, gather_tokens(): lax.ppermute(tokens, 'col', [(i, i ^ other) for i in range(devices)])  11.8 us
    ppermute x5, starting transfers between devices, outward(): lax.ppermute(value, 'row', [(left - hop, left - hop - 1), (right + hop, r...  6.44 us
  transfers between devices with their start and end apart: 20, of which 11 were waited for; matrix products, arithmetic and copies ran while one was open for 0% of the time, Pallas kernels for 33%

profile of v3, /device:TPU:0, one launch (start us, length us, event | category | flops | bytes accessed | tf_op | source)
XLA Modules:
  0.0 236.8 jit_solution(8682223622817487405)
XLA Ops:
  7.2 4.0 %collective-permute-start.2 = (bf16[64,2048]{1,0:T(8,128)(2,1)}, bf16[64,2048]{1,0:T(8,128)(2,1)S(1)}, u32[]{:S(2)}, u32[]{:S(2)}) collective-permute-start(bf16[64,2048]{1,0:T(8,128)(2,1)} %param.5), channel_id=1, source_target_pairs={{0,6},{1,7},{2,4},{3,5},{4,2},{5,3},{6,0},{7,1},{8,14},{9,15},{10,... | collective-permute-start | bytes 786440 | tf_op jit(solution)/shard_map/ppermute | solution.py:224
  11.8 6.7 %collective-permute-done.2 = bf16[64,2048]{1,0:T(8,128)(2,1)S(1)} collective-permute-done((bf16[64,2048]{1,0:T(8,128)(2,1)}, bf16[64,2048]{1,0:T(8,128)(2,1)S(1)}, u32[]{:S(2)}, u32[]{:S(2)}) %collective-permute-start.2) | collective-permute-done | bytes 262176 | tf_op jit(solution)/shard_map/ppermute | solution.py:224
  18.6 4.7 %collective-permute-done.1 = bf16[64,2048]{1,0:T(8,128)(2,1)S(1)} collective-permute-done((bf16[64,2048]{1,0:T(8,128)(2,1)}, bf16[64,2048]{1,0:T(8,128)(2,1)S(1)}, u32[]{:S(2)}, u32[]{:S(2)}) %collective-permute-start.1) | collective-permute-done | bytes 262176 | tf_op jit(solution)/shard_map/ppermute | solution.py:224
  23.6 1.0 pad_maximum_fusion
  25.0 2.4 %collective-permute-done.3 = bf16[256,2048]{1,0:T(8,128)(2,1)S(1)} collective-permute-done((bf16[256,2048]{1,0:T(8,128)(2,1)S(1)}, bf16[256,2048]{1,0:T(8,128)(2,1)S(1)}, u32[]{:S(2)}, u32[]{:S(2)}) %collective-permute-start.3) | collective-permute-done | bytes 1048608 | tf_op jit(solution)/shard_map/ppermute | solution.py:226
  27.5 3.9 %forward.5.a_ref = s16[528,512]{1,0:T(8,128)(2,1)S(1)} custom-call(s32[2]{0:T(128)S(1)} %pad_add_fusion.place_ref, s32[16,16]{1,0:T(8,128)S(1)} %copy-done.8, bf16[512,2048]{1,0:T(8,128)(2,1)S(1)} %constant_dynamic-update-slice_fusion.tokens_ref.value_ref, bf16[2048,2048]{1,0:T(8,128)(2,1)} %gate_ref.9, bf16[2048,2048]{1,0:T(8,128)(2,1)} %up_ref.9), custom_call_target="tpu_custom_call" | custom-call | flops 4000000000 | bytes 10000000 | tf_op jit(solution)/shard_map/forward/pallas_call | solution.py:77
  31.4 3.5 %collective-permute-start.4 = (s16[528,512]{1,0:T(8,128)(2,1)S(1)}, s16[528,512]{1,0:T(8,128)(2,1)S(1)}, u32[]{:S(2)}, u32[]{:S(2)}) collective-permute-start(s16[528,512]{1,0:T(8,128)(2,1)S(1)} %forward.5.a_ref), channel_id=1, source_target_pairs={{0,8},{24,16},{1,9},{25,17},{2,10},{26,18},{3,11},{27,19},{4,12},{... | collective-permute-start | bytes 1622024 | tf_op jit(solution)/shard_map/ppermute | solution.py:246
  34.9 5.7 %forward.6.a_ref = s16[528,1024]{1,0:T(8,128)(2,1)S(1)} custom-call(s32[2]{0:T(128)S(1)} %pad_add_fusion.place_ref, s32[16,16]{1,0:T(8,128)S(1)} %copy-done.8, bf16[512,2048]{1,0:T(8,128)(2,1)S(1)} %constant_dynamic-update-slice_fusion.tokens_ref.value_ref, bf16[2048,2048]{1,0:T(8,128)(2,1)} %gate_ref.9, bf16[2048,2048]{1,0:T(8,128)(2,1)} %up_ref.9), custom_call_target="tpu_custom_call" | custom-call | flops 4000000000 | bytes 10000000 | tf_op jit(solution)/shard_map/forward/pallas_call | solution.py:77
  40.6 1.5 collective-permute-start.5
  42.0 5.7 %forward.7.a_ref = s16[528,1024]{1,0:T(8,128)(2,1)S(1)} custom-call(s32[2]{0:T(128)S(1)} %pad_add_fusion.place_ref, s32[16,16]{1,0:T(8,128)S(1)} %copy-done.8, bf16[512,2048]{1,0:T(8,128)(2,1)S(1)} %constant_dynamic-update-slice_fusion.tokens_ref.value_ref, bf16[2048,2048]{1,0:T(8,128)(2,1)} %gate_ref.9, bf16[2048,2048]{1,0:T(8,128)(2,1)} %up_ref.9), custom_call_target="tpu_custom_call" | custom-call | flops 4000000000 | bytes 10000000 | tf_op jit(solution)/shard_map/forward/pallas_call | solution.py:77
  47.7 5.7 %forward.8.a_ref = s16[528,1024]{1,0:T(8,128)(2,1)S(1)} custom-call(s32[2]{0:T(128)S(1)} %pad_add_fusion.place_ref, s32[16,16]{1,0:T(8,128)S(1)} %copy-done.8, bf16[512,2048]{1,0:T(8,128)(2,1)S(1)} %constant_dynamic-update-slice_fusion.tokens_ref.value_ref, bf16[2048,2048]{1,0:T(8,128)(2,1)} %gate_ref.9, bf16[2048,2048]{1,0:T(8,128)(2,1)} %up_ref.9), custom_call_target="tpu_custom_call" | custom-call | flops 4000000000 | bytes 10000000 | tf_op jit(solution)/shard_map/forward/pallas_call | solution.py:77
  53.4 1.5 turn.1.turned_ref
  54.9 4.1 %collective-permute-done.4.b_ref = s16[528,512]{1,0:T(8,128)(2,1)S(1)} collective-permute-done((s16[528,512]{1,0:T(8,128)(2,1)S(1)}, s16[528,512]{1,0:T(8,128)(2,1)S(1)}, u32[]{:S(2)}, u32[]{:S(2)}) %collective-permute-start.4) | collective-permute-done | bytes 540704 | tf_op jit(solution)/shard_map/ppermute | solution.py:246
  59.0 1.1 add.12.rest_0_
  60.9 6.8 %collective-permute-start.7 = (s16[528,1024]{1,0:T(8,128)(2,1)S(1)}, s16[528,1024]{1,0:T(8,128)(2,1)S(1)}, u32[]{:S(2)}, u32[]{:S(2)}) collective-permute-start(s16[528,1024]{1,0:T(8,128)(2,1)S(1)} %forward.7.a_ref), channel_id=1, source_target_pairs={{0,8},{24,16},{1,9},{25,17},{2,10},{26,18},{3,11},{27,19},{4,12},{... | collective-permute-start | bytes 3244040 | tf_op jit(solution)/shard_map/ppermute | solution.py:246
  67.7 4.7 %forward.9.a_ref = s16[528,512]{1,0:T(8,128)(2,1)} custom-call(s32[2]{0:T(128)S(1)} %pad_add_fusion.place_ref, s32[16,16]{1,0:T(8,128)S(1)} %copy-done.8, bf16[512,2048]{1,0:T(8,128)(2,1)S(1)} %constant_dynamic-update-slice_fusion.tokens_ref.value_ref, bf16[2048,2048]{1,0:T(8,128)(2,1)} %gate_ref.9, bf16[2048,2048]{1,0:T(8,128)(2,1)} %up_ref.9), custom_call_target="tpu_custom_call" | custom-call | flops 4000000000 | bytes 10000000 | tf_op jit(solution)/shard_map/forward/pallas_call | solution.py:77
  72.4 30.1 %collective-permute-done.5.b_ref = s16[528,1024]{1,0:T(8,128)(2,1)S(1)} collective-permute-done((s16[528,1024]{1,0:T(8,128)(2,1)S(1)}, s16[528,1024]{1,0:T(8,128)(2,1)S(1)}, u32[]{:S(2)}, u32[]{:S(2)}) %collective-permute-start.5) | collective-permute-done | bytes 1081376 | tf_op jit(solution)/shard_map/ppermute | solution.py:246
  102.5 1.9 add.13.rest_0_
  105.2 9.2 %collective-permute-start.10 = (s16[528,1024]{1,0:T(8,128)(2,1)S(1)}, s16[528,1024]{1,0:T(8,128)(2,1)}, u32[]{:S(2)}, u32[]{:S(2)}) collective-permute-start(s16[528,1024]{1,0:T(8,128)(2,1)S(1)} %forward.8.a_ref), channel_id=1, source_target_pairs={{0,8},{24,16},{1,9},{25,17},{2,10},{26,18},{3,11},{27,19},{4,12},{... | collective-permute-start | bytes 3244040 | tf_op jit(solution)/shard_map/ppermute | solution.py:246
  114.4 1.1 add.14
  115.6 1.3 collective-permute-start.9
  116.9 8.8 %collective-permute-done.7.b_ref = s16[528,1024]{1,0:T(8,128)(2,1)S(1)} collective-permute-done((s16[528,1024]{1,0:T(8,128)(2,1)S(1)}, s16[528,1024]{1,0:T(8,128)(2,1)S(1)}, u32[]{:S(2)}, u32[]{:S(2)}) %collective-permute-start.7) | collective-permute-done | bytes 1081376 | tf_op jit(solution)/shard_map/ppermute | solution.py:246
  125.7 2.7 %add.15.rest_0_ = s16[528,1024]{1,0:T(8,128)(2,1)} custom-call(s32[2]{0:T(128)S(1)} %pad_add_fusion.place_ref, s16[528,1024]{1,0:T(8,128)(2,1)S(1)} %forward.7.a_ref, s16[528,1024]{1,0:T(8,128)(2,1)S(1)} %collective-permute-done.7.b_ref), custom_call_target="tpu_custom_call" | custom-call | flops 4000000000 | bytes 10000000 | tf_op jit(solution)/shard_map/add/pallas_call | solution.py:100
  128.4 1.6 collective-permute-start.11
  130.1 8.0 %collective-permute-start.13 = (s16[528,512]{1,0:T(8,128)(2,1)}, s16[528,512]{1,0:T(8,128)(2,1)}, u32[]{:S(2)}, u32[]{:S(2)}) collective-permute-start(s16[528,512]{1,0:T(8,128)(2,1)} %forward.9.a_ref), channel_id=1, source_target_pairs={{0,8},{24,16},{1,9},{25,17},{2,10},{26,18},{3,11},{27,19},{4,12},{... | collective-permute-start | bytes 1622024 | tf_op jit(solution)/shard_map/ppermute | solution.py:246
  138.1 2.7 %add.16 = s16[528,1024]{1,0:T(8,128)(2,1)} custom-call(s32[2]{0:T(128)S(1)} %pad_add_fusion.place_ref, s16[528,1024]{1,0:T(8,128)(2,1)S(1)} %forward.6.a_ref, s16[528,1024]{1,0:T(8,128)(2,1)S(1)} %collective-permute-done.8.b_ref.rest_1_), custom_call_target="tpu_custom_call" | custom-call | flops 4000000000 | bytes 10000000 | tf_op jit(solution)/shard_map/add/pallas_call | solution.py:100
  140.8 1.3 collective-permute-start.12
  142.9 1.6 copy-done
  144.5 1.0 copy-done.10
  145.6 1.0 copy-done.12
  146.6 1.0 copy-done.14
  147.7 4.2 %weight_grads.5 = (bf16[128,2048]{1,0:T(8,128)(2,1)}, f32[2048,2048]{1,0:T(8,128)}, f32[2048,2048]{1,0:T(8,128)}) custom-call(s32[2]{0:T(128)S(1)} %pad_add_fusion.place_ref, s32[16,16]{1,0:T(8,128)S(1)} %copy-done.8, bf16[2048,512]{1,0:T(8,128)(2,1)S(1)} %turn.1.turned_ref, bf16[512,2048]{1,0:T(8,128)(2,1)S(1)} %copy-done, s16[528,512]{1,0:T(8,128)(2,1)S(1)} %copy-done.10, ...), custom_call_target="tpu_custom_call" | custom-call | flops 4000000000 | bytes 10000000 | tf_op jit(solution)/shard_map/weight_grads/pallas_call | solution.py:188
  151.8 2.9 %add.17.rest_0_ = s16[528,1024]{1,0:T(8,128)(2,1)S(1)} custom-call(s32[2]{0:T(128)S(1)} %pad_add_fusion.place_ref, s16[528,1024]{1,0:T(8,128)(2,1)S(1)} %forward.8.a_ref, s16[528,1024]{1,0:T(8,128)(2,1)} %collective-permute-done.10.b_ref), custom_call_target="tpu_custom_call" | custom-call | flops 4000000000 | bytes 10000000 | tf_op jit(solution)/shard_map/add/pallas_call | solution.py:100
  155.6 3.6 %add.18 = s16[528,1024]{1,0:T(8,128)(2,1)} custom-call(s32[2]{0:T(128)S(1)} %pad_add_fusion.place_ref, s16[528,1024]{1,0:T(8,128)(2,1)S(1)} %copy-done.3, s16[528,1024]{1,0:T(8,128)(2,1)} %collective-permute-done.11.b_ref.rest_1_), custom_call_target="tpu_custom_call" | custom-call | flops 4000000000 | bytes 10000000 | tf_op jit(solution)/shard_map/add/pallas_call | solution.py:100
  159.2 1.3 collective-permute-start.15
  160.5 9.3 %collective-permute-done.12.rest_2_ = s16[528,1024]{1,0:T(8,128)(2,1)} collective-permute-done((s16[528,1024]{1,0:T(8,128)(2,1)}, s16[528,1024]{1,0:T(8,128)(2,1)}, u32[]{:S(2)}, u32[]{:S(2)}) %collective-permute-start.12) | collective-permute-done | bytes 1081376 | tf_op jit(solution)/shard_map/ppermute | solution.py:243
  169.8 8.4 %weight_grads.6 = (bf16[128,2048]{1,0:T(8,128)(2,1)}, f32[2048,2048]{1,0:T(8,128)}, f32[2048,2048]{1,0:T(8,128)}) custom-call(s32[2]{0:T(128)S(1)} %pad_add_fusion.place_ref, s32[16,16]{1,0:T(8,128)S(1)} %copy-done.8, bf16[2048,512]{1,0:T(8,128)(2,1)S(1)} %turn.1.turned_ref, ...), custom_call_target="tpu_custom_call", output_to_operand_aliasing={{0}: (7, {}), {1}: (8, {}), {2}: (9, {})} | custom-call | flops 4000000000 | bytes 10000000 | tf_op jit(solution)/shard_map/weight_grads/pallas_call | solution.py:188
  178.2 2.3 add.19.rest_0_
  180.6 1.9 add.20
  182.5 1.3 collective-permute-start.17
  184.5 8.4 %collective-permute-done.15.rest_2_ = s16[528,1024]{1,0:T(8,128)(2,1)S(1)} collective-permute-done((s16[528,1024]{1,0:T(8,128)(2,1)}, s16[528,1024]{1,0:T(8,128)(2,1)S(1)}, u32[]{:S(2)}, u32[]{:S(2)}) %collective-permute-start.15) | collective-permute-done | bytes 1081376 | tf_op jit(solution)/shard_map/ppermute | solution.py:243
  192.9 9.1 %weight_grads.7 = (bf16[128,2048]{1,0:T(8,128)(2,1)}, f32[2048,2048]{1,0:T(8,128)}, f32[2048,2048]{1,0:T(8,128)}) custom-call(s32[2]{0:T(128)S(1)} %pad_add_fusion.place_ref, s32[16,16]{1,0:T(8,128)S(1)} %copy-done.8, bf16[2048,512]{1,0:T(8,128)(2,1)S(1)} %turn.1.turned_ref, ...), custom_call_target="tpu_custom_call", output_to_operand_aliasing={{0}: (7, {}), {1}: (8, {}), {2}: (9, {})} | custom-call | flops 4000000000 | bytes 10000000 | tf_op jit(solution)/shard_map/weight_grads/pallas_call | solution.py:188
  202.0 2.2 add.21
  204.2 1.3 collective-permute-start.18
  205.5 10.6 %collective-permute-done.17.rest_2_ = s16[528,1024]{1,0:T(8,128)(2,1)S(1)} collective-permute-done((s16[528,1024]{1,0:T(8,128)(2,1)S(1)}, s16[528,1024]{1,0:T(8,128)(2,1)S(1)}, u32[]{:S(2)}, u32[]{:S(2)}) %collective-permute-start.17) | collective-permute-done | bytes 1081376 | tf_op jit(solution)/shard_map/ppermute | solution.py:243
  216.1 7.7 %weight_grads.8 = (bf16[128,2048]{1,0:T(8,128)(2,1)}, f32[2048,2048]{1,0:T(8,128)}, f32[2048,2048]{1,0:T(8,128)}) custom-call(s32[2]{0:T(128)S(1)} %pad_add_fusion.place_ref, s32[16,16]{1,0:T(8,128)S(1)} %copy-done.8, bf16[2048,512]{1,0:T(8,128)(2,1)S(1)} %turn.1.turned_ref, ...), custom_call_target="tpu_custom_call", output_to_operand_aliasing={{0}: (7, {}), {1}: (8, {}), {2}: (9, {})} | custom-call | flops 4000000000 | bytes 10000000 | tf_op jit(solution)/shard_map/weight_grads/pallas_call | solution.py:188
  223.8 2.0 collective-permute-done.18.rest_2_
  225.8 4.2 %weight_grads.9 = (bf16[128,2048]{1,0:T(8,128)(2,1)}, f32[2048,2048]{1,0:T(8,128)}, f32[2048,2048]{1,0:T(8,128)}) custom-call(s32[2]{0:T(128)S(1)} %pad_add_fusion.place_ref, s32[16,16]{1,0:T(8,128)S(1)} %copy-done.8, bf16[2048,512]{1,0:T(8,128)(2,1)S(1)} %turn.1.turned_ref, ...), custom_call_target="tpu_custom_call", output_to_operand_aliasing={{0}: (7, {}), {1}: (8, {}), {2}: (9, {})} | custom-call | flops 4000000000 | bytes 10000000 | tf_op jit(solution)/shard_map/weight_grads/pallas_call | solution.py:188
  (53 shorter events, 5.1 us)
Async XLA Ops:
  7.2 17.7 %copy-start.15 = (bf16[64,2048]{1,0:T(8,128)(2,1)S(1)}, bf16[64,2048]{1,0:T(8,128)(2,1)}, u32[]{:S(2)}) copy-start(bf16[64,2048]{1,0:T(8,128)(2,1)} %param.5) | copy-start | bytes 786436
  7.2 135.8 %all-gather.2.cloned.1.call-start = ((), (), s32[]{:S(2)}) async-start(), calls=%async_computation | async-start | bytes 2621440 | tf_op jit(solution)/shard_map/all_gather | solution.py:251
  7.2 11.3 %collective-permute-start.2 = (bf16[64,2048]{1,0:T(8,128)(2,1)}, bf16[64,2048]{1,0:T(8,128)(2,1)S(1)}, u32[]{:S(2)}, u32[]{:S(2)}) collective-permute-start(bf16[64,2048]{1,0:T(8,128)(2,1)} %param.5), channel_id=1, source_target_pairs={{0,6},{1,7},{2,4},{3,5},{4,2},{5,3},{6,0},{7,1},{8,14},{9,15},{10,... | collective-permute-start | bytes 786440 | tf_op jit(solution)/shard_map/ppermute | solution.py:224
  11.2 12.1 %collective-permute-start.1 = (bf16[64,2048]{1,0:T(8,128)(2,1)}, bf16[64,2048]{1,0:T(8,128)(2,1)S(1)}, u32[]{:S(2)}, u32[]{:S(2)}) collective-permute-start(bf16[64,2048]{1,0:T(8,128)(2,1)} %param.5), channel_id=1, source_target_pairs={{0,4},{1,5},{2,6},{3,7},{4,0},{5,1},{6,2},{7,3},{8,12},{9,13},{10,... | collective-permute-start | bytes 786440 | tf_op jit(solution)/shard_map/ppermute | solution.py:224
  11.7 11.9 %collective-permute-start = (bf16[64,2048]{1,0:T(8,128)(2,1)}, bf16[64,2048]{1,0:T(8,128)(2,1)S(1)}, u32[]{:S(2)}, u32[]{:S(2)}) collective-permute-start(bf16[64,2048]{1,0:T(8,128)(2,1)} %param.5), channel_id=1, source_target_pairs={{0,2},{1,3},{2,0},{3,1},{4,6},{5,7},{6,4},{7,5},{8,10},{9,11},{10,... | collective-permute-start | bytes 786440 | tf_op jit(solution)/shard_map/ppermute | solution.py:224
  24.7 2.7 %collective-permute-start.3 = (bf16[256,2048]{1,0:T(8,128)(2,1)S(1)}, bf16[256,2048]{1,0:T(8,128)(2,1)S(1)}, u32[]{:S(2)}, u32[]{:S(2)}) collective-permute-start(bf16[256,2048]{1,0:T(8,128)(2,1)S(1)} %pad_maximum_fusion), channel_id=1, source_target_pairs={{0,1},{1,0},{2,3},{3,2},{4,5},{5,4},{6,7},{7,6},{8,9},{9,8},{10,11... | collective-permute-start | bytes 3145736 | tf_op jit(solution)/shard_map/ppermute | solution.py:226
  24.8 2.6 %copy-start.8 = (s32[16,16]{1,0:T(8,128)S(1)}, s32[16,16]{1,0:T(8,128)}, u32[]{:S(2)}) copy-start(s32[16,16]{1,0:T(8,128)} %mask_ref.19) | copy-start | bytes 3076
  31.4 27.7 %collective-permute-start.4 = (s16[528,512]{1,0:T(8,128)(2,1)S(1)}, s16[528,512]{1,0:T(8,128)(2,1)S(1)}, u32[]{:S(2)}, u32[]{:S(2)}) collective-permute-start(s16[528,512]{1,0:T(8,128)(2,1)S(1)} %forward.5.a_ref), channel_id=1, source_target_pairs={{0,8},{24,16},{1,9},{25,17},{2,10},{26,18},{3,11},{27,19},{4,12},{... | collective-permute-start | bytes 1622024 | tf_op jit(solution)/shard_map/ppermute | solution.py:246
  40.6 62.0 %collective-permute-start.5 = (s16[528,1024]{1,0:T(8,128)(2,1)S(1)}, s16[528,1024]{1,0:T(8,128)(2,1)S(1)}, u32[]{:S(2)}, u32[]{:S(2)}) collective-permute-start(s16[528,1024]{1,0:T(8,128)(2,1)S(1)} %forward.6.a_ref), channel_id=1, source_target_pairs={{0,8},{24,16},{1,9},{25,17},{2,10},{26,18},{3,11},{27,19},{4,12},{... | collective-permute-start | bytes 3244040 | tf_op jit(solution)/shard_map/ppermute | solution.py:246
  47.7 78.0 %copy-start.2 = (s16[528,1024]{1,0:T(8,128)(2,1)}, s16[528,1024]{1,0:T(8,128)(2,1)S(1)}, u32[]{:S(2)}) copy-start(s16[528,1024]{1,0:T(8,128)(2,1)S(1)} %forward.7.a_ref) | copy-start | bytes 3244036
  60.1 12.2 %copy-start.9 = (s16[528,512]{1,0:T(8,128)(2,1)}, s16[528,512]{1,0:T(8,128)(2,1)S(1)}, u32[]{:S(2)}) copy-start(s16[528,512]{1,0:T(8,128)(2,1)S(1)} %add.12.rest_0_) | copy-start | bytes 1622020
  60.2 54.3 %collective-permute-start.6 = (s16[528,512]{1,0:T(8,128)(2,1)S(1)}, s16[528,512]{1,0:T(8,128)(2,1)S(1)}, u32[]{:S(2)}, u32[]{:S(2)}) collective-permute-start(s16[528,512]{1,0:T(8,128)(2,1)S(1)} %add.12.rest_0_), channel_id=1, source_target_pairs={{8,16},{16,8},{9,17},{17,9},{10,18},{18,10},{11,19},{19,11},{12,20... | collective-permute-start | bytes 1622024 | tf_op jit(solution)/shard_map/ppermute | solution.py:249
  60.9 64.8 %collective-permute-start.7 = (s16[528,1024]{1,0:T(8,128)(2,1)S(1)}, s16[528,1024]{1,0:T(8,128)(2,1)S(1)}, u32[]{:S(2)}, u32[]{:S(2)}) collective-permute-start(s16[528,1024]{1,0:T(8,128)(2,1)S(1)} %forward.7.a_ref), channel_id=1, source_target_pairs={{0,8},{24,16},{1,9},{25,17},{2,10},{26,18},{3,11},{27,19},{4,12},{... | collective-permute-start | bytes 3244040 | tf_op jit(solution)/shard_map/ppermute | solution.py:246
  104.5 11.1 %copy-start.4 = (s16[528,1024]{1,0:T(8,128)(2,1)}, s16[528,1024]{1,0:T(8,128)(2,1)S(1)}, u32[]{:S(2)}) copy-start(s16[528,1024]{1,0:T(8,128)(2,1)S(1)} %add.13.rest_0_) | copy-start | bytes 3244036
  104.5 33.6 %collective-permute-start.8 = (s16[528,1024]{1,0:T(8,128)(2,1)S(1)}, s16[528,1024]{1,0:T(8,128)(2,1)S(1)}, u32[]{:S(2)}, u32[]{:S(2)}) collective-permute-start(s16[528,1024]{1,0:T(8,128)(2,1)S(1)} %add.13.rest_0_), channel_id=1, source_target_pairs={{8,16},{16,8},{9,17},{17,9},{10,18},{18,10},{11,19},{19,11},{12,20... | collective-permute-start | bytes 3244040 | tf_op jit(solution)/shard_map/ppermute | solution.py:249
  105.2 46.6 %collective-permute-start.10 = (s16[528,1024]{1,0:T(8,128)(2,1)S(1)}, s16[528,1024]{1,0:T(8,128)(2,1)}, u32[]{:S(2)}, u32[]{:S(2)}) collective-permute-start(s16[528,1024]{1,0:T(8,128)(2,1)S(1)} %forward.8.a_ref), channel_id=1, source_target_pairs={{0,8},{24,16},{1,9},{25,17},{2,10},{26,18},{3,11},{27,19},{4,12},{... | collective-permute-start | bytes 3244040 | tf_op jit(solution)/shard_map/ppermute | solution.py:246
  114.4 1.1 copy-start.11
  115.6 26.5 %collective-permute-start.9 = (s16[528,512]{1,0:T(8,128)(2,1)S(1)}, s16[528,512]{1,0:T(8,128)(2,1)S(1)}, u32[]{:S(2)}, u32[]{:S(2)}) collective-permute-start(s16[528,512]{1,0:T(8,128)(2,1)S(1)} %add.14), channel_id=1, source_target_pairs={{8,0},{16,24},{9,1},{17,25},{10,2},{18,26},{11,3},{19,27},{12,4},{... | collective-permute-start | bytes 1622024 | tf_op jit(solution)/shard_map/ppermute | solution.py:243
  128.4 27.2 %collective-permute-start.11 = (s16[528,1024]{1,0:T(8,128)(2,1)}, s16[528,1024]{1,0:T(8,128)(2,1)}, u32[]{:S(2)}, u32[]{:S(2)}) collective-permute-start(s16[528,1024]{1,0:T(8,128)(2,1)} %add.15.rest_0_), channel_id=1, source_target_pairs={{8,16},{16,8},{9,17},{17,9},{10,18},{18,10},{11,19},{19,11},{12,20... | collective-permute-start | bytes 3244040 | tf_op jit(solution)/shard_map/ppermute | solution.py:249
  130.1 48.2 %collective-permute-start.13 = (s16[528,512]{1,0:T(8,128)(2,1)}, s16[528,512]{1,0:T(8,128)(2,1)}, u32[]{:S(2)}, u32[]{:S(2)}) collective-permute-start(s16[528,512]{1,0:T(8,128)(2,1)} %forward.9.a_ref), channel_id=1, source_target_pairs={{0,8},{24,16},{1,9},{25,17},{2,10},{26,18},{3,11},{27,19},{4,12},{... | collective-permute-start | bytes 1622024 | tf_op jit(solution)/shard_map/ppermute | solution.py:246
  138.1 2.7 %copy-start.6 = (s16[528,1024]{1,0:T(8,128)(2,1)}, s16[528,1024]{1,0:T(8,128)(2,1)S(1)}, u32[]{:S(2)}) copy-start(s16[528,1024]{1,0:T(8,128)(2,1)S(1)} %collective-permute-done.8.b_ref.rest_1_) | copy-start | bytes 3244036
  140.8 29.0 %collective-permute-start.12 = (s16[528,1024]{1,0:T(8,128)(2,1)}, s16[528,1024]{1,0:T(8,128)(2,1)}, u32[]{:S(2)}, u32[]{:S(2)}) collective-permute-start(s16[528,1024]{1,0:T(8,128)(2,1)} %add.16), channel_id=1, source_target_pairs={{8,0},{16,24},{9,1},{17,25},{10,2},{18,26},{11,3},{19,27},{12,4},{... | collective-permute-start | bytes 3244040 | tf_op jit(solution)/shard_map/ppermute | solution.py:243
  142.1 0.8 copy-start.13
  142.9 1.6 copy-start
  144.5 1.0 copy-start.10
  145.6 1.0 copy-start.12
  146.6 1.0 copy-start.14
  151.8 3.8 %copy-start.3 = (s16[528,1024]{1,0:T(8,128)(2,1)S(1)}, s16[528,1024]{1,0:T(8,128)(2,1)}, u32[]{:S(2)}) copy-start(s16[528,1024]{1,0:T(8,128)(2,1)} %copy-done.2) | copy-start | bytes 3244036
  154.7 15.1 %copy-start.5 = (s16[528,1024]{1,0:T(8,128)(2,1)S(1)}, s16[528,1024]{1,0:T(8,128)(2,1)}, u32[]{:S(2)}) copy-start(s16[528,1024]{1,0:T(8,128)(2,1)} %copy-done.4) | copy-start | bytes 3244036
  154.7 15.1 %copy-start.7 = (s16[528,1024]{1,0:T(8,128)(2,1)S(1)}, s16[528,1024]{1,0:T(8,128)(2,1)}, u32[]{:S(2)}) copy-start(s16[528,1024]{1,0:T(8,128)(2,1)} %copy-done.6) | copy-start | bytes 3244036
  154.7 25.8 %collective-permute-start.14 = (s16[528,1024]{1,0:T(8,128)(2,1)S(1)}, s16[528,1024]{1,0:T(8,128)(2,1)S(1)}, u32[]{:S(2)}, u32[]{:S(2)}) collective-permute-start(s16[528,1024]{1,0:T(8,128)(2,1)S(1)} %add.17.rest_0_), channel_id=1, source_target_pairs={{8,16},{16,8},{9,17},{17,9},{10,18},{18,10},{11,19},{19,11},{12,20... | collective-permute-start | bytes 3244040 | tf_op jit(solution)/shard_map/ppermute | solution.py:249
  159.2 33.6 %collective-permute-start.15 = (s16[528,1024]{1,0:T(8,128)(2,1)}, s16[528,1024]{1,0:T(8,128)(2,1)S(1)}, u32[]{:S(2)}, u32[]{:S(2)}) collective-permute-start(s16[528,1024]{1,0:T(8,128)(2,1)} %add.18), channel_id=1, source_target_pairs={{8,0},{16,24},{9,1},{17,25},{10,2},{18,26},{11,3},{19,27},{12,4},{... | collective-permute-start | bytes 3244040 | tf_op jit(solution)/shard_map/ppermute | solution.py:243
  182.5 33.5 %collective-permute-start.17 = (s16[528,1024]{1,0:T(8,128)(2,1)S(1)}, s16[528,1024]{1,0:T(8,128)(2,1)S(1)}, u32[]{:S(2)}, u32[]{:S(2)}) collective-permute-start(s16[528,1024]{1,0:T(8,128)(2,1)S(1)} %add.20), channel_id=1, source_target_pairs={{8,0},{16,24},{9,1},{17,25},{10,2},{18,26},{11,3},{19,27},{12,4},{... | collective-permute-start | bytes 3244040 | tf_op jit(solution)/shard_map/ppermute | solution.py:243
  183.8 18.2 %collective-permute-start.16 = (s16[528,512]{1,0:T(8,128)(2,1)S(1)}, s16[528,512]{1,0:T(8,128)(2,1)S(1)}, u32[]{:S(2)}, u32[]{:S(2)}) collective-permute-start(s16[528,512]{1,0:T(8,128)(2,1)S(1)} %add.19.rest_0_), channel_id=1, source_target_pairs={{8,16},{16,8},{9,17},{17,9},{10,18},{18,10},{11,19},{19,11},{12,20... | collective-permute-start | bytes 1622024 | tf_op jit(solution)/shard_map/ppermute | solution.py:249
  204.2 21.6 %collective-permute-start.18 = (s16[528,512]{1,0:T(8,128)(2,1)S(1)}, s16[528,512]{1,0:T(8,128)(2,1)S(1)}, u32[]{:S(2)}, u32[]{:S(2)}) collective-permute-start(s16[528,512]{1,0:T(8,128)(2,1)S(1)} %add.21), channel_id=1, source_target_pairs={{8,0},{16,24},{9,1},{17,25},{10,2},{18,26},{11,3},{19,27},{12,4},{... | collective-permute-start | bytes 1622024 | tf_op jit(solution)/shard_map/ppermute | solution.py:243
  216.1 9.7 %copy-start.1 = (bf16[512,2048]{1,0:T(8,128)(2,1)S(1)}, bf16[512,2048]{1,0:T(8,128)(2,1)}, u32[]{:S(2)}) copy-start(bf16[512,2048]{1,0:T(8,128)(2,1)} %all-gather.2.cloned.1.call-done.back_ref) | copy-start | bytes 6291460
Sparse Core Ops, SparseCore 0:
  24.9 74.9 all-gather.1

commit v4 on v3

--- a/solution.py
+++ b/solution.py
@@ -140,6 +140,8 @@
     count = deltas.shape[0]
     share = count // devices
     col, row = place_ref[0], place_ref[1]
+    owned = hidden_ref.shape[0]
+    ahead = (count // owned - 1 - row) * owned
 
     @pl.when(step == 0)
     def _():
@@ -155,14 +157,13 @@
             gate, up = both[:, :width], both[:, width:]
             slot = at // share
             other = (slot % (devices // 2)) * 2 + slot // (devices // 2)
-            start = pl.multiple_of(jnp.bitwise_xor(col, other) * share + at % share, size)
+            start = pl.multiple_of(ahead + jnp.bitwise_xor(col, other) * share + at % share, size)
             back = back_ref[pl.ds(start, size), :].astype(jnp.float32)
             sig = jax.nn.sigmoid(gate)
             silu = gate * sig
             hidden[rows, :] = (silu * up).astype(jnp.bfloat16)
             deltas[rows, :width] = (back * up * sig * (1.0 + gate * (1.0 - sig))).astype(jnp.bfloat16)
             deltas[rows, width:] = (back * silu).astype(jnp.bfloat16)
-        owned = hidden_ref.shape[0]
         for at in range(0, owned, share):
             other = jnp.bitwise_xor(col, row * (owned // share) + at // share)
             slot = (other % 2) * (devices // 2) + other // 2
@@ -192,7 +193,7 @@
             grid=(width // part, depth // deep),
             in_specs=[
                 pl.BlockSpec((deep, count), lambda j, m, place, mask: (m, 0)),
-                pl.BlockSpec((count, part), lambda j, m, place, mask: (0, start // part + j)),
+                pl.BlockSpec((back.shape[0], part), lambda j, m, place, mask: (0, start // part + j)),
             ]
             + [message] * len(coded)
             + [pl.BlockSpec(memory_space=pl.ANY)] * len(previous),
@@ -218,11 +219,11 @@
     return lax.select(jnp.broadcast_to(condition, a.shape), a, b)
 
 
-def gather_tokens(tokens, devices):
+def gather_tokens(tokens, devices, others):
     pieces = [tokens]
     for other in range(2, devices, 2):
         pieces.append(lax.ppermute(tokens, "col", [(i, i ^ other) for i in range(devices)]))
-    mine = jnp.concatenate(pieces, axis=0)
+    mine = tie(jnp.concatenate(pieces, axis=0), *others)
     return jnp.concatenate([mine, lax.ppermute(mine, "col", [(i, i ^ 1) for i in range(devices)])], axis=0)
 
 
@@ -248,13 +249,19 @@
     def swap(value):
         return lax.ppermute(value, "row", [(left, right), (right, left)])
 
-    back = lax.all_gather(hidden_grad, "row", axis=0, tiled=True)
-    gathered = gather_tokens(tokens, devices)
 
     part = part_width(local)
     widths = chunk_widths(local)
     starts = [sum(widths[:c]) for c in range(len(widths))]
     chunks = len(widths)
+    before, after = [hidden_grad], [hidden_grad]
+
+    def pass_on(sources):
+        before.append(lax.ppermute(sources[0], "row", [(i, i + 1) for i in range(ring - 1)]))
+        after.append(lax.ppermute(sources[1], "row", [(i + 1, i) for i in range(ring - 1)]))
+
+    pass_on((hidden_grad, hidden_grad))
+    gathered = gather_tokens(tokens, devices, (before[-1], after[-1]))
     own, came, sums, across, terms = [], [], [], [], []
     outs = ()
     turned = None
@@ -299,9 +306,16 @@
         terms.append(parts)
 
     ahead = min(AHEAD, chunks)
-    for c in range(min(ahead, chunks)):
+    for hop in range(2, ring):
+        if hop == 2:
+            pass_on((before[-1], after[-1]))
+            run_forward(0)
+        else:
+            pass_on(lax.optimization_barrier((before[-1], after[-1], place))[:2])
+    for c in range(len(own), ahead):
         run_forward(c)
     turned = ordered(turn, gathered)
+    back = jnp.concatenate(lax.optimization_barrier((*before[:0:-1], *after, place))[:-1], axis=0)
     for c in range(chunks + 2):
         if c < chunks:
             run_in(c)

time: 238 us -> 224 us (0.941)
  starting transfers between devices: 44.8 us -> 58.7 us
  between operations: 14.4 us -> 1.2 us
  waiting for transfers between devices: 87.5 us -> 77.8 us
  Pallas kernels: 83.2 us -> 80 us
    ppermute x5, waiting for transfers between devices: 43.1 us -> 13.2 us  [inward(): lax.ppermute(value, 'row', [(left - hop - 1, left - hop), (right + hop +...]
    ppermute x0 -> x6, waiting for transfers between devices: none -> 23.5 us  [the longest x3 23.4 us: pass_on(): lax.ppermute(sources[0], 'row', [(i, i + 1) for i in range(ring - 1)])]
    ppermute x0 -> x6, starting transfers between devices: none -> 16.2 us  [the longest x3 12.3 us: pass_on(): lax.ppermute(sources[0], 'row', [(i, i + 1) for i in range(ring - 1)])]
    pallas_call x10, Pallas kernels: 22.5 us -> 18.9 us  [add(): pl.pallas_call(add_kernel, grid_spec=pltpu.PrefetchScalarGridSpec(num_sca...]
    ppermute x1, waiting for transfers between devices: 2.43 us -> 0.01 us  [gather_tokens(): lax.ppermute(mine, 'col', [(i, i ^ 1) for i in range(devices)])]
    unnamed x36 -> x29, local copies, waits for them, and re-layouts: 5.67 us -> 3.4 us
  transfers between devices with their start and end apart: 20 -> 25, of which waited for: 11 -> 10; matrix products, arithmetic and copies ran while one was open for 0% -> 1% of each run, Pallas kernels for 33% -> 34%
where the time goes in v4:
time: 224 us; the launch traced here: 222 us
  Pallas kernels  80 us (36%)
  waiting for transfers between devices  77.8 us (35%)
  starting transfers between devices  58.7 us (26%)
  local copies, waits for them, and re-layouts  3.53 us (2%)
    pallas_call x5, Pallas kernels, weight_grads(): pl.pallas_call(functools.partial(weights_kernel, first=start // BLOCK, te...  34.8 us
    ppermute x5, waiting for transfers between devices, outward(): lax.ppermute(value, 'row', [(left - hop, left - hop - 1), (right + hop, r...  29.9 us
    ppermute x5, starting transfers between devices, inward(): lax.ppermute(value, 'row', [(left - hop - 1, left - hop), (right + hop +...  27.6 us
    pallas_call x5, Pallas kernels, forward(): pl.pallas_call(functools.partial(forward_kernel, first=start // BLOCK), g...  24.8 us
    ppermute x3, waiting for transfers between devices, pass_on(): lax.ppermute(sources[0], 'row', [(i, i + 1) for i in range(ring - 1)])  23.4 us
    pallas_call x10, Pallas kernels, add(): pl.pallas_call(add_kernel, grid_spec=pltpu.PrefetchScalarGridSpec(num_sca...  18.9 us
    ppermute x5, waiting for transfers between devices, inward(): lax.ppermute(value, 'row', [(left - hop - 1, left - hop), (right + hop +...  13.2 us
    ppermute x3, starting transfers between devices, pass_on(): lax.ppermute(sources[0], 'row', [(i, i + 1) for i in range(ring - 1)])  12.3 us
  transfers between devices with their start and end apart: 25, of which 10 were waited for; matrix products, arithmetic and copies ran while one was open for 1% of the time, Pallas kernels for 34%

profile of v4, /device:TPU:0, one launch (start us, length us, event | category | flops | bytes accessed | tf_op | source)
XLA Modules:
  0.0 222.4 jit_solution(16723711203866183448)
XLA Ops:
  0.6 5.0 %collective-permute-start.3 = (bf16[128,2048]{1,0:T(8,128)(2,1)}, bf16[128,2048]{1,0:T(8,128)(2,1)S(1)}, u32[]{:S(2)}, u32[]{:S(2)}) collective-permute-start(bf16[128,2048]{1,0:T(8,128)(2,1)} %param.9), channel_id=1, source_target_pairs={{0,8},{8,16},{16,24},{1,9},{9,17},{17,25},{2,10},{10,18},{18,26},{... | collective-permute-start | bytes 1572872 | tf_op jit(solution)/shard_map/ppermute | solution.py:260
  5.6 1.3 collective-permute-start.4
  6.9 1.6 collective-permute-start.1
  8.5 1.5 collective-permute-start
  10.5 5.1 %collective-permute-done.1 = bf16[64,2048]{1,0:T(8,128)(2,1)S(1)} collective-permute-done((bf16[64,2048]{1,0:T(8,128)(2,1)}, bf16[64,2048]{1,0:T(8,128)(2,1)S(1)}, u32[]{:S(2)}, u32[]{:S(2)}) %collective-permute-start.1) | collective-permute-done | bytes 262176 | tf_op jit(solution)/shard_map/ppermute | solution.py:225
  15.5 2.4 %collective-permute-done = bf16[64,2048]{1,0:T(8,128)(2,1)S(1)} collective-permute-done((bf16[64,2048]{1,0:T(8,128)(2,1)}, bf16[64,2048]{1,0:T(8,128)(2,1)S(1)}, u32[]{:S(2)}, u32[]{:S(2)}) %collective-permute-start) | collective-permute-done | bytes 262176 | tf_op jit(solution)/shard_map/ppermute | solution.py:225
  18.0 3.8 %collective-permute-done.2 = bf16[64,2048]{1,0:T(8,128)(2,1)S(1)} collective-permute-done((bf16[64,2048]{1,0:T(8,128)(2,1)}, bf16[64,2048]{1,0:T(8,128)(2,1)S(1)}, u32[]{:S(2)}, u32[]{:S(2)}) %collective-permute-start.2) | collective-permute-done | bytes 262176 | tf_op jit(solution)/shard_map/ppermute | solution.py:225
  23.0 4.3 %collective-permute-start.11 = (bf16[128,2048]{1,0:T(8,128)(2,1)S(1)}, bf16[128,2048]{1,0:T(8,128)(2,1)S(1)}, u32[]{:S(2)}, u32[]{:S(2)}) collective-permute-start(bf16[128,2048]{1,0:T(8,128)(2,1)S(1)} %collective-permute-done.3), channel_id=1, source_target_pairs={{0,8},{8,16},{16,24},{1,9},{9,17},{17,25},{2,10},{10,18},{18,26},{... | collective-permute-start | bytes 1572872 | tf_op jit(solution)/shard_map/ppermute | solution.py:260
  27.3 1.3 collective-permute-start.12
  28.9 3.9 %forward.5.a_ref = s16[528,512]{1,0:T(8,128)(2,1)S(1)} custom-call(s32[2]{0:T(128)S(1)} %pad_add_fusion.place_ref, s32[16,16]{1,0:T(8,128)S(1)} %copy-done, bf16[512,2048]{1,0:T(8,128)(2,1)S(1)} %constant_dynamic-update-slice_fusion.tokens_ref.value_ref, bf16[2048,2048]{1,0:T(8,128)(2,1)} %gate_ref.9, bf16[2048,2048]{1,0:T(8,128)(2,1)} %up_ref.9), custom_call_target="tpu_custom_call" | custom-call | flops 4000000000 | bytes 10000000 | tf_op jit(solution)/shard_map/forward/pallas_call | solution.py:77
  32.8 4.6 %collective-permute-start.6 = (s16[528,512]{1,0:T(8,128)(2,1)S(1)}, s16[528,512]{1,0:T(8,128)(2,1)S(1)}, u32[]{:S(2)}, u32[]{:S(2)}) collective-permute-start(s16[528,512]{1,0:T(8,128)(2,1)S(1)} %forward.5.a_ref), channel_id=1, source_target_pairs={{0,8},{24,16},{1,9},{25,17},{2,10},{26,18},{3,11},{27,19},{4,12},{... | collective-permute-start | bytes 1622024 | tf_op jit(solution)/shard_map/ppermute | solution.py:247
  37.4 5.7 %forward.6.a_ref = s16[528,1024]{1,0:T(8,128)(2,1)S(1)} custom-call(s32[2]{0:T(128)S(1)} %pad_add_fusion.place_ref, s32[16,16]{1,0:T(8,128)S(1)} %copy-done, bf16[512,2048]{1,0:T(8,128)(2,1)S(1)} %constant_dynamic-update-slice_fusion.tokens_ref.value_ref, bf16[2048,2048]{1,0:T(8,128)(2,1)} %gate_ref.9, bf16[2048,2048]{1,0:T(8,128)(2,1)} %up_ref.9), custom_call_target="tpu_custom_call" | custom-call | flops 4000000000 | bytes 10000000 | tf_op jit(solution)/shard_map/forward/pallas_call | solution.py:77
  43.0 1.4 collective-permute-start.7
  44.4 3.0 %collective-permute-start.13 = (bf16[128,2048]{1,0:T(8,128)(2,1)S(1)}, bf16[128,2048]{1,0:T(8,128)(2,1)}, u32[]{:S(2)}, u32[]{:S(2)}) collective-permute-start(bf16[128,2048]{1,0:T(8,128)(2,1)S(1)} %collective-permute-done.11), channel_id=1, source_target_pairs={{0,8},{8,16},{16,24},{1,9},{9,17},{17,25},{2,10},{10,18},{18,26},{... | collective-permute-start | bytes 1572872 | tf_op jit(solution)/shard_map/ppermute | solution.py:260
  47.5 1.3 collective-permute-start.14
  48.8 5.7 %forward.7.a_ref = s16[528,1024]{1,0:T(8,128)(2,1)S(1)} custom-call(s32[2]{0:T(128)S(1)} %pad_add_fusion.place_ref, s32[16,16]{1,0:T(8,128)S(1)} %copy-done, bf16[512,2048]{1,0:T(8,128)(2,1)S(1)} %constant_dynamic-update-slice_fusion.tokens_ref.value_ref, bf16[2048,2048]{1,0:T(8,128)(2,1)} %gate_ref.9, bf16[2048,2048]{1,0:T(8,128)(2,1)} %up_ref.9), custom_call_target="tpu_custom_call" | custom-call | flops 4000000000 | bytes 10000000 | tf_op jit(solution)/shard_map/forward/pallas_call | solution.py:77
  54.5 5.7 %forward.8.a_ref = s16[528,1024]{1,0:T(8,128)(2,1)S(1)} custom-call(s32[2]{0:T(128)S(1)} %pad_add_fusion.place_ref, s32[16,16]{1,0:T(8,128)S(1)} %copy-done, bf16[512,2048]{1,0:T(8,128)(2,1)S(1)} %constant_dynamic-update-slice_fusion.tokens_ref.value_ref, bf16[2048,2048]{1,0:T(8,128)(2,1)} %gate_ref.9, bf16[2048,2048]{1,0:T(8,128)(2,1)} %up_ref.9), custom_call_target="tpu_custom_call" | custom-call | flops 4000000000 | bytes 10000000 | tf_op jit(solution)/shard_map/forward/pallas_call | solution.py:77
  60.2 1.5 turn.1.turned_ref
  61.7 23.4 %collective-permute-done.13 = bf16[128,2048]{1,0:T(8,128)(2,1)} collective-permute-done((bf16[128,2048]{1,0:T(8,128)(2,1)S(1)}, bf16[128,2048]{1,0:T(8,128)(2,1)}, u32[]{:S(2)}, u32[]{:S(2)}) %collective-permute-start.13) | collective-permute-done | bytes 524320 | tf_op jit(solution)/shard_map/ppermute | solution.py:260
  88.5 10.5 %collective-permute-start.9 = (s16[528,1024]{1,0:T(8,128)(2,1)S(1)}, s16[528,1024]{1,0:T(8,128)(2,1)S(1)}, u32[]{:S(2)}, u32[]{:S(2)}) collective-permute-start(s16[528,1024]{1,0:T(8,128)(2,1)S(1)} %forward.7.a_ref), channel_id=1, source_target_pairs={{0,8},{24,16},{1,9},{25,17},{2,10},{26,18},{3,11},{27,19},{4,12},{... | collective-permute-start | bytes 3244040 | tf_op jit(solution)/shard_map/ppermute | solution.py:247
  98.9 3.9 %forward.9.a_ref = s16[528,512]{1,0:T(8,128)(2,1)S(1)} custom-call(s32[2]{0:T(128)S(1)} %pad_add_fusion.place_ref, s32[16,16]{1,0:T(8,128)S(1)} %copy-done, bf16[512,2048]{1,0:T(8,128)(2,1)S(1)} %constant_dynamic-update-slice_fusion.tokens_ref.value_ref, bf16[2048,2048]{1,0:T(8,128)(2,1)} %gate_ref.9, bf16[2048,2048]{1,0:T(8,128)(2,1)} %up_ref.9), custom_call_target="tpu_custom_call" | custom-call | flops 4000000000 | bytes 10000000 | tf_op jit(solution)/shard_map/forward/pallas_call | solution.py:77
  102.9 1.9 add.13.rest_0_
  105.7 1.8 copy-done.3
  108.6 1.3 collective-permute-start.15
  109.9 4.8 %collective-permute-start.16 = (s16[528,1024]{1,0:T(8,128)(2,1)S(1)}, s16[528,1024]{1,0:T(8,128)(2,1)S(1)}, u32[]{:S(2)}, u32[]{:S(2)}) collective-permute-start(s16[528,1024]{1,0:T(8,128)(2,1)S(1)} %forward.8.a_ref), channel_id=1, source_target_pairs={{0,8},{24,16},{1,9},{25,17},{2,10},{26,18},{3,11},{27,19},{4,12},{... | collective-permute-start | bytes 3244040 | tf_op jit(solution)/shard_map/ppermute | solution.py:247
  114.7 8.5 %collective-permute-done.9.b_ref = s16[528,1024]{1,0:T(8,128)(2,1)S(1)} collective-permute-done((s16[528,1024]{1,0:T(8,128)(2,1)S(1)}, s16[528,1024]{1,0:T(8,128)(2,1)S(1)}, u32[]{:S(2)}, u32[]{:S(2)}) %collective-permute-start.9) | collective-permute-done | bytes 1081376 | tf_op jit(solution)/shard_map/ppermute | solution.py:247
  123.1 1.9 add.15.rest_0_
  126.0 6.4 %collective-permute-start.19 = (s16[528,512]{1,0:T(8,128)(2,1)S(1)}, s16[528,512]{1,0:T(8,128)(2,1)}, u32[]{:S(2)}, u32[]{:S(2)}) collective-permute-start(s16[528,512]{1,0:T(8,128)(2,1)S(1)} %forward.9.a_ref), channel_id=1, source_target_pairs={{0,8},{24,16},{1,9},{25,17},{2,10},{26,18},{3,11},{27,19},{4,12},{... | collective-permute-start | bytes 1622024 | tf_op jit(solution)/shard_map/ppermute | solution.py:247
  132.4 2.8 %add.16 = s16[528,1024]{1,0:T(8,128)(2,1)} custom-call(s32[2]{0:T(128)S(1)} %pad_add_fusion.place_ref, s16[528,1024]{1,0:T(8,128)(2,1)S(1)} %forward.6.a_ref, s16[528,1024]{1,0:T(8,128)(2,1)S(1)} %collective-permute-done.10.b_ref.rest_1_), custom_call_target="tpu_custom_call" | custom-call | flops 4000000000 | bytes 10000000 | tf_op jit(solution)/shard_map/add/pallas_call | solution.py:100
  135.2 1.3 collective-permute-start.18
  136.5 5.1 %weight_grads.5 = (bf16[128,2048]{1,0:T(8,128)(2,1)}, f32[2048,2048]{1,0:T(8,128)}, f32[2048,2048]{1,0:T(8,128)}) custom-call(s32[2]{0:T(128)S(1)} %pad_add_fusion.place_ref, s32[16,16]{1,0:T(8,128)S(1)} %copy-done, bf16[2048,512]{1,0:T(8,128)(2,1)S(1)} %turn.1.turned_ref, bf16[896,2048]{1,0:T(8,128)(2,1)} %copy-done.3, s16[528,512]{1,0:T(8,128)(2,1)S(1)} %copy-done.2, ...), custom_call_target="tpu_custom_call" | custom-call | flops 4000000000 | bytes 10000000 | tf_op jit(solution)/shard_map/weight_grads/pallas_call | solution.py:189
  141.6 4.7 %collective-permute-done.16.b_ref = s16[528,1024]{1,0:T(8,128)(2,1)S(1)} collective-permute-done((s16[528,1024]{1,0:T(8,128)(2,1)S(1)}, s16[528,1024]{1,0:T(8,128)(2,1)S(1)}, u32[]{:S(2)}, u32[]{:S(2)}) %collective-permute-start.16) | collective-permute-done | bytes 1081376 | tf_op jit(solution)/shard_map/ppermute | solution.py:247
  146.3 1.9 add.17.rest_0_
  148.3 1.6 collective-permute-start.20
  149.9 1.9 add.18
  151.9 1.3 collective-permute-start.21
  153.2 7.4 %collective-permute-done.18.rest_2_ = s16[528,1024]{1,0:T(8,128)(2,1)S(1)} collective-permute-done((s16[528,1024]{1,0:T(8,128)(2,1)}, s16[528,1024]{1,0:T(8,128)(2,1)S(1)}, u32[]{:S(2)}, u32[]{:S(2)}) %collective-permute-start.18) | collective-permute-done | bytes 1081376 | tf_op jit(solution)/shard_map/ppermute | solution.py:244
  160.5 7.9 %weight_grads.6 = (bf16[128,2048]{1,0:T(8,128)(2,1)}, f32[2048,2048]{1,0:T(8,128)}, f32[2048,2048]{1,0:T(8,128)}) custom-call(s32[2]{0:T(128)S(1)} %pad_add_fusion.place_ref, s32[16,16]{1,0:T(8,128)S(1)} %copy-done, bf16[2048,512]{1,0:T(8,128)(2,1)S(1)} %turn.1.turned_ref, ...), custom_call_target="tpu_custom_call", output_to_operand_aliasing={{0}: (7, {}), {1}: (8, {}), {2}: (9, {})} | custom-call | flops 4000000000 | bytes 10000000 | tf_op jit(solution)/shard_map/weight_grads/pallas_call | solution.py:189
  168.5 2.2 add.19.rest_0_
  170.7 2.9 %add.20 = s16[528,1024]{1,0:T(8,128)(2,1)S(1)} custom-call(s32[2]{0:T(128)S(1)} %pad_add_fusion.place_ref, s16[528,1024]{1,0:T(8,128)(2,1)S(1)} %forward.8.a_ref, s16[528,1024]{1,0:T(8,128)(2,1)} %collective-permute-done.20.b_ref.rest_1_), custom_call_target="tpu_custom_call" | custom-call | flops 4000000000 | bytes 10000000 | tf_op jit(solution)/shard_map/add/pallas_call | solution.py:100
  173.5 1.3 collective-permute-start.23
  175.5 7.3 %collective-permute-done.21.rest_2_ = s16[528,1024]{1,0:T(8,128)(2,1)S(1)} collective-permute-done((s16[528,1024]{1,0:T(8,128)(2,1)S(1)}, s16[528,1024]{1,0:T(8,128)(2,1)S(1)}, u32[]{:S(2)}, u32[]{:S(2)}) %collective-permute-start.21) | collective-permute-done | bytes 1081376 | tf_op jit(solution)/shard_map/ppermute | solution.py:244
  182.8 7.9 %weight_grads.7 = (bf16[128,2048]{1,0:T(8,128)(2,1)}, f32[2048,2048]{1,0:T(8,128)}, f32[2048,2048]{1,0:T(8,128)}) custom-call(s32[2]{0:T(128)S(1)} %pad_add_fusion.place_ref, s32[16,16]{1,0:T(8,128)S(1)} %copy-done, bf16[2048,512]{1,0:T(8,128)(2,1)S(1)} %turn.1.turned_ref, ...), custom_call_target="tpu_custom_call", output_to_operand_aliasing={{0}: (7, {}), {1}: (8, {}), {2}: (9, {})} | custom-call | flops 4000000000 | bytes 10000000 | tf_op jit(solution)/shard_map/weight_grads/pallas_call | solution.py:189
  191.8 1.5 collective-permute-start.24
  193.4 13.9 %collective-permute-done.23.rest_2_ = s16[528,1024]{1,0:T(8,128)(2,1)S(1)} collective-permute-done((s16[528,1024]{1,0:T(8,128)(2,1)S(1)}, s16[528,1024]{1,0:T(8,128)(2,1)S(1)}, u32[]{:S(2)}, u32[]{:S(2)}) %collective-permute-start.23) | collective-permute-done | bytes 1081376 | tf_op jit(solution)/shard_map/ppermute | solution.py:244
  207.3 8.7 %weight_grads.8 = (bf16[128,2048]{1,0:T(8,128)(2,1)}, f32[2048,2048]{1,0:T(8,128)}, f32[2048,2048]{1,0:T(8,128)}) custom-call(s32[2]{0:T(128)S(1)} %pad_add_fusion.place_ref, s32[16,16]{1,0:T(8,128)S(1)} %copy-done, bf16[2048,512]{1,0:T(8,128)(2,1)S(1)} %turn.1.turned_ref, ...), custom_call_target="tpu_custom_call", output_to_operand_aliasing={{0}: (7, {}), {1}: (8, {}), {2}: (9, {})} | custom-call | flops 4000000000 | bytes 10000000 | tf_op jit(solution)/shard_map/weight_grads/pallas_call | solution.py:189
  216.0 1.3 collective-permute-done.24.rest_2_
  217.3 5.1 %weight_grads.9 = (bf16[128,2048]{1,0:T(8,128)(2,1)}, f32[2048,2048]{1,0:T(8,128)}, f32[2048,2048]{1,0:T(8,128)}) custom-call(s32[2]{0:T(128)S(1)} %pad_add_fusion.place_ref, s32[16,16]{1,0:T(8,128)S(1)} %copy-done, bf16[2048,512]{1,0:T(8,128)(2,1)S(1)} %turn.1.turned_ref, ...), custom_call_target="tpu_custom_call", output_to_operand_aliasing={{0}: (7, {}), {1}: (8, {}), {2}: (9, {})} | custom-call | flops 4000000000 | bytes 10000000 | tf_op jit(solution)/shard_map/weight_grads/pallas_call | solution.py:189
  (56 shorter events, 9.8 us)
Async XLA Ops:
  0.6 28.2 %copy-start = (s32[16,16]{1,0:T(8,128)S(1)}, s32[16,16]{1,0:T(8,128)}, u32[]{:S(2)}) copy-start(s32[16,16]{1,0:T(8,128)} %mask_ref.19) | copy-start | bytes 3076
  0.6 22.2 %collective-permute-start.3 = (bf16[128,2048]{1,0:T(8,128)(2,1)}, bf16[128,2048]{1,0:T(8,128)(2,1)S(1)}, u32[]{:S(2)}, u32[]{:S(2)}) collective-permute-start(bf16[128,2048]{1,0:T(8,128)(2,1)} %param.9), channel_id=1, source_target_pairs={{0,8},{8,16},{16,24},{1,9},{9,17},{17,25},{2,10},{10,18},{18,26},{... | collective-permute-start | bytes 1572872 | tf_op jit(solution)/shard_map/ppermute | solution.py:260
  5.6 17.3 %collective-permute-start.4 = (bf16[128,2048]{1,0:T(8,128)(2,1)}, bf16[128,2048]{1,0:T(8,128)(2,1)S(1)}, u32[]{:S(2)}, u32[]{:S(2)}) collective-permute-start(bf16[128,2048]{1,0:T(8,128)(2,1)} %param.9), channel_id=1, source_target_pairs={{8,0},{16,8},{24,16},{9,1},{17,9},{25,17},{10,2},{18,10},{26,18},{... | collective-permute-start | bytes 1572872 | tf_op jit(solution)/shard_map/ppermute | solution.py:261
  6.9 8.6 %collective-permute-start.1 = (bf16[64,2048]{1,0:T(8,128)(2,1)}, bf16[64,2048]{1,0:T(8,128)(2,1)S(1)}, u32[]{:S(2)}, u32[]{:S(2)}) collective-permute-start(bf16[64,2048]{1,0:T(8,128)(2,1)} %param.5), channel_id=1, source_target_pairs={{0,4},{1,5},{2,6},{3,7},{4,0},{5,1},{6,2},{7,3},{8,12},{9,13},{10,... | collective-permute-start | bytes 786440 | tf_op jit(solution)/shard_map/ppermute | solution.py:225
  8.5 9.5 %collective-permute-start = (bf16[64,2048]{1,0:T(8,128)(2,1)}, bf16[64,2048]{1,0:T(8,128)(2,1)S(1)}, u32[]{:S(2)}, u32[]{:S(2)}) collective-permute-start(bf16[64,2048]{1,0:T(8,128)(2,1)} %param.5), channel_id=1, source_target_pairs={{0,2},{1,3},{2,0},{3,1},{4,6},{5,7},{6,4},{7,5},{8,10},{9,11},{10,... | collective-permute-start | bytes 786440 | tf_op jit(solution)/shard_map/ppermute | solution.py:225
  10.0 11.8 %collective-permute-start.2 = (bf16[64,2048]{1,0:T(8,128)(2,1)}, bf16[64,2048]{1,0:T(8,128)(2,1)S(1)}, u32[]{:S(2)}, u32[]{:S(2)}) collective-permute-start(bf16[64,2048]{1,0:T(8,128)(2,1)} %param.5), channel_id=1, source_target_pairs={{0,6},{1,7},{2,4},{3,5},{4,2},{5,3},{6,0},{7,1},{8,14},{9,15},{10,... | collective-permute-start | bytes 786440 | tf_op jit(solution)/shard_map/ppermute | solution.py:225
  22.9 9.9 %copy-start.5 = (bf16[128,2048]{1,0:T(8,128)(2,1)}, bf16[128,2048]{1,0:T(8,128)(2,1)S(1)}, u32[]{:S(2)}) copy-start(bf16[128,2048]{1,0:T(8,128)(2,1)S(1)} %collective-permute-done.3) | copy-start | bytes 1572868
  22.9 5.9 %collective-permute-start.5 = (bf16[256,2048]{1,0:T(8,128)(2,1)S(1)}, bf16[256,2048]{1,0:T(8,128)(2,1)S(1)}, u32[]{:S(2)}, u32[]{:S(2)}) collective-permute-start(bf16[256,2048]{1,0:T(8,128)(2,1)S(1)} %pad_maximum_fusion), channel_id=1, source_target_pairs={{0,1},{1,0},{2,3},{3,2},{4,5},{5,4},{6,7},{7,6},{8,9},{9,8},{10,11... | collective-permute-start | bytes 3145736 | tf_op jit(solution)/shard_map/ppermute | solution.py:227
  23.0 21.4 %collective-permute-start.11 = (bf16[128,2048]{1,0:T(8,128)(2,1)S(1)}, bf16[128,2048]{1,0:T(8,128)(2,1)S(1)}, u32[]{:S(2)}, u32[]{:S(2)}) collective-permute-start(bf16[128,2048]{1,0:T(8,128)(2,1)S(1)} %collective-permute-done.3), channel_id=1, source_target_pairs={{0,8},{8,16},{16,24},{1,9},{9,17},{17,25},{2,10},{10,18},{18,26},{... | collective-permute-start | bytes 1572872 | tf_op jit(solution)/shard_map/ppermute | solution.py:260
  27.3 17.1 %collective-permute-start.12 = (bf16[128,2048]{1,0:T(8,128)(2,1)S(1)}, bf16[128,2048]{1,0:T(8,128)(2,1)S(1)}, u32[]{:S(2)}, u32[]{:S(2)}) collective-permute-start(bf16[128,2048]{1,0:T(8,128)(2,1)S(1)} %collective-permute-done.4), channel_id=1, source_target_pairs={{8,0},{16,8},{24,16},{9,1},{17,9},{25,17},{10,2},{18,10},{26,18},{... | collective-permute-start | bytes 1572872 | tf_op jit(solution)/shard_map/ppermute | solution.py:261
  32.8 53.8 %collective-permute-start.6 = (s16[528,512]{1,0:T(8,128)(2,1)S(1)}, s16[528,512]{1,0:T(8,128)(2,1)S(1)}, u32[]{:S(2)}, u32[]{:S(2)}) collective-permute-start(s16[528,512]{1,0:T(8,128)(2,1)S(1)} %forward.5.a_ref), channel_id=1, source_target_pairs={{0,8},{24,16},{1,9},{25,17},{2,10},{26,18},{3,11},{27,19},{4,12},{... | collective-permute-start | bytes 1622024 | tf_op jit(solution)/shard_map/ppermute | solution.py:247
  43.0 59.8 %collective-permute-start.7 = (s16[528,1024]{1,0:T(8,128)(2,1)S(1)}, s16[528,1024]{1,0:T(8,128)(2,1)S(1)}, u32[]{:S(2)}, u32[]{:S(2)}) collective-permute-start(s16[528,1024]{1,0:T(8,128)(2,1)S(1)} %forward.6.a_ref), channel_id=1, source_target_pairs={{0,8},{24,16},{1,9},{25,17},{2,10},{26,18},{3,11},{27,19},{4,12},{... | collective-permute-start | bytes 3244040 | tf_op jit(solution)/shard_map/ppermute | solution.py:247
  44.4 10.0 %copy-start.7 = (bf16[128,2048]{1,0:T(8,128)(2,1)}, bf16[128,2048]{1,0:T(8,128)(2,1)S(1)}, u32[]{:S(2)}) copy-start(bf16[128,2048]{1,0:T(8,128)(2,1)S(1)} %collective-permute-done.12) | copy-start | bytes 1572868
  44.4 40.7 %collective-permute-start.13 = (bf16[128,2048]{1,0:T(8,128)(2,1)S(1)}, bf16[128,2048]{1,0:T(8,128)(2,1)}, u32[]{:S(2)}, u32[]{:S(2)}) collective-permute-start(bf16[128,2048]{1,0:T(8,128)(2,1)S(1)} %collective-permute-done.11), channel_id=1, source_target_pairs={{0,8},{8,16},{16,24},{1,9},{9,17},{17,25},{2,10},{10,18},{18,26},{... | collective-permute-start | bytes 1572872 | tf_op jit(solution)/shard_map/ppermute | solution.py:260
  47.5 37.6 %collective-permute-start.14 = (bf16[128,2048]{1,0:T(8,128)(2,1)S(1)}, bf16[128,2048]{1,0:T(8,128)(2,1)S(1)}, u32[]{:S(2)}, u32[]{:S(2)}) collective-permute-start(bf16[128,2048]{1,0:T(8,128)(2,1)S(1)} %collective-permute-done.12), channel_id=1, source_target_pairs={{8,0},{16,8},{24,16},{9,1},{17,9},{25,17},{10,2},{18,10},{26,18},{... | collective-permute-start | bytes 1572872 | tf_op jit(solution)/shard_map/ppermute | solution.py:261
  60.1 26.3 %copy-start.6 = (bf16[128,2048]{1,0:T(8,128)(2,1)S(1)}, bf16[128,2048]{1,0:T(8,128)(2,1)}, u32[]{:S(2)}) copy-start(bf16[128,2048]{1,0:T(8,128)(2,1)} %copy-done.5) | copy-start | bytes 1572868
  60.2 26.3 %copy-start.4 = (bf16[128,2048]{1,0:T(8,128)(2,1)S(1)}, bf16[128,2048]{1,0:T(8,128)(2,1)}, u32[]{:S(2)}) copy-start(bf16[128,2048]{1,0:T(8,128)(2,1)} %param.9) | copy-start | bytes 1572868
  85.1 2.6 %copy-start.9 = (bf16[128,2048]{1,0:T(8,128)(2,1)}, bf16[128,2048]{1,0:T(8,128)(2,1)S(1)}, u32[]{:S(2)}) copy-start(bf16[128,2048]{1,0:T(8,128)(2,1)S(1)} %collective-permute-done.14) | copy-start | bytes 1572868
  87.7 15.1 %copy-start.1 = (s16[528,512]{1,0:T(8,128)(2,1)}, s16[528,512]{1,0:T(8,128)(2,1)S(1)}, u32[]{:S(2)}) copy-start(s16[528,512]{1,0:T(8,128)(2,1)S(1)} %add.12.rest_0_) | copy-start | bytes 1622020
  87.8 19.7 %collective-permute-start.8 = (s16[528,512]{1,0:T(8,128)(2,1)S(1)}, s16[528,512]{1,0:T(8,128)(2,1)S(1)}, u32[]{:S(2)}, u32[]{:S(2)}) collective-permute-start(s16[528,512]{1,0:T(8,128)(2,1)S(1)} %add.12.rest_0_), channel_id=1, source_target_pairs={{8,16},{16,8},{9,17},{17,9},{10,18},{18,10},{11,19},{19,11},{12,20... | collective-permute-start | bytes 1622024 | tf_op jit(solution)/shard_map/ppermute | solution.py:250
  88.5 34.7 %collective-permute-start.9 = (s16[528,1024]{1,0:T(8,128)(2,1)S(1)}, s16[528,1024]{1,0:T(8,128)(2,1)S(1)}, u32[]{:S(2)}, u32[]{:S(2)}) collective-permute-start(s16[528,1024]{1,0:T(8,128)(2,1)S(1)} %forward.7.a_ref), channel_id=1, source_target_pairs={{0,8},{24,16},{1,9},{25,17},{2,10},{26,18},{3,11},{27,19},{4,12},{... | collective-permute-start | bytes 3244040 | tf_op jit(solution)/shard_map/ppermute | solution.py:247
  102.8 2.7 %copy-start.8 = (bf16[128,2048]{1,0:T(8,128)(2,1)S(1)}, bf16[128,2048]{1,0:T(8,128)(2,1)}, u32[]{:S(2)}) copy-start(bf16[128,2048]{1,0:T(8,128)(2,1)} %copy-done.7) | copy-start | bytes 1572868
  102.8 2.8 %copy-start.10 = (bf16[128,2048]{1,0:T(8,128)(2,1)S(1)}, bf16[128,2048]{1,0:T(8,128)(2,1)}, u32[]{:S(2)}) copy-start(bf16[128,2048]{1,0:T(8,128)(2,1)} %copy-done.9) | copy-start | bytes 1572868
  104.8 27.6 %collective-permute-start.10 = (s16[528,1024]{1,0:T(8,128)(2,1)S(1)}, s16[528,1024]{1,0:T(8,128)(2,1)S(1)}, u32[]{:S(2)}, u32[]{:S(2)}) collective-permute-start(s16[528,1024]{1,0:T(8,128)(2,1)S(1)} %add.13.rest_0_), channel_id=1, source_target_pairs={{8,16},{16,8},{9,17},{17,9},{10,18},{18,10},{11,19},{19,11},{12,20... | collective-permute-start | bytes 3244040 | tf_op jit(solution)/shard_map/ppermute | solution.py:250
  105.7 1.8 copy-start.3
  108.6 27.9 %collective-permute-start.15 = (s16[528,512]{1,0:T(8,128)(2,1)S(1)}, s16[528,512]{1,0:T(8,128)(2,1)S(1)}, u32[]{:S(2)}, u32[]{:S(2)}) collective-permute-start(s16[528,512]{1,0:T(8,128)(2,1)S(1)} %add.14), channel_id=1, source_target_pairs={{8,0},{16,24},{9,1},{17,25},{10,2},{18,26},{11,3},{19,27},{12,4},{... | collective-permute-start | bytes 1622024 | tf_op jit(solution)/shard_map/ppermute | solution.py:244
  109.9 36.5 %collective-permute-start.16 = (s16[528,1024]{1,0:T(8,128)(2,1)S(1)}, s16[528,1024]{1,0:T(8,128)(2,1)S(1)}, u32[]{:S(2)}, u32[]{:S(2)}) collective-permute-start(s16[528,1024]{1,0:T(8,128)(2,1)S(1)} %forward.8.a_ref), channel_id=1, source_target_pairs={{0,8},{24,16},{1,9},{25,17},{2,10},{26,18},{3,11},{27,19},{4,12},{... | collective-permute-start | bytes 3244040 | tf_op jit(solution)/shard_map/ppermute | solution.py:247
  125.1 11.4 %copy-start.2 = (s16[528,512]{1,0:T(8,128)(2,1)S(1)}, s16[528,512]{1,0:T(8,128)(2,1)}, u32[]{:S(2)}) copy-start(s16[528,512]{1,0:T(8,128)(2,1)} %copy-done.1) | copy-start | bytes 1622020
  125.1 24.8 %collective-permute-start.17 = (s16[528,1024]{1,0:T(8,128)(2,1)S(1)}, s16[528,1024]{1,0:T(8,128)(2,1)S(1)}, u32[]{:S(2)}, u32[]{:S(2)}) collective-permute-start(s16[528,1024]{1,0:T(8,128)(2,1)S(1)} %add.15.rest_0_), channel_id=1, source_target_pairs={{8,16},{16,8},{9,17},{17,9},{10,18},{18,10},{11,19},{19,11},{12,20... | collective-permute-start | bytes 3244040 | tf_op jit(solution)/shard_map/ppermute | solution.py:250
  126.0 42.5 %collective-permute-start.19 = (s16[528,512]{1,0:T(8,128)(2,1)S(1)}, s16[528,512]{1,0:T(8,128)(2,1)}, u32[]{:S(2)}, u32[]{:S(2)}) collective-permute-start(s16[528,512]{1,0:T(8,128)(2,1)S(1)} %forward.9.a_ref), channel_id=1, source_target_pairs={{0,8},{24,16},{1,9},{25,17},{2,10},{26,18},{3,11},{27,19},{4,12},{... | collective-permute-start | bytes 1622024 | tf_op jit(solution)/shard_map/ppermute | solution.py:247
  135.2 25.4 %collective-permute-start.18 = (s16[528,1024]{1,0:T(8,128)(2,1)}, s16[528,1024]{1,0:T(8,128)(2,1)S(1)}, u32[]{:S(2)}, u32[]{:S(2)}) collective-permute-start(s16[528,1024]{1,0:T(8,128)(2,1)} %add.16), channel_id=1, source_target_pairs={{8,0},{16,24},{9,1},{17,25},{10,2},{18,26},{11,3},{19,27},{12,4},{... | collective-permute-start | bytes 3244040 | tf_op jit(solution)/shard_map/ppermute | solution.py:244
  148.3 22.4 %collective-permute-start.20 = (s16[528,1024]{1,0:T(8,128)(2,1)S(1)}, s16[528,1024]{1,0:T(8,128)(2,1)}, u32[]{:S(2)}, u32[]{:S(2)}) collective-permute-start(s16[528,1024]{1,0:T(8,128)(2,1)S(1)} %add.17.rest_0_), channel_id=1, source_target_pairs={{8,16},{16,8},{9,17},{17,9},{10,18},{18,10},{11,19},{19,11},{12,20... | collective-permute-start | bytes 3244040 | tf_op jit(solution)/shard_map/ppermute | solution.py:250
  151.9 30.9 %collective-permute-start.21 = (s16[528,1024]{1,0:T(8,128)(2,1)S(1)}, s16[528,1024]{1,0:T(8,128)(2,1)S(1)}, u32[]{:S(2)}, u32[]{:S(2)}) collective-permute-start(s16[528,1024]{1,0:T(8,128)(2,1)S(1)} %add.18), channel_id=1, source_target_pairs={{8,0},{16,24},{9,1},{17,25},{10,2},{18,26},{11,3},{19,27},{12,4},{... | collective-permute-start | bytes 3244040 | tf_op jit(solution)/shard_map/ppermute | solution.py:244
  173.5 33.8 %collective-permute-start.23 = (s16[528,1024]{1,0:T(8,128)(2,1)S(1)}, s16[528,1024]{1,0:T(8,128)(2,1)S(1)}, u32[]{:S(2)}, u32[]{:S(2)}) collective-permute-start(s16[528,1024]{1,0:T(8,128)(2,1)S(1)} %add.20), channel_id=1, source_target_pairs={{8,0},{16,24},{9,1},{17,25},{10,2},{18,26},{11,3},{19,27},{12,4},{... | collective-permute-start | bytes 3244040 | tf_op jit(solution)/shard_map/ppermute | solution.py:244
  174.8 15.9 %collective-permute-start.22 = (s16[528,512]{1,0:T(8,128)(2,1)S(1)}, s16[528,512]{1,0:T(8,128)(2,1)S(1)}, u32[]{:S(2)}, u32[]{:S(2)}) collective-permute-start(s16[528,512]{1,0:T(8,128)(2,1)S(1)} %add.19.rest_0_), channel_id=1, source_target_pairs={{8,16},{16,8},{9,17},{17,9},{10,18},{18,10},{11,19},{19,11},{12,20... | collective-permute-start | bytes 1622024 | tf_op jit(solution)/shard_map/ppermute | solution.py:250
  191.8 25.4 %collective-permute-start.24 = (s16[528,512]{1,0:T(8,128)(2,1)S(1)}, s16[528,512]{1,0:T(8,128)(2,1)S(1)}, u32[]{:S(2)}, u32[]{:S(2)}) collective-permute-start(s16[528,512]{1,0:T(8,128)(2,1)S(1)} %add.21), channel_id=1, source_target_pairs={{8,0},{16,24},{9,1},{17,25},{10,2},{18,26},{11,3},{19,27},{12,4},{... | collective-permute-start | bytes 1622024 | tf_op jit(solution)/shard_map/ppermute | solution.py:244

commit v5 on v3

v5 whole, which is shorter than its diff:
```python
import functools

import jax
import jax.numpy as jnp
from jax import lax
from jax.experimental import pallas as pl
from jax.experimental.pallas import tpu as pltpu
from jax.sharding import PartitionSpec as P

BLOCK = 128
GROUPS = 16
CHUNK = 3
AHEAD = 3
LAG = 3
ROWS = 512
VMEM_LIMIT = 48 * 1024 * 1024


def params():
    return pltpu.CompilerParams(vmem_limit_bytes=VMEM_LIMIT)


def cost(megaflops=1):
    return pl.CostEstimate(flops=megaflops * 10**6, bytes_accessed=megaflops * 2500, transcendentals=0)


def chunk_widths(local):
    units = local // BLOCK
    rest = [CHUNK] * ((units - 1) // CHUNK)
    return [BLOCK * u for u in [units - sum(rest), *rest]]


def put(ref, value):
    rows, cols = value.shape
    grouped = value.reshape(GROUPS, rows // GROUPS, cols)
    top = jnp.max(jnp.abs(grouped), axis=1)
    power = jnp.floor(jnp.log2(jnp.maximum(top, 1e-30))) + 1.0
    codes = jnp.round(grouped * jnp.exp2(15.0 - power)[:, None, :])
    codes = jnp.clip(codes, -32767.0, 32767.0).reshape(rows, cols)
    ref[0:rows, :] = codes.astype(jnp.int32).astype(jnp.int16)
    ref[rows : rows + GROUPS, :] = power.astype(jnp.int32).astype(jnp.int16)


def scales(ref):
    rows = ref.shape[0] - GROUPS
    return jnp.exp2(ref[rows : rows + GROUPS, :].astype(jnp.int32).astype(jnp.float32) - 15.0)


def get(ref):
    rows = ref.shape[0] - GROUPS
    cols = ref.shape[1]
    codes = ref[0:rows, :].astype(jnp.int32).astype(jnp.float32)
    grouped = codes.reshape(GROUPS, rows // GROUPS, cols) * scales(ref)[:, None, :]
    return grouped.reshape(rows, cols)


def forward_kernel(place_ref, mask_ref, tokens_ref, gate_ref, up_ref, out_ref, held, *, first):
    depth = gate_ref.shape[0]
    for r in range(depth // BLOCK):
        rows = slice(r * BLOCK, (r + 1) * BLOCK)
        keep = mask_ref[r, first + pl.program_id(0)].astype(jnp.float32)
        keep = jnp.full((BLOCK, BLOCK), keep).astype(jnp.bfloat16)
        held[rows, :BLOCK] = gate_ref[rows, :] * keep
        held[rows, BLOCK:] = up_ref[rows, :] * keep
    put(out_ref, jnp.dot(tokens_ref[...], held[...], preferred_element_type=jnp.float32))


def forward(place, mask, tokens, gate_weight, up_weight, start, width):
    count, depth = tokens.shape
    weight = pl.BlockSpec((depth, BLOCK), lambda j, place, mask: (0, start // BLOCK + j))
    return pl.pallas_call(
        functools.partial(forward_kernel, first=start // BLOCK),
        grid_spec=pltpu.PrefetchScalarGridSpec(
            num_scalar_prefetch=2,
            grid=(width // BLOCK,),
            in_specs=[pl.BlockSpec((count, depth), lambda j, place, mask: (0, 0)), weight, weight],
            out_specs=pl.BlockSpec((count + GROUPS, 2 * BLOCK), lambda j, place, mask: (0, j)),
            scratch_shapes=[pltpu.VMEM((depth, 2 * BLOCK), jnp.bfloat16)],
        ),
        out_shape=jax.ShapeDtypeStruct((count + GROUPS, 2 * width), jnp.int16),
        compiler_params=params(),
        cost_estimate=cost(8000),
        name="forward",
    )(place, mask, tokens, gate_weight, up_weight)


def add_kernel(place_ref, a_ref, b_ref, out_ref):
    inner = place_ref[2] != 0

    @pl.when(inner)
    def _():
        put(out_ref, get(a_ref) + get(b_ref))

    @pl.when(jnp.logical_not(inner))
    def _():
        out_ref[...] = a_ref[...]


def add(place, a, b):
    return pl.pallas_call(
        add_kernel,
        grid_spec=pltpu.PrefetchScalarGridSpec(
            num_scalar_prefetch=1,
            grid=(1,),
            in_specs=[pl.BlockSpec(x.shape, lambda j, place: (0, 0)) for x in (a, b)],
            out_specs=pl.BlockSpec(a.shape, lambda j, place: (0, 0)),
        ),
        out_shape=jax.ShapeDtypeStruct(a.shape, a.dtype),
        compiler_params=params(),
        cost_estimate=cost(),
        name="add",
    )(place, a, b)


def reply_kernel(place_ref, a_ref, b_ref, next_ref, out_ref):
    inner = place_ref[2] != 0

    @pl.when(inner)
    def _():
        put(out_ref.at[:, 0 : a_ref.shape[1]], get(a_ref) + get(b_ref))

    @pl.when(jnp.logical_not(inner))
    def _():
        out_ref[...] = next_ref[...]


def reply(place, a, b, following):
    return pl.pallas_call(
        reply_kernel,
        grid_spec=pltpu.PrefetchScalarGridSpec(
            num_scalar_prefetch=1,
            grid=(1,),
            in_specs=[pl.BlockSpec(x.shape, lambda j, place: (0, 0)) for x in (a, b, following)],
            out_specs=pl.BlockSpec(following.shape, lambda j, place: (0, 0)),
        ),
        out_shape=jax.ShapeDtypeStruct(following.shape, a.dtype),
        compiler_params=params(),
        cost_estimate=cost(),
        name="reply",
    )(place, a, b, following)


def turn_kernel(place_ref, value_ref, out_ref):
    out_ref[...] = value_ref[...].T


def turn(place, value):
    rows, cols = value.shape
    deep = min(512, cols)
    return pl.pallas_call(
        turn_kernel,
        grid_spec=pltpu.PrefetchScalarGridSpec(
            num_scalar_prefetch=1,
            grid=(cols // deep,),
            in_specs=[pl.BlockSpec((rows, deep), lambda i, place: (0, i))],
            out_specs=pl.BlockSpec((deep, rows), lambda i, place: (i, 0)),
        ),
        out_shape=jax.ShapeDtypeStruct((cols, rows), value.dtype),
        compiler_params=params(),
        cost_estimate=cost(8000),
        name="turn",
    )(place, value)


def weights_kernel(place_ref, mask_ref, turned_ref, back_ref, own_ref, across_ref, out_ref, *rest, first, devices):
    hidden_ref, gate_ref, up_ref, deltas, hidden = rest[-5:]
    step = pl.program_id(0)
    depth, width = gate_ref.shape
    count = deltas.shape[0]
    share = count // devices
    col, row, inner = place_ref[0], place_ref[1], place_ref[2] != 0
    owned = hidden_ref.shape[0]

    @pl.when(step == 0)
    def _():
        span = 2 * width
        power = jnp.where(inner, across_ref[count : count + GROUPS, :span], out_ref[count : count + GROUPS, :span])
        scale = jnp.exp2(power.astype(jnp.int32).astype(jnp.float32) - 15.0)
        own_scale = scales(own_ref)
        size = min(share, count // GROUPS)
        for at in range(0, count, size):
            rows = slice(at, at + size)
            group = at // (count // GROUPS)
            slot = at // share
            other = (slot % (devices // 2)) * 2 + slot // (devices // 2)
            token = jnp.bitwise_xor(col, other) * share + at % share
            source = place_ref[3 + token // owned]
            start = pl.multiple_of(source * owned + token % owned, size)
            codes = jnp.where(inner, across_ref[rows, :span], out_ref[rows, :span])
            both = (
                own_ref[rows, :].astype(jnp.int32).astype(jnp.float32) * own_scale[group : group + 1, :]
                + codes.astype(jnp.int32).astype(jnp.float32) * scale[group : group + 1, :]
            )
            for q in range(width // BLOCK):
                cols = slice(q * BLOCK, (q + 1) * BLOCK)
                gate = both[:, 2 * q * BLOCK : (2 * q + 1) * BLOCK]
                up = both[:, (2 * q + 1) * BLOCK : (2 * q + 2) * BLOCK]
                back = back_ref[pl.ds(start, size), cols].astype(jnp.float32)
                sig = jax.nn.sigmoid(gate)
                silu = gate * sig
                hidden[rows, cols] = (silu * up).astype(jnp.bfloat16)
                delta = back * up * sig * (1.0 + gate * (1.0 - sig))
                deltas[rows, 2 * q * BLOCK : (2 * q + 1) * BLOCK] = delta.astype(jnp.bfloat16)
                deltas[rows, (2 * q + 1) * BLOCK : (2 * q + 2) * BLOCK] = (back * silu).astype(jnp.bfloat16)
        for at in range(0, owned, share):
            other = jnp.bitwise_xor(col, row * (owned // share) + at // share)
            slot = (other % 2) * (devices // 2) + other // 2
            hidden_ref[at : at + share, :] = hidden[pl.ds(pl.multiple_of(slot * share, share), share), :]

    total = jnp.dot(turned_ref[...], deltas[...], preferred_element_type=jnp.float32)
    for r in range(depth // BLOCK):
        rows = slice(r * BLOCK, (r + 1) * BLOCK)
        for q in range(width // BLOCK):
            cols = slice(q * BLOCK, (q + 1) * BLOCK)
            keep = mask_ref[step * (depth // BLOCK) + r, first + q].astype(jnp.float32)
            gate_ref[rows, cols] = total[rows, 2 * q * BLOCK : (2 * q + 1) * BLOCK] * keep
            up_ref[rows, cols] = total[rows, (2 * q + 1) * BLOCK : (2 * q + 2) * BLOCK] * keep


def weight_grads(place, mask, turned, back, coded, previous, shapes, start, width, devices):
    depth, count = turned.shape
    owned = shapes[0].shape[0]
    deep = min(ROWS, depth)
    place_of = lambda m, place, mask: (0, 0)
    first = start // BLOCK
    column = pl.Element(width)
    out = pl.BlockSpec((pl.Element(deep), column), lambda m, place, mask: (m * deep, start))
    return pl.pallas_call(
        functools.partial(weights_kernel, first=first, devices=devices),
        grid_spec=pltpu.PrefetchScalarGridSpec(
            num_scalar_prefetch=2,
            grid=(depth // deep,),
            in_specs=[
                pl.BlockSpec((deep, count), lambda m, place, mask: (m, 0)),
                pl.BlockSpec((pl.Element(back.shape[0]), column), lambda m, place, mask: (0, start)),
            ]
            + [pl.BlockSpec(x.shape, place_of) for x in coded]
            + [pl.BlockSpec(memory_space=pl.ANY)] * len(previous),
            out_specs=[pl.BlockSpec((pl.Element(owned), column), lambda m, place, mask: (0, start)), out, out],
            scratch_shapes=[
                pltpu.VMEM((count, 2 * width), jnp.bfloat16),
                pltpu.VMEM((count, width), jnp.bfloat16),
            ],
        ),
        out_shape=shapes,
        input_output_aliases={4 + len(coded) + i: i for i in range(len(previous))},
        compiler_params=params(),
        cost_estimate=cost(),
        name="weight_grads",
    )(place, mask, turned, back, *coded, *previous)


def tie(value, *others):
    return lax.optimization_barrier((value, *others))[0]


def pick(condition, a, b):
    return lax.select(jnp.broadcast_to(condition, a.shape), a, b)


def gather_tokens(tokens, devices, others):
    pieces = [tokens]
    for other in range(2, devices, 2):
        pieces.append(lax.ppermute(tokens, "col", [(i, i ^ other) for i in range(devices)]))
    mine = tie(jnp.concatenate(pieces, axis=0), *others)
    return jnp.concatenate([mine, lax.ppermute(mine, "col", [(i, i ^ 1) for i in range(devices)])], axis=0)


def on_device(tokens, gate_weight, up_weight, block_mask, hidden_grad, *, ring, devices):
    me = lax.axis_index("row")
    depth, local = gate_weight.shape
    left, right = ring // 2 - 1, ring // 2
    reach = ring // 2 - 1
    short = reach == 1
    distance = jnp.where(me >= right, me - right, left - me)
    shapes = [
        jax.ShapeDtypeStruct(hidden_grad.shape, jnp.bfloat16),
        jax.ShapeDtypeStruct((depth, local), jnp.float32),
        jax.ShapeDtypeStruct((depth, local), jnp.float32),
    ]
    widths = chunk_widths(local)
    starts = [sum(widths[:c]) for c in range(len(widths))]
    chunks = len(widths)

    def outward(value, hop):
        return lax.ppermute(value, "row", [(left - hop, left - hop - 1), (right + hop, right + hop + 1)])

    def inward(value, hop):
        return lax.ppermute(value, "row", [(left - hop - 1, left - hop), (right + hop + 1, right + hop)])

    def swap(value):
        return lax.ppermute(value, "row", [(left, right), (right, left)])

    def exchange(value):
        return lax.ppermute(value, "row", [(i, i ^ 1) for i in range(ring)])

    pair = [exchange(hidden_grad)] if short else []
    gathered = gather_tokens(tokens, devices, pair)
    on_left = me < right
    if short:
        sources = [jnp.where(on_left, i != me, 3 - i) for i in range(2)]
        sources += [jnp.where(on_left, i, i != me) for i in range(2, 4)]
    else:
        sources = list(range(ring))
    inner = (distance == 0) if short else 1
    place = jnp.stack([lax.axis_index("col"), me, inner, *sources]).astype(jnp.int32)
    own, sums, across, arrived, terms = [], [], [], [], []
    outs = ()

    def ordered(kernel, *args):
        nonlocal place
        out = kernel(place, *args)
        place = tie(place, out[0] if isinstance(out, (list, tuple)) else out)
        return out

    def run_forward(c):
        own.append(ordered(forward, block_mask, gathered, gate_weight, up_weight, starts[c], widths[c]))

    def run_weights(c, coded, back):
        nonlocal outs
        outs = ordered(
            weight_grads, block_mask, turned, back, coded, outs, shapes, starts[c], widths[c], devices
        )

    if not short:
        back = lax.all_gather(hidden_grad, "row", axis=0, tiled=True)
        turned = ordered(turn, gathered)
        for c in range(chunks):
            run_forward(c)
            total = own[c]
            for hop in reversed(range(reach)):
                new = ordered(add, own[c], inward(total, hop))
                total = pick(distance == hop, new, total)
            coming = swap(total)
            for hop in range(reach):
                came = outward(ordered(add, own[c], coming), hop)
                coming = pick(distance == hop + 1, came, coming)
            run_weights(c, (total, coming, coming), back)
        return tuple(outs)

    ahead = min(AHEAD, chunks)
    run_forward(0)
    arrived.append(inward(own[0], 0))
    half = jnp.concatenate([hidden_grad, *pair], axis=0)
    other_half = swap(tie(half, place))
    for c in range(1, ahead):
        run_forward(c)
        if c == 1:
            arrived.append(inward(own[1], 0))
    turned = ordered(turn, gathered)
    for s in range(chunks + LAG):
        if s < chunks:
            if s + 2 < min(chunks, LAG):
                arrived.append(inward(tie(own[s + 2], arrived[s]), 0))
            sums.append(ordered(add, own[s], arrived[s]))
            across.append(swap(sums[s]))
        if s == 0:
            moved = outward(tie(other_half, place), 0)
        if s + ahead < chunks:
            run_forward(s + ahead)
        if s == LAG:
            there, moved = lax.optimization_barrier((other_half, moved, place))[:2]
            back = jnp.concatenate([half, pick(distance == 0, there, moved)], axis=0)
        if s >= LAG:
            c = s - LAG
            run_weights(c, (sums[c], across[c], arrived[s]), back)
        c = s - 1
        if 0 <= c < chunks:
            both_ways = c + LAG < chunks
            message = ordered(reply, own[c], across[c], own[c + LAG] if both_ways else own[c])
            arrived.append(exchange(message) if both_ways else outward(message, 0))
    return tuple(outs)


def solution(mesh):
    placed = (P("col", "row"), P("row", "col"), P("row", "col"), P("row", "col"), P("row", "col"))
    return jax.shard_map(
        functools.partial(on_device, ring=mesh.shape["row"], devices=mesh.shape["col"]),
        mesh=mesh,
        in_specs=placed,
        out_specs=(P("row", "col"), P("row", "col"), P("row", "col")),
        check_vma=False,
    )
```

time: 238 us -> 204 us (0.86)
  waiting for transfers between devices: 87.5 us -> 68.8 us
  between operations: 14.4 us -> 1.12 us
  Pallas kernels: 83.2 us -> 73.3 us
  starting transfers between devices: 44.8 us -> 53.1 us
  local copies, waits for them, and re-layouts: 5.73 us -> 1.51 us
  other arithmetic: 1.12 us -> 4.77 us
    ppermute x5 -> x3, waiting for transfers between devices: 43.1 us -> 0.01 us  [inward(): lax.ppermute(value, 'row', [(left - hop - 1, left - hop), (right + hop +...]
    ppermute x0 -> x4, waiting for transfers between devices: none -> 30.5 us  [exchange(): return lax.ppermute(value, 'row', [(i, i ^ 1) for i in range(ring)])]
    ppermute x0 -> x4, starting transfers between devices: none -> 28.5 us  [exchange(): return lax.ppermute(value, 'row', [(i, i ^ 1) for i in range(ring)])]
    pallas_call x10 -> x6, Pallas kernels: 22.5 us -> 3.57 us  [add(): pl.pallas_call(add_kernel, grid_spec=pltpu.PrefetchScalarGridSpec(num_sca...]
    ppermute x5 -> x3, starting transfers between devices: 29 us -> 10.4 us  [inward(): lax.ppermute(value, 'row', [(left - hop - 1, left - hop), (right + hop +...]
    pallas_call x5 -> x12, Pallas kernels: 33.6 us -> 40.8 us  [the longest x6 36.3 us: weight_grads(): pl.pallas_call(functools.partial(weights_kernel, first=first, devices=dev...]
    unnamed x36 -> x13, local copies, waits for them, and re-layouts: 5.67 us -> 0.14 us
    ppermute x5 -> x4, waiting for transfers between devices: 30.2 us -> 25.5 us  [outward(): lax.ppermute(value, 'row', [(left - hop, left - hop - 1), (right + hop, r...]
  transfers between devices with their start and end apart: 20 -> 22, of which waited for: 11 -> 9; matrix products, arithmetic and copies ran while one was open for 0% -> 2% of each run, Pallas kernels for 33% -> 32%
where the time goes in v5:
time: 204 us; the launch traced here: 203 us
  Pallas kernels  73.3 us (36%)
  waiting for transfers between devices  68.8 us (34%)
  starting transfers between devices  53.1 us (26%)
  other arithmetic  4.77 us (2%)
    pallas_call x6, Pallas kernels, weight_grads(): pl.pallas_call(functools.partial(weights_kernel, first=first, devices=dev...  36.3 us
    ppermute x4, waiting for transfers between devices, exchange(): return lax.ppermute(value, 'row', [(i, i ^ 1) for i in range(ring)])  30.5 us
    ppermute x4, starting transfers between devices, exchange(): return lax.ppermute(value, 'row', [(i, i ^ 1) for i in range(ring)])  28.5 us
    pallas_call x6, Pallas kernels, forward(): pl.pallas_call(functools.partial(forward_kernel, first=start // BLOCK), g...  27.4 us
    ppermute x4, waiting for transfers between devices, outward(): lax.ppermute(value, 'row', [(left - hop, left - hop - 1), (right + hop, r...  25.5 us
    ppermute x3, waiting for transfers between devices, gather_tokens(): lax.ppermute(tokens, 'col', [(i, i ^ other) for i in range(devices)])  11.3 us
    ppermute x3, starting transfers between devices, inward(): lax.ppermute(value, 'row', [(left - hop - 1, left - hop), (right + hop +...  10.4 us
    ppermute x4, starting transfers between devices, outward(): lax.ppermute(value, 'row', [(left - hop, left - hop - 1), (right + hop, r...  5.39 us
  transfers between devices with their start and end apart: 22, of which 9 were waited for; matrix products, arithmetic and copies ran while one was open for 2% of the time, Pallas kernels for 32%

profile of v5, /device:TPU:0, one launch (start us, length us, event | category | flops | bytes accessed | tf_op | source)
XLA Modules:
  0.0 202.6 jit_solution(13157141541494198955)
XLA Ops:
  0.6 3.1 %collective-permute-start.3 = (bf16[128,2048]{1,0:T(8,128)(2,1)}, bf16[128,2048]{1,0:T(8,128)(2,1)}, u32[]{:S(2)}, u32[]{:S(2)}) collective-permute-start(bf16[128,2048]{1,0:T(8,128)(2,1)} %param.9), channel_id=1, source_target_pairs={{0,8},{8,0},{16,24},{24,16},{1,9},{9,1},{17,25},{25,17},{2,10},{10... | collective-permute-start | bytes 1572872 | tf_op jit(solution)/shard_map/ppermute | solution.py:295
  3.7 1.5 collective-permute-start
  5.2 1.5 collective-permute-start.1
  7.2 6.0 %collective-permute-done = bf16[64,2048]{1,0:T(8,128)(2,1)S(1)} collective-permute-done((bf16[64,2048]{1,0:T(8,128)(2,1)}, bf16[64,2048]{1,0:T(8,128)(2,1)S(1)}, u32[]{:S(2)}, u32[]{:S(2)}) %collective-permute-start) | collective-permute-done | bytes 262176 | tf_op jit(solution)/shard_map/ppermute | solution.py:264
  13.2 5.4 %collective-permute-done.1 = bf16[64,2048]{1,0:T(8,128)(2,1)S(1)} collective-permute-done((bf16[64,2048]{1,0:T(8,128)(2,1)}, bf16[64,2048]{1,0:T(8,128)(2,1)S(1)}, u32[]{:S(2)}, u32[]{:S(2)}) %collective-permute-start.1) | collective-permute-done | bytes 262176 | tf_op jit(solution)/shard_map/ppermute | solution.py:264
  18.5 1.1 pad_maximum_fusion.1
  19.9 1.1 pad_maximum_fusion.2
  21.1 1.4 collective-permute-done.4
  22.5 1.3 constant_dynamic-update-slice_fusion.tokens_ref.value_ref
  23.8 2.8 %forward.6.a_ref = s16[528,256]{1,0:T(8,128)(2,1)S(1)} custom-call(s32[7]{0:T(128)S(1)} %stack.35.place_ref, s32[16,16]{1,0:T(8,128)S(1)} %copy-done.3, bf16[512,2048]{1,0:T(8,128)(2,1)S(1)} %constant_dynamic-update-slice_fusion.tokens_ref.value_ref, bf16[2048,2048]{1,0:T(8,128)(2,1)} %gate_ref.11, bf16[2048,2048]{1,0:T(8,128)(2,1)} %up_ref.11), custom_call_target="tpu_custom_call" | custom-call | flops 8000000000 | bytes 20000000 | tf_op jit(solution)/shard_map/forward/pallas_call | solution.py:71
  26.6 2.4 %collective-permute-start.5 = (s16[528,256]{1,0:T(8,128)(2,1)S(1)}, s16[528,256]{1,0:T(8,128)(2,1)S(1)}, u32[]{:S(2)}, u32[]{:S(2)}) collective-permute-start(s16[528,256]{1,0:T(8,128)(2,1)S(1)} %forward.6.a_ref), channel_id=1, source_target_pairs={{0,8},{24,16},{1,9},{25,17},{2,10},{26,18},{3,11},{27,19},{4,12},{... | collective-permute-start | bytes 811016 | tf_op jit(solution)/shard_map/ppermute | solution.py:289
  29.0 4.9 %forward.7.a_ref = s16[528,768]{1,0:T(8,128)(2,1)S(1)} custom-call(s32[7]{0:T(128)S(1)} %stack.35.place_ref, s32[16,16]{1,0:T(8,128)S(1)} %copy-done.3, bf16[512,2048]{1,0:T(8,128)(2,1)S(1)} %constant_dynamic-update-slice_fusion.tokens_ref.value_ref, bf16[2048,2048]{1,0:T(8,128)(2,1)} %gate_ref.11, bf16[2048,2048]{1,0:T(8,128)(2,1)} %up_ref.11), custom_call_target="tpu_custom_call" | custom-call | flops 8000000000 | bytes 20000000 | tf_op jit(solution)/shard_map/forward/pallas_call | solution.py:71
  33.9 1.3 collective-permute-start.6
  35.3 4.9 %forward.8.a_ref = s16[528,768]{1,0:T(8,128)(2,1)S(1)} custom-call(s32[7]{0:T(128)S(1)} %stack.35.place_ref, s32[16,16]{1,0:T(8,128)S(1)} %copy-done.3, bf16[512,2048]{1,0:T(8,128)(2,1)S(1)} %constant_dynamic-update-slice_fusion.tokens_ref.value_ref, bf16[2048,2048]{1,0:T(8,128)(2,1)} %gate_ref.11, bf16[2048,2048]{1,0:T(8,128)(2,1)} %up_ref.11), custom_call_target="tpu_custom_call" | custom-call | flops 8000000000 | bytes 20000000 | tf_op jit(solution)/shard_map/forward/pallas_call | solution.py:71
  40.2 0.7 collective-permute-start.11
  40.9 1.5 turn.1.turned_ref
  43.0 0.7 collective-permute-start.7
  43.7 6.7 %collective-permute-start.8 = (s16[528,768]{1,0:T(8,128)(2,1)S(1)}, s16[528,768]{1,0:T(8,128)(2,1)S(1)}, u32[]{:S(2)}, u32[]{:S(2)}) collective-permute-start(s16[528,768]{1,0:T(8,128)(2,1)S(1)} %forward.8.a_ref), channel_id=1, source_target_pairs={{0,8},{24,16},{1,9},{25,17},{2,10},{26,18},{3,11},{27,19},{4,12},{... | collective-permute-start | bytes 2433032 | tf_op jit(solution)/shard_map/ppermute | solution.py:289
  50.4 4.9 %forward.9.next_ref.a_ref = s16[528,768]{1,0:T(8,128)(2,1)S(1)} custom-call(s32[7]{0:T(128)S(1)} %stack.35.place_ref, s32[16,16]{1,0:T(8,128)S(1)} %copy-done.3, bf16[512,2048]{1,0:T(8,128)(2,1)S(1)} %constant_dynamic-update-slice_fusion.tokens_ref.value_ref, bf16[2048,2048]{1,0:T(8,128)(2,1)} %gate_ref.11, bf16[2048,2048]{1,0:T(8,128)(2,1)} %up_ref.11), custom_call_target="tpu_custom_call" | custom-call | flops 8000000000 | bytes 20000000 | tf_op jit(solution)/shard_map/forward/pallas_call | solution.py:71
  56.0 0.7 collective-permute-start.9
  56.7 1.3 collective-permute-start.12
  58.0 4.9 %forward.10.next_ref.a_ref = s16[528,768]{1,0:T(8,128)(2,1)S(1)} custom-call(s32[7]{0:T(128)S(1)} %stack.35.place_ref, s32[16,16]{1,0:T(8,128)S(1)} %copy-done.3, bf16[512,2048]{1,0:T(8,128)(2,1)S(1)} %copy-done.2, bf16[2048,2048]{1,0:T(8,128)(2,1)} %gate_ref.11, bf16[2048,2048]{1,0:T(8,128)(2,1)} %up_ref.11), custom_call_target="tpu_custom_call" | custom-call | flops 8000000000 | bytes 20000000 | tf_op jit(solution)/shard_map/forward/pallas_call | solution.py:71
  63.6 12.6 %collective-permute-start.10 = (s16[528,768]{1,0:T(8,128)(2,1)S(1)}, s16[528,768]{1,0:T(8,128)(2,1)S(1)}, u32[]{:S(2)}, u32[]{:S(2)}) collective-permute-start(s16[528,768]{1,0:T(8,128)(2,1)S(1)} %reply.6), channel_id=1, source_target_pairs={{0,8},{8,0},{16,24},{24,16},{1,9},{9,1},{17,25},{25,17},{2,10},{10... | collective-permute-start | bytes 2433032 | tf_op jit(solution)/shard_map/ppermute | solution.py:295
  76.8 0.7 collective-permute-start.13
  77.5 4.9 %forward.11.next_ref.a_ref = s16[528,768]{1,0:T(8,128)(2,1)S(1)} custom-call(s32[7]{0:T(128)S(1)} %stack.35.place_ref, s32[16,16]{1,0:T(8,128)S(1)} %copy-done.3, bf16[512,2048]{1,0:T(8,128)(2,1)S(1)} %copy-done.2, bf16[2048,2048]{1,0:T(8,128)(2,1)} %gate_ref.11, bf16[2048,2048]{1,0:T(8,128)(2,1)} %up_ref.11), custom_call_target="tpu_custom_call" | custom-call | flops 8000000000 | bytes 20000000 | tf_op jit(solution)/shard_map/forward/pallas_call | solution.py:71
  82.5 1.5 reply.7
  84.0 9.5 %collective-permute-start.14 = (s16[528,768]{1,0:T(8,128)(2,1)}, s16[528,768]{1,0:T(8,128)(2,1)S(1)}, u32[]{:S(2)}, u32[]{:S(2)}) collective-permute-start(s16[528,768]{1,0:T(8,128)(2,1)} %reply.7), channel_id=1, source_target_pairs={{0,8},{8,0},{16,24},{24,16},{1,9},{9,1},{17,25},{25,17},{2,10},{10... | collective-permute-start | bytes 2433032 | tf_op jit(solution)/shard_map/ppermute | solution.py:295
  93.5 17.3 %collective-permute-done.10.b_ref.out_ref = s16[528,768]{1,0:T(8,128)(2,1)S(1)} collective-permute-done((s16[528,768]{1,0:T(8,128)(2,1)S(1)}, s16[528,768]{1,0:T(8,128)(2,1)S(1)}, u32[]{:S(2)}, u32[]{:S(2)}) %collective-permute-start.10) | collective-permute-done | bytes 811040 | tf_op jit(solution)/shard_map/ppermute | solution.py:295
  111.4 1.0 collective-permute-start.15
  112.5 1.3 broadcast_select_fusion
  113.8 1.2 pad_maximum_fusion.back_ref
  115.1 3.5 %weight_grads.6 = (bf16[128,2048]{1,0:T(8,128)(2,1)}, f32[2048,2048]{1,0:T(8,128)}, f32[2048,2048]{1,0:T(8,128)}) custom-call(s32[7]{0:T(128)S(1)} %stack.35.place_ref, s32[16,16]{1,0:T(8,128)S(1)} %copy-done.3, bf16[2048,512]{1,0:T(8,128)(2,1)S(1)} %turn.1.turned_ref, bf16[512,2048]{1,0:T(8,128)(2,1)S(1)} %pad_maximum_fusion.back_ref, ...), custom_call_target="tpu_custom_call" | custom-call | flops 1000000 | bytes 2500 | tf_op jit(solution)/shard_map/weight_grads/pallas_call | solution.py:228
  119.2 3.2 %collective-permute-start.16 = (s16[528,768]{1,0:T(8,128)(2,1)S(1)}, s16[528,768]{1,0:T(8,128)(2,1)S(1)}, u32[]{:S(2)}, u32[]{:S(2)}) collective-permute-start(s16[528,768]{1,0:T(8,128)(2,1)S(1)} %reply.8), channel_id=1, source_target_pairs={{0,8},{8,0},{16,24},{24,16},{1,9},{9,1},{17,25},{25,17},{2,10},{10... | collective-permute-start | bytes 2433032 | tf_op jit(solution)/shard_map/ppermute | solution.py:295
  122.5 5.7 %collective-permute-done.14.b_ref.out_ref = s16[528,768]{1,0:T(8,128)(2,1)S(1)} collective-permute-done((s16[528,768]{1,0:T(8,128)(2,1)}, s16[528,768]{1,0:T(8,128)(2,1)S(1)}, u32[]{:S(2)}, u32[]{:S(2)}) %collective-permute-start.14) | collective-permute-done | bytes 811040 | tf_op jit(solution)/shard_map/ppermute | solution.py:295
  128.8 0.7 collective-permute-start.17
  129.5 6.6 %weight_grads.7 = (bf16[128,2048]{1,0:T(8,128)(2,1)}, f32[2048,2048]{1,0:T(8,128)}, f32[2048,2048]{1,0:T(8,128)}) custom-call(s32[7]{0:T(128)S(1)} %stack.35.place_ref, s32[16,16]{1,0:T(8,128)S(1)} %copy-done.3, bf16[2048,512]{1,0:T(8,128)(2,1)S(1)} %turn.1.turned_ref, ...), custom_call_target="tpu_custom_call", output_to_operand_aliasing={{0}: (7, {}), {1}: (8, {}), {2}: (9, {})} | custom-call | flops 1000000 | bytes 2500 | tf_op jit(solution)/shard_map/weight_grads/pallas_call | solution.py:228
  136.7 1.3 collective-permute-start.18
  138.0 7.6 %collective-permute-done.16.b_ref.out_ref = s16[528,768]{1,0:T(8,128)(2,1)S(1)} collective-permute-done((s16[528,768]{1,0:T(8,128)(2,1)S(1)}, s16[528,768]{1,0:T(8,128)(2,1)S(1)}, u32[]{:S(2)}, u32[]{:S(2)}) %collective-permute-start.16) | collective-permute-done | bytes 811040 | tf_op jit(solution)/shard_map/ppermute | solution.py:295
  146.2 0.7 collective-permute-start.19
  146.9 6.6 %weight_grads.8 = (bf16[128,2048]{1,0:T(8,128)(2,1)}, f32[2048,2048]{1,0:T(8,128)}, f32[2048,2048]{1,0:T(8,128)}) custom-call(s32[7]{0:T(128)S(1)} %stack.35.place_ref, s32[16,16]{1,0:T(8,128)S(1)} %copy-done.3, bf16[2048,512]{1,0:T(8,128)(2,1)S(1)} %turn.1.turned_ref, ...), custom_call_target="tpu_custom_call", output_to_operand_aliasing={{0}: (7, {}), {1}: (8, {}), {2}: (9, {})} | custom-call | flops 1000000 | bytes 2500 | tf_op jit(solution)/shard_map/weight_grads/pallas_call | solution.py:228
  154.0 1.3 collective-permute-start.20
  155.3 7.6 %collective-permute-done.18.out_ref = s16[528,768]{1,0:T(8,128)(2,1)S(1)} collective-permute-done((s16[528,768]{1,0:T(8,128)(2,1)S(1)}, s16[528,768]{1,0:T(8,128)(2,1)S(1)}, u32[]{:S(2)}, u32[]{:S(2)}) %collective-permute-start.18) | collective-permute-done | bytes 811040 | tf_op jit(solution)/shard_map/ppermute | solution.py:286
  162.9 6.6 %weight_grads.9 = (bf16[128,2048]{1,0:T(8,128)(2,1)}, f32[2048,2048]{1,0:T(8,128)}, f32[2048,2048]{1,0:T(8,128)}) custom-call(s32[7]{0:T(128)S(1)} %stack.35.place_ref, s32[16,16]{1,0:T(8,128)S(1)} %copy-done.3, bf16[2048,512]{1,0:T(8,128)(2,1)S(1)} %turn.1.turned_ref, ...), custom_call_target="tpu_custom_call", output_to_operand_aliasing={{0}: (7, {}), {1}: (8, {}), {2}: (9, {})} | custom-call | flops 1000000 | bytes 2500 | tf_op jit(solution)/shard_map/weight_grads/pallas_call | solution.py:228
  170.1 1.5 collective-permute-start.21
  171.6 8.7 %collective-permute-done.20.out_ref = s16[528,768]{1,0:T(8,128)(2,1)S(1)} collective-permute-done((s16[528,768]{1,0:T(8,128)(2,1)S(1)}, s16[528,768]{1,0:T(8,128)(2,1)S(1)}, u32[]{:S(2)}, u32[]{:S(2)}) %collective-permute-start.20) | collective-permute-done | bytes 811040 | tf_op jit(solution)/shard_map/ppermute | solution.py:286
  180.3 6.5 %weight_grads.10 = (bf16[128,2048]{1,0:T(8,128)(2,1)}, f32[2048,2048]{1,0:T(8,128)}, f32[2048,2048]{1,0:T(8,128)}) custom-call(s32[7]{0:T(128)S(1)} %stack.35.place_ref, s32[16,16]{1,0:T(8,128)S(1)} %copy-done.3, bf16[2048,512]{1,0:T(8,128)(2,1)S(1)} %turn.1.turned_ref, ...), custom_call_target="tpu_custom_call", output_to_operand_aliasing={{0}: (7, {}), {1}: (8, {}), {2}: (9, {})} | custom-call | flops 1000000 | bytes 2500 | tf_op jit(solution)/shard_map/weight_grads/pallas_call | solution.py:228
  186.9 9.2 %collective-permute-done.21.out_ref = s16[528,768]{1,0:T(8,128)(2,1)S(1)} collective-permute-done((s16[528,768]{1,0:T(8,128)(2,1)S(1)}, s16[528,768]{1,0:T(8,128)(2,1)S(1)}, u32[]{:S(2)}, u32[]{:S(2)}) %collective-permute-start.21) | collective-permute-done | bytes 811040 | tf_op jit(solution)/shard_map/ppermute | solution.py:286
  196.1 6.6 %weight_grads.11 = (bf16[128,2048]{1,0:T(8,128)(2,1)}, f32[2048,2048]{1,0:T(8,128)}, f32[2048,2048]{1,0:T(8,128)}) custom-call(s32[7]{0:T(128)S(1)} %stack.35.place_ref, s32[16,16]{1,0:T(8,128)S(1)} %copy-done.3, bf16[2048,512]{1,0:T(8,128)(2,1)S(1)} %turn.1.turned_ref, ...), custom_call_target="tpu_custom_call", output_to_operand_aliasing={{0}: (7, {}), {1}: (8, {}), {2}: (9, {})} | custom-call | flops 1000000 | bytes 2500 | tf_op jit(solution)/shard_map/weight_grads/pallas_call | solution.py:228
  (40 shorter events, 7.4 us)
Async XLA Ops:
  0.6 19.3 %copy-start.4 = (bf16[128,2048]{1,0:T(8,128)(2,1)S(1)}, bf16[128,2048]{1,0:T(8,128)(2,1)}, u32[]{:S(2)}) copy-start(bf16[128,2048]{1,0:T(8,128)(2,1)} %param.9) | copy-start | bytes 1572868
  0.6 19.0 %collective-permute-start.3 = (bf16[128,2048]{1,0:T(8,128)(2,1)}, bf16[128,2048]{1,0:T(8,128)(2,1)}, u32[]{:S(2)}, u32[]{:S(2)}) collective-permute-start(bf16[128,2048]{1,0:T(8,128)(2,1)} %param.9), channel_id=1, source_target_pairs={{0,8},{8,0},{16,24},{24,16},{1,9},{9,1},{17,25},{25,17},{2,10},{10... | collective-permute-start | bytes 1572872 | tf_op jit(solution)/shard_map/ppermute | solution.py:295
  3.7 9.4 %collective-permute-start = (bf16[64,2048]{1,0:T(8,128)(2,1)}, bf16[64,2048]{1,0:T(8,128)(2,1)S(1)}, u32[]{:S(2)}, u32[]{:S(2)}) collective-permute-start(bf16[64,2048]{1,0:T(8,128)(2,1)} %param.5), channel_id=1, source_target_pairs={{0,2},{1,3},{2,0},{3,1},{4,6},{5,7},{6,4},{7,5},{8,10},{9,11},{10,... | collective-permute-start | bytes 786440 | tf_op jit(solution)/shard_map/ppermute | solution.py:264
  5.2 13.3 %collective-permute-start.1 = (bf16[64,2048]{1,0:T(8,128)(2,1)}, bf16[64,2048]{1,0:T(8,128)(2,1)S(1)}, u32[]{:S(2)}, u32[]{:S(2)}) collective-permute-start(bf16[64,2048]{1,0:T(8,128)(2,1)} %param.5), channel_id=1, source_target_pairs={{0,4},{1,5},{2,6},{3,7},{4,0},{5,1},{6,2},{7,3},{8,12},{9,13},{10,... | collective-permute-start | bytes 786440 | tf_op jit(solution)/shard_map/ppermute | solution.py:264
  6.7 11.8 %collective-permute-start.2 = (bf16[64,2048]{1,0:T(8,128)(2,1)}, bf16[64,2048]{1,0:T(8,128)(2,1)S(1)}, u32[]{:S(2)}, u32[]{:S(2)}) collective-permute-start(bf16[64,2048]{1,0:T(8,128)(2,1)} %param.5), channel_id=1, source_target_pairs={{0,6},{1,7},{2,4},{3,5},{4,2},{5,3},{6,0},{7,1},{8,14},{9,15},{10,... | collective-permute-start | bytes 786440 | tf_op jit(solution)/shard_map/ppermute | solution.py:264
  19.6 2.9 %collective-permute-start.4 = (bf16[256,2048]{1,0:T(8,128)(2,1)S(1)}, bf16[256,2048]{1,0:T(8,128)(2,1)}, u32[]{:S(2)}, u32[]{:S(2)}) collective-permute-start(bf16[256,2048]{1,0:T(8,128)(2,1)S(1)} %pad_maximum_fusion.1), channel_id=1, source_target_pairs={{0,1},{1,0},{2,3},{3,2},{4,5},{5,4},{6,7},{7,6},{8,9},{9,8},{10,11... | collective-permute-start | bytes 3145736 | tf_op jit(solution)/shard_map/ppermute | solution.py:266
  19.9 3.8 %copy-start.3 = (s32[16,16]{1,0:T(8,128)S(1)}, s32[16,16]{1,0:T(8,128)}, u32[]{:S(2)}) copy-start(s32[16,16]{1,0:T(8,128)} %mask_ref.23) | copy-start | bytes 3076
  23.8 26.6 %copy-start.1 = (bf16[512,2048]{1,0:T(8,128)(2,1)}, bf16[512,2048]{1,0:T(8,128)(2,1)S(1)}, u32[]{:S(2)}) copy-start(bf16[512,2048]{1,0:T(8,128)(2,1)S(1)} %constant_dynamic-update-slice_fusion.tokens_ref.value_ref) | copy-start | bytes 6291460
  26.6 15.8 %collective-permute-start.5 = (s16[528,256]{1,0:T(8,128)(2,1)S(1)}, s16[528,256]{1,0:T(8,128)(2,1)S(1)}, u32[]{:S(2)}, u32[]{:S(2)}) collective-permute-start(s16[528,256]{1,0:T(8,128)(2,1)S(1)} %forward.6.a_ref), channel_id=1, source_target_pairs={{0,8},{24,16},{1,9},{25,17},{2,10},{26,18},{3,11},{27,19},{4,12},{... | collective-permute-start | bytes 811016 | tf_op jit(solution)/shard_map/ppermute | solution.py:289
  33.9 21.4 %collective-permute-start.6 = (s16[528,768]{1,0:T(8,128)(2,1)S(1)}, s16[528,768]{1,0:T(8,128)(2,1)S(1)}, u32[]{:S(2)}, u32[]{:S(2)}) collective-permute-start(s16[528,768]{1,0:T(8,128)(2,1)S(1)} %forward.7.a_ref), channel_id=1, source_target_pairs={{0,8},{24,16},{1,9},{25,17},{2,10},{26,18},{3,11},{27,19},{4,12},{... | collective-permute-start | bytes 2433032 | tf_op jit(solution)/shard_map/ppermute | solution.py:289
  40.2 16.5 %collective-permute-start.11 = (bf16[256,2048]{1,0:T(8,128)(2,1)S(1)}, bf16[256,2048]{1,0:T(8,128)(2,1)S(1)}, u32[]{:S(2)}, u32[]{:S(2)}) collective-permute-start(bf16[256,2048]{1,0:T(8,128)(2,1)S(1)} %pad_maximum_fusion.2), channel_id=1, source_target_pairs={{8,16},{16,8},{9,17},{17,9},{10,18},{18,10},{11,19},{19,11},{12,20... | collective-permute-start | bytes 3145736 | tf_op jit(solution)/shard_map/ppermute | solution.py:292
  43.0 19.9 %collective-permute-start.7 = (s16[528,256]{1,0:T(8,128)(2,1)S(1)}, s16[528,256]{1,0:T(8,128)(2,1)S(1)}, u32[]{:S(2)}, u32[]{:S(2)}) collective-permute-start(s16[528,256]{1,0:T(8,128)(2,1)S(1)} %add.7.own_ref), channel_id=1, source_target_pairs={{8,16},{16,8},{9,17},{17,9},{10,18},{18,10},{11,19},{19,11},{12,20... | collective-permute-start | bytes 811016 | tf_op jit(solution)/shard_map/ppermute | solution.py:292
  43.7 32.5 %collective-permute-start.8 = (s16[528,768]{1,0:T(8,128)(2,1)S(1)}, s16[528,768]{1,0:T(8,128)(2,1)S(1)}, u32[]{:S(2)}, u32[]{:S(2)}) collective-permute-start(s16[528,768]{1,0:T(8,128)(2,1)S(1)} %forward.8.a_ref), channel_id=1, source_target_pairs={{0,8},{24,16},{1,9},{25,17},{2,10},{26,18},{3,11},{27,19},{4,12},{... | collective-permute-start | bytes 2433032 | tf_op jit(solution)/shard_map/ppermute | solution.py:289
  55.3 2.7 %copy-start.2 = (bf16[512,2048]{1,0:T(8,128)(2,1)S(1)}, bf16[512,2048]{1,0:T(8,128)(2,1)}, u32[]{:S(2)}) copy-start(bf16[512,2048]{1,0:T(8,128)(2,1)} %copy-done.1) | copy-start | bytes 6291460
  56.0 26.5 %collective-permute-start.9 = (s16[528,768]{1,0:T(8,128)(2,1)S(1)}, s16[528,768]{1,0:T(8,128)(2,1)S(1)}, u32[]{:S(2)}, u32[]{:S(2)}) collective-permute-start(s16[528,768]{1,0:T(8,128)(2,1)S(1)} %add.8.own_ref), channel_id=1, source_target_pairs={{8,16},{16,8},{9,17},{17,9},{10,18},{18,10},{11,19},{19,11},{12,20... | collective-permute-start | bytes 2433032 | tf_op jit(solution)/shard_map/ppermute | solution.py:292
  56.7 55.7 %collective-permute-start.12 = (bf16[256,2048]{1,0:T(8,128)(2,1)S(1)}, bf16[256,2048]{1,0:T(8,128)(2,1)}, u32[]{:S(2)}, u32[]{:S(2)}) collective-permute-start(bf16[256,2048]{1,0:T(8,128)(2,1)S(1)} %collective-permute-done.11), channel_id=1, source_target_pairs={{8,0},{16,24},{9,1},{17,25},{10,2},{18,26},{11,3},{19,27},{12,4},{... | collective-permute-start | bytes 3145736 | tf_op jit(solution)/shard_map/ppermute | solution.py:286
  63.6 47.2 %collective-permute-start.10 = (s16[528,768]{1,0:T(8,128)(2,1)S(1)}, s16[528,768]{1,0:T(8,128)(2,1)S(1)}, u32[]{:S(2)}, u32[]{:S(2)}) collective-permute-start(s16[528,768]{1,0:T(8,128)(2,1)S(1)} %reply.6), channel_id=1, source_target_pairs={{0,8},{8,0},{16,24},{24,16},{1,9},{9,1},{17,25},{25,17},{2,10},{10... | collective-permute-start | bytes 2433032 | tf_op jit(solution)/shard_map/ppermute | solution.py:295
  76.8 41.8 %collective-permute-start.13 = (s16[528,768]{1,0:T(8,128)(2,1)S(1)}, s16[528,768]{1,0:T(8,128)(2,1)S(1)}, u32[]{:S(2)}, u32[]{:S(2)}) collective-permute-start(s16[528,768]{1,0:T(8,128)(2,1)S(1)} %add.9.own_ref), channel_id=1, source_target_pairs={{8,16},{16,8},{9,17},{17,9},{10,18},{18,10},{11,19},{19,11},{12,20... | collective-permute-start | bytes 2433032 | tf_op jit(solution)/shard_map/ppermute | solution.py:292
  84.0 44.2 %collective-permute-start.14 = (s16[528,768]{1,0:T(8,128)(2,1)}, s16[528,768]{1,0:T(8,128)(2,1)S(1)}, u32[]{:S(2)}, u32[]{:S(2)}) collective-permute-start(s16[528,768]{1,0:T(8,128)(2,1)} %reply.7), channel_id=1, source_target_pairs={{0,8},{8,0},{16,24},{24,16},{1,9},{9,1},{17,25},{25,17},{2,10},{10... | collective-permute-start | bytes 2433032 | tf_op jit(solution)/shard_map/ppermute | solution.py:295
  111.4 2.4 %copy-start.5 = (bf16[128,2048]{1,0:T(8,128)(2,1)S(1)}, bf16[128,2048]{1,0:T(8,128)(2,1)}, u32[]{:S(2)}) copy-start(bf16[128,2048]{1,0:T(8,128)(2,1)} %param.9) | copy-start | bytes 1572868
  111.4 24.6 %collective-permute-start.15 = (s16[528,768]{1,0:T(8,128)(2,1)S(1)}, s16[528,768]{1,0:T(8,128)(2,1)S(1)}, u32[]{:S(2)}, u32[]{:S(2)}) collective-permute-start(s16[528,768]{1,0:T(8,128)(2,1)S(1)} %add.10.own_ref), channel_id=1, source_target_pairs={{8,16},{16,8},{9,17},{17,9},{10,18},{18,10},{11,19},{19,11},{12,20... | collective-permute-start | bytes 2433032 | tf_op jit(solution)/shard_map/ppermute | solution.py:292
  115.1 3.6 %copy-start = (bf16[512,2048]{1,0:T(8,128)(2,1)}, bf16[512,2048]{1,0:T(8,128)(2,1)S(1)}, u32[]{:S(2)}) copy-start(bf16[512,2048]{1,0:T(8,128)(2,1)S(1)} %pad_maximum_fusion.back_ref) | copy-start | bytes 6291460
  119.2 26.3 %collective-permute-start.16 = (s16[528,768]{1,0:T(8,128)(2,1)S(1)}, s16[528,768]{1,0:T(8,128)(2,1)S(1)}, u32[]{:S(2)}, u32[]{:S(2)}) collective-permute-start(s16[528,768]{1,0:T(8,128)(2,1)S(1)} %reply.8), channel_id=1, source_target_pairs={{0,8},{8,0},{16,24},{24,16},{1,9},{9,1},{17,25},{25,17},{2,10},{10... | collective-permute-start | bytes 2433032 | tf_op jit(solution)/shard_map/ppermute | solution.py:295
  128.8 24.7 %collective-permute-start.17 = (s16[528,768]{1,0:T(8,128)(2,1)S(1)}, s16[528,768]{1,0:T(8,128)(2,1)S(1)}, u32[]{:S(2)}, u32[]{:S(2)}) collective-permute-start(s16[528,768]{1,0:T(8,128)(2,1)S(1)} %add.11.own_ref), channel_id=1, source_target_pairs={{8,16},{16,8},{9,17},{17,9},{10,18},{18,10},{11,19},{19,11},{12,20... | collective-permute-start | bytes 2433032 | tf_op jit(solution)/shard_map/ppermute | solution.py:292
  136.7 26.3 %collective-permute-start.18 = (s16[528,768]{1,0:T(8,128)(2,1)S(1)}, s16[528,768]{1,0:T(8,128)(2,1)S(1)}, u32[]{:S(2)}, u32[]{:S(2)}) collective-permute-start(s16[528,768]{1,0:T(8,128)(2,1)S(1)} %reply.9), channel_id=1, source_target_pairs={{8,0},{16,24},{9,1},{17,25},{10,2},{18,26},{11,3},{19,27},{12,4},{... | collective-permute-start | bytes 2433032 | tf_op jit(solution)/shard_map/ppermute | solution.py:286
  146.2 23.3 %collective-permute-start.19 = (s16[528,768]{1,0:T(8,128)(2,1)S(1)}, s16[528,768]{1,0:T(8,128)(2,1)S(1)}, u32[]{:S(2)}, u32[]{:S(2)}) collective-permute-start(s16[528,768]{1,0:T(8,128)(2,1)S(1)} %add.12.own_ref), channel_id=1, source_target_pairs={{8,16},{16,8},{9,17},{17,9},{10,18},{18,10},{11,19},{19,11},{12,20... | collective-permute-start | bytes 2433032 | tf_op jit(solution)/shard_map/ppermute | solution.py:292
  154.0 26.3 %collective-permute-start.20 = (s16[528,768]{1,0:T(8,128)(2,1)S(1)}, s16[528,768]{1,0:T(8,128)(2,1)S(1)}, u32[]{:S(2)}, u32[]{:S(2)}) collective-permute-start(s16[528,768]{1,0:T(8,128)(2,1)S(1)} %reply.10), channel_id=1, source_target_pairs={{8,0},{16,24},{9,1},{17,25},{10,2},{18,26},{11,3},{19,27},{12,4},{... | collective-permute-start | bytes 2433032 | tf_op jit(solution)/shard_map/ppermute | solution.py:286
  170.1 26.0 %collective-permute-start.21 = (s16[528,768]{1,0:T(8,128)(2,1)S(1)}, s16[528,768]{1,0:T(8,128)(2,1)S(1)}, u32[]{:S(2)}, u32[]{:S(2)}) collective-permute-start(s16[528,768]{1,0:T(8,128)(2,1)S(1)} %reply.11), channel_id=1, source_target_pairs={{8,0},{16,24},{9,1},{17,25},{10,2},{18,26},{11,3},{19,27},{12,4},{... | collective-permute-start | bytes 2433032 | tf_op jit(solution)/shard_map/ppermute | solution.py:286

commit v6 on v5

--- a/solution.py
+++ b/solution.py
@@ -12,6 +12,7 @@
 CHUNK = 3
 AHEAD = 3
 LAG = 3
+EARLY, LATE, TURN = 8000, 1, 8000
 ROWS = 512
 VMEM_LIMIT = 48 * 1024 * 1024
 
@@ -54,34 +55,45 @@
     return grouped.reshape(rows, cols)
 
 
-def forward_kernel(place_ref, mask_ref, tokens_ref, gate_ref, up_ref, out_ref, held, *, first):
+def forward_kernel(place_ref, mask_ref, low_ref, high_ref, gate_ref, up_ref, out_ref, joined, held, *, first):
     depth = gate_ref.shape[0]
+    half = low_ref.shape[0]
+
+    @pl.when(pl.program_id(0) == 0)
+    def _():
+        joined[0:half, :] = low_ref[...]
+        joined[half : 2 * half, :] = high_ref[...]
+
     for r in range(depth // BLOCK):
         rows = slice(r * BLOCK, (r + 1) * BLOCK)
         keep = mask_ref[r, first + pl.program_id(0)].astype(jnp.float32)
         keep = jnp.full((BLOCK, BLOCK), keep).astype(jnp.bfloat16)
         held[rows, :BLOCK] = gate_ref[rows, :] * keep
         held[rows, BLOCK:] = up_ref[rows, :] * keep
-    put(out_ref, jnp.dot(tokens_ref[...], held[...], preferred_element_type=jnp.float32))
+    put(out_ref, jnp.dot(joined[...], held[...], preferred_element_type=jnp.float32))
 
 
 def forward(place, mask, tokens, gate_weight, up_weight, start, width):
-    count, depth = tokens.shape
+    half, depth = tokens[0].shape
+    count = 2 * half
     weight = pl.BlockSpec((depth, BLOCK), lambda j, place, mask: (0, start // BLOCK + j))
     return pl.pallas_call(
         functools.partial(forward_kernel, first=start // BLOCK),
         grid_spec=pltpu.PrefetchScalarGridSpec(
             num_scalar_prefetch=2,
             grid=(width // BLOCK,),
-            in_specs=[pl.BlockSpec((count, depth), lambda j, place, mask: (0, 0)), weight, weight],
+            in_specs=[pl.BlockSpec((half, depth), lambda j, place, mask: (0, 0))] * 2 + [weight] * 2,
             out_specs=pl.BlockSpec((count + GROUPS, 2 * BLOCK), lambda j, place, mask: (0, j)),
-            scratch_shapes=[pltpu.VMEM((depth, 2 * BLOCK), jnp.bfloat16)],
+            scratch_shapes=[
+                pltpu.VMEM((count, depth), jnp.bfloat16),
+                pltpu.VMEM((depth, 2 * BLOCK), jnp.bfloat16),
+            ],
         ),
         out_shape=jax.ShapeDtypeStruct((count + GROUPS, 2 * width), jnp.int16),
         compiler_params=params(),
-        cost_estimate=cost(8000),
+        cost_estimate=cost(EARLY if start < 2 * width else LATE),
         name="forward",
-    )(place, mask, tokens, gate_weight, up_weight)
+    )(place, mask, *tokens, gate_weight, up_weight)
 
 
 def add_kernel(place_ref, a_ref, b_ref, out_ref):
@@ -140,26 +152,28 @@
     )(place, a, b, following)
 
 
-def turn_kernel(place_ref, value_ref, out_ref):
-    out_ref[...] = value_ref[...].T
-
-
-def turn(place, value):
-    rows, cols = value.shape
+def turn_kernel(place_ref, low_ref, high_ref, out_ref):
+    half = low_ref.shape[0]
+    out_ref[:, 0:half] = low_ref[...].T
+    out_ref[:, half : 2 * half] = high_ref[...].T
+
+
+def turn(place, low, high):
+    half, cols = low.shape
     deep = min(512, cols)
     return pl.pallas_call(
         turn_kernel,
         grid_spec=pltpu.PrefetchScalarGridSpec(
             num_scalar_prefetch=1,
             grid=(cols // deep,),
-            in_specs=[pl.BlockSpec((rows, deep), lambda i, place: (0, i))],
-            out_specs=pl.BlockSpec((deep, rows), lambda i, place: (i, 0)),
+            in_specs=[pl.BlockSpec((half, deep), lambda i, place: (0, i))] * 2,
+            out_specs=pl.BlockSpec((deep, 2 * half), lambda i, place: (i, 0)),
         ),
-        out_shape=jax.ShapeDtypeStruct((cols, rows), value.dtype),
+        out_shape=jax.ShapeDtypeStruct((cols, 2 * half), low.dtype),
         compiler_params=params(),
-        cost_estimate=cost(8000),
+        cost_estimate=cost(TURN),
         name="turn",
-    )(place, value)
+    )(place, low, high)
 
 
 def weights_kernel(place_ref, mask_ref, turned_ref, back_ref, own_ref, across_ref, out_ref, *rest, first, devices):
@@ -263,7 +277,7 @@
     for other in range(2, devices, 2):
         pieces.append(lax.ppermute(tokens, "col", [(i, i ^ other) for i in range(devices)]))
     mine = tie(jnp.concatenate(pieces, axis=0), *others)
-    return jnp.concatenate([mine, lax.ppermute(mine, "col", [(i, i ^ 1) for i in range(devices)])], axis=0)
+    return mine, lax.ppermute(mine, "col", [(i, i ^ 1) for i in range(devices)])
 
 
 def on_device(tokens, gate_weight, up_weight, block_mask, hidden_grad, *, ring, devices):
@@ -324,7 +338,7 @@
 
     if not short:
         back = lax.all_gather(hidden_grad, "row", axis=0, tiled=True)
-        turned = ordered(turn, gathered)
+        turned = ordered(turn, *gathered)
         for c in range(chunks):
             run_forward(c)
             total = own[c]
@@ -342,25 +356,27 @@
     run_forward(0)
     arrived.append(inward(own[0], 0))
     half = jnp.concatenate([hidden_grad, *pair], axis=0)
-    other_half = swap(tie(half, place))
+    other_half = swap(half)
     for c in range(1, ahead):
         run_forward(c)
         if c == 1:
             arrived.append(inward(own[1], 0))
-    turned = ordered(turn, gathered)
+    turned = ordered(turn, *gathered)
     for s in range(chunks + LAG):
         if s < chunks:
+            if s == 1:
+                place = tie(place, other_half)
+            if s == LAG:
+                place = tie(place, moved)
             if s + 2 < min(chunks, LAG):
                 arrived.append(inward(tie(own[s + 2], arrived[s]), 0))
             sums.append(ordered(add, own[s], arrived[s]))
             across.append(swap(sums[s]))
         if s == 0:
             moved = outward(tie(other_half, place), 0)
-        if s + ahead < chunks:
-            run_forward(s + ahead)
         if s == LAG:
-            there, moved = lax.optimization_barrier((other_half, moved, place))[:2]
-            back = jnp.concatenate([half, pick(distance == 0, there, moved)], axis=0)
+            far_half = pick(distance == 0, *lax.optimization_barrier((other_half, moved, place))[:2])
+            back = jnp.concatenate([half, far_half], axis=0)
         if s >= LAG:
             c = s - LAG
             run_weights(c, (sums[c], across[c], arrived[s]), back)
@@ -369,6 +385,8 @@
             both_ways = c + LAG < chunks
             message = ordered(reply, own[c], across[c], own[c + LAG] if both_ways else own[c])
             arrived.append(exchange(message) if both_ways else outward(message, 0))
+        if s + ahead < chunks:
+            run_forward(s + ahead)
     return tuple(outs)
 
 

time: 204 us -> 186 us (0.912)
  waiting for transfers between devices: 68.8 us -> 60.1 us
  starting transfers between devices: 53.1 us -> 45.4 us
  Pallas kernels: 73.3 us -> 76 us
  other arithmetic: 4.77 us -> 2.44 us
    ppermute x4, waiting for transfers between devices: 30.5 us -> 18.4 us  [exchange(): return lax.ppermute(value, 'row', [(i, i ^ 1) for i in range(ring)])]
    ppermute x4, starting transfers between devices: 28.5 us -> 17.4 us  [exchange(): return lax.ppermute(value, 'row', [(i, i ^ 1) for i in range(ring)])]
    ppermute x3, waiting for transfers between devices: 0.01 us -> 3.91 us  [inward(): lax.ppermute(value, 'row', [(left - hop - 1, left - hop), (right + hop +...]
    ppermute x3, starting transfers between devices: 10.4 us -> 14 us  [inward(): lax.ppermute(value, 'row', [(left - hop - 1, left - hop), (right + hop +...]
  transfers between devices with their start and end apart: 22 -> 22, of which waited for: 9 -> 10; matrix products, arithmetic and copies ran while one was open for 2% -> 1% of each run, Pallas kernels for 32% -> 38%
where the time goes in v6:
time: 186 us; the launch traced here: 185 us
  Pallas kernels  76 us (41%)
  waiting for transfers between devices  60.1 us (32%)
  starting transfers between devices  45.4 us (24%)
  other arithmetic  2.44 us (1%)
    pallas_call x6, Pallas kernels, weight_grads(): pl.pallas_call(functools.partial(weights_kernel, first=first, devices=dev...  36.6 us
    pallas_call x6, Pallas kernels, forward(): pl.pallas_call(functools.partial(forward_kernel, first=start // BLOCK), g...  27.8 us
    ppermute x4, waiting for transfers between devices, outward(): lax.ppermute(value, 'row', [(left - hop, left - hop - 1), (right + hop, r...  25.8 us
    ppermute x4, waiting for transfers between devices, exchange(): return lax.ppermute(value, 'row', [(i, i ^ 1) for i in range(ring)])  18.4 us
    ppermute x4, starting transfers between devices, exchange(): return lax.ppermute(value, 'row', [(i, i ^ 1) for i in range(ring)])  17.4 us
    ppermute x3, starting transfers between devices, inward(): lax.ppermute(value, 'row', [(left - hop - 1, left - hop), (right + hop +...  14 us
    ppermute x3, waiting for transfers between devices, gather_tokens(): lax.ppermute(tokens, 'col', [(i, i ^ other) for i in range(devices)])  11.3 us
    pallas_call x6, Pallas kernels, reply(): pl.pallas_call(reply_kernel, grid_spec=pltpu.PrefetchScalarGridSpec(num_s...  5.41 us
  transfers between devices with their start and end apart: 22, of which 10 were waited for; matrix products, arithmetic and copies ran while one was open for 1% of the time, Pallas kernels for 38%

profile of v6, /device:TPU:0, one launch (start us, length us, event | category | flops | bytes accessed | tf_op | source)
XLA Modules:
  0.0 185.1 jit_solution(8538910058104943579)
XLA Ops:
  0.6 3.1 %collective-permute-start.3 = (bf16[128,2048]{1,0:T(8,128)(2,1)}, bf16[128,2048]{1,0:T(8,128)(2,1)S(1)}, u32[]{:S(2)}, u32[]{:S(2)}) collective-permute-start(bf16[128,2048]{1,0:T(8,128)(2,1)} %param.9), channel_id=1, source_target_pairs={{0,8},{8,0},{16,24},{24,16},{1,9},{9,1},{17,25},{25,17},{2,10},{10... | collective-permute-start | bytes 1572872 | tf_op jit(solution)/shard_map/ppermute | solution.py:309
  3.7 1.5 collective-permute-start
  5.2 1.5 collective-permute-start.1
  7.2 6.0 %collective-permute-done = bf16[64,2048]{1,0:T(8,128)(2,1)S(1)} collective-permute-done((bf16[64,2048]{1,0:T(8,128)(2,1)}, bf16[64,2048]{1,0:T(8,128)(2,1)S(1)}, u32[]{:S(2)}, u32[]{:S(2)}) %collective-permute-start) | collective-permute-done | bytes 262176 | tf_op jit(solution)/shard_map/ppermute | solution.py:278
  13.2 5.4 %collective-permute-done.1 = bf16[64,2048]{1,0:T(8,128)(2,1)S(1)} collective-permute-done((bf16[64,2048]{1,0:T(8,128)(2,1)}, bf16[64,2048]{1,0:T(8,128)(2,1)S(1)}, u32[]{:S(2)}, u32[]{:S(2)}) %collective-permute-start.1) | collective-permute-done | bytes 262176 | tf_op jit(solution)/shard_map/ppermute | solution.py:278
  18.5 1.0 pad_maximum_fusion.1.low_ref
  19.8 1.1 pad_maximum_fusion.2
  20.9 0.7 collective-permute-start.6
  22.3 2.7 %forward.6.a_ref = s16[528,256]{1,0:T(8,128)(2,1)S(1)} custom-call(s32[7]{0:T(128)S(1)} %stack.35.place_ref, s32[16,16]{1,0:T(8,128)S(1)} %copy-done.3, bf16[256,2048]{1,0:T(8,128)(2,1)S(1)} %pad_maximum_fusion.1.low_ref, bf16[256,2048]{1,0:T(8,128)(2,1)S(1)} %collective-permute-done.4.high_ref, bf16[2048,2048]{1,0:T(8,128)(2,1)} %gate_ref.11, ...), custom_call_target="tpu_custom_call" | custom-call | flops 8000000000 | bytes 20000000 | tf_op jit(solution)/shard_map/forward/pallas_call | solution.py:80
  25.1 5.6 %collective-permute-start.5 = (s16[528,256]{1,0:T(8,128)(2,1)S(1)}, s16[528,256]{1,0:T(8,128)(2,1)S(1)}, u32[]{:S(2)}, u32[]{:S(2)}) collective-permute-start(s16[528,256]{1,0:T(8,128)(2,1)S(1)} %forward.6.a_ref), channel_id=1, source_target_pairs={{0,8},{24,16},{1,9},{25,17},{2,10},{26,18},{3,11},{27,19},{4,12},{... | collective-permute-start | bytes 811016 | tf_op jit(solution)/shard_map/ppermute | solution.py:303
  30.7 5.0 %forward.7.a_ref = s16[528,768]{1,0:T(8,128)(2,1)S(1)} custom-call(s32[7]{0:T(128)S(1)} %stack.35.place_ref, s32[16,16]{1,0:T(8,128)S(1)} %copy-done.3, bf16[256,2048]{1,0:T(8,128)(2,1)S(1)} %pad_maximum_fusion.1.low_ref, bf16[256,2048]{1,0:T(8,128)(2,1)S(1)} %collective-permute-done.4.high_ref, bf16[2048,2048]{1,0:T(8,128)(2,1)} %gate_ref.11, ...), custom_call_target="tpu_custom_call" | custom-call | flops 8000000000 | bytes 20000000 | tf_op jit(solution)/shard_map/forward/pallas_call | solution.py:80
  35.8 1.3 collective-permute-start.7
  37.1 5.0 %forward.8.a_ref = s16[528,768]{1,0:T(8,128)(2,1)S(1)} custom-call(s32[7]{0:T(128)S(1)} %stack.35.place_ref, s32[16,16]{1,0:T(8,128)S(1)} %copy-done.3, bf16[256,2048]{1,0:T(8,128)(2,1)S(1)} %pad_maximum_fusion.1.low_ref, bf16[256,2048]{1,0:T(8,128)(2,1)S(1)} %collective-permute-done.4.high_ref, bf16[2048,2048]{1,0:T(8,128)(2,1)} %gate_ref.11, ...), custom_call_target="tpu_custom_call" | custom-call | flops 8000000000 | bytes 20000000 | tf_op jit(solution)/shard_map/forward/pallas_call | solution.py:80
  42.1 1.5 turn.1.turned_ref
  44.2 0.7 collective-permute-start.8
  44.9 1.3 collective-permute-start.11
  46.2 7.1 %collective-permute-start.9 = (s16[528,768]{1,0:T(8,128)(2,1)S(1)}, s16[528,768]{1,0:T(8,128)(2,1)S(1)}, u32[]{:S(2)}, u32[]{:S(2)}) collective-permute-start(s16[528,768]{1,0:T(8,128)(2,1)S(1)} %forward.8.a_ref), channel_id=1, source_target_pairs={{0,8},{24,16},{1,9},{25,17},{2,10},{26,18},{3,11},{27,19},{4,12},{... | collective-permute-start | bytes 2433032 | tf_op jit(solution)/shard_map/ppermute | solution.py:303
  53.3 5.0 %forward.9.next_ref.a_ref = s16[528,768]{1,0:T(8,128)(2,1)S(1)} custom-call(s32[7]{0:T(128)S(1)} %stack.35.place_ref, s32[16,16]{1,0:T(8,128)S(1)} %copy-done.3, bf16[256,2048]{1,0:T(8,128)(2,1)S(1)} %pad_maximum_fusion.1.low_ref, bf16[256,2048]{1,0:T(8,128)(2,1)S(1)} %collective-permute-done.4.high_ref, bf16[2048,2048]{1,0:T(8,128)(2,1)} %gate_ref.11, ...), custom_call_target="tpu_custom_call" | custom-call | flops 1000000 | bytes 2500 | tf_op jit(solution)/shard_map/forward/pallas_call | solution.py:80
  59.0 0.7 collective-permute-start.10
  60.3 3.6 %collective-permute-start.12 = (s16[528,768]{1,0:T(8,128)(2,1)S(1)}, s16[528,768]{1,0:T(8,128)(2,1)S(1)}, u32[]{:S(2)}, u32[]{:S(2)}) collective-permute-start(s16[528,768]{1,0:T(8,128)(2,1)S(1)} %reply.6), channel_id=1, source_target_pairs={{0,8},{8,0},{16,24},{24,16},{1,9},{9,1},{17,25},{25,17},{2,10},{10... | collective-permute-start | bytes 2433032 | tf_op jit(solution)/shard_map/ppermute | solution.py:309
  63.9 5.0 %forward.10.next_ref.a_ref = s16[528,768]{1,0:T(8,128)(2,1)S(1)} custom-call(s32[7]{0:T(128)S(1)} %stack.35.place_ref, s32[16,16]{1,0:T(8,128)S(1)} %copy-done.3, bf16[256,2048]{1,0:T(8,128)(2,1)S(1)} %pad_maximum_fusion.1.low_ref, bf16[256,2048]{1,0:T(8,128)(2,1)S(1)} %collective-permute-done.4.high_ref, bf16[2048,2048]{1,0:T(8,128)(2,1)} %gate_ref.11, ...), custom_call_target="tpu_custom_call" | custom-call | flops 1000000 | bytes 2500 | tf_op jit(solution)/shard_map/forward/pallas_call | solution.py:80
  68.9 3.9 %collective-permute-done.9.b_ref = s16[528,768]{1,0:T(8,128)(2,1)S(1)} collective-permute-done((s16[528,768]{1,0:T(8,128)(2,1)S(1)}, s16[528,768]{1,0:T(8,128)(2,1)S(1)}, u32[]{:S(2)}, u32[]{:S(2)}) %collective-permute-start.9) | collective-permute-done | bytes 811040 | tf_op jit(solution)/shard_map/ppermute | solution.py:303
  72.8 1.5 add.9.own_ref
  74.3 0.7 collective-permute-start.13
  75.0 1.5 reply.7
  76.6 6.4 %collective-permute-start.14 = (s16[528,768]{1,0:T(8,128)(2,1)}, s16[528,768]{1,0:T(8,128)(2,1)S(1)}, u32[]{:S(2)}, u32[]{:S(2)}) collective-permute-start(s16[528,768]{1,0:T(8,128)(2,1)} %reply.7), channel_id=1, source_target_pairs={{0,8},{8,0},{16,24},{24,16},{1,9},{9,1},{17,25},{25,17},{2,10},{10... | collective-permute-start | bytes 2433032 | tf_op jit(solution)/shard_map/ppermute | solution.py:309
  83.0 5.0 %forward.11.next_ref.a_ref = s16[528,768]{1,0:T(8,128)(2,1)S(1)} custom-call(s32[7]{0:T(128)S(1)} %stack.35.place_ref, s32[16,16]{1,0:T(8,128)S(1)} %copy-done.3, bf16[256,2048]{1,0:T(8,128)(2,1)S(1)} %pad_maximum_fusion.1.low_ref, bf16[256,2048]{1,0:T(8,128)(2,1)S(1)} %collective-permute-done.4.high_ref, bf16[2048,2048]{1,0:T(8,128)(2,1)} %gate_ref.11, ...), custom_call_target="tpu_custom_call" | custom-call | flops 1000000 | bytes 2500 | tf_op jit(solution)/shard_map/forward/pallas_call | solution.py:80
  88.0 4.7 %collective-permute-done.12.b_ref.out_ref = s16[528,768]{1,0:T(8,128)(2,1)S(1)} collective-permute-done((s16[528,768]{1,0:T(8,128)(2,1)S(1)}, s16[528,768]{1,0:T(8,128)(2,1)S(1)}, u32[]{:S(2)}, u32[]{:S(2)}) %collective-permute-start.12) | collective-permute-done | bytes 811040 | tf_op jit(solution)/shard_map/ppermute | solution.py:309
  92.7 0.8 add.10.own_ref
  93.5 0.7 collective-permute-start.15
  94.5 3.5 %weight_grads.6 = (bf16[128,2048]{1,0:T(8,128)(2,1)}, f32[2048,2048]{1,0:T(8,128)}, f32[2048,2048]{1,0:T(8,128)}) custom-call(s32[7]{0:T(128)S(1)} %stack.35.place_ref, s32[16,16]{1,0:T(8,128)S(1)} %copy-done.3, bf16[2048,512]{1,0:T(8,128)(2,1)S(1)} %turn.1.turned_ref, bf16[512,2048]{1,0:T(8,128)(2,1)S(1)} %pad_maximum_fusion.back_ref, ...), custom_call_target="tpu_custom_call" | custom-call | flops 1000000 | bytes 2500 | tf_op jit(solution)/shard_map/weight_grads/pallas_call | solution.py:242
  98.0 1.5 reply.8
  99.5 4.3 %collective-permute-start.16 = (s16[528,768]{1,0:T(8,128)(2,1)}, s16[528,768]{1,0:T(8,128)(2,1)S(1)}, u32[]{:S(2)}, u32[]{:S(2)}) collective-permute-start(s16[528,768]{1,0:T(8,128)(2,1)} %reply.8), channel_id=1, source_target_pairs={{0,8},{8,0},{16,24},{24,16},{1,9},{9,1},{17,25},{25,17},{2,10},{10... | collective-permute-start | bytes 2433032 | tf_op jit(solution)/shard_map/ppermute | solution.py:309
  103.9 6.2 %collective-permute-done.14.b_ref.out_ref = s16[528,768]{1,0:T(8,128)(2,1)S(1)} collective-permute-done((s16[528,768]{1,0:T(8,128)(2,1)}, s16[528,768]{1,0:T(8,128)(2,1)S(1)}, u32[]{:S(2)}, u32[]{:S(2)}) %collective-permute-start.14) | collective-permute-done | bytes 811040 | tf_op jit(solution)/shard_map/ppermute | solution.py:309
  110.7 0.7 collective-permute-start.17
  111.4 6.6 %weight_grads.7 = (bf16[128,2048]{1,0:T(8,128)(2,1)}, f32[2048,2048]{1,0:T(8,128)}, f32[2048,2048]{1,0:T(8,128)}) custom-call(s32[7]{0:T(128)S(1)} %stack.35.place_ref, s32[16,16]{1,0:T(8,128)S(1)} %copy-done.3, bf16[2048,512]{1,0:T(8,128)(2,1)S(1)} %turn.1.turned_ref, ...), custom_call_target="tpu_custom_call", output_to_operand_aliasing={{0}: (7, {}), {1}: (8, {}), {2}: (9, {})} | custom-call | flops 1000000 | bytes 2500 | tf_op jit(solution)/shard_map/weight_grads/pallas_call | solution.py:242
  118.6 1.3 collective-permute-start.18
  119.9 7.6 %collective-permute-done.16.b_ref.out_ref = s16[528,768]{1,0:T(8,128)(2,1)S(1)} collective-permute-done((s16[528,768]{1,0:T(8,128)(2,1)}, s16[528,768]{1,0:T(8,128)(2,1)S(1)}, u32[]{:S(2)}, u32[]{:S(2)}) %collective-permute-start.16) | collective-permute-done | bytes 811040 | tf_op jit(solution)/shard_map/ppermute | solution.py:309
  128.0 0.7 collective-permute-start.19
  128.8 6.9 %weight_grads.8 = (bf16[128,2048]{1,0:T(8,128)(2,1)}, f32[2048,2048]{1,0:T(8,128)}, f32[2048,2048]{1,0:T(8,128)}) custom-call(s32[7]{0:T(128)S(1)} %stack.35.place_ref, s32[16,16]{1,0:T(8,128)S(1)} %copy-done.3, bf16[2048,512]{1,0:T(8,128)(2,1)S(1)} %turn.1.turned_ref, ...), custom_call_target="tpu_custom_call", output_to_operand_aliasing={{0}: (7, {}), {1}: (8, {}), {2}: (9, {})} | custom-call | flops 1000000 | bytes 2500 | tf_op jit(solution)/shard_map/weight_grads/pallas_call | solution.py:242
  136.2 1.3 collective-permute-start.20
  137.5 7.3 %collective-permute-done.18.out_ref = s16[528,768]{1,0:T(8,128)(2,1)S(1)} collective-permute-done((s16[528,768]{1,0:T(8,128)(2,1)S(1)}, s16[528,768]{1,0:T(8,128)(2,1)S(1)}, u32[]{:S(2)}, u32[]{:S(2)}) %collective-permute-start.18) | collective-permute-done | bytes 811040 | tf_op jit(solution)/shard_map/ppermute | solution.py:300
  144.8 6.6 %weight_grads.9 = (bf16[128,2048]{1,0:T(8,128)(2,1)}, f32[2048,2048]{1,0:T(8,128)}, f32[2048,2048]{1,0:T(8,128)}) custom-call(s32[7]{0:T(128)S(1)} %stack.35.place_ref, s32[16,16]{1,0:T(8,128)S(1)} %copy-done.3, bf16[2048,512]{1,0:T(8,128)(2,1)S(1)} %turn.1.turned_ref, ...), custom_call_target="tpu_custom_call", output_to_operand_aliasing={{0}: (7, {}), {1}: (8, {}), {2}: (9, {})} | custom-call | flops 1000000 | bytes 2500 | tf_op jit(solution)/shard_map/weight_grads/pallas_call | solution.py:242
  152.0 1.5 collective-permute-start.21
  153.5 8.7 %collective-permute-done.20.out_ref = s16[528,768]{1,0:T(8,128)(2,1)S(1)} collective-permute-done((s16[528,768]{1,0:T(8,128)(2,1)S(1)}, s16[528,768]{1,0:T(8,128)(2,1)S(1)}, u32[]{:S(2)}, u32[]{:S(2)}) %collective-permute-start.20) | collective-permute-done | bytes 811040 | tf_op jit(solution)/shard_map/ppermute | solution.py:300
  162.2 6.6 %weight_grads.10 = (bf16[128,2048]{1,0:T(8,128)(2,1)}, f32[2048,2048]{1,0:T(8,128)}, f32[2048,2048]{1,0:T(8,128)}) custom-call(s32[7]{0:T(128)S(1)} %stack.35.place_ref, s32[16,16]{1,0:T(8,128)S(1)} %copy-done.3, bf16[2048,512]{1,0:T(8,128)(2,1)S(1)} %turn.1.turned_ref, ...), custom_call_target="tpu_custom_call", output_to_operand_aliasing={{0}: (7, {}), {1}: (8, {}), {2}: (9, {})} | custom-call | flops 1000000 | bytes 2500 | tf_op jit(solution)/shard_map/weight_grads/pallas_call | solution.py:242
  168.8 9.8 %collective-permute-done.21.out_ref = s16[528,768]{1,0:T(8,128)(2,1)S(1)} collective-permute-done((s16[528,768]{1,0:T(8,128)(2,1)S(1)}, s16[528,768]{1,0:T(8,128)(2,1)S(1)}, u32[]{:S(2)}, u32[]{:S(2)}) %collective-permute-start.21) | collective-permute-done | bytes 811040 | tf_op jit(solution)/shard_map/ppermute | solution.py:300
  178.5 6.5 %weight_grads.11 = (bf16[128,2048]{1,0:T(8,128)(2,1)}, f32[2048,2048]{1,0:T(8,128)}, f32[2048,2048]{1,0:T(8,128)}) custom-call(s32[7]{0:T(128)S(1)} %stack.35.place_ref, s32[16,16]{1,0:T(8,128)S(1)} %copy-done.3, bf16[2048,512]{1,0:T(8,128)(2,1)S(1)} %turn.1.turned_ref, ...), custom_call_target="tpu_custom_call", output_to_operand_aliasing={{0}: (7, {}), {1}: (8, {}), {2}: (9, {})} | custom-call | flops 1000000 | bytes 2500 | tf_op jit(solution)/shard_map/weight_grads/pallas_call | solution.py:242
  (40 shorter events, 6.4 us)
Async XLA Ops:
  0.6 21.7 %copy-start.3 = (s32[16,16]{1,0:T(8,128)S(1)}, s32[16,16]{1,0:T(8,128)}, u32[]{:S(2)}) copy-start(s32[16,16]{1,0:T(8,128)} %mask_ref.23) | copy-start | bytes 3076
  0.6 19.0 %collective-permute-start.3 = (bf16[128,2048]{1,0:T(8,128)(2,1)}, bf16[128,2048]{1,0:T(8,128)(2,1)S(1)}, u32[]{:S(2)}, u32[]{:S(2)}) collective-permute-start(bf16[128,2048]{1,0:T(8,128)(2,1)} %param.9), channel_id=1, source_target_pairs={{0,8},{8,0},{16,24},{24,16},{1,9},{9,1},{17,25},{25,17},{2,10},{10... | collective-permute-start | bytes 1572872 | tf_op jit(solution)/shard_map/ppermute | solution.py:309
  3.7 9.4 %collective-permute-start = (bf16[64,2048]{1,0:T(8,128)(2,1)}, bf16[64,2048]{1,0:T(8,128)(2,1)S(1)}, u32[]{:S(2)}, u32[]{:S(2)}) collective-permute-start(bf16[64,2048]{1,0:T(8,128)(2,1)} %param.5), channel_id=1, source_target_pairs={{0,2},{1,3},{2,0},{3,1},{4,6},{5,7},{6,4},{7,5},{8,10},{9,11},{10,... | collective-permute-start | bytes 786440 | tf_op jit(solution)/shard_map/ppermute | solution.py:278
  5.2 13.3 %collective-permute-start.1 = (bf16[64,2048]{1,0:T(8,128)(2,1)}, bf16[64,2048]{1,0:T(8,128)(2,1)S(1)}, u32[]{:S(2)}, u32[]{:S(2)}) collective-permute-start(bf16[64,2048]{1,0:T(8,128)(2,1)} %param.5), channel_id=1, source_target_pairs={{0,4},{1,5},{2,6},{3,7},{4,0},{5,1},{6,2},{7,3},{8,12},{9,13},{10,... | collective-permute-start | bytes 786440 | tf_op jit(solution)/shard_map/ppermute | solution.py:278
  6.7 11.8 %collective-permute-start.2 = (bf16[64,2048]{1,0:T(8,128)(2,1)}, bf16[64,2048]{1,0:T(8,128)(2,1)S(1)}, u32[]{:S(2)}, u32[]{:S(2)}) collective-permute-start(bf16[64,2048]{1,0:T(8,128)(2,1)} %param.5), channel_id=1, source_target_pairs={{0,6},{1,7},{2,4},{3,5},{4,2},{5,3},{6,0},{7,1},{8,14},{9,15},{10,... | collective-permute-start | bytes 786440 | tf_op jit(solution)/shard_map/ppermute | solution.py:278
  19.6 5.5 %copy-start.5 = (bf16[128,2048]{1,0:T(8,128)(2,1)}, bf16[128,2048]{1,0:T(8,128)(2,1)S(1)}, u32[]{:S(2)}) copy-start(bf16[128,2048]{1,0:T(8,128)(2,1)S(1)} %collective-permute-done.3) | copy-start | bytes 1572868
  19.6 2.7 %collective-permute-start.4 = (bf16[256,2048]{1,0:T(8,128)(2,1)S(1)}, bf16[256,2048]{1,0:T(8,128)(2,1)S(1)}, u32[]{:S(2)}, u32[]{:S(2)}) collective-permute-start(bf16[256,2048]{1,0:T(8,128)(2,1)S(1)} %pad_maximum_fusion.1.low_ref), channel_id=1, source_target_pairs={{0,1},{1,0},{2,3},{3,2},{4,5},{5,4},{6,7},{7,6},{8,9},{9,8},{10,11... | collective-permute-start | bytes 3145736 | tf_op jit(solution)/shard_map/ppermute | solution.py:280
  20.9 24.0 %collective-permute-start.6 = (bf16[256,2048]{1,0:T(8,128)(2,1)S(1)}, bf16[256,2048]{1,0:T(8,128)(2,1)S(1)}, u32[]{:S(2)}, u32[]{:S(2)}) collective-permute-start(bf16[256,2048]{1,0:T(8,128)(2,1)S(1)} %pad_maximum_fusion.2), channel_id=1, source_target_pairs={{8,16},{16,8},{9,17},{17,9},{10,18},{18,10},{11,19},{19,11},{12,20... | collective-permute-start | bytes 3145736 | tf_op jit(solution)/shard_map/ppermute | solution.py:306
  25.1 18.5 %collective-permute-start.5 = (s16[528,256]{1,0:T(8,128)(2,1)S(1)}, s16[528,256]{1,0:T(8,128)(2,1)S(1)}, u32[]{:S(2)}, u32[]{:S(2)}) collective-permute-start(s16[528,256]{1,0:T(8,128)(2,1)S(1)} %forward.6.a_ref), channel_id=1, source_target_pairs={{0,8},{24,16},{1,9},{25,17},{2,10},{26,18},{3,11},{27,19},{4,12},{... | collective-permute-start | bytes 811016 | tf_op jit(solution)/shard_map/ppermute | solution.py:303
  35.8 22.6 %collective-permute-start.7 = (s16[528,768]{1,0:T(8,128)(2,1)S(1)}, s16[528,768]{1,0:T(8,128)(2,1)S(1)}, u32[]{:S(2)}, u32[]{:S(2)}) collective-permute-start(s16[528,768]{1,0:T(8,128)(2,1)S(1)} %forward.7.a_ref), channel_id=1, source_target_pairs={{0,8},{24,16},{1,9},{25,17},{2,10},{26,18},{3,11},{27,19},{4,12},{... | collective-permute-start | bytes 2433032 | tf_op jit(solution)/shard_map/ppermute | solution.py:303
  44.2 15.5 %collective-permute-start.8 = (s16[528,256]{1,0:T(8,128)(2,1)S(1)}, s16[528,256]{1,0:T(8,128)(2,1)S(1)}, u32[]{:S(2)}, u32[]{:S(2)}) collective-permute-start(s16[528,256]{1,0:T(8,128)(2,1)S(1)} %add.7.own_ref), channel_id=1, source_target_pairs={{8,16},{16,8},{9,17},{17,9},{10,18},{18,10},{11,19},{19,11},{12,20... | collective-permute-start | bytes 811016 | tf_op jit(solution)/shard_map/ppermute | solution.py:306
  44.9 43.1 %collective-permute-start.11 = (bf16[256,2048]{1,0:T(8,128)(2,1)S(1)}, bf16[256,2048]{1,0:T(8,128)(2,1)S(1)}, u32[]{:S(2)}, u32[]{:S(2)}) collective-permute-start(bf16[256,2048]{1,0:T(8,128)(2,1)S(1)} %collective-permute-done.6), channel_id=1, source_target_pairs={{8,0},{16,24},{9,1},{17,25},{10,2},{18,26},{11,3},{19,27},{12,4},{... | collective-permute-start | bytes 3145736 | tf_op jit(solution)/shard_map/ppermute | solution.py:300
  46.2 26.6 %collective-permute-start.9 = (s16[528,768]{1,0:T(8,128)(2,1)S(1)}, s16[528,768]{1,0:T(8,128)(2,1)S(1)}, u32[]{:S(2)}, u32[]{:S(2)}) collective-permute-start(s16[528,768]{1,0:T(8,128)(2,1)S(1)} %forward.8.a_ref), channel_id=1, source_target_pairs={{0,8},{24,16},{1,9},{25,17},{2,10},{26,18},{3,11},{27,19},{4,12},{... | collective-permute-start | bytes 2433032 | tf_op jit(solution)/shard_map/ppermute | solution.py:303
  59.0 10.0 %copy-start.1 = (s16[528,768]{1,0:T(8,128)(2,1)}, s16[528,768]{1,0:T(8,128)(2,1)S(1)}, u32[]{:S(2)}) copy-start(s16[528,768]{1,0:T(8,128)(2,1)S(1)} %add.8.own_ref) | copy-start | bytes 2433028
  59.0 16.1 %collective-permute-start.10 = (s16[528,768]{1,0:T(8,128)(2,1)S(1)}, s16[528,768]{1,0:T(8,128)(2,1)S(1)}, u32[]{:S(2)}, u32[]{:S(2)}) collective-permute-start(s16[528,768]{1,0:T(8,128)(2,1)S(1)} %add.8.own_ref), channel_id=1, source_target_pairs={{8,16},{16,8},{9,17},{17,9},{10,18},{18,10},{11,19},{19,11},{12,20... | collective-permute-start | bytes 2433032 | tf_op jit(solution)/shard_map/ppermute | solution.py:306
  60.3 32.3 %collective-permute-start.12 = (s16[528,768]{1,0:T(8,128)(2,1)S(1)}, s16[528,768]{1,0:T(8,128)(2,1)S(1)}, u32[]{:S(2)}, u32[]{:S(2)}) collective-permute-start(s16[528,768]{1,0:T(8,128)(2,1)S(1)} %reply.6), channel_id=1, source_target_pairs={{0,8},{8,0},{16,24},{24,16},{1,9},{9,1},{17,25},{25,17},{2,10},{10... | collective-permute-start | bytes 2433032 | tf_op jit(solution)/shard_map/ppermute | solution.py:309
  74.3 23.7 %collective-permute-start.13 = (s16[528,768]{1,0:T(8,128)(2,1)}, s16[528,768]{1,0:T(8,128)(2,1)S(1)}, u32[]{:S(2)}, u32[]{:S(2)}) collective-permute-start(s16[528,768]{1,0:T(8,128)(2,1)} %add.9.own_ref), channel_id=1, source_target_pairs={{8,16},{16,8},{9,17},{17,9},{10,18},{18,10},{11,19},{19,11},{12,20... | collective-permute-start | bytes 2433032 | tf_op jit(solution)/shard_map/ppermute | solution.py:306
  76.6 33.5 %collective-permute-start.14 = (s16[528,768]{1,0:T(8,128)(2,1)}, s16[528,768]{1,0:T(8,128)(2,1)S(1)}, u32[]{:S(2)}, u32[]{:S(2)}) collective-permute-start(s16[528,768]{1,0:T(8,128)(2,1)} %reply.7), channel_id=1, source_target_pairs={{0,8},{8,0},{16,24},{24,16},{1,9},{9,1},{17,25},{25,17},{2,10},{10... | collective-permute-start | bytes 2433032 | tf_op jit(solution)/shard_map/ppermute | solution.py:309
  88.0 6.3 %copy-start.4 = (bf16[128,2048]{1,0:T(8,128)(2,1)S(1)}, bf16[128,2048]{1,0:T(8,128)(2,1)}, u32[]{:S(2)}) copy-start(bf16[128,2048]{1,0:T(8,128)(2,1)} %param.9) | copy-start | bytes 1572868
  88.0 6.3 %copy-start.6 = (bf16[128,2048]{1,0:T(8,128)(2,1)S(1)}, bf16[128,2048]{1,0:T(8,128)(2,1)}, u32[]{:S(2)}) copy-start(bf16[128,2048]{1,0:T(8,128)(2,1)} %copy-done.5) | copy-start | bytes 1572868
  93.5 24.5 %collective-permute-start.15 = (s16[528,768]{1,0:T(8,128)(2,1)S(1)}, s16[528,768]{1,0:T(8,128)(2,1)S(1)}, u32[]{:S(2)}, u32[]{:S(2)}) collective-permute-start(s16[528,768]{1,0:T(8,128)(2,1)S(1)} %add.10.own_ref), channel_id=1, source_target_pairs={{8,16},{16,8},{9,17},{17,9},{10,18},{18,10},{11,19},{19,11},{12,20... | collective-permute-start | bytes 2433032 | tf_op jit(solution)/shard_map/ppermute | solution.py:306
  94.5 5.1 %copy-start = (bf16[512,2048]{1,0:T(8,128)(2,1)}, bf16[512,2048]{1,0:T(8,128)(2,1)S(1)}, u32[]{:S(2)}) copy-start(bf16[512,2048]{1,0:T(8,128)(2,1)S(1)} %pad_maximum_fusion.back_ref) | copy-start | bytes 6291460
  98.0 13.3 %copy-start.2 = (s16[528,768]{1,0:T(8,128)(2,1)S(1)}, s16[528,768]{1,0:T(8,128)(2,1)}, u32[]{:S(2)}) copy-start(s16[528,768]{1,0:T(8,128)(2,1)} %copy-done.1) | copy-start | bytes 2433028
  99.5 27.9 %collective-permute-start.16 = (s16[528,768]{1,0:T(8,128)(2,1)}, s16[528,768]{1,0:T(8,128)(2,1)S(1)}, u32[]{:S(2)}, u32[]{:S(2)}) collective-permute-start(s16[528,768]{1,0:T(8,128)(2,1)} %reply.8), channel_id=1, source_target_pairs={{0,8},{8,0},{16,24},{24,16},{1,9},{9,1},{17,25},{25,17},{2,10},{10... | collective-permute-start | bytes 2433032 | tf_op jit(solution)/shard_map/ppermute | solution.py:309
  110.7 25.0 %collective-permute-start.17 = (s16[528,768]{1,0:T(8,128)(2,1)S(1)}, s16[528,768]{1,0:T(8,128)(2,1)S(1)}, u32[]{:S(2)}, u32[]{:S(2)}) collective-permute-start(s16[528,768]{1,0:T(8,128)(2,1)S(1)} %add.11.own_ref), channel_id=1, source_target_pairs={{8,16},{16,8},{9,17},{17,9},{10,18},{18,10},{11,19},{19,11},{12,20... | collective-permute-start | bytes 2433032 | tf_op jit(solution)/shard_map/ppermute | solution.py:306
  118.6 26.2 %collective-permute-start.18 = (s16[528,768]{1,0:T(8,128)(2,1)S(1)}, s16[528,768]{1,0:T(8,128)(2,1)S(1)}, u32[]{:S(2)}, u32[]{:S(2)}) collective-permute-start(s16[528,768]{1,0:T(8,128)(2,1)S(1)} %reply.9), channel_id=1, source_target_pairs={{8,0},{16,24},{9,1},{17,25},{10,2},{18,26},{11,3},{19,27},{12,4},{... | collective-permute-start | bytes 2433032 | tf_op jit(solution)/shard_map/ppermute | solution.py:300
  128.0 23.3 %collective-permute-start.19 = (s16[528,768]{1,0:T(8,128)(2,1)S(1)}, s16[528,768]{1,0:T(8,128)(2,1)S(1)}, u32[]{:S(2)}, u32[]{:S(2)}) collective-permute-start(s16[528,768]{1,0:T(8,128)(2,1)S(1)} %add.12.own_ref), channel_id=1, source_target_pairs={{8,16},{16,8},{9,17},{17,9},{10,18},{18,10},{11,19},{19,11},{12,20... | collective-permute-start | bytes 2433032 | tf_op jit(solution)/shard_map/ppermute | solution.py:306
  136.2 26.0 %collective-permute-start.20 = (s16[528,768]{1,0:T(8,128)(2,1)S(1)}, s16[528,768]{1,0:T(8,128)(2,1)S(1)}, u32[]{:S(2)}, u32[]{:S(2)}) collective-permute-start(s16[528,768]{1,0:T(8,128)(2,1)S(1)} %reply.10), channel_id=1, source_target_pairs={{8,0},{16,24},{9,1},{17,25},{10,2},{18,26},{11,3},{19,27},{12,4},{... | collective-permute-start | bytes 2433032 | tf_op jit(solution)/shard_map/ppermute | solution.py:300
  152.0 26.6 %collective-permute-start.21 = (s16[528,768]{1,0:T(8,128)(2,1)S(1)}, s16[528,768]{1,0:T(8,128)(2,1)S(1)}, u32[]{:S(2)}, u32[]{:S(2)}) collective-permute-start(s16[528,768]{1,0:T(8,128)(2,1)S(1)} %reply.11), channel_id=1, source_target_pairs={{8,0},{16,24},{9,1},{17,25},{10,2},{18,26},{11,3},{19,27},{12,4},{... | collective-permute-start | bytes 2433032 | tf_op jit(solution)/shard_map/ppermute | solution.py:300

commit v7 on v6

--- a/solution.py
+++ b/solution.py
@@ -9,7 +9,7 @@
 
 BLOCK = 128
 GROUPS = 16
-CHUNK = 3
+CHUNK = 2
 AHEAD = 3
 LAG = 3
 EARLY, LATE, TURN = 8000, 1, 8000
@@ -355,7 +355,7 @@
     ahead = min(AHEAD, chunks)
     run_forward(0)
     arrived.append(inward(own[0], 0))
-    half = jnp.concatenate([hidden_grad, *pair], axis=0)
+    half = jnp.concatenate([tie(hidden_grad, place), *pair], axis=0)
     other_half = swap(half)
     for c in range(1, ahead):
         run_forward(c)
@@ -374,17 +374,22 @@
             across.append(swap(sums[s]))
         if s == 0:
             moved = outward(tie(other_half, place), 0)
+        def weights_of(s):
+            c = s - LAG
+            run_weights(c, (sums[c], across[c], arrived[s]), back)
+
         if s == LAG:
             far_half = pick(distance == 0, *lax.optimization_barrier((other_half, moved, place))[:2])
             back = jnp.concatenate([half, far_half], axis=0)
-        if s >= LAG:
-            c = s - LAG
-            run_weights(c, (sums[c], across[c], arrived[s]), back)
+        if LAG <= s < chunks - 1:
+            weights_of(s)
         c = s - 1
         if 0 <= c < chunks:
             both_ways = c + LAG < chunks
             message = ordered(reply, own[c], across[c], own[c + LAG] if both_ways else own[c])
             arrived.append(exchange(message) if both_ways else outward(message, 0))
+        if s >= max(LAG, chunks - 1):
+            weights_of(s)
         if s + ahead < chunks:
             run_forward(s + ahead)
     return tuple(outs)

time: 186 us -> 184 us (0.989)
  waiting for transfers between devices: 60.1 us -> 39.6 us
  starting transfers between devices: 45.4 us -> 60.6 us
  Pallas kernels: 76 us -> 79.1 us
    ppermute x4 -> x6, waiting for transfers between devices: 18.4 us -> 5.32 us  [exchange(): return lax.ppermute(value, 'row', [(i, i ^ 1) for i in range(ring)])]
    ppermute x4, waiting for transfers between devices: 25.8 us -> 17.3 us  [outward(): lax.ppermute(value, 'row', [(left - hop, left - hop - 1), (right + hop, r...]
    ppermute x3, starting transfers between devices: 14 us -> 21 us  [inward(): lax.ppermute(value, 'row', [(left - hop - 1, left - hop), (right + hop +...]
    ppermute x4 -> x6, starting transfers between devices: 17.4 us -> 24.4 us  [exchange(): return lax.ppermute(value, 'row', [(i, i ^ 1) for i in range(ring)])]
    pallas_call x6 -> x8, Pallas kernels: 27.8 us -> 30.5 us  [forward(): pl.pallas_call(functools.partial(forward_kernel, first=start // BLOCK), g...]
    ppermute x1, waiting for transfers between devices: 0.66 us -> 2.53 us  [gather_tokens(): lax.ppermute(mine, 'col', [(i, i ^ 1) for i in range(devices)])]
    ppermute x7 -> x9, starting transfers between devices: 4.96 us -> 6.47 us  [swap(): return lax.ppermute(value, 'row', [(left, right), (right, left)])]
    pallas_call x6 -> x8, Pallas kernels: 5.41 us -> 5.7 us  [reply(): pl.pallas_call(reply_kernel, grid_spec=pltpu.PrefetchScalarGridSpec(num_s...]
  transfers between devices with their start and end apart: 22 -> 26, of which waited for: 10 -> 9; matrix products, arithmetic and copies ran while one was open for 1% -> 1% of each run, Pallas kernels for 38% -> 39%
where the time goes in v7:
time: 184 us; the launch traced here: 183 us
  Pallas kernels  79.1 us (43%)
  starting transfers between devices  60.6 us (33%)
  waiting for transfers between devices  39.6 us (22%)
    pallas_call x8, Pallas kernels, weight_grads(): pl.pallas_call(functools.partial(weights_kernel, first=first, devices=dev...  36.8 us
    pallas_call x8, Pallas kernels, forward(): pl.pallas_call(functools.partial(forward_kernel, first=start // BLOCK), g...  30.5 us
    ppermute x6, starting transfers between devices, exchange(): return lax.ppermute(value, 'row', [(i, i ^ 1) for i in range(ring)])  24.4 us
    ppermute x3, starting transfers between devices, inward(): lax.ppermute(value, 'row', [(left - hop - 1, left - hop), (right + hop +...  21 us
    ppermute x4, waiting for transfers between devices, outward(): lax.ppermute(value, 'row', [(left - hop, left - hop - 1), (right + hop, r...  17.3 us
    ppermute x3, waiting for transfers between devices, gather_tokens(): lax.ppermute(tokens, 'col', [(i, i ^ other) for i in range(devices)])  11.3 us
    ppermute x9, starting transfers between devices, swap(): return lax.ppermute(value, 'row', [(left, right), (right, left)])  6.47 us
    pallas_call x8, Pallas kernels, reply(): pl.pallas_call(reply_kernel, grid_spec=pltpu.PrefetchScalarGridSpec(num_s...  5.7 us
  transfers between devices with their start and end apart: 26, of which 9 were waited for; matrix products, arithmetic and copies ran while one was open for 1% of the time, Pallas kernels for 39%

profile of v7, /device:TPU:0, one launch (start us, length us, event | category | flops | bytes accessed | tf_op | source)
XLA Modules:
  0.0 182.8 jit_solution(2213571329408125175)
XLA Ops:
  0.6 3.1 %collective-permute-start.3 = (bf16[128,2048]{1,0:T(8,128)(2,1)}, bf16[128,2048]{1,0:T(8,128)(2,1)S(1)}, u32[]{:S(2)}, u32[]{:S(2)}) collective-permute-start(bf16[128,2048]{1,0:T(8,128)(2,1)} %param.9), channel_id=1, source_target_pairs={{0,8},{8,0},{16,24},{24,16},{1,9},{9,1},{17,25},{25,17},{2,10},{10... | collective-permute-start | bytes 1572872 | tf_op jit(solution)/shard_map/ppermute | solution.py:309
  3.7 1.5 collective-permute-start
  5.2 1.5 collective-permute-start.1
  7.2 6.0 %collective-permute-done = bf16[64,2048]{1,0:T(8,128)(2,1)S(1)} collective-permute-done((bf16[64,2048]{1,0:T(8,128)(2,1)}, bf16[64,2048]{1,0:T(8,128)(2,1)S(1)}, u32[]{:S(2)}, u32[]{:S(2)}) %collective-permute-start) | collective-permute-done | bytes 262176 | tf_op jit(solution)/shard_map/ppermute | solution.py:278
  13.2 5.4 %collective-permute-done.1 = bf16[64,2048]{1,0:T(8,128)(2,1)S(1)} collective-permute-done((bf16[64,2048]{1,0:T(8,128)(2,1)}, bf16[64,2048]{1,0:T(8,128)(2,1)S(1)}, u32[]{:S(2)}, u32[]{:S(2)}) %collective-permute-start.1) | collective-permute-done | bytes 262176 | tf_op jit(solution)/shard_map/ppermute | solution.py:278
  18.5 1.0 pad_maximum_fusion.1.low_ref
  19.8 2.5 %collective-permute-done.4.high_ref = bf16[256,2048]{1,0:T(8,128)(2,1)S(1)} collective-permute-done((bf16[256,2048]{1,0:T(8,128)(2,1)S(1)}, bf16[256,2048]{1,0:T(8,128)(2,1)S(1)}, u32[]{:S(2)}, u32[]{:S(2)}) %collective-permute-start.4) | collective-permute-done | bytes 1048608 | tf_op jit(solution)/shard_map/ppermute | solution.py:280
  22.3 0.7 copy-done.4
  23.0 3.8 %forward.8.a_ref = s16[528,512]{1,0:T(8,128)(2,1)S(1)} custom-call(s32[7]{0:T(128)S(1)} %stack.35.place_ref, s32[16,16]{1,0:T(8,128)S(1)} %copy-done.4, bf16[256,2048]{1,0:T(8,128)(2,1)S(1)} %pad_maximum_fusion.1.low_ref, bf16[256,2048]{1,0:T(8,128)(2,1)S(1)} %collective-permute-done.4.high_ref, bf16[2048,2048]{1,0:T(8,128)(2,1)} %gate_ref.15, ...), custom_call_target="tpu_custom_call" | custom-call | flops 8000000000 | bytes 20000000 | tf_op jit(solution)/shard_map/forward/pallas_call | solution.py:80
  26.8 2.4 %collective-permute-start.5 = (s16[528,512]{1,0:T(8,128)(2,1)S(1)}, s16[528,512]{1,0:T(8,128)(2,1)S(1)}, u32[]{:S(2)}, u32[]{:S(2)}) collective-permute-start(s16[528,512]{1,0:T(8,128)(2,1)S(1)} %forward.8.a_ref), channel_id=1, source_target_pairs={{0,8},{24,16},{1,9},{25,17},{2,10},{26,18},{3,11},{27,19},{4,12},{... | collective-permute-start | bytes 1622024 | tf_op jit(solution)/shard_map/ppermute | solution.py:303
  29.3 0.7 collective-permute-start.6
  30.1 3.8 %forward.9.a_ref = s16[528,512]{1,0:T(8,128)(2,1)S(1)} custom-call(s32[7]{0:T(128)S(1)} %stack.35.place_ref, s32[16,16]{1,0:T(8,128)S(1)} %copy-done.4, bf16[256,2048]{1,0:T(8,128)(2,1)S(1)} %pad_maximum_fusion.1.low_ref, bf16[256,2048]{1,0:T(8,128)(2,1)S(1)} %collective-permute-done.4.high_ref, bf16[2048,2048]{1,0:T(8,128)(2,1)} %gate_ref.15, ...), custom_call_target="tpu_custom_call" | custom-call | flops 8000000000 | bytes 20000000 | tf_op jit(solution)/shard_map/forward/pallas_call | solution.py:80
  33.9 5.2 %collective-permute-start.7 = (s16[528,512]{1,0:T(8,128)(2,1)S(1)}, s16[528,512]{1,0:T(8,128)(2,1)S(1)}, u32[]{:S(2)}, u32[]{:S(2)}) collective-permute-start(s16[528,512]{1,0:T(8,128)(2,1)S(1)} %forward.9.a_ref), channel_id=1, source_target_pairs={{0,8},{24,16},{1,9},{25,17},{2,10},{26,18},{3,11},{27,19},{4,12},{... | collective-permute-start | bytes 1622024 | tf_op jit(solution)/shard_map/ppermute | solution.py:303
  39.1 3.8 %forward.10.a_ref = s16[528,512]{1,0:T(8,128)(2,1)S(1)} custom-call(s32[7]{0:T(128)S(1)} %stack.35.place_ref, s32[16,16]{1,0:T(8,128)S(1)} %copy-done.4, bf16[256,2048]{1,0:T(8,128)(2,1)S(1)} %pad_maximum_fusion.1.low_ref, bf16[256,2048]{1,0:T(8,128)(2,1)S(1)} %collective-permute-done.4.high_ref, bf16[2048,2048]{1,0:T(8,128)(2,1)} %gate_ref.15, ...), custom_call_target="tpu_custom_call" | custom-call | flops 1000000 | bytes 2500 | tf_op jit(solution)/shard_map/forward/pallas_call | solution.py:80
  42.9 1.5 turn.1.turned_ref
  45.0 0.7 collective-permute-start.8
  45.7 1.3 collective-permute-start.11
  47.1 3.8 %forward.11.next_ref.a_ref = s16[528,512]{1,0:T(8,128)(2,1)S(1)} custom-call(s32[7]{0:T(128)S(1)} %stack.35.place_ref, s32[16,16]{1,0:T(8,128)S(1)} %copy-done.5, bf16[256,2048]{1,0:T(8,128)(2,1)S(1)} %pad_maximum_fusion.1.low_ref, bf16[256,2048]{1,0:T(8,128)(2,1)S(1)} %collective-permute-done.4.high_ref, bf16[2048,2048]{1,0:T(8,128)(2,1)} %gate_ref.15, ...), custom_call_target="tpu_custom_call" | custom-call | flops 1000000 | bytes 2500 | tf_op jit(solution)/shard_map/forward/pallas_call | solution.py:80
  50.9 13.5 %collective-permute-start.9 = (s16[528,512]{1,0:T(8,128)(2,1)S(1)}, s16[528,512]{1,0:T(8,128)(2,1)S(1)}, u32[]{:S(2)}, u32[]{:S(2)}) collective-permute-start(s16[528,512]{1,0:T(8,128)(2,1)S(1)} %forward.10.a_ref), channel_id=1, source_target_pairs={{0,8},{24,16},{1,9},{25,17},{2,10},{26,18},{3,11},{27,19},{4,12},{... | collective-permute-start | bytes 1622024 | tf_op jit(solution)/shard_map/ppermute | solution.py:303
  66.3 3.8 %collective-permute-start.12 = (s16[528,512]{1,0:T(8,128)(2,1)S(1)}, s16[528,512]{1,0:T(8,128)(2,1)S(1)}, u32[]{:S(2)}, u32[]{:S(2)}) collective-permute-start(s16[528,512]{1,0:T(8,128)(2,1)S(1)} %reply.8), channel_id=1, source_target_pairs={{0,8},{8,0},{16,24},{24,16},{1,9},{9,1},{17,25},{25,17},{2,10},{10... | collective-permute-start | bytes 1622024 | tf_op jit(solution)/shard_map/ppermute | solution.py:309
  70.0 3.8 %forward.12.next_ref.a_ref = s16[528,512]{1,0:T(8,128)(2,1)S(1)} custom-call(s32[7]{0:T(128)S(1)} %stack.35.place_ref, s32[16,16]{1,0:T(8,128)S(1)} %copy-done.5, bf16[256,2048]{1,0:T(8,128)(2,1)S(1)} %pad_maximum_fusion.1.low_ref, bf16[256,2048]{1,0:T(8,128)(2,1)S(1)} %collective-permute-done.4.high_ref, bf16[2048,2048]{1,0:T(8,128)(2,1)} %gate_ref.15, ...), custom_call_target="tpu_custom_call" | custom-call | flops 1000000 | bytes 2500 | tf_op jit(solution)/shard_map/forward/pallas_call | solution.py:80
  73.9 3.2 %collective-permute-done.9.b_ref = s16[528,512]{1,0:T(8,128)(2,1)S(1)} collective-permute-done((s16[528,512]{1,0:T(8,128)(2,1)S(1)}, s16[528,512]{1,0:T(8,128)(2,1)S(1)}, u32[]{:S(2)}, u32[]{:S(2)}) %collective-permute-start.9) | collective-permute-done | bytes 540704 | tf_op jit(solution)/shard_map/ppermute | solution.py:303
  79.0 6.9 %collective-permute-start.14 = (s16[528,512]{1,0:T(8,128)(2,1)S(1)}, s16[528,512]{1,0:T(8,128)(2,1)S(1)}, u32[]{:S(2)}, u32[]{:S(2)}) collective-permute-start(s16[528,512]{1,0:T(8,128)(2,1)S(1)} %reply.9), channel_id=1, source_target_pairs={{0,8},{8,0},{16,24},{24,16},{1,9},{9,1},{17,25},{25,17},{2,10},{10... | collective-permute-start | bytes 1622024 | tf_op jit(solution)/shard_map/ppermute | solution.py:309
  85.8 3.8 %forward.13.next_ref.a_ref = s16[528,512]{1,0:T(8,128)(2,1)S(1)} custom-call(s32[7]{0:T(128)S(1)} %stack.35.place_ref, s32[16,16]{1,0:T(8,128)S(1)} %copy-done.5, bf16[256,2048]{1,0:T(8,128)(2,1)S(1)} %pad_maximum_fusion.1.low_ref, bf16[256,2048]{1,0:T(8,128)(2,1)S(1)} %collective-permute-done.4.high_ref, bf16[2048,2048]{1,0:T(8,128)(2,1)} %gate_ref.15, ...), custom_call_target="tpu_custom_call" | custom-call | flops 1000000 | bytes 2500 | tf_op jit(solution)/shard_map/forward/pallas_call | solution.py:80
  89.7 4.5 %collective-permute-done.12.b_ref.out_ref = s16[528,512]{1,0:T(8,128)(2,1)S(1)} collective-permute-done((s16[528,512]{1,0:T(8,128)(2,1)S(1)}, s16[528,512]{1,0:T(8,128)(2,1)S(1)}, u32[]{:S(2)}, u32[]{:S(2)}) %collective-permute-start.12) | collective-permute-done | bytes 540704 | tf_op jit(solution)/shard_map/ppermute | solution.py:309
  94.8 0.9 collective-permute-start.15
  95.9 4.6 %weight_grads.8 = (bf16[128,2048]{1,0:T(8,128)(2,1)}, f32[2048,2048]{1,0:T(8,128)}, f32[2048,2048]{1,0:T(8,128)}) custom-call(s32[7]{0:T(128)S(1)} %stack.35.place_ref, s32[16,16]{1,0:T(8,128)S(1)} %copy-done.5, bf16[2048,512]{1,0:T(8,128)(2,1)S(1)} %turn.1.turned_ref, bf16[512,2048]{1,0:T(8,128)(2,1)S(1)} %pad_maximum_fusion.back_ref, ...), custom_call_target="tpu_custom_call" | custom-call | flops 1000000 | bytes 2500 | tf_op jit(solution)/shard_map/weight_grads/pallas_call | solution.py:242
  100.5 1.4 reply.10
  101.9 3.9 %collective-permute-start.16 = (s16[528,512]{1,0:T(8,128)(2,1)}, s16[528,512]{1,0:T(8,128)(2,1)S(1)}, u32[]{:S(2)}, u32[]{:S(2)}) collective-permute-start(s16[528,512]{1,0:T(8,128)(2,1)} %reply.10), channel_id=1, source_target_pairs={{0,8},{8,0},{16,24},{24,16},{1,9},{9,1},{17,25},{25,17},{2,10},{10... | collective-permute-start | bytes 1622024 | tf_op jit(solution)/shard_map/ppermute | solution.py:309
  105.8 3.8 %forward.14.next_ref.a_ref = s16[528,512]{1,0:T(8,128)(2,1)S(1)} custom-call(s32[7]{0:T(128)S(1)} %stack.35.place_ref, s32[16,16]{1,0:T(8,128)S(1)} %copy-done.5, bf16[256,2048]{1,0:T(8,128)(2,1)S(1)} %pad_maximum_fusion.1.low_ref, bf16[256,2048]{1,0:T(8,128)(2,1)S(1)} %collective-permute-done.4.high_ref, bf16[2048,2048]{1,0:T(8,128)(2,1)} %gate_ref.15, ...), custom_call_target="tpu_custom_call" | custom-call | flops 1000000 | bytes 2500 | tf_op jit(solution)/shard_map/forward/pallas_call | solution.py:80
  111.0 4.6 %weight_grads.9 = (bf16[128,2048]{1,0:T(8,128)(2,1)}, f32[2048,2048]{1,0:T(8,128)}, f32[2048,2048]{1,0:T(8,128)}) custom-call(s32[7]{0:T(128)S(1)} %stack.35.place_ref, s32[16,16]{1,0:T(8,128)S(1)} %copy-done.5, bf16[2048,512]{1,0:T(8,128)(2,1)S(1)} %turn.1.turned_ref, ...), custom_call_target="tpu_custom_call", output_to_operand_aliasing={{0}: (7, {}), {1}: (8, {}), {2}: (9, {})} | custom-call | flops 1000000 | bytes 2500 | tf_op jit(solution)/shard_map/weight_grads/pallas_call | solution.py:242
  116.2 2.5 %collective-permute-start.18 = (s16[528,512]{1,0:T(8,128)(2,1)S(1)}, s16[528,512]{1,0:T(8,128)(2,1)S(1)}, u32[]{:S(2)}, u32[]{:S(2)}) collective-permute-start(s16[528,512]{1,0:T(8,128)(2,1)S(1)} %reply.11), channel_id=1, source_target_pairs={{0,8},{8,0},{16,24},{24,16},{1,9},{9,1},{17,25},{25,17},{2,10},{10... | collective-permute-start | bytes 1622024 | tf_op jit(solution)/shard_map/ppermute | solution.py:309
  118.7 3.8 %forward.15.next_ref.a_ref = s16[528,512]{1,0:T(8,128)(2,1)S(1)} custom-call(s32[7]{0:T(128)S(1)} %stack.35.place_ref, s32[16,16]{1,0:T(8,128)S(1)} %copy-done.5, bf16[256,2048]{1,0:T(8,128)(2,1)S(1)} %pad_maximum_fusion.1.low_ref, bf16[256,2048]{1,0:T(8,128)(2,1)S(1)} %collective-permute-done.4.high_ref, bf16[2048,2048]{1,0:T(8,128)(2,1)} %gate_ref.15, ...), custom_call_target="tpu_custom_call" | custom-call | flops 1000000 | bytes 2500 | tf_op jit(solution)/shard_map/forward/pallas_call | solution.py:80
  123.8 4.6 %weight_grads.10 = (bf16[128,2048]{1,0:T(8,128)(2,1)}, f32[2048,2048]{1,0:T(8,128)}, f32[2048,2048]{1,0:T(8,128)}) custom-call(s32[7]{0:T(128)S(1)} %stack.35.place_ref, s32[16,16]{1,0:T(8,128)S(1)} %copy-done.5, bf16[2048,512]{1,0:T(8,128)(2,1)S(1)} %turn.1.turned_ref, ...), custom_call_target="tpu_custom_call", output_to_operand_aliasing={{0}: (7, {}), {1}: (8, {}), {2}: (9, {})} | custom-call | flops 1000000 | bytes 2500 | tf_op jit(solution)/shard_map/weight_grads/pallas_call | solution.py:242
  129.0 4.2 %collective-permute-start.20 = (s16[528,512]{1,0:T(8,128)(2,1)S(1)}, s16[528,512]{1,0:T(8,128)(2,1)S(1)}, u32[]{:S(2)}, u32[]{:S(2)}) collective-permute-start(s16[528,512]{1,0:T(8,128)(2,1)S(1)} %reply.12), channel_id=1, source_target_pairs={{0,8},{8,0},{16,24},{24,16},{1,9},{9,1},{17,25},{25,17},{2,10},{10... | collective-permute-start | bytes 1622024 | tf_op jit(solution)/shard_map/ppermute | solution.py:309
  134.6 4.6 %weight_grads.11 = (bf16[128,2048]{1,0:T(8,128)(2,1)}, f32[2048,2048]{1,0:T(8,128)}, f32[2048,2048]{1,0:T(8,128)}) custom-call(s32[7]{0:T(128)S(1)} %stack.35.place_ref, s32[16,16]{1,0:T(8,128)S(1)} %copy-done.5, bf16[2048,512]{1,0:T(8,128)(2,1)S(1)} %turn.1.turned_ref, ...), custom_call_target="tpu_custom_call", output_to_operand_aliasing={{0}: (7, {}), {1}: (8, {}), {2}: (9, {})} | custom-call | flops 1000000 | bytes 2500 | tf_op jit(solution)/shard_map/weight_grads/pallas_call | solution.py:242
  139.8 0.8 collective-permute-done.20.b_ref.out_ref
  141.9 1.3 collective-permute-start.23
  143.2 0.8 reply.14
  144.0 1.3 collective-permute-start.24
  145.3 4.6 %weight_grads.12 = (bf16[128,2048]{1,0:T(8,128)(2,1)}, f32[2048,2048]{1,0:T(8,128)}, f32[2048,2048]{1,0:T(8,128)}) custom-call(s32[7]{0:T(128)S(1)} %stack.35.place_ref, s32[16,16]{1,0:T(8,128)S(1)} %copy-done.5, bf16[2048,512]{1,0:T(8,128)(2,1)S(1)} %turn.1.turned_ref, ...), custom_call_target="tpu_custom_call", output_to_operand_aliasing={{0}: (7, {}), {1}: (8, {}), {2}: (9, {})} | custom-call | flops 1000000 | bytes 2500 | tf_op jit(solution)/shard_map/weight_grads/pallas_call | solution.py:242
  150.5 1.3 collective-permute-start.25
  151.8 9.8 %collective-permute-done.23.out_ref = s16[528,512]{1,0:T(8,128)(2,1)S(1)} collective-permute-done((s16[528,512]{1,0:T(8,128)(2,1)S(1)}, s16[528,512]{1,0:T(8,128)(2,1)S(1)}, u32[]{:S(2)}, u32[]{:S(2)}) %collective-permute-start.23) | collective-permute-done | bytes 540704 | tf_op jit(solution)/shard_map/ppermute | solution.py:300
  161.6 4.6 %weight_grads.13 = (bf16[128,2048]{1,0:T(8,128)(2,1)}, f32[2048,2048]{1,0:T(8,128)}, f32[2048,2048]{1,0:T(8,128)}) custom-call(s32[7]{0:T(128)S(1)} %stack.35.place_ref, s32[16,16]{1,0:T(8,128)S(1)} %copy-done.5, bf16[2048,512]{1,0:T(8,128)(2,1)S(1)} %turn.1.turned_ref, ...), custom_call_target="tpu_custom_call", output_to_operand_aliasing={{0}: (7, {}), {1}: (8, {}), {2}: (9, {})} | custom-call | flops 1000000 | bytes 2500 | tf_op jit(solution)/shard_map/weight_grads/pallas_call | solution.py:242
  166.2 6.2 %collective-permute-done.24.out_ref = s16[528,512]{1,0:T(8,128)(2,1)S(1)} collective-permute-done((s16[528,512]{1,0:T(8,128)(2,1)S(1)}, s16[528,512]{1,0:T(8,128)(2,1)S(1)}, u32[]{:S(2)}, u32[]{:S(2)}) %collective-permute-start.24) | collective-permute-done | bytes 540704 | tf_op jit(solution)/shard_map/ppermute | solution.py:300
  172.4 4.6 %weight_grads.14 = (bf16[128,2048]{1,0:T(8,128)(2,1)}, f32[2048,2048]{1,0:T(8,128)}, f32[2048,2048]{1,0:T(8,128)}) custom-call(s32[7]{0:T(128)S(1)} %stack.35.place_ref, s32[16,16]{1,0:T(8,128)S(1)} %copy-done.5, bf16[2048,512]{1,0:T(8,128)(2,1)S(1)} %turn.1.turned_ref, ...), custom_call_target="tpu_custom_call", output_to_operand_aliasing={{0}: (7, {}), {1}: (8, {}), {2}: (9, {})} | custom-call | flops 1000000 | bytes 2500 | tf_op jit(solution)/shard_map/weight_grads/pallas_call | solution.py:242
  177.0 1.2 collective-permute-done.25.out_ref
  178.2 4.6 %weight_grads.15 = (bf16[128,2048]{1,0:T(8,128)(2,1)}, f32[2048,2048]{1,0:T(8,128)}, f32[2048,2048]{1,0:T(8,128)}) custom-call(s32[7]{0:T(128)S(1)} %stack.35.place_ref, s32[16,16]{1,0:T(8,128)S(1)} %copy-done.5, bf16[2048,512]{1,0:T(8,128)(2,1)S(1)} %turn.1.turned_ref, ...), custom_call_target="tpu_custom_call", output_to_operand_aliasing={{0}: (7, {}), {1}: (8, {}), {2}: (9, {})} | custom-call | flops 1000000 | bytes 2500 | tf_op jit(solution)/shard_map/weight_grads/pallas_call | solution.py:242
  (56 shorter events, 13.4 us)
Async XLA Ops:
  0.6 19.0 %collective-permute-start.3 = (bf16[128,2048]{1,0:T(8,128)(2,1)}, bf16[128,2048]{1,0:T(8,128)(2,1)S(1)}, u32[]{:S(2)}, u32[]{:S(2)}) collective-permute-start(bf16[128,2048]{1,0:T(8,128)(2,1)} %param.9), channel_id=1, source_target_pairs={{0,8},{8,0},{16,24},{24,16},{1,9},{9,1},{17,25},{25,17},{2,10},{10... | collective-permute-start | bytes 1572872 | tf_op jit(solution)/shard_map/ppermute | solution.py:309
  3.7 9.4 %collective-permute-start = (bf16[64,2048]{1,0:T(8,128)(2,1)}, bf16[64,2048]{1,0:T(8,128)(2,1)S(1)}, u32[]{:S(2)}, u32[]{:S(2)}) collective-permute-start(bf16[64,2048]{1,0:T(8,128)(2,1)} %param.5), channel_id=1, source_target_pairs={{0,2},{1,3},{2,0},{3,1},{4,6},{5,7},{6,4},{7,5},{8,10},{9,11},{10,... | collective-permute-start | bytes 786440 | tf_op jit(solution)/shard_map/ppermute | solution.py:278
  5.2 13.3 %collective-permute-start.1 = (bf16[64,2048]{1,0:T(8,128)(2,1)}, bf16[64,2048]{1,0:T(8,128)(2,1)S(1)}, u32[]{:S(2)}, u32[]{:S(2)}) collective-permute-start(bf16[64,2048]{1,0:T(8,128)(2,1)} %param.5), channel_id=1, source_target_pairs={{0,4},{1,5},{2,6},{3,7},{4,0},{5,1},{6,2},{7,3},{8,12},{9,13},{10,... | collective-permute-start | bytes 786440 | tf_op jit(solution)/shard_map/ppermute | solution.py:278
  6.7 11.8 %collective-permute-start.2 = (bf16[64,2048]{1,0:T(8,128)(2,1)}, bf16[64,2048]{1,0:T(8,128)(2,1)S(1)}, u32[]{:S(2)}, u32[]{:S(2)}) collective-permute-start(bf16[64,2048]{1,0:T(8,128)(2,1)} %param.5), channel_id=1, source_target_pairs={{0,6},{1,7},{2,4},{3,5},{4,2},{5,3},{6,0},{7,1},{8,14},{9,15},{10,... | collective-permute-start | bytes 786440 | tf_op jit(solution)/shard_map/ppermute | solution.py:278
  19.6 2.7 %collective-permute-start.4 = (bf16[256,2048]{1,0:T(8,128)(2,1)S(1)}, bf16[256,2048]{1,0:T(8,128)(2,1)S(1)}, u32[]{:S(2)}, u32[]{:S(2)}) collective-permute-start(bf16[256,2048]{1,0:T(8,128)(2,1)S(1)} %pad_maximum_fusion.1.low_ref), channel_id=1, source_target_pairs={{0,1},{1,0},{2,3},{3,2},{4,5},{5,4},{6,7},{7,6},{8,9},{9,8},{10,11... | collective-permute-start | bytes 3145736 | tf_op jit(solution)/shard_map/ppermute | solution.py:280
  22.3 0.7 copy-start.4
  23.0 6.2 %copy-start.6 = (bf16[128,2048]{1,0:T(8,128)(2,1)S(1)}, bf16[128,2048]{1,0:T(8,128)(2,1)}, u32[]{:S(2)}) copy-start(bf16[128,2048]{1,0:T(8,128)(2,1)} %param.9) | copy-start | bytes 1572868
  26.8 17.6 %collective-permute-start.5 = (s16[528,512]{1,0:T(8,128)(2,1)S(1)}, s16[528,512]{1,0:T(8,128)(2,1)S(1)}, u32[]{:S(2)}, u32[]{:S(2)}) collective-permute-start(s16[528,512]{1,0:T(8,128)(2,1)S(1)} %forward.8.a_ref), channel_id=1, source_target_pairs={{0,8},{24,16},{1,9},{25,17},{2,10},{26,18},{3,11},{27,19},{4,12},{... | collective-permute-start | bytes 1622024 | tf_op jit(solution)/shard_map/ppermute | solution.py:303
  29.3 16.4 %collective-permute-start.6 = (bf16[256,2048]{1,0:T(8,128)(2,1)S(1)}, bf16[256,2048]{1,0:T(8,128)(2,1)S(1)}, u32[]{:S(2)}, u32[]{:S(2)}) collective-permute-start(bf16[256,2048]{1,0:T(8,128)(2,1)S(1)} %pad_maximum_fusion.2), channel_id=1, source_target_pairs={{8,16},{16,8},{9,17},{17,9},{10,18},{18,10},{11,19},{19,11},{12,20... | collective-permute-start | bytes 3145736 | tf_op jit(solution)/shard_map/ppermute | solution.py:306
  33.9 30.5 %collective-permute-start.7 = (s16[528,512]{1,0:T(8,128)(2,1)S(1)}, s16[528,512]{1,0:T(8,128)(2,1)S(1)}, u32[]{:S(2)}, u32[]{:S(2)}) collective-permute-start(s16[528,512]{1,0:T(8,128)(2,1)S(1)} %forward.9.a_ref), channel_id=1, source_target_pairs={{0,8},{24,16},{1,9},{25,17},{2,10},{26,18},{3,11},{27,19},{4,12},{... | collective-permute-start | bytes 1622024 | tf_op jit(solution)/shard_map/ppermute | solution.py:303
  42.9 4.1 %copy-start.5 = (s32[16,16]{1,0:T(8,128)S(1)}, s32[16,16]{1,0:T(8,128)}, u32[]{:S(2)}) copy-start(s32[16,16]{1,0:T(8,128)} %mask_ref.31) | copy-start | bytes 3076
  45.0 20.6 %collective-permute-start.8 = (s16[528,512]{1,0:T(8,128)(2,1)S(1)}, s16[528,512]{1,0:T(8,128)(2,1)S(1)}, u32[]{:S(2)}, u32[]{:S(2)}) collective-permute-start(s16[528,512]{1,0:T(8,128)(2,1)S(1)} %add.9.own_ref), channel_id=1, source_target_pairs={{8,16},{16,8},{9,17},{17,9},{10,18},{18,10},{11,19},{19,11},{12,20... | collective-permute-start | bytes 1622024 | tf_op jit(solution)/shard_map/ppermute | solution.py:306
  45.7 43.9 %collective-permute-start.11 = (bf16[256,2048]{1,0:T(8,128)(2,1)S(1)}, bf16[256,2048]{1,0:T(8,128)(2,1)S(1)}, u32[]{:S(2)}, u32[]{:S(2)}) collective-permute-start(bf16[256,2048]{1,0:T(8,128)(2,1)S(1)} %collective-permute-done.6), channel_id=1, source_target_pairs={{8,0},{16,24},{9,1},{17,25},{10,2},{18,26},{11,3},{19,27},{12,4},{... | collective-permute-start | bytes 3145736 | tf_op jit(solution)/shard_map/ppermute | solution.py:300
  50.9 26.2 %collective-permute-start.9 = (s16[528,512]{1,0:T(8,128)(2,1)S(1)}, s16[528,512]{1,0:T(8,128)(2,1)S(1)}, u32[]{:S(2)}, u32[]{:S(2)}) collective-permute-start(s16[528,512]{1,0:T(8,128)(2,1)S(1)} %forward.10.a_ref), channel_id=1, source_target_pairs={{0,8},{24,16},{1,9},{25,17},{2,10},{26,18},{3,11},{27,19},{4,12},{... | collective-permute-start | bytes 1622024 | tf_op jit(solution)/shard_map/ppermute | solution.py:303
  65.0 13.4 %collective-permute-start.10 = (s16[528,512]{1,0:T(8,128)(2,1)S(1)}, s16[528,512]{1,0:T(8,128)(2,1)S(1)}, u32[]{:S(2)}, u32[]{:S(2)}) collective-permute-start(s16[528,512]{1,0:T(8,128)(2,1)S(1)} %add.10.own_ref), channel_id=1, source_target_pairs={{8,16},{16,8},{9,17},{17,9},{10,18},{18,10},{11,19},{19,11},{12,20... | collective-permute-start | bytes 1622024 | tf_op jit(solution)/shard_map/ppermute | solution.py:306
  66.3 27.9 %collective-permute-start.12 = (s16[528,512]{1,0:T(8,128)(2,1)S(1)}, s16[528,512]{1,0:T(8,128)(2,1)S(1)}, u32[]{:S(2)}, u32[]{:S(2)}) collective-permute-start(s16[528,512]{1,0:T(8,128)(2,1)S(1)} %reply.8), channel_id=1, source_target_pairs={{0,8},{8,0},{16,24},{24,16},{1,9},{9,1},{17,25},{25,17},{2,10},{10... | collective-permute-start | bytes 1622024 | tf_op jit(solution)/shard_map/ppermute | solution.py:309
  77.6 22.9 %collective-permute-start.13 = (s16[528,512]{1,0:T(8,128)(2,1)S(1)}, s16[528,512]{1,0:T(8,128)(2,1)S(1)}, u32[]{:S(2)}, u32[]{:S(2)}) collective-permute-start(s16[528,512]{1,0:T(8,128)(2,1)S(1)} %add.11.own_ref), channel_id=1, source_target_pairs={{8,16},{16,8},{9,17},{17,9},{10,18},{18,10},{11,19},{19,11},{12,20... | collective-permute-start | bytes 1622024 | tf_op jit(solution)/shard_map/ppermute | solution.py:306
  78.4 11.3 %copy-start.2 = (s16[528,512]{1,0:T(8,128)(2,1)}, s16[528,512]{1,0:T(8,128)(2,1)S(1)}, u32[]{:S(2)}) copy-start(s16[528,512]{1,0:T(8,128)(2,1)S(1)} %collective-permute-done.10.b_ref.across_ref) | copy-start | bytes 1622020
  79.0 30.7 %collective-permute-start.14 = (s16[528,512]{1,0:T(8,128)(2,1)S(1)}, s16[528,512]{1,0:T(8,128)(2,1)S(1)}, u32[]{:S(2)}, u32[]{:S(2)}) collective-permute-start(s16[528,512]{1,0:T(8,128)(2,1)S(1)} %reply.9), channel_id=1, source_target_pairs={{0,8},{8,0},{16,24},{24,16},{1,9},{9,1},{17,25},{25,17},{2,10},{10... | collective-permute-start | bytes 1622024 | tf_op jit(solution)/shard_map/ppermute | solution.py:309
  94.8 20.8 %collective-permute-start.15 = (s16[528,512]{1,0:T(8,128)(2,1)S(1)}, s16[528,512]{1,0:T(8,128)(2,1)S(1)}, u32[]{:S(2)}, u32[]{:S(2)}) collective-permute-start(s16[528,512]{1,0:T(8,128)(2,1)S(1)} %add.12.own_ref), channel_id=1, source_target_pairs={{8,16},{16,8},{9,17},{17,9},{10,18},{18,10},{11,19},{19,11},{12,20... | collective-permute-start | bytes 1622024 | tf_op jit(solution)/shard_map/ppermute | solution.py:306
  100.5 9.1 %copy-start = (s16[528,512]{1,0:T(8,128)(2,1)}, s16[528,512]{1,0:T(8,128)(2,1)S(1)}, u32[]{:S(2)}) copy-start(s16[528,512]{1,0:T(8,128)(2,1)S(1)} %collective-permute-done.13.b_ref.across_ref) | copy-start | bytes 1622020
  101.9 9.0 %copy-start.3 = (s16[528,512]{1,0:T(8,128)(2,1)S(1)}, s16[528,512]{1,0:T(8,128)(2,1)}, u32[]{:S(2)}) copy-start(s16[528,512]{1,0:T(8,128)(2,1)} %copy-done.2) | copy-start | bytes 1622020
  101.9 20.6 %collective-permute-start.16 = (s16[528,512]{1,0:T(8,128)(2,1)}, s16[528,512]{1,0:T(8,128)(2,1)S(1)}, u32[]{:S(2)}, u32[]{:S(2)}) collective-permute-start(s16[528,512]{1,0:T(8,128)(2,1)} %reply.10), channel_id=1, source_target_pairs={{0,8},{8,0},{16,24},{24,16},{1,9},{9,1},{17,25},{25,17},{2,10},{10... | collective-permute-start | bytes 1622024 | tf_op jit(solution)/shard_map/ppermute | solution.py:309
  110.2 18.2 %collective-permute-start.17 = (s16[528,512]{1,0:T(8,128)(2,1)S(1)}, s16[528,512]{1,0:T(8,128)(2,1)S(1)}, u32[]{:S(2)}, u32[]{:S(2)}) collective-permute-start(s16[528,512]{1,0:T(8,128)(2,1)S(1)} %add.13.own_ref), channel_id=1, source_target_pairs={{8,16},{16,8},{9,17},{17,9},{10,18},{18,10},{11,19},{19,11},{12,20... | collective-permute-start | bytes 1622024 | tf_op jit(solution)/shard_map/ppermute | solution.py:306
  116.2 7.7 %copy-start.1 = (s16[528,512]{1,0:T(8,128)(2,1)S(1)}, s16[528,512]{1,0:T(8,128)(2,1)}, u32[]{:S(2)}) copy-start(s16[528,512]{1,0:T(8,128)(2,1)} %copy-done) | copy-start | bytes 1622020
  116.2 17.1 %collective-permute-start.18 = (s16[528,512]{1,0:T(8,128)(2,1)S(1)}, s16[528,512]{1,0:T(8,128)(2,1)S(1)}, u32[]{:S(2)}, u32[]{:S(2)}) collective-permute-start(s16[528,512]{1,0:T(8,128)(2,1)S(1)} %reply.11), channel_id=1, source_target_pairs={{0,8},{8,0},{16,24},{24,16},{1,9},{9,1},{17,25},{25,17},{2,10},{10... | collective-permute-start | bytes 1622024 | tf_op jit(solution)/shard_map/ppermute | solution.py:309
  123.1 16.0 %collective-permute-start.19 = (s16[528,512]{1,0:T(8,128)(2,1)S(1)}, s16[528,512]{1,0:T(8,128)(2,1)S(1)}, u32[]{:S(2)}, u32[]{:S(2)}) collective-permute-start(s16[528,512]{1,0:T(8,128)(2,1)S(1)} %add.14.own_ref), channel_id=1, source_target_pairs={{8,16},{16,8},{9,17},{17,9},{10,18},{18,10},{11,19},{19,11},{12,20... | collective-permute-start | bytes 1622024 | tf_op jit(solution)/shard_map/ppermute | solution.py:306
  129.0 11.5 %collective-permute-start.20 = (s16[528,512]{1,0:T(8,128)(2,1)S(1)}, s16[528,512]{1,0:T(8,128)(2,1)S(1)}, u32[]{:S(2)}, u32[]{:S(2)}) collective-permute-start(s16[528,512]{1,0:T(8,128)(2,1)S(1)} %reply.12), channel_id=1, source_target_pairs={{0,8},{8,0},{16,24},{24,16},{1,9},{9,1},{17,25},{25,17},{2,10},{10... | collective-permute-start | bytes 1622024 | tf_op jit(solution)/shard_map/ppermute | solution.py:309
  133.9 9.3 %collective-permute-start.21 = (s16[528,512]{1,0:T(8,128)(2,1)S(1)}, s16[528,512]{1,0:T(8,128)(2,1)S(1)}, u32[]{:S(2)}, u32[]{:S(2)}) collective-permute-start(s16[528,512]{1,0:T(8,128)(2,1)S(1)} %add.15.own_ref), channel_id=1, source_target_pairs={{8,16},{16,8},{9,17},{17,9},{10,18},{18,10},{11,19},{19,11},{12,20... | collective-permute-start | bytes 1622024 | tf_op jit(solution)/shard_map/ppermute | solution.py:306
  141.2 8.7 %collective-permute-start.22 = (s16[528,512]{1,0:T(8,128)(2,1)S(1)}, s16[528,512]{1,0:T(8,128)(2,1)S(1)}, u32[]{:S(2)}, u32[]{:S(2)}) collective-permute-start(s16[528,512]{1,0:T(8,128)(2,1)S(1)} %add.16.own_ref), channel_id=1, source_target_pairs={{8,16},{16,8},{9,17},{17,9},{10,18},{18,10},{11,19},{19,11},{12,20... | collective-permute-start | bytes 1622024 | tf_op jit(solution)/shard_map/ppermute | solution.py:306
  141.9 19.7 %collective-permute-start.23 = (s16[528,512]{1,0:T(8,128)(2,1)S(1)}, s16[528,512]{1,0:T(8,128)(2,1)S(1)}, u32[]{:S(2)}, u32[]{:S(2)}) collective-permute-start(s16[528,512]{1,0:T(8,128)(2,1)S(1)} %reply.13), channel_id=1, source_target_pairs={{8,0},{16,24},{9,1},{17,25},{10,2},{18,26},{11,3},{19,27},{12,4},{... | collective-permute-start | bytes 1622024 | tf_op jit(solution)/shard_map/ppermute | solution.py:300
  144.0 28.4 %collective-permute-start.24 = (s16[528,512]{1,0:T(8,128)(2,1)S(1)}, s16[528,512]{1,0:T(8,128)(2,1)S(1)}, u32[]{:S(2)}, u32[]{:S(2)}) collective-permute-start(s16[528,512]{1,0:T(8,128)(2,1)S(1)} %reply.14), channel_id=1, source_target_pairs={{8,0},{16,24},{9,1},{17,25},{10,2},{18,26},{11,3},{19,27},{12,4},{... | collective-permute-start | bytes 1622024 | tf_op jit(solution)/shard_map/ppermute | solution.py:300
  150.5 27.7 %collective-permute-start.25 = (s16[528,512]{1,0:T(8,128)(2,1)S(1)}, s16[528,512]{1,0:T(8,128)(2,1)S(1)}, u32[]{:S(2)}, u32[]{:S(2)}) collective-permute-start(s16[528,512]{1,0:T(8,128)(2,1)S(1)} %reply.15), channel_id=1, source_target_pairs={{8,0},{16,24},{9,1},{17,25},{10,2},{18,26},{11,3},{19,27},{12,4},{... | collective-permute-start | bytes 1622024 | tf_op jit(solution)/shard_map/ppermute | solution.py:300

commit v8 on v7

--- a/solution.py
+++ b/solution.py
@@ -10,9 +10,9 @@
 BLOCK = 128
 GROUPS = 16
 CHUNK = 2
-AHEAD = 3
+AHEAD = 5
 LAG = 3
-EARLY, LATE, TURN = 8000, 1, 8000
+EARLY, LATE, TURN = 8000, 1, 1
 ROWS = 512
 VMEM_LIMIT = 48 * 1024 * 1024
 
@@ -55,43 +55,62 @@
     return grouped.reshape(rows, cols)
 
 
-def forward_kernel(place_ref, mask_ref, low_ref, high_ref, gate_ref, up_ref, out_ref, joined, held, *, first):
+def forward_kernel(place_ref, mask_ref, low_ref, high_ref, gate_ref, up_ref, *rest, first, spans):
+    *outs, joined, held, coded = rest
+    step = pl.program_id(0)
     depth = gate_ref.shape[0]
     half = low_ref.shape[0]
 
-    @pl.when(pl.program_id(0) == 0)
+    @pl.when(step == 0)
     def _():
         joined[0:half, :] = low_ref[...]
         joined[half : 2 * half, :] = high_ref[...]
 
     for r in range(depth // BLOCK):
         rows = slice(r * BLOCK, (r + 1) * BLOCK)
-        keep = mask_ref[r, first + pl.program_id(0)].astype(jnp.float32)
+        keep = mask_ref[r, first + step].astype(jnp.float32)
         keep = jnp.full((BLOCK, BLOCK), keep).astype(jnp.bfloat16)
         held[rows, :BLOCK] = gate_ref[rows, :] * keep
         held[rows, BLOCK:] = up_ref[rows, :] * keep
-    put(out_ref, jnp.dot(joined[...], held[...], preferred_element_type=jnp.float32))
-
-
-def forward(place, mask, tokens, gate_weight, up_weight, start, width):
+    total = jnp.dot(joined[...], held[...], preferred_element_type=jnp.float32)
+    if len(outs) == 1:
+        put(outs[0], total)
+        return
+    put(coded, total)
+    for out_ref, (begin, end) in zip(outs, spans):
+
+        @pl.when(jnp.logical_and(step >= begin, step < end))
+        def _(out_ref=out_ref):
+            out_ref[...] = coded[...]
+
+
+def forward(place, mask, tokens, gate_weight, up_weight, start, widths):
     half, depth = tokens[0].shape
     count = 2 * half
+    ends = [sum(widths[: c + 1]) // BLOCK for c in range(len(widths))]
+    spans = list(zip([0, *ends], ends))
     weight = pl.BlockSpec((depth, BLOCK), lambda j, place, mask: (0, start // BLOCK + j))
+
+    def out(begin, end):
+        block = (count + GROUPS, 2 * BLOCK)
+        return pl.BlockSpec(block, lambda j, place, mask: (0, jnp.clip(j, begin, end - 1) - begin))
+
     return pl.pallas_call(
-        functools.partial(forward_kernel, first=start // BLOCK),
+        functools.partial(forward_kernel, first=start // BLOCK, spans=spans),
         grid_spec=pltpu.PrefetchScalarGridSpec(
             num_scalar_prefetch=2,
-            grid=(width // BLOCK,),
+            grid=(ends[-1],),
             in_specs=[pl.BlockSpec((half, depth), lambda j, place, mask: (0, 0))] * 2 + [weight] * 2,
-            out_specs=pl.BlockSpec((count + GROUPS, 2 * BLOCK), lambda j, place, mask: (0, j)),
+            out_specs=[out(*span) for span in spans],
             scratch_shapes=[
                 pltpu.VMEM((count, depth), jnp.bfloat16),
                 pltpu.VMEM((depth, 2 * BLOCK), jnp.bfloat16),
+                pltpu.VMEM((count + GROUPS, 2 * BLOCK), jnp.int16),
             ],
         ),
-        out_shape=jax.ShapeDtypeStruct((count + GROUPS, 2 * width), jnp.int16),
+        out_shape=[jax.ShapeDtypeStruct((count + GROUPS, 2 * w), jnp.int16) for w in widths],
         compiler_params=params(),
-        cost_estimate=cost(EARLY if start < 2 * width else LATE),
+        cost_estimate=cost(EARLY if start < 2 * widths[0] else LATE),
         name="forward",
     )(place, mask, *tokens, gate_weight, up_weight)
 
@@ -308,8 +327,8 @@
     def exchange(value):
         return lax.ppermute(value, "row", [(i, i ^ 1) for i in range(ring)])
 
-    pair = [exchange(hidden_grad)] if short else []
-    gathered = gather_tokens(tokens, devices, pair)
+    near = [exchange(hidden_grad), swap(hidden_grad)] if short else []
+    gathered = gather_tokens(tokens, devices, near)
     on_left = me < right
     if short:
         sources = [jnp.where(on_left, i != me, 3 - i) for i in range(2)]
@@ -327,8 +346,8 @@
         place = tie(place, out[0] if isinstance(out, (list, tuple)) else out)
         return out
 
-    def run_forward(c):
-        own.append(ordered(forward, block_mask, gathered, gate_weight, up_weight, starts[c], widths[c]))
+    def run_forward(c, end):
+        own.extend(ordered(forward, block_mask, gathered, gate_weight, up_weight, starts[c], widths[c:end]))
 
     def run_weights(c, coded, back):
         nonlocal outs
@@ -340,7 +359,7 @@
         back = lax.all_gather(hidden_grad, "row", axis=0, tiled=True)
         turned = ordered(turn, *gathered)
         for c in range(chunks):
-            run_forward(c)
+            run_forward(c, c + 1)
             total = own[c]
             for hop in reversed(range(reach)):
                 new = ordered(add, own[c], inward(total, hop))
@@ -353,34 +372,32 @@
         return tuple(outs)
 
     ahead = min(AHEAD, chunks)
-    run_forward(0)
+    far = [near[1], swap(near[0])]
+    moved = [outward(near[1], 0)]
+    run_forward(0, 1)
     arrived.append(inward(own[0], 0))
-    half = jnp.concatenate([tie(hidden_grad, place), *pair], axis=0)
-    other_half = swap(half)
-    for c in range(1, ahead):
-        run_forward(c)
-        if c == 1:
-            arrived.append(inward(own[1], 0))
+    place = tie(place, far[1], moved[0])
+    run_forward(1, 2)
+    arrived.append(inward(own[1], 0))
+    moved.append(outward(tie(far[1], place), 0))
+    run_forward(2, ahead)
     turned = ordered(turn, *gathered)
     for s in range(chunks + LAG):
         if s < chunks:
-            if s == 1:
-                place = tie(place, other_half)
-            if s == LAG:
-                place = tie(place, moved)
+            if s == 0:
+                place = tie(place, moved[1])
             if s + 2 < min(chunks, LAG):
                 arrived.append(inward(tie(own[s + 2], arrived[s]), 0))
             sums.append(ordered(add, own[s], arrived[s]))
             across.append(swap(sums[s]))
-        if s == 0:
-            moved = outward(tie(other_half, place), 0)
         def weights_of(s):
             c = s - LAG
             run_weights(c, (sums[c], across[c], arrived[s]), back)
 
         if s == LAG:
-            far_half = pick(distance == 0, *lax.optimization_barrier((other_half, moved, place))[:2])
-            back = jnp.concatenate([half, far_half], axis=0)
+            *late, _ = lax.optimization_barrier((*far, *moved, place))
+            others = [pick(distance == 0, a, b) for a, b in zip(late[:2], late[2:])]
+            back = jnp.concatenate([hidden_grad, near[0], *others], axis=0)
         if LAG <= s < chunks - 1:
             weights_of(s)
         c = s - 1
@@ -391,7 +408,7 @@
         if s >= max(LAG, chunks - 1):
             weights_of(s)
         if s + ahead < chunks:
-            run_forward(s + ahead)
+            run_forward(s + ahead, s + ahead + 1)
     return tuple(outs)
 
 

time: 184 us -> 183 us (level)
  local copies, waits for them, and re-layouts: 0.81 us -> 2.68 us
    ppermute x4 -> x5, waiting for transfers between devices: 17.3 us -> 23.8 us  [outward(): lax.ppermute(value, 'row', [(left - hop, left - hop - 1), (right + hop, r...]
    ppermute x3, starting transfers between devices: 21 us -> 16.4 us  [inward(): lax.ppermute(value, 'row', [(left - hop - 1, left - hop), (right + hop +...]
    ppermute x3, waiting for transfers between devices: 3.2 us -> 0.01 us  [inward(): lax.ppermute(value, 'row', [(left - hop - 1, left - hop), (right + hop +...]
    pallas_call x8 -> x6, Pallas kernels: 30.5 us -> 27.6 us  [forward(): pl.pallas_call(functools.partial(forward_kernel, first=start // BLOCK, sp...]
    ppermute x6, waiting for transfers between devices: 5.32 us -> 3.05 us  [exchange(): return lax.ppermute(value, 'row', [(i, i ^ 1) for i in range(ring)])]
    ppermute x1, waiting for transfers between devices: 2.53 us -> 0.54 us  [gather_tokens(): lax.ppermute(mine, 'col', [(i, i ^ 1) for i in range(devices)])]
    unnamed x14 -> x22, local copies, waits for them, and re-layouts: 0.72 us -> 2.59 us
    ppermute x9 -> x10, starting transfers between devices: 6.47 us -> 7.88 us  [swap(): return lax.ppermute(value, 'row', [(left, right), (right, left)])]
  transfers between devices with their start and end apart: 26 -> 28, of which waited for: 9 -> 8; matrix products, arithmetic and copies ran while one was open for 1% -> 1% of each run, Pallas kernels for 39% -> 40%
where the time goes in v8:
time: 183 us
  Pallas kernels  78.3 us (43%)
  starting transfers between devices  60.3 us (33%)
  waiting for transfers between devices  38.8 us (21%)
  local copies, waits for them, and re-layouts  2.68 us (1%)
    pallas_call x8, Pallas kernels, weight_grads(): pl.pallas_call(functools.partial(weights_kernel, first=first, devices=dev...  37.7 us
    pallas_call x6, Pallas kernels, forward(): pl.pallas_call(functools.partial(forward_kernel, first=start // BLOCK, sp...  27.6 us
    ppermute x6, starting transfers between devices, exchange(): return lax.ppermute(value, 'row', [(i, i ^ 1) for i in range(ring)])  25.9 us
    ppermute x5, waiting for transfers between devices, outward(): lax.ppermute(value, 'row', [(left - hop, left - hop - 1), (right + hop, r...  23.8 us
    ppermute x3, starting transfers between devices, inward(): lax.ppermute(value, 'row', [(left - hop - 1, left - hop), (right + hop +...  16.4 us
    ppermute x3, waiting for transfers between devices, gather_tokens(): lax.ppermute(tokens, 'col', [(i, i ^ other) for i in range(devices)])  11.3 us
    ppermute x10, starting transfers between devices, swap(): return lax.ppermute(value, 'row', [(left, right), (right, left)])  7.88 us
    pallas_call x8, Pallas kernels, reply(): pl.pallas_call(reply_kernel, grid_spec=pltpu.PrefetchScalarGridSpec(num_s...  6.75 us
  transfers between devices with their start and end apart: 28, of which 8 were waited for; matrix products, arithmetic and copies ran while one was open for 1% of the time, Pallas kernels for 40%

profile of v8, /device:TPU:0, one launch (start us, length us, event | category | flops | bytes accessed | tf_op | source)
XLA Modules:
  0.0 182.5 jit_solution(13700992226457038678)
XLA Ops:
  0.6 3.1 %collective-permute-start.3 = (bf16[128,2048]{1,0:T(8,128)(2,1)}, bf16[128,2048]{1,0:T(8,128)(2,1)S(1)}, u32[]{:S(2)}, u32[]{:S(2)}) collective-permute-start(bf16[128,2048]{1,0:T(8,128)(2,1)} %param.9), channel_id=1, source_target_pairs={{0,8},{8,0},{16,24},{24,16},{1,9},{9,1},{17,25},{25,17},{2,10},{10... | collective-permute-start | bytes 1572872 | tf_op jit(solution)/shard_map/ppermute | solution.py:328
  4.4 1.6 collective-permute-start
  6.0 1.5 collective-permute-start.1
  8.0 6.0 %collective-permute-done = bf16[64,2048]{1,0:T(8,128)(2,1)S(1)} collective-permute-done((bf16[64,2048]{1,0:T(8,128)(2,1)}, bf16[64,2048]{1,0:T(8,128)(2,1)S(1)}, u32[]{:S(2)}, u32[]{:S(2)}) %collective-permute-start) | collective-permute-done | bytes 262176 | tf_op jit(solution)/shard_map/ppermute | solution.py:297
  13.9 5.4 %collective-permute-done.1 = bf16[64,2048]{1,0:T(8,128)(2,1)S(1)} collective-permute-done((bf16[64,2048]{1,0:T(8,128)(2,1)}, bf16[64,2048]{1,0:T(8,128)(2,1)S(1)}, u32[]{:S(2)}, u32[]{:S(2)}) %collective-permute-start.1) | collective-permute-done | bytes 262176 | tf_op jit(solution)/shard_map/ppermute | solution.py:297
  19.3 1.0 pad_maximum_fusion.1.low_ref
  21.3 1.3 collective-permute-start.7
  23.1 0.7 copy-done.4
  23.8 3.9 %forward.6.a_ref = s16[528,512]{1,0:T(8,128)(2,1)S(1)} custom-call(s32[7]{0:T(128)S(1)} %stack.35.place_ref, s32[16,16]{1,0:T(8,128)S(1)} %copy-done.4, bf16[256,2048]{1,0:T(8,128)(2,1)S(1)} %pad_maximum_fusion.1.low_ref, bf16[256,2048]{1,0:T(8,128)(2,1)S(1)} %collective-permute-done.5.high_ref, bf16[2048,2048]{1,0:T(8,128)(2,1)} %gate_ref.11, ...), custom_call_target="tpu_custom_call" | custom-call | flops 8000000000 | bytes 20000000 | tf_op jit(solution)/shard_map/forward/pallas_call | solution.py:98
  27.7 7.0 %collective-permute-start.9 = (s16[528,512]{1,0:T(8,128)(2,1)S(1)}, s16[528,512]{1,0:T(8,128)(2,1)S(1)}, u32[]{:S(2)}, u32[]{:S(2)}) collective-permute-start(s16[528,512]{1,0:T(8,128)(2,1)S(1)} %forward.6.a_ref), channel_id=1, source_target_pairs={{0,8},{24,16},{1,9},{25,17},{2,10},{26,18},{3,11},{27,19},{4,12},{... | collective-permute-start | bytes 1622024 | tf_op jit(solution)/shard_map/ppermute | solution.py:322
  34.8 5.7 %collective-permute-done.7 = bf16[128,2048]{1,0:T(8,128)(2,1)S(1)} collective-permute-done((bf16[128,2048]{1,0:T(8,128)(2,1)S(1)}, bf16[128,2048]{1,0:T(8,128)(2,1)S(1)}, u32[]{:S(2)}, u32[]{:S(2)}) %collective-permute-start.7) | collective-permute-done | bytes 524320 | tf_op jit(solution)/shard_map/ppermute | solution.py:319
  40.4 3.8 %forward.7.a_ref = s16[528,512]{1,0:T(8,128)(2,1)S(1)} custom-call(s32[7]{0:T(128)S(1)} %stack.35.place_ref, s32[16,16]{1,0:T(8,128)S(1)} %copy-done.4, bf16[256,2048]{1,0:T(8,128)(2,1)S(1)} %pad_maximum_fusion.1.low_ref, bf16[256,2048]{1,0:T(8,128)(2,1)S(1)} %collective-permute-done.5.high_ref, bf16[2048,2048]{1,0:T(8,128)(2,1)} %gate_ref.11, ...), custom_call_target="tpu_custom_call" | custom-call | flops 8000000000 | bytes 20000000 | tf_op jit(solution)/shard_map/forward/pallas_call | solution.py:98
  44.3 1.3 collective-permute-start.8
  45.6 4.6 %collective-permute-start.10 = (s16[528,512]{1,0:T(8,128)(2,1)S(1)}, s16[528,512]{1,0:T(8,128)(2,1)S(1)}, u32[]{:S(2)}, u32[]{:S(2)}) collective-permute-start(s16[528,512]{1,0:T(8,128)(2,1)S(1)} %forward.7.a_ref), channel_id=1, source_target_pairs={{0,8},{24,16},{1,9},{25,17},{2,10},{26,18},{3,11},{27,19},{4,12},{... | collective-permute-start | bytes 1622024 | tf_op jit(solution)/shard_map/ppermute | solution.py:322
  50.2 8.4 %forward.8 = (s16[528,512]{1,0:T(8,128)(2,1)S(1)}, s16[528,512]{1,0:T(8,128)(2,1)S(1)}, s16[528,512]{1,0:T(8,128)(2,1)S(1)}) custom-call(s32[7]{0:T(128)S(1)} %stack.35.place_ref, s32[16,16]{1,0:T(8,128)S(1)} %copy-done.4, bf16[256,2048]{1,0:T(8,128)(2,1)S(1)} %pad_maximum_fusion.1.low_ref, bf16[256,2048]{1,0:T(8,128)(2,1)S(1)} %collective-permute-done.5.high_ref, ...), custom_call_target="tpu_custom_call" | custom-call | flops 1000000 | bytes 2500 | tf_op jit(solution)/shard_map/forward/pallas_call | solution.py:98
  58.6 1.5 turn.1.turned_ref
  60.7 0.7 collective-permute-start.11
  61.4 4.8 %collective-permute-start.12 = (s16[528,512]{1,0:T(8,128)(2,1)S(1)}, s16[528,512]{1,0:T(8,128)(2,1)S(1)}, u32[]{:S(2)}, u32[]{:S(2)}) collective-permute-start(s16[528,512]{1,0:T(8,128)(2,1)S(1)} %get-tuple-element.81.a_ref), channel_id=1, source_target_pairs={{0,8},{24,16},{1,9},{25,17},{2,10},{26,18},{3,11},{27,19},{4,12},{... | collective-permute-start | bytes 1622024 | tf_op jit(solution)/shard_map/ppermute | solution.py:322
  66.2 3.9 %forward.9.next_ref.a_ref = s16[528,512]{1,0:T(8,128)(2,1)S(1)} custom-call(s32[7]{0:T(128)S(1)} %stack.35.place_ref, s32[16,16]{1,0:T(8,128)S(1)} %copy-done.4, bf16[256,2048]{1,0:T(8,128)(2,1)S(1)} %pad_maximum_fusion.1.low_ref, bf16[256,2048]{1,0:T(8,128)(2,1)S(1)} %collective-permute-done.5.high_ref, bf16[2048,2048]{1,0:T(8,128)(2,1)} %gate_ref.11, ...), custom_call_target="tpu_custom_call" | custom-call | flops 1000000 | bytes 2500 | tf_op jit(solution)/shard_map/forward/pallas_call | solution.py:98
  72.0 6.9 %collective-permute-start.14 = (s16[528,512]{1,0:T(8,128)(2,1)S(1)}, s16[528,512]{1,0:T(8,128)(2,1)S(1)}, u32[]{:S(2)}, u32[]{:S(2)}) collective-permute-start(s16[528,512]{1,0:T(8,128)(2,1)S(1)} %reply.8), channel_id=1, source_target_pairs={{0,8},{8,0},{16,24},{24,16},{1,9},{9,1},{17,25},{25,17},{2,10},{10... | collective-permute-start | bytes 1622024 | tf_op jit(solution)/shard_map/ppermute | solution.py:328
  78.9 3.8 %forward.10.next_ref.a_ref = s16[528,512]{1,0:T(8,128)(2,1)S(1)} custom-call(s32[7]{0:T(128)S(1)} %stack.35.place_ref, s32[16,16]{1,0:T(8,128)S(1)} %copy-done.5, bf16[256,2048]{1,0:T(8,128)(2,1)S(1)} %pad_maximum_fusion.1.low_ref, bf16[256,2048]{1,0:T(8,128)(2,1)S(1)} %collective-permute-done.5.high_ref, bf16[2048,2048]{1,0:T(8,128)(2,1)} %gate_ref.11, ...), custom_call_target="tpu_custom_call" | custom-call | flops 1000000 | bytes 2500 | tf_op jit(solution)/shard_map/forward/pallas_call | solution.py:98
  83.4 1.5 collective-permute-start.15
  84.8 1.4 reply.9
  86.3 5.0 %collective-permute-start.16 = (s16[528,512]{1,0:T(8,128)(2,1)}, s16[528,512]{1,0:T(8,128)(2,1)S(1)}, u32[]{:S(2)}, u32[]{:S(2)}) collective-permute-start(s16[528,512]{1,0:T(8,128)(2,1)} %reply.9), channel_id=1, source_target_pairs={{0,8},{8,0},{16,24},{24,16},{1,9},{9,1},{17,25},{25,17},{2,10},{10... | collective-permute-start | bytes 1622024 | tf_op jit(solution)/shard_map/ppermute | solution.py:328
  91.2 3.8 %forward.11.next_ref.a_ref = s16[528,512]{1,0:T(8,128)(2,1)S(1)} custom-call(s32[7]{0:T(128)S(1)} %stack.35.place_ref, s32[16,16]{1,0:T(8,128)S(1)} %copy-done.5, bf16[256,2048]{1,0:T(8,128)(2,1)S(1)} %pad_maximum_fusion.1.low_ref, bf16[256,2048]{1,0:T(8,128)(2,1)S(1)} %collective-permute-done.5.high_ref, bf16[2048,2048]{1,0:T(8,128)(2,1)} %gate_ref.11, ...), custom_call_target="tpu_custom_call" | custom-call | flops 1000000 | bytes 2500 | tf_op jit(solution)/shard_map/forward/pallas_call | solution.py:98
  95.7 0.9 collective-permute-start.17
  96.9 4.6 %weight_grads.8 = (bf16[128,2048]{1,0:T(8,128)(2,1)}, f32[2048,2048]{1,0:T(8,128)}, f32[2048,2048]{1,0:T(8,128)}) custom-call(s32[7]{0:T(128)S(1)} %stack.35.place_ref, s32[16,16]{1,0:T(8,128)S(1)} %copy-done.5, bf16[2048,512]{1,0:T(8,128)(2,1)S(1)} %turn.1.turned_ref, bf16[512,2048]{1,0:T(8,128)(2,1)S(1)} %pad_maximum_fusion.back_ref, ...), custom_call_target="tpu_custom_call" | custom-call | flops 1000000 | bytes 2500 | tf_op jit(solution)/shard_map/weight_grads/pallas_call | solution.py:261
  101.5 1.6 reply.10
  103.1 4.1 %collective-permute-start.18 = (s16[528,512]{1,0:T(8,128)(2,1)S(1)}, s16[528,512]{1,0:T(8,128)(2,1)S(1)}, u32[]{:S(2)}, u32[]{:S(2)}) collective-permute-start(s16[528,512]{1,0:T(8,128)(2,1)S(1)} %reply.10), channel_id=1, source_target_pairs={{0,8},{8,0},{16,24},{24,16},{1,9},{9,1},{17,25},{25,17},{2,10},{10... | collective-permute-start | bytes 1622024 | tf_op jit(solution)/shard_map/ppermute | solution.py:328
  107.8 0.8 copy-done
  109.3 1.0 copy-done.1
  110.4 4.6 %weight_grads.9 = (bf16[128,2048]{1,0:T(8,128)(2,1)}, f32[2048,2048]{1,0:T(8,128)}, f32[2048,2048]{1,0:T(8,128)}) custom-call(s32[7]{0:T(128)S(1)} %stack.35.place_ref, s32[16,16]{1,0:T(8,128)S(1)} %copy-done.5, bf16[2048,512]{1,0:T(8,128)(2,1)S(1)} %turn.1.turned_ref, ...), custom_call_target="tpu_custom_call", output_to_operand_aliasing={{0}: (7, {}), {1}: (8, {}), {2}: (9, {})} | custom-call | flops 1000000 | bytes 2500 | tf_op jit(solution)/shard_map/weight_grads/pallas_call | solution.py:261
  115.6 2.7 %collective-permute-start.20 = (s16[528,512]{1,0:T(8,128)(2,1)S(1)}, s16[528,512]{1,0:T(8,128)(2,1)S(1)}, u32[]{:S(2)}, u32[]{:S(2)}) collective-permute-start(s16[528,512]{1,0:T(8,128)(2,1)S(1)} %reply.11), channel_id=1, source_target_pairs={{0,8},{8,0},{16,24},{24,16},{1,9},{9,1},{17,25},{25,17},{2,10},{10... | collective-permute-start | bytes 1622024 | tf_op jit(solution)/shard_map/ppermute | solution.py:328
  119.5 5.6 %weight_grads.10 = (bf16[128,2048]{1,0:T(8,128)(2,1)}, f32[2048,2048]{1,0:T(8,128)}, f32[2048,2048]{1,0:T(8,128)}) custom-call(s32[7]{0:T(128)S(1)} %stack.35.place_ref, s32[16,16]{1,0:T(8,128)S(1)} %copy-done.5, bf16[2048,512]{1,0:T(8,128)(2,1)S(1)} %turn.1.turned_ref, ...), custom_call_target="tpu_custom_call", output_to_operand_aliasing={{0}: (7, {}), {1}: (8, {}), {2}: (9, {})} | custom-call | flops 1000000 | bytes 2500 | tf_op jit(solution)/shard_map/weight_grads/pallas_call | solution.py:261
  125.8 4.1 %collective-permute-start.22 = (s16[528,512]{1,0:T(8,128)(2,1)S(1)}, s16[528,512]{1,0:T(8,128)(2,1)S(1)}, u32[]{:S(2)}, u32[]{:S(2)}) collective-permute-start(s16[528,512]{1,0:T(8,128)(2,1)S(1)} %reply.12), channel_id=1, source_target_pairs={{0,8},{8,0},{16,24},{24,16},{1,9},{9,1},{17,25},{25,17},{2,10},{10... | collective-permute-start | bytes 1622024 | tf_op jit(solution)/shard_map/ppermute | solution.py:328
  131.2 4.6 %weight_grads.11 = (bf16[128,2048]{1,0:T(8,128)(2,1)}, f32[2048,2048]{1,0:T(8,128)}, f32[2048,2048]{1,0:T(8,128)}) custom-call(s32[7]{0:T(128)S(1)} %stack.35.place_ref, s32[16,16]{1,0:T(8,128)S(1)} %copy-done.5, bf16[2048,512]{1,0:T(8,128)(2,1)S(1)} %turn.1.turned_ref, ...), custom_call_target="tpu_custom_call", output_to_operand_aliasing={{0}: (7, {}), {1}: (8, {}), {2}: (9, {})} | custom-call | flops 1000000 | bytes 2500 | tf_op jit(solution)/shard_map/weight_grads/pallas_call | solution.py:261
  136.3 3.0 %collective-permute-done.22.b_ref.out_ref = s16[528,512]{1,0:T(8,128)(2,1)S(1)} collective-permute-done((s16[528,512]{1,0:T(8,128)(2,1)S(1)}, s16[528,512]{1,0:T(8,128)(2,1)S(1)}, u32[]{:S(2)}, u32[]{:S(2)}) %collective-permute-start.22) | collective-permute-done | bytes 540704 | tf_op jit(solution)/shard_map/ppermute | solution.py:328
  140.7 1.3 collective-permute-start.25
  142.6 1.3 collective-permute-start.26
  143.9 4.6 %weight_grads.12 = (bf16[128,2048]{1,0:T(8,128)(2,1)}, f32[2048,2048]{1,0:T(8,128)}, f32[2048,2048]{1,0:T(8,128)}) custom-call(s32[7]{0:T(128)S(1)} %stack.35.place_ref, s32[16,16]{1,0:T(8,128)S(1)} %copy-done.5, bf16[2048,512]{1,0:T(8,128)(2,1)S(1)} %turn.1.turned_ref, ...), custom_call_target="tpu_custom_call", output_to_operand_aliasing={{0}: (7, {}), {1}: (8, {}), {2}: (9, {})} | custom-call | flops 1000000 | bytes 2500 | tf_op jit(solution)/shard_map/weight_grads/pallas_call | solution.py:261
  148.5 0.8 reply.15
  149.3 1.3 collective-permute-start.27
  150.6 8.9 %collective-permute-done.25.out_ref = s16[528,512]{1,0:T(8,128)(2,1)S(1)} collective-permute-done((s16[528,512]{1,0:T(8,128)(2,1)S(1)}, s16[528,512]{1,0:T(8,128)(2,1)S(1)}, u32[]{:S(2)}, u32[]{:S(2)}) %collective-permute-start.25) | collective-permute-done | bytes 540704 | tf_op jit(solution)/shard_map/ppermute | solution.py:319
  159.5 4.6 %weight_grads.13 = (bf16[128,2048]{1,0:T(8,128)(2,1)}, f32[2048,2048]{1,0:T(8,128)}, f32[2048,2048]{1,0:T(8,128)}) custom-call(s32[7]{0:T(128)S(1)} %stack.35.place_ref, s32[16,16]{1,0:T(8,128)S(1)} %copy-done.5, bf16[2048,512]{1,0:T(8,128)(2,1)S(1)} %turn.1.turned_ref, ...), custom_call_target="tpu_custom_call", output_to_operand_aliasing={{0}: (7, {}), {1}: (8, {}), {2}: (9, {})} | custom-call | flops 1000000 | bytes 2500 | tf_op jit(solution)/shard_map/weight_grads/pallas_call | solution.py:261
  164.1 7.0 %collective-permute-done.26.out_ref = s16[528,512]{1,0:T(8,128)(2,1)S(1)} collective-permute-done((s16[528,512]{1,0:T(8,128)(2,1)S(1)}, s16[528,512]{1,0:T(8,128)(2,1)S(1)}, u32[]{:S(2)}, u32[]{:S(2)}) %collective-permute-start.26) | collective-permute-done | bytes 540704 | tf_op jit(solution)/shard_map/ppermute | solution.py:319
  171.1 4.6 %weight_grads.14 = (bf16[128,2048]{1,0:T(8,128)(2,1)}, f32[2048,2048]{1,0:T(8,128)}, f32[2048,2048]{1,0:T(8,128)}) custom-call(s32[7]{0:T(128)S(1)} %stack.35.place_ref, s32[16,16]{1,0:T(8,128)S(1)} %copy-done.5, bf16[2048,512]{1,0:T(8,128)(2,1)S(1)} %turn.1.turned_ref, ...), custom_call_target="tpu_custom_call", output_to_operand_aliasing={{0}: (7, {}), {1}: (8, {}), {2}: (9, {})} | custom-call | flops 1000000 | bytes 2500 | tf_op jit(solution)/shard_map/weight_grads/pallas_call | solution.py:261
  175.7 2.2 %collective-permute-done.27.out_ref = s16[528,512]{1,0:T(8,128)(2,1)S(1)} collective-permute-done((s16[528,512]{1,0:T(8,128)(2,1)S(1)}, s16[528,512]{1,0:T(8,128)(2,1)S(1)}, u32[]{:S(2)}, u32[]{:S(2)}) %collective-permute-start.27) | collective-permute-done | bytes 540704 | tf_op jit(solution)/shard_map/ppermute | solution.py:319
  177.9 4.6 %weight_grads.15 = (bf16[128,2048]{1,0:T(8,128)(2,1)}, f32[2048,2048]{1,0:T(8,128)}, f32[2048,2048]{1,0:T(8,128)}) custom-call(s32[7]{0:T(128)S(1)} %stack.35.place_ref, s32[16,16]{1,0:T(8,128)S(1)} %copy-done.5, bf16[2048,512]{1,0:T(8,128)(2,1)S(1)} %turn.1.turned_ref, ...), custom_call_target="tpu_custom_call", output_to_operand_aliasing={{0}: (7, {}), {1}: (8, {}), {2}: (9, {})} | custom-call | flops 1000000 | bytes 2500 | tf_op jit(solution)/shard_map/weight_grads/pallas_call | solution.py:261
  (65 shorter events, 13.9 us)
Async XLA Ops:
  0.6 19.7 %collective-permute-start.3 = (bf16[128,2048]{1,0:T(8,128)(2,1)}, bf16[128,2048]{1,0:T(8,128)(2,1)S(1)}, u32[]{:S(2)}, u32[]{:S(2)}) collective-permute-start(bf16[128,2048]{1,0:T(8,128)(2,1)} %param.9), channel_id=1, source_target_pairs={{0,8},{8,0},{16,24},{24,16},{1,9},{9,1},{17,25},{25,17},{2,10},{10... | collective-permute-start | bytes 1572872 | tf_op jit(solution)/shard_map/ppermute | solution.py:328
  3.7 16.6 %collective-permute-start.4 = (bf16[128,2048]{1,0:T(8,128)(2,1)}, bf16[128,2048]{1,0:T(8,128)(2,1)S(1)}, u32[]{:S(2)}, u32[]{:S(2)}) collective-permute-start(bf16[128,2048]{1,0:T(8,128)(2,1)} %param.9), channel_id=1, source_target_pairs={{8,16},{16,8},{9,17},{17,9},{10,18},{18,10},{11,19},{19,11},{12,20... | collective-permute-start | bytes 1572872 | tf_op jit(solution)/shard_map/ppermute | solution.py:325
  4.4 9.5 %collective-permute-start = (bf16[64,2048]{1,0:T(8,128)(2,1)}, bf16[64,2048]{1,0:T(8,128)(2,1)S(1)}, u32[]{:S(2)}, u32[]{:S(2)}) collective-permute-start(bf16[64,2048]{1,0:T(8,128)(2,1)} %param.5), channel_id=1, source_target_pairs={{0,2},{1,3},{2,0},{3,1},{4,6},{5,7},{6,4},{7,5},{8,10},{9,11},{10,... | collective-permute-start | bytes 786440 | tf_op jit(solution)/shard_map/ppermute | solution.py:297
  6.0 13.3 %collective-permute-start.1 = (bf16[64,2048]{1,0:T(8,128)(2,1)}, bf16[64,2048]{1,0:T(8,128)(2,1)S(1)}, u32[]{:S(2)}, u32[]{:S(2)}) collective-permute-start(bf16[64,2048]{1,0:T(8,128)(2,1)} %param.5), channel_id=1, source_target_pairs={{0,4},{1,5},{2,6},{3,7},{4,0},{5,1},{6,2},{7,3},{8,12},{9,13},{10,... | collective-permute-start | bytes 786440 | tf_op jit(solution)/shard_map/ppermute | solution.py:297
  7.5 11.8 %collective-permute-start.2 = (bf16[64,2048]{1,0:T(8,128)(2,1)}, bf16[64,2048]{1,0:T(8,128)(2,1)S(1)}, u32[]{:S(2)}, u32[]{:S(2)}) collective-permute-start(bf16[64,2048]{1,0:T(8,128)(2,1)} %param.5), channel_id=1, source_target_pairs={{0,6},{1,7},{2,4},{3,5},{4,2},{5,3},{6,0},{7,1},{8,14},{9,15},{10,... | collective-permute-start | bytes 786440 | tf_op jit(solution)/shard_map/ppermute | solution.py:297
  20.4 7.3 %copy-start.9 = (bf16[128,2048]{1,0:T(8,128)(2,1)}, bf16[128,2048]{1,0:T(8,128)(2,1)S(1)}, u32[]{:S(2)}) copy-start(bf16[128,2048]{1,0:T(8,128)(2,1)S(1)} %collective-permute-done.3) | copy-start | bytes 1572868
  20.4 7.3 %copy-start.6 = (bf16[128,2048]{1,0:T(8,128)(2,1)}, bf16[128,2048]{1,0:T(8,128)(2,1)S(1)}, u32[]{:S(2)}) copy-start(bf16[128,2048]{1,0:T(8,128)(2,1)S(1)} %collective-permute-done.4) | copy-start | bytes 1572868
  20.4 2.7 %collective-permute-start.5 = (bf16[256,2048]{1,0:T(8,128)(2,1)S(1)}, bf16[256,2048]{1,0:T(8,128)(2,1)S(1)}, u32[]{:S(2)}, u32[]{:S(2)}) collective-permute-start(bf16[256,2048]{1,0:T(8,128)(2,1)S(1)} %pad_maximum_fusion.1.low_ref), channel_id=1, source_target_pairs={{0,1},{1,0},{2,3},{3,2},{4,5},{5,4},{6,7},{7,6},{8,9},{9,8},{10,11... | collective-permute-start | bytes 3145736 | tf_op jit(solution)/shard_map/ppermute | solution.py:299
  20.6 14.2 %collective-permute-start.6 = (bf16[128,2048]{1,0:T(8,128)(2,1)S(1)}, bf16[128,2048]{1,0:T(8,128)(2,1)S(1)}, u32[]{:S(2)}, u32[]{:S(2)}) collective-permute-start(bf16[128,2048]{1,0:T(8,128)(2,1)S(1)} %collective-permute-done.3), channel_id=1, source_target_pairs={{8,16},{16,8},{9,17},{17,9},{10,18},{18,10},{11,19},{19,11},{12,20... | collective-permute-start | bytes 1572872 | tf_op jit(solution)/shard_map/ppermute | solution.py:325
  21.3 19.1 %collective-permute-start.7 = (bf16[128,2048]{1,0:T(8,128)(2,1)S(1)}, bf16[128,2048]{1,0:T(8,128)(2,1)S(1)}, u32[]{:S(2)}, u32[]{:S(2)}) collective-permute-start(bf16[128,2048]{1,0:T(8,128)(2,1)S(1)} %collective-permute-done.4), channel_id=1, source_target_pairs={{8,0},{16,24},{9,1},{17,25},{10,2},{18,26},{11,3},{19,27},{12,4},{... | collective-permute-start | bytes 1572872 | tf_op jit(solution)/shard_map/ppermute | solution.py:319
  23.1 0.7 copy-start.4
  27.7 32.4 %collective-permute-start.9 = (s16[528,512]{1,0:T(8,128)(2,1)S(1)}, s16[528,512]{1,0:T(8,128)(2,1)S(1)}, u32[]{:S(2)}, u32[]{:S(2)}) collective-permute-start(s16[528,512]{1,0:T(8,128)(2,1)S(1)} %forward.6.a_ref), channel_id=1, source_target_pairs={{0,8},{24,16},{1,9},{25,17},{2,10},{26,18},{3,11},{27,19},{4,12},{... | collective-permute-start | bytes 1622024 | tf_op jit(solution)/shard_map/ppermute | solution.py:322
  44.3 15.8 %collective-permute-start.8 = (bf16[128,2048]{1,0:T(8,128)(2,1)S(1)}, bf16[128,2048]{1,0:T(8,128)(2,1)S(1)}, u32[]{:S(2)}, u32[]{:S(2)}) collective-permute-start(bf16[128,2048]{1,0:T(8,128)(2,1)S(1)} %collective-permute-done.6), channel_id=1, source_target_pairs={{8,0},{16,24},{9,1},{17,25},{10,2},{18,26},{11,3},{19,27},{12,4},{... | collective-permute-start | bytes 1572872 | tf_op jit(solution)/shard_map/ppermute | solution.py:319
  45.6 24.5 %collective-permute-start.10 = (s16[528,512]{1,0:T(8,128)(2,1)S(1)}, s16[528,512]{1,0:T(8,128)(2,1)S(1)}, u32[]{:S(2)}, u32[]{:S(2)}) collective-permute-start(s16[528,512]{1,0:T(8,128)(2,1)S(1)} %forward.7.a_ref), channel_id=1, source_target_pairs={{0,8},{24,16},{1,9},{25,17},{2,10},{26,18},{3,11},{27,19},{4,12},{... | collective-permute-start | bytes 1622024 | tf_op jit(solution)/shard_map/ppermute | solution.py:322
  60.7 18.2 %copy-start.5 = (s32[16,16]{1,0:T(8,128)S(1)}, s32[16,16]{1,0:T(8,128)}, u32[]{:S(2)}) copy-start(s32[16,16]{1,0:T(8,128)} %mask_ref.27) | copy-start | bytes 3076
  60.7 10.7 %collective-permute-start.11 = (s16[528,512]{1,0:T(8,128)(2,1)S(1)}, s16[528,512]{1,0:T(8,128)(2,1)S(1)}, u32[]{:S(2)}, u32[]{:S(2)}) collective-permute-start(s16[528,512]{1,0:T(8,128)(2,1)S(1)} %add.9.own_ref), channel_id=1, source_target_pairs={{8,16},{16,8},{9,17},{17,9},{10,18},{18,10},{11,19},{19,11},{12,20... | collective-permute-start | bytes 1622024 | tf_op jit(solution)/shard_map/ppermute | solution.py:325
  61.4 21.3 %collective-permute-start.12 = (s16[528,512]{1,0:T(8,128)(2,1)S(1)}, s16[528,512]{1,0:T(8,128)(2,1)S(1)}, u32[]{:S(2)}, u32[]{:S(2)}) collective-permute-start(s16[528,512]{1,0:T(8,128)(2,1)S(1)} %get-tuple-element.81.a_ref), channel_id=1, source_target_pairs={{0,8},{24,16},{1,9},{25,17},{2,10},{26,18},{3,11},{27,19},{4,12},{... | collective-permute-start | bytes 1622024 | tf_op jit(solution)/shard_map/ppermute | solution.py:322
  70.7 14.2 %collective-permute-start.13 = (s16[528,512]{1,0:T(8,128)(2,1)S(1)}, s16[528,512]{1,0:T(8,128)(2,1)S(1)}, u32[]{:S(2)}, u32[]{:S(2)}) collective-permute-start(s16[528,512]{1,0:T(8,128)(2,1)S(1)} %add.10.own_ref), channel_id=1, source_target_pairs={{8,16},{16,8},{9,17},{17,9},{10,18},{18,10},{11,19},{19,11},{12,20... | collective-permute-start | bytes 1622024 | tf_op jit(solution)/shard_map/ppermute | solution.py:325
  72.0 23.2 %collective-permute-start.14 = (s16[528,512]{1,0:T(8,128)(2,1)S(1)}, s16[528,512]{1,0:T(8,128)(2,1)S(1)}, u32[]{:S(2)}, u32[]{:S(2)}) collective-permute-start(s16[528,512]{1,0:T(8,128)(2,1)S(1)} %reply.8), channel_id=1, source_target_pairs={{0,8},{8,0},{16,24},{24,16},{1,9},{9,1},{17,25},{25,17},{2,10},{10... | collective-permute-start | bytes 1622024 | tf_op jit(solution)/shard_map/ppermute | solution.py:328
  83.4 18.1 %collective-permute-start.15 = (s16[528,512]{1,0:T(8,128)(2,1)S(1)}, s16[528,512]{1,0:T(8,128)(2,1)}, u32[]{:S(2)}, u32[]{:S(2)}) collective-permute-start(s16[528,512]{1,0:T(8,128)(2,1)S(1)} %add.11.own_ref), channel_id=1, source_target_pairs={{8,16},{16,8},{9,17},{17,9},{10,18},{18,10},{11,19},{19,11},{12,20... | collective-permute-start | bytes 1622024 | tf_op jit(solution)/shard_map/ppermute | solution.py:325
  84.8 10.3 %copy-start.2 = (s16[528,512]{1,0:T(8,128)(2,1)}, s16[528,512]{1,0:T(8,128)(2,1)S(1)}, u32[]{:S(2)}) copy-start(s16[528,512]{1,0:T(8,128)(2,1)S(1)} %collective-permute-done.13.b_ref.across_ref) | copy-start | bytes 1622020
  86.3 10.4 %copy-start.7 = (bf16[128,2048]{1,0:T(8,128)(2,1)S(1)}, bf16[128,2048]{1,0:T(8,128)(2,1)}, u32[]{:S(2)}) copy-start(bf16[128,2048]{1,0:T(8,128)(2,1)} %copy-done.6) | copy-start | bytes 1572868
  86.3 21.0 %collective-permute-start.16 = (s16[528,512]{1,0:T(8,128)(2,1)}, s16[528,512]{1,0:T(8,128)(2,1)S(1)}, u32[]{:S(2)}, u32[]{:S(2)}) collective-permute-start(s16[528,512]{1,0:T(8,128)(2,1)} %reply.9), channel_id=1, source_target_pairs={{0,8},{8,0},{16,24},{24,16},{1,9},{9,1},{17,25},{25,17},{2,10},{10... | collective-permute-start | bytes 1622024 | tf_op jit(solution)/shard_map/ppermute | solution.py:328
  95.1 1.6 copy-start.8
  95.1 1.6 copy-start.10
  95.7 19.2 %collective-permute-start.17 = (s16[528,512]{1,0:T(8,128)(2,1)S(1)}, s16[528,512]{1,0:T(8,128)(2,1)S(1)}, u32[]{:S(2)}, u32[]{:S(2)}) collective-permute-start(s16[528,512]{1,0:T(8,128)(2,1)S(1)} %add.12.own_ref), channel_id=1, source_target_pairs={{8,16},{16,8},{9,17},{17,9},{10,18},{18,10},{11,19},{19,11},{12,20... | collective-permute-start | bytes 1622024 | tf_op jit(solution)/shard_map/ppermute | solution.py:325
  96.9 12.4 %copy-start.3 = (s16[528,512]{1,0:T(8,128)(2,1)S(1)}, s16[528,512]{1,0:T(8,128)(2,1)}, u32[]{:S(2)}) copy-start(s16[528,512]{1,0:T(8,128)(2,1)} %copy-done.2) | copy-start | bytes 1622020
  103.1 15.1 %collective-permute-start.18 = (s16[528,512]{1,0:T(8,128)(2,1)S(1)}, s16[528,512]{1,0:T(8,128)(2,1)S(1)}, u32[]{:S(2)}, u32[]{:S(2)}) collective-permute-start(s16[528,512]{1,0:T(8,128)(2,1)S(1)} %reply.10), channel_id=1, source_target_pairs={{0,8},{8,0},{16,24},{24,16},{1,9},{9,1},{17,25},{25,17},{2,10},{10... | collective-permute-start | bytes 1622024 | tf_op jit(solution)/shard_map/ppermute | solution.py:328
  107.8 0.8 copy-start
  108.6 16.5 %collective-permute-start.19 = (s16[528,512]{1,0:T(8,128)(2,1)S(1)}, s16[528,512]{1,0:T(8,128)(2,1)S(1)}, u32[]{:S(2)}, u32[]{:S(2)}) collective-permute-start(s16[528,512]{1,0:T(8,128)(2,1)S(1)} %add.13.own_ref), channel_id=1, source_target_pairs={{8,16},{16,8},{9,17},{17,9},{10,18},{18,10},{11,19},{19,11},{12,20... | collective-permute-start | bytes 1622024 | tf_op jit(solution)/shard_map/ppermute | solution.py:325
  109.3 1.0 copy-start.1
  115.6 14.3 %collective-permute-start.20 = (s16[528,512]{1,0:T(8,128)(2,1)S(1)}, s16[528,512]{1,0:T(8,128)(2,1)S(1)}, u32[]{:S(2)}, u32[]{:S(2)}) collective-permute-start(s16[528,512]{1,0:T(8,128)(2,1)S(1)} %reply.11), channel_id=1, source_target_pairs={{0,8},{8,0},{16,24},{24,16},{1,9},{9,1},{17,25},{25,17},{2,10},{10... | collective-permute-start | bytes 1622024 | tf_op jit(solution)/shard_map/ppermute | solution.py:328
  118.8 16.9 %collective-permute-start.21 = (s16[528,512]{1,0:T(8,128)(2,1)S(1)}, s16[528,512]{1,0:T(8,128)(2,1)S(1)}, u32[]{:S(2)}, u32[]{:S(2)}) collective-permute-start(s16[528,512]{1,0:T(8,128)(2,1)S(1)} %add.14.own_ref), channel_id=1, source_target_pairs={{8,16},{16,8},{9,17},{17,9},{10,18},{18,10},{11,19},{19,11},{12,20... | collective-permute-start | bytes 1622024 | tf_op jit(solution)/shard_map/ppermute | solution.py:325
  125.8 13.6 %collective-permute-start.22 = (s16[528,512]{1,0:T(8,128)(2,1)S(1)}, s16[528,512]{1,0:T(8,128)(2,1)S(1)}, u32[]{:S(2)}, u32[]{:S(2)}) collective-permute-start(s16[528,512]{1,0:T(8,128)(2,1)S(1)} %reply.12), channel_id=1, source_target_pairs={{0,8},{8,0},{16,24},{24,16},{1,9},{9,1},{17,25},{25,17},{2,10},{10... | collective-permute-start | bytes 1622024 | tf_op jit(solution)/shard_map/ppermute | solution.py:328
  130.5 11.5 %collective-permute-start.23 = (s16[528,512]{1,0:T(8,128)(2,1)S(1)}, s16[528,512]{1,0:T(8,128)(2,1)S(1)}, u32[]{:S(2)}, u32[]{:S(2)}) collective-permute-start(s16[528,512]{1,0:T(8,128)(2,1)S(1)} %add.15.own_ref), channel_id=1, source_target_pairs={{8,16},{16,8},{9,17},{17,9},{10,18},{18,10},{11,19},{19,11},{12,20... | collective-permute-start | bytes 1622024 | tf_op jit(solution)/shard_map/ppermute | solution.py:325
  140.0 8.5 %collective-permute-start.24 = (s16[528,512]{1,0:T(8,128)(2,1)S(1)}, s16[528,512]{1,0:T(8,128)(2,1)S(1)}, u32[]{:S(2)}, u32[]{:S(2)}) collective-permute-start(s16[528,512]{1,0:T(8,128)(2,1)S(1)} %add.16.own_ref), channel_id=1, source_target_pairs={{8,16},{16,8},{9,17},{17,9},{10,18},{18,10},{11,19},{19,11},{12,20... | collective-permute-start | bytes 1622024 | tf_op jit(solution)/shard_map/ppermute | solution.py:325
  140.7 18.8 %collective-permute-start.25 = (s16[528,512]{1,0:T(8,128)(2,1)S(1)}, s16[528,512]{1,0:T(8,128)(2,1)S(1)}, u32[]{:S(2)}, u32[]{:S(2)}) collective-permute-start(s16[528,512]{1,0:T(8,128)(2,1)S(1)} %reply.13), channel_id=1, source_target_pairs={{8,0},{16,24},{9,1},{17,25},{10,2},{18,26},{11,3},{19,27},{12,4},{... | collective-permute-start | bytes 1622024 | tf_op jit(solution)/shard_map/ppermute | solution.py:319
  142.6 28.5 %collective-permute-start.26 = (s16[528,512]{1,0:T(8,128)(2,1)S(1)}, s16[528,512]{1,0:T(8,128)(2,1)S(1)}, u32[]{:S(2)}, u32[]{:S(2)}) collective-permute-start(s16[528,512]{1,0:T(8,128)(2,1)S(1)} %reply.14), channel_id=1, source_target_pairs={{8,0},{16,24},{9,1},{17,25},{10,2},{18,26},{11,3},{19,27},{12,4},{... | collective-permute-start | bytes 1622024 | tf_op jit(solution)/shard_map/ppermute | solution.py:319
  149.3 28.6 %collective-permute-start.27 = (s16[528,512]{1,0:T(8,128)(2,1)S(1)}, s16[528,512]{1,0:T(8,128)(2,1)S(1)}, u32[]{:S(2)}, u32[]{:S(2)}) collective-permute-start(s16[528,512]{1,0:T(8,128)(2,1)S(1)} %reply.15), channel_id=1, source_target_pairs={{8,0},{16,24},{9,1},{17,25},{10,2},{18,26},{11,3},{19,27},{12,4},{... | collective-permute-start | bytes 1622024 | tf_op jit(solution)/shard_map/ppermute | solution.py:319

commit v9 on v8

--- a/solution.py
+++ b/solution.py
@@ -12,7 +12,7 @@
 CHUNK = 2
 AHEAD = 5
 LAG = 3
-EARLY, LATE, TURN = 8000, 1, 1
+EARLY, LATE, TURN = 8000, 1, 8000
 ROWS = 512
 VMEM_LIMIT = 48 * 1024 * 1024
 
@@ -327,7 +327,7 @@
     def exchange(value):
         return lax.ppermute(value, "row", [(i, i ^ 1) for i in range(ring)])
 
-    near = [exchange(hidden_grad), swap(hidden_grad)] if short else []
+    near = [exchange(hidden_grad)] if short else []
     gathered = gather_tokens(tokens, devices, near)
     on_left = me < right
     if short:
@@ -372,20 +372,18 @@
         return tuple(outs)
 
     ahead = min(AHEAD, chunks)
-    far = [near[1], swap(near[0])]
-    moved = [outward(near[1], 0)]
     run_forward(0, 1)
     arrived.append(inward(own[0], 0))
-    place = tie(place, far[1], moved[0])
+    half = jnp.concatenate([tie(hidden_grad, place), *near], axis=0)
+    far_half = swap(half)
     run_forward(1, 2)
     arrived.append(inward(own[1], 0))
-    moved.append(outward(tie(far[1], place), 0))
     run_forward(2, ahead)
     turned = ordered(turn, *gathered)
     for s in range(chunks + LAG):
         if s < chunks:
-            if s == 0:
-                place = tie(place, moved[1])
+            if s == LAG:
+                place = tie(place, moved)
             if s + 2 < min(chunks, LAG):
                 arrived.append(inward(tie(own[s + 2], arrived[s]), 0))
             sums.append(ordered(add, own[s], arrived[s]))
@@ -395,9 +393,8 @@
             run_weights(c, (sums[c], across[c], arrived[s]), back)
 
         if s == LAG:
-            *late, _ = lax.optimization_barrier((*far, *moved, place))
-            others = [pick(distance == 0, a, b) for a, b in zip(late[:2], late[2:])]
-            back = jnp.concatenate([hidden_grad, near[0], *others], axis=0)
+            far_half = pick(distance == 0, *lax.optimization_barrier((far_half, moved, place))[:2])
+            back = jnp.concatenate([half, far_half], axis=0)
         if LAG <= s < chunks - 1:
             weights_of(s)
         c = s - 1
@@ -407,8 +404,10 @@
             arrived.append(exchange(message) if both_ways else outward(message, 0))
         if s >= max(LAG, chunks - 1):
             weights_of(s)
-        if s + ahead < chunks:
-            run_forward(s + ahead, s + ahead + 1)
+        if len(own) < chunks:
+            run_forward(len(own), len(own) + 1)
+        if s == 0:
+            moved = outward(tie(far_half, place), 0)
     return tuple(outs)
 
 

time: 183 us -> 182 us (level)
  waiting for transfers between devices: 38.8 us -> 46.1 us
  starting transfers between devices: 60.3 us -> 54.5 us
  Pallas kernels: 78.3 us -> 75.4 us
    ppermute x6, waiting for transfers between devices: 3.05 us -> 14.6 us  [exchange(): return lax.ppermute(value, 'row', [(i, i ^ 1) for i in range(ring)])]
    ppermute x5 -> x4, waiting for transfers between devices: 23.8 us -> 17.7 us  [outward(): lax.ppermute(value, 'row', [(left - hop, left - hop - 1), (right + hop, r...]
    ppermute x3, starting transfers between devices: 16.4 us -> 12.6 us  [inward(): lax.ppermute(value, 'row', [(left - hop - 1, left - hop), (right + hop +...]
    ppermute x1, waiting for transfers between devices: 0.54 us -> 2.53 us  [gather_tokens(): lax.ppermute(mine, 'col', [(i, i ^ 1) for i in range(devices)])]
    pallas_call x8, Pallas kernels: 6.75 us -> 4.9 us  [reply(): pl.pallas_call(reply_kernel, grid_spec=pltpu.PrefetchScalarGridSpec(num_s...]
    ppermute x10 -> x9, starting transfers between devices: 7.88 us -> 6.46 us  [swap(): return lax.ppermute(value, 'row', [(left, right), (right, left)])]
    ppermute x5 -> x4, starting transfers between devices: 6.46 us -> 5.17 us  [outward(): lax.ppermute(value, 'row', [(left - hop, left - hop - 1), (right + hop, r...]
  transfers between devices with their start and end apart: 28 -> 26, of which waited for: 8 -> 10; matrix products, arithmetic and copies ran while one was open for 1% -> 1% of each run, Pallas kernels for 40% -> 37%
where the time goes in v9:
time: 182 us
  Pallas kernels  75.4 us (41%)
  starting transfers between devices  54.5 us (30%)
  waiting for transfers between devices  46.1 us (25%)
  local copies, waits for them, and re-layouts  2.91 us (2%)
    pallas_call x8, Pallas kernels, weight_grads(): pl.pallas_call(functools.partial(weights_kernel, first=first, devices=dev...  36.7 us
    pallas_call x6, Pallas kernels, forward(): pl.pallas_call(functools.partial(forward_kernel, first=start // BLOCK, sp...  27.6 us
    ppermute x6, starting transfers between devices, exchange(): return lax.ppermute(value, 'row', [(i, i ^ 1) for i in range(ring)])  26.7 us
    ppermute x4, waiting for transfers between devices, outward(): lax.ppermute(value, 'row', [(left - hop, left - hop - 1), (right + hop, r...  17.7 us
    ppermute x6, waiting for transfers between devices, exchange(): return lax.ppermute(value, 'row', [(i, i ^ 1) for i in range(ring)])  14.6 us
    ppermute x3, starting transfers between devices, inward(): lax.ppermute(value, 'row', [(left - hop - 1, left - hop), (right + hop +...  12.6 us
    ppermute x3, waiting for transfers between devices, gather_tokens(): lax.ppermute(tokens, 'col', [(i, i ^ other) for i in range(devices)])  11.3 us
    ppermute x9, starting transfers between devices, swap(): return lax.ppermute(value, 'row', [(left, right), (right, left)])  6.46 us
  transfers between devices with their start and end apart: 26, of which 10 were waited for; matrix products, arithmetic and copies ran while one was open for 1% of the time, Pallas kernels for 37%

profile of v9, /device:TPU:0, one launch (start us, length us, event | category | flops | bytes accessed | tf_op | source)
XLA Modules:
  0.0 181.6 jit_solution(548745220393319233)
XLA Ops:
  0.6 3.1 %collective-permute-start.3 = (bf16[128,2048]{1,0:T(8,128)(2,1)}, bf16[128,2048]{1,0:T(8,128)(2,1)S(1)}, u32[]{:S(2)}, u32[]{:S(2)}) collective-permute-start(bf16[128,2048]{1,0:T(8,128)(2,1)} %param.9), channel_id=1, source_target_pairs={{0,8},{8,0},{16,24},{24,16},{1,9},{9,1},{17,25},{25,17},{2,10},{10... | collective-permute-start | bytes 1572872 | tf_op jit(solution)/shard_map/ppermute | solution.py:328
  3.7 1.5 collective-permute-start
  5.2 1.5 collective-permute-start.1
  7.2 6.0 %collective-permute-done = bf16[64,2048]{1,0:T(8,128)(2,1)S(1)} collective-permute-done((bf16[64,2048]{1,0:T(8,128)(2,1)}, bf16[64,2048]{1,0:T(8,128)(2,1)S(1)}, u32[]{:S(2)}, u32[]{:S(2)}) %collective-permute-start) | collective-permute-done | bytes 262176 | tf_op jit(solution)/shard_map/ppermute | solution.py:297
  13.2 5.4 %collective-permute-done.1 = bf16[64,2048]{1,0:T(8,128)(2,1)S(1)} collective-permute-done((bf16[64,2048]{1,0:T(8,128)(2,1)}, bf16[64,2048]{1,0:T(8,128)(2,1)S(1)}, u32[]{:S(2)}, u32[]{:S(2)}) %collective-permute-start.1) | collective-permute-done | bytes 262176 | tf_op jit(solution)/shard_map/ppermute | solution.py:297
  18.5 1.0 pad_maximum_fusion.1.low_ref
  19.8 2.5 %collective-permute-done.4.high_ref = bf16[256,2048]{1,0:T(8,128)(2,1)S(1)} collective-permute-done((bf16[256,2048]{1,0:T(8,128)(2,1)S(1)}, bf16[256,2048]{1,0:T(8,128)(2,1)S(1)}, u32[]{:S(2)}, u32[]{:S(2)}) %collective-permute-start.4) | collective-permute-done | bytes 1048608 | tf_op jit(solution)/shard_map/ppermute | solution.py:299
  22.3 0.7 copy-done.6
  23.0 3.9 %forward.6.a_ref = s16[528,512]{1,0:T(8,128)(2,1)S(1)} custom-call(s32[7]{0:T(128)S(1)} %stack.35.place_ref, s32[16,16]{1,0:T(8,128)S(1)} %copy-done.6, bf16[256,2048]{1,0:T(8,128)(2,1)S(1)} %pad_maximum_fusion.1.low_ref, bf16[256,2048]{1,0:T(8,128)(2,1)S(1)} %collective-permute-done.4.high_ref, bf16[2048,2048]{1,0:T(8,128)(2,1)} %gate_ref.11, ...), custom_call_target="tpu_custom_call" | custom-call | flops 8000000000 | bytes 20000000 | tf_op jit(solution)/shard_map/forward/pallas_call | solution.py:98
  26.9 2.4 %collective-permute-start.5 = (s16[528,512]{1,0:T(8,128)(2,1)S(1)}, s16[528,512]{1,0:T(8,128)(2,1)S(1)}, u32[]{:S(2)}, u32[]{:S(2)}) collective-permute-start(s16[528,512]{1,0:T(8,128)(2,1)S(1)} %forward.6.a_ref), channel_id=1, source_target_pairs={{0,8},{24,16},{1,9},{25,17},{2,10},{26,18},{3,11},{27,19},{4,12},{... | collective-permute-start | bytes 1622024 | tf_op jit(solution)/shard_map/ppermute | solution.py:322
  29.4 0.7 collective-permute-start.10
  30.2 3.9 %forward.7.a_ref = s16[528,512]{1,0:T(8,128)(2,1)S(1)} custom-call(s32[7]{0:T(128)S(1)} %stack.35.place_ref, s32[16,16]{1,0:T(8,128)S(1)} %copy-done.6, bf16[256,2048]{1,0:T(8,128)(2,1)S(1)} %pad_maximum_fusion.1.low_ref, bf16[256,2048]{1,0:T(8,128)(2,1)S(1)} %collective-permute-done.4.high_ref, bf16[2048,2048]{1,0:T(8,128)(2,1)} %gate_ref.11, ...), custom_call_target="tpu_custom_call" | custom-call | flops 8000000000 | bytes 20000000 | tf_op jit(solution)/shard_map/forward/pallas_call | solution.py:98
  34.0 5.2 %collective-permute-start.6 = (s16[528,512]{1,0:T(8,128)(2,1)S(1)}, s16[528,512]{1,0:T(8,128)(2,1)S(1)}, u32[]{:S(2)}, u32[]{:S(2)}) collective-permute-start(s16[528,512]{1,0:T(8,128)(2,1)S(1)} %forward.7.a_ref), channel_id=1, source_target_pairs={{0,8},{24,16},{1,9},{25,17},{2,10},{26,18},{3,11},{27,19},{4,12},{... | collective-permute-start | bytes 1622024 | tf_op jit(solution)/shard_map/ppermute | solution.py:322
  39.2 8.4 %forward.8 = (s16[528,512]{1,0:T(8,128)(2,1)S(1)}, s16[528,512]{1,0:T(8,128)(2,1)S(1)}, s16[528,512]{1,0:T(8,128)(2,1)S(1)}) custom-call(s32[7]{0:T(128)S(1)} %stack.35.place_ref, s32[16,16]{1,0:T(8,128)S(1)} %copy-done.7, bf16[256,2048]{1,0:T(8,128)(2,1)S(1)} %pad_maximum_fusion.1.low_ref, bf16[256,2048]{1,0:T(8,128)(2,1)S(1)} %collective-permute-done.4.high_ref, ...), custom_call_target="tpu_custom_call" | custom-call | flops 1000000 | bytes 2500 | tf_op jit(solution)/shard_map/forward/pallas_call | solution.py:98
  47.6 1.5 turn.1.turned_ref
  49.7 0.7 collective-permute-start.7
  50.4 3.9 %forward.9.next_ref.a_ref = s16[528,512]{1,0:T(8,128)(2,1)S(1)} custom-call(s32[7]{0:T(128)S(1)} %stack.35.place_ref, s32[16,16]{1,0:T(8,128)S(1)} %copy-done.7, bf16[256,2048]{1,0:T(8,128)(2,1)S(1)} %pad_maximum_fusion.1.low_ref, bf16[256,2048]{1,0:T(8,128)(2,1)S(1)} %collective-permute-done.4.high_ref, bf16[2048,2048]{1,0:T(8,128)(2,1)} %gate_ref.11, ...), custom_call_target="tpu_custom_call" | custom-call | flops 1000000 | bytes 2500 | tf_op jit(solution)/shard_map/forward/pallas_call | solution.py:98
  54.3 1.3 collective-permute-start.11
  55.6 5.0 %collective-permute-start.8 = (s16[528,512]{1,0:T(8,128)(2,1)S(1)}, s16[528,512]{1,0:T(8,128)(2,1)S(1)}, u32[]{:S(2)}, u32[]{:S(2)}) collective-permute-start(s16[528,512]{1,0:T(8,128)(2,1)S(1)} %get-tuple-element.76.a_ref), channel_id=1, source_target_pairs={{0,8},{24,16},{1,9},{25,17},{2,10},{26,18},{3,11},{27,19},{4,12},{... | collective-permute-start | bytes 1622024 | tf_op jit(solution)/shard_map/ppermute | solution.py:322
  61.2 0.7 collective-permute-start.9
  62.5 7.6 %collective-permute-start.12 = (s16[528,512]{1,0:T(8,128)(2,1)S(1)}, s16[528,512]{1,0:T(8,128)(2,1)S(1)}, u32[]{:S(2)}, u32[]{:S(2)}) collective-permute-start(s16[528,512]{1,0:T(8,128)(2,1)S(1)} %reply.8), channel_id=1, source_target_pairs={{0,8},{8,0},{16,24},{24,16},{1,9},{9,1},{17,25},{25,17},{2,10},{10... | collective-permute-start | bytes 1622024 | tf_op jit(solution)/shard_map/ppermute | solution.py:328
  70.1 3.8 %forward.10.next_ref.a_ref = s16[528,512]{1,0:T(8,128)(2,1)S(1)} custom-call(s32[7]{0:T(128)S(1)} %stack.35.place_ref, s32[16,16]{1,0:T(8,128)S(1)} %copy-done.7, bf16[256,2048]{1,0:T(8,128)(2,1)S(1)} %pad_maximum_fusion.1.low_ref, bf16[256,2048]{1,0:T(8,128)(2,1)S(1)} %collective-permute-done.4.high_ref, bf16[2048,2048]{1,0:T(8,128)(2,1)} %gate_ref.11, ...), custom_call_target="tpu_custom_call" | custom-call | flops 1000000 | bytes 2500 | tf_op jit(solution)/shard_map/forward/pallas_call | solution.py:98
  76.1 5.6 %collective-permute-start.14 = (s16[528,512]{1,0:T(8,128)(2,1)S(1)}, s16[528,512]{1,0:T(8,128)(2,1)S(1)}, u32[]{:S(2)}, u32[]{:S(2)}) collective-permute-start(s16[528,512]{1,0:T(8,128)(2,1)S(1)} %reply.9), channel_id=1, source_target_pairs={{0,8},{8,0},{16,24},{24,16},{1,9},{9,1},{17,25},{25,17},{2,10},{10... | collective-permute-start | bytes 1622024 | tf_op jit(solution)/shard_map/ppermute | solution.py:328
  81.7 3.8 %forward.11.next_ref.a_ref = s16[528,512]{1,0:T(8,128)(2,1)S(1)} custom-call(s32[7]{0:T(128)S(1)} %stack.35.place_ref, s32[16,16]{1,0:T(8,128)S(1)} %copy-done.7, bf16[256,2048]{1,0:T(8,128)(2,1)S(1)} %pad_maximum_fusion.1.low_ref, bf16[256,2048]{1,0:T(8,128)(2,1)S(1)} %collective-permute-done.4.high_ref, bf16[2048,2048]{1,0:T(8,128)(2,1)} %gate_ref.11, ...), custom_call_target="tpu_custom_call" | custom-call | flops 1000000 | bytes 2500 | tf_op jit(solution)/shard_map/forward/pallas_call | solution.py:98
  85.6 8.7 %collective-permute-done.12.b_ref.out_ref = s16[528,512]{1,0:T(8,128)(2,1)S(1)} collective-permute-done((s16[528,512]{1,0:T(8,128)(2,1)S(1)}, s16[528,512]{1,0:T(8,128)(2,1)S(1)}, u32[]{:S(2)}, u32[]{:S(2)}) %collective-permute-start.12) | collective-permute-done | bytes 540704 | tf_op jit(solution)/shard_map/ppermute | solution.py:328
  94.8 0.9 collective-permute-start.15
  96.1 4.6 %weight_grads.8 = (bf16[128,2048]{1,0:T(8,128)(2,1)}, f32[2048,2048]{1,0:T(8,128)}, f32[2048,2048]{1,0:T(8,128)}) custom-call(s32[7]{0:T(128)S(1)} %stack.35.place_ref, s32[16,16]{1,0:T(8,128)S(1)} %copy-done.7, bf16[2048,512]{1,0:T(8,128)(2,1)S(1)} %turn.1.turned_ref, bf16[512,2048]{1,0:T(8,128)(2,1)S(1)} %pad_maximum_fusion.back_ref, ...), custom_call_target="tpu_custom_call" | custom-call | flops 1000000 | bytes 2500 | tf_op jit(solution)/shard_map/weight_grads/pallas_call | solution.py:261
  101.3 3.9 %collective-permute-start.16 = (s16[528,512]{1,0:T(8,128)(2,1)S(1)}, s16[528,512]{1,0:T(8,128)(2,1)S(1)}, u32[]{:S(2)}, u32[]{:S(2)}) collective-permute-start(s16[528,512]{1,0:T(8,128)(2,1)S(1)} %reply.10), channel_id=1, source_target_pairs={{0,8},{8,0},{16,24},{24,16},{1,9},{9,1},{17,25},{25,17},{2,10},{10... | collective-permute-start | bytes 1622024 | tf_op jit(solution)/shard_map/ppermute | solution.py:328
  106.4 0.8 copy-done
  108.0 1.0 copy-done.1
  109.0 4.6 %weight_grads.9 = (bf16[128,2048]{1,0:T(8,128)(2,1)}, f32[2048,2048]{1,0:T(8,128)}, f32[2048,2048]{1,0:T(8,128)}) custom-call(s32[7]{0:T(128)S(1)} %stack.35.place_ref, s32[16,16]{1,0:T(8,128)S(1)} %copy-done.7, bf16[2048,512]{1,0:T(8,128)(2,1)S(1)} %turn.1.turned_ref, ...), custom_call_target="tpu_custom_call", output_to_operand_aliasing={{0}: (7, {}), {1}: (8, {}), {2}: (9, {})} | custom-call | flops 1000000 | bytes 2500 | tf_op jit(solution)/shard_map/weight_grads/pallas_call | solution.py:261
  114.2 4.0 %collective-permute-start.18 = (s16[528,512]{1,0:T(8,128)(2,1)S(1)}, s16[528,512]{1,0:T(8,128)(2,1)S(1)}, u32[]{:S(2)}, u32[]{:S(2)}) collective-permute-start(s16[528,512]{1,0:T(8,128)(2,1)S(1)} %reply.11), channel_id=1, source_target_pairs={{0,8},{8,0},{16,24},{24,16},{1,9},{9,1},{17,25},{25,17},{2,10},{10... | collective-permute-start | bytes 1622024 | tf_op jit(solution)/shard_map/ppermute | solution.py:328
  119.4 4.6 %weight_grads.10 = (bf16[128,2048]{1,0:T(8,128)(2,1)}, f32[2048,2048]{1,0:T(8,128)}, f32[2048,2048]{1,0:T(8,128)}) custom-call(s32[7]{0:T(128)S(1)} %stack.35.place_ref, s32[16,16]{1,0:T(8,128)S(1)} %copy-done.7, bf16[2048,512]{1,0:T(8,128)(2,1)S(1)} %turn.1.turned_ref, ...), custom_call_target="tpu_custom_call", output_to_operand_aliasing={{0}: (7, {}), {1}: (8, {}), {2}: (9, {})} | custom-call | flops 1000000 | bytes 2500 | tf_op jit(solution)/shard_map/weight_grads/pallas_call | solution.py:261
  124.6 2.6 %collective-permute-start.20 = (s16[528,512]{1,0:T(8,128)(2,1)S(1)}, s16[528,512]{1,0:T(8,128)(2,1)S(1)}, u32[]{:S(2)}, u32[]{:S(2)}) collective-permute-start(s16[528,512]{1,0:T(8,128)(2,1)S(1)} %reply.12), channel_id=1, source_target_pairs={{0,8},{8,0},{16,24},{24,16},{1,9},{9,1},{17,25},{25,17},{2,10},{10... | collective-permute-start | bytes 1622024 | tf_op jit(solution)/shard_map/ppermute | solution.py:328
  127.2 3.4 %collective-permute-done.18.b_ref.out_ref = s16[528,512]{1,0:T(8,128)(2,1)S(1)} collective-permute-done((s16[528,512]{1,0:T(8,128)(2,1)S(1)}, s16[528,512]{1,0:T(8,128)(2,1)S(1)}, u32[]{:S(2)}, u32[]{:S(2)}) %collective-permute-start.18) | collective-permute-done | bytes 540704 | tf_op jit(solution)/shard_map/ppermute | solution.py:328
  131.9 4.6 %weight_grads.11 = (bf16[128,2048]{1,0:T(8,128)(2,1)}, f32[2048,2048]{1,0:T(8,128)}, f32[2048,2048]{1,0:T(8,128)}) custom-call(s32[7]{0:T(128)S(1)} %stack.35.place_ref, s32[16,16]{1,0:T(8,128)S(1)} %copy-done.7, bf16[2048,512]{1,0:T(8,128)(2,1)S(1)} %turn.1.turned_ref, ...), custom_call_target="tpu_custom_call", output_to_operand_aliasing={{0}: (7, {}), {1}: (8, {}), {2}: (9, {})} | custom-call | flops 1000000 | bytes 2500 | tf_op jit(solution)/shard_map/weight_grads/pallas_call | solution.py:261
  137.1 1.9 %collective-permute-done.20.b_ref.out_ref = s16[528,512]{1,0:T(8,128)(2,1)S(1)} collective-permute-done((s16[528,512]{1,0:T(8,128)(2,1)S(1)}, s16[528,512]{1,0:T(8,128)(2,1)S(1)}, u32[]{:S(2)}, u32[]{:S(2)}) %collective-permute-start.20) | collective-permute-done | bytes 540704 | tf_op jit(solution)/shard_map/ppermute | solution.py:328
  140.3 1.3 collective-permute-start.23
  142.2 1.3 collective-permute-start.24
  143.5 4.6 %weight_grads.12 = (bf16[128,2048]{1,0:T(8,128)(2,1)}, f32[2048,2048]{1,0:T(8,128)}, f32[2048,2048]{1,0:T(8,128)}) custom-call(s32[7]{0:T(128)S(1)} %stack.35.place_ref, s32[16,16]{1,0:T(8,128)S(1)} %copy-done.7, bf16[2048,512]{1,0:T(8,128)(2,1)S(1)} %turn.1.turned_ref, ...), custom_call_target="tpu_custom_call", output_to_operand_aliasing={{0}: (7, {}), {1}: (8, {}), {2}: (9, {})} | custom-call | flops 1000000 | bytes 2500 | tf_op jit(solution)/shard_map/weight_grads/pallas_call | solution.py:261
  148.1 0.8 reply.15
  148.9 1.3 collective-permute-start.25
  150.2 8.2 %collective-permute-done.23.out_ref = s16[528,512]{1,0:T(8,128)(2,1)S(1)} collective-permute-done((s16[528,512]{1,0:T(8,128)(2,1)S(1)}, s16[528,512]{1,0:T(8,128)(2,1)S(1)}, u32[]{:S(2)}, u32[]{:S(2)}) %collective-permute-start.23) | collective-permute-done | bytes 540704 | tf_op jit(solution)/shard_map/ppermute | solution.py:319
  158.4 4.6 %weight_grads.13 = (bf16[128,2048]{1,0:T(8,128)(2,1)}, f32[2048,2048]{1,0:T(8,128)}, f32[2048,2048]{1,0:T(8,128)}) custom-call(s32[7]{0:T(128)S(1)} %stack.35.place_ref, s32[16,16]{1,0:T(8,128)S(1)} %copy-done.7, bf16[2048,512]{1,0:T(8,128)(2,1)S(1)} %turn.1.turned_ref, ...), custom_call_target="tpu_custom_call", output_to_operand_aliasing={{0}: (7, {}), {1}: (8, {}), {2}: (9, {})} | custom-call | flops 1000000 | bytes 2500 | tf_op jit(solution)/shard_map/weight_grads/pallas_call | solution.py:261
  163.0 7.0 %collective-permute-done.24.out_ref = s16[528,512]{1,0:T(8,128)(2,1)S(1)} collective-permute-done((s16[528,512]{1,0:T(8,128)(2,1)S(1)}, s16[528,512]{1,0:T(8,128)(2,1)S(1)}, u32[]{:S(2)}, u32[]{:S(2)}) %collective-permute-start.24) | collective-permute-done | bytes 540704 | tf_op jit(solution)/shard_map/ppermute | solution.py:319
  170.0 4.6 %weight_grads.14 = (bf16[128,2048]{1,0:T(8,128)(2,1)}, f32[2048,2048]{1,0:T(8,128)}, f32[2048,2048]{1,0:T(8,128)}) custom-call(s32[7]{0:T(128)S(1)} %stack.35.place_ref, s32[16,16]{1,0:T(8,128)S(1)} %copy-done.7, bf16[2048,512]{1,0:T(8,128)(2,1)S(1)} %turn.1.turned_ref, ...), custom_call_target="tpu_custom_call", output_to_operand_aliasing={{0}: (7, {}), {1}: (8, {}), {2}: (9, {})} | custom-call | flops 1000000 | bytes 2500 | tf_op jit(solution)/shard_map/weight_grads/pallas_call | solution.py:261
  174.6 2.4 %collective-permute-done.25.out_ref = s16[528,512]{1,0:T(8,128)(2,1)S(1)} collective-permute-done((s16[528,512]{1,0:T(8,128)(2,1)S(1)}, s16[528,512]{1,0:T(8,128)(2,1)S(1)}, u32[]{:S(2)}, u32[]{:S(2)}) %collective-permute-start.25) | collective-permute-done | bytes 540704 | tf_op jit(solution)/shard_map/ppermute | solution.py:319
  177.0 4.6 %weight_grads.15 = (bf16[128,2048]{1,0:T(8,128)(2,1)}, f32[2048,2048]{1,0:T(8,128)}, f32[2048,2048]{1,0:T(8,128)}) custom-call(s32[7]{0:T(128)S(1)} %stack.35.place_ref, s32[16,16]{1,0:T(8,128)S(1)} %copy-done.7, bf16[2048,512]{1,0:T(8,128)(2,1)S(1)} %turn.1.turned_ref, ...), custom_call_target="tpu_custom_call", output_to_operand_aliasing={{0}: (7, {}), {1}: (8, {}), {2}: (9, {})} | custom-call | flops 1000000 | bytes 2500 | tf_op jit(solution)/shard_map/weight_grads/pallas_call | solution.py:261
  (62 shorter events, 14.2 us)
Async XLA Ops:
  0.6 19.0 %collective-permute-start.3 = (bf16[128,2048]{1,0:T(8,128)(2,1)}, bf16[128,2048]{1,0:T(8,128)(2,1)S(1)}, u32[]{:S(2)}, u32[]{:S(2)}) collective-permute-start(bf16[128,2048]{1,0:T(8,128)(2,1)} %param.9), channel_id=1, source_target_pairs={{0,8},{8,0},{16,24},{24,16},{1,9},{9,1},{17,25},{25,17},{2,10},{10... | collective-permute-start | bytes 1572872 | tf_op jit(solution)/shard_map/ppermute | solution.py:328
  3.7 9.4 %collective-permute-start = (bf16[64,2048]{1,0:T(8,128)(2,1)}, bf16[64,2048]{1,0:T(8,128)(2,1)S(1)}, u32[]{:S(2)}, u32[]{:S(2)}) collective-permute-start(bf16[64,2048]{1,0:T(8,128)(2,1)} %param.5), channel_id=1, source_target_pairs={{0,2},{1,3},{2,0},{3,1},{4,6},{5,7},{6,4},{7,5},{8,10},{9,11},{10,... | collective-permute-start | bytes 786440 | tf_op jit(solution)/shard_map/ppermute | solution.py:297
  5.2 13.3 %collective-permute-start.1 = (bf16[64,2048]{1,0:T(8,128)(2,1)}, bf16[64,2048]{1,0:T(8,128)(2,1)S(1)}, u32[]{:S(2)}, u32[]{:S(2)}) collective-permute-start(bf16[64,2048]{1,0:T(8,128)(2,1)} %param.5), channel_id=1, source_target_pairs={{0,4},{1,5},{2,6},{3,7},{4,0},{5,1},{6,2},{7,3},{8,12},{9,13},{10,... | collective-permute-start | bytes 786440 | tf_op jit(solution)/shard_map/ppermute | solution.py:297
  6.7 11.8 %collective-permute-start.2 = (bf16[64,2048]{1,0:T(8,128)(2,1)}, bf16[64,2048]{1,0:T(8,128)(2,1)S(1)}, u32[]{:S(2)}, u32[]{:S(2)}) collective-permute-start(bf16[64,2048]{1,0:T(8,128)(2,1)} %param.5), channel_id=1, source_target_pairs={{0,6},{1,7},{2,4},{3,5},{4,2},{5,3},{6,0},{7,1},{8,14},{9,15},{10,... | collective-permute-start | bytes 786440 | tf_op jit(solution)/shard_map/ppermute | solution.py:297
  19.6 9.7 %copy-start.9 = (bf16[128,2048]{1,0:T(8,128)(2,1)}, bf16[128,2048]{1,0:T(8,128)(2,1)S(1)}, u32[]{:S(2)}) copy-start(bf16[128,2048]{1,0:T(8,128)(2,1)S(1)} %collective-permute-done.3) | copy-start | bytes 1572868
  19.6 2.7 %collective-permute-start.4 = (bf16[256,2048]{1,0:T(8,128)(2,1)S(1)}, bf16[256,2048]{1,0:T(8,128)(2,1)S(1)}, u32[]{:S(2)}, u32[]{:S(2)}) collective-permute-start(bf16[256,2048]{1,0:T(8,128)(2,1)S(1)} %pad_maximum_fusion.1.low_ref), channel_id=1, source_target_pairs={{0,1},{1,0},{2,3},{3,2},{4,5},{5,4},{6,7},{7,6},{8,9},{9,8},{10,11... | collective-permute-start | bytes 3145736 | tf_op jit(solution)/shard_map/ppermute | solution.py:299
  22.3 0.7 copy-start.6
  23.0 6.3 %copy-start.8 = (bf16[128,2048]{1,0:T(8,128)(2,1)S(1)}, bf16[128,2048]{1,0:T(8,128)(2,1)}, u32[]{:S(2)}) copy-start(bf16[128,2048]{1,0:T(8,128)(2,1)} %param.9) | copy-start | bytes 1572868
  26.9 22.2 %collective-permute-start.5 = (s16[528,512]{1,0:T(8,128)(2,1)S(1)}, s16[528,512]{1,0:T(8,128)(2,1)S(1)}, u32[]{:S(2)}, u32[]{:S(2)}) collective-permute-start(s16[528,512]{1,0:T(8,128)(2,1)S(1)} %forward.6.a_ref), channel_id=1, source_target_pairs={{0,8},{24,16},{1,9},{25,17},{2,10},{26,18},{3,11},{27,19},{4,12},{... | collective-permute-start | bytes 1622024 | tf_op jit(solution)/shard_map/ppermute | solution.py:322
  29.4 9.8 %copy-start.7 = (s32[16,16]{1,0:T(8,128)S(1)}, s32[16,16]{1,0:T(8,128)}, u32[]{:S(2)}) copy-start(s32[16,16]{1,0:T(8,128)} %mask_ref.27) | copy-start | bytes 3076
  29.4 24.9 %collective-permute-start.10 = (bf16[256,2048]{1,0:T(8,128)(2,1)S(1)}, bf16[256,2048]{1,0:T(8,128)(2,1)S(1)}, u32[]{:S(2)}, u32[]{:S(2)}) collective-permute-start(bf16[256,2048]{1,0:T(8,128)(2,1)S(1)} %pad_maximum_fusion.2), channel_id=1, source_target_pairs={{8,16},{16,8},{9,17},{17,9},{10,18},{18,10},{11,19},{19,11},{12,20... | collective-permute-start | bytes 3145736 | tf_op jit(solution)/shard_map/ppermute | solution.py:325
  34.0 26.6 %collective-permute-start.6 = (s16[528,512]{1,0:T(8,128)(2,1)S(1)}, s16[528,512]{1,0:T(8,128)(2,1)S(1)}, u32[]{:S(2)}, u32[]{:S(2)}) collective-permute-start(s16[528,512]{1,0:T(8,128)(2,1)S(1)} %forward.7.a_ref), channel_id=1, source_target_pairs={{0,8},{24,16},{1,9},{25,17},{2,10},{26,18},{3,11},{27,19},{4,12},{... | collective-permute-start | bytes 1622024 | tf_op jit(solution)/shard_map/ppermute | solution.py:322
  49.7 12.2 %collective-permute-start.7 = (s16[528,512]{1,0:T(8,128)(2,1)S(1)}, s16[528,512]{1,0:T(8,128)(2,1)S(1)}, u32[]{:S(2)}, u32[]{:S(2)}) collective-permute-start(s16[528,512]{1,0:T(8,128)(2,1)S(1)} %add.9.own_ref), channel_id=1, source_target_pairs={{8,16},{16,8},{9,17},{17,9},{10,18},{18,10},{11,19},{19,11},{12,20... | collective-permute-start | bytes 1622024 | tf_op jit(solution)/shard_map/ppermute | solution.py:325
  54.3 31.3 %collective-permute-start.11 = (bf16[256,2048]{1,0:T(8,128)(2,1)S(1)}, bf16[256,2048]{1,0:T(8,128)(2,1)S(1)}, u32[]{:S(2)}, u32[]{:S(2)}) collective-permute-start(bf16[256,2048]{1,0:T(8,128)(2,1)S(1)} %collective-permute-done.10), channel_id=1, source_target_pairs={{8,0},{16,24},{9,1},{17,25},{10,2},{18,26},{11,3},{19,27},{12,4},{... | collective-permute-start | bytes 3145736 | tf_op jit(solution)/shard_map/ppermute | solution.py:319
  55.6 18.4 %collective-permute-start.8 = (s16[528,512]{1,0:T(8,128)(2,1)S(1)}, s16[528,512]{1,0:T(8,128)(2,1)S(1)}, u32[]{:S(2)}, u32[]{:S(2)}) collective-permute-start(s16[528,512]{1,0:T(8,128)(2,1)S(1)} %get-tuple-element.76.a_ref), channel_id=1, source_target_pairs={{0,8},{24,16},{1,9},{25,17},{2,10},{26,18},{3,11},{27,19},{4,12},{... | collective-permute-start | bytes 1622024 | tf_op jit(solution)/shard_map/ppermute | solution.py:322
  61.2 14.0 %collective-permute-start.9 = (s16[528,512]{1,0:T(8,128)(2,1)S(1)}, s16[528,512]{1,0:T(8,128)(2,1)S(1)}, u32[]{:S(2)}, u32[]{:S(2)}) collective-permute-start(s16[528,512]{1,0:T(8,128)(2,1)S(1)} %add.10.own_ref), channel_id=1, source_target_pairs={{8,16},{16,8},{9,17},{17,9},{10,18},{18,10},{11,19},{19,11},{12,20... | collective-permute-start | bytes 1622024 | tf_op jit(solution)/shard_map/ppermute | solution.py:325
  62.5 31.7 %collective-permute-start.12 = (s16[528,512]{1,0:T(8,128)(2,1)S(1)}, s16[528,512]{1,0:T(8,128)(2,1)S(1)}, u32[]{:S(2)}, u32[]{:S(2)}) collective-permute-start(s16[528,512]{1,0:T(8,128)(2,1)S(1)} %reply.8), channel_id=1, source_target_pairs={{0,8},{8,0},{16,24},{24,16},{1,9},{9,1},{17,25},{25,17},{2,10},{10... | collective-permute-start | bytes 1622024 | tf_op jit(solution)/shard_map/ppermute | solution.py:328
  74.6 26.1 %collective-permute-start.13 = (s16[528,512]{1,0:T(8,128)(2,1)S(1)}, s16[528,512]{1,0:T(8,128)(2,1)S(1)}, u32[]{:S(2)}, u32[]{:S(2)}) collective-permute-start(s16[528,512]{1,0:T(8,128)(2,1)S(1)} %add.11.own_ref), channel_id=1, source_target_pairs={{8,16},{16,8},{9,17},{17,9},{10,18},{18,10},{11,19},{19,11},{12,20... | collective-permute-start | bytes 1622024 | tf_op jit(solution)/shard_map/ppermute | solution.py:325
  75.3 0.8 copy-start.4
  76.1 29.7 %collective-permute-start.14 = (s16[528,512]{1,0:T(8,128)(2,1)S(1)}, s16[528,512]{1,0:T(8,128)(2,1)S(1)}, u32[]{:S(2)}, u32[]{:S(2)}) collective-permute-start(s16[528,512]{1,0:T(8,128)(2,1)S(1)} %reply.9), channel_id=1, source_target_pairs={{0,8},{8,0},{16,24},{24,16},{1,9},{9,1},{17,25},{25,17},{2,10},{10... | collective-permute-start | bytes 1622024 | tf_op jit(solution)/shard_map/ppermute | solution.py:328
  85.6 10.3 %copy-start.10 = (bf16[128,2048]{1,0:T(8,128)(2,1)S(1)}, bf16[128,2048]{1,0:T(8,128)(2,1)}, u32[]{:S(2)}) copy-start(bf16[128,2048]{1,0:T(8,128)(2,1)} %copy-done.9) | copy-start | bytes 1572868
  94.8 18.7 %collective-permute-start.15 = (s16[528,512]{1,0:T(8,128)(2,1)S(1)}, s16[528,512]{1,0:T(8,128)(2,1)S(1)}, u32[]{:S(2)}, u32[]{:S(2)}) collective-permute-start(s16[528,512]{1,0:T(8,128)(2,1)S(1)} %add.12.own_ref), channel_id=1, source_target_pairs={{8,16},{16,8},{9,17},{17,9},{10,18},{18,10},{11,19},{19,11},{12,20... | collective-permute-start | bytes 1622024 | tf_op jit(solution)/shard_map/ppermute | solution.py:325
  96.1 11.8 %copy-start.5 = (s16[528,512]{1,0:T(8,128)(2,1)S(1)}, s16[528,512]{1,0:T(8,128)(2,1)}, u32[]{:S(2)}) copy-start(s16[528,512]{1,0:T(8,128)(2,1)} %copy-done.4) | copy-start | bytes 1622020
  100.7 4.5 %copy-start.2 = (s16[528,512]{1,0:T(8,128)(2,1)}, s16[528,512]{1,0:T(8,128)(2,1)S(1)}, u32[]{:S(2)}) copy-start(s16[528,512]{1,0:T(8,128)(2,1)S(1)} %collective-permute-done.13.b_ref.across_ref) | copy-start | bytes 1622020
  101.3 16.9 %collective-permute-start.16 = (s16[528,512]{1,0:T(8,128)(2,1)S(1)}, s16[528,512]{1,0:T(8,128)(2,1)S(1)}, u32[]{:S(2)}, u32[]{:S(2)}) collective-permute-start(s16[528,512]{1,0:T(8,128)(2,1)S(1)} %reply.10), channel_id=1, source_target_pairs={{0,8},{8,0},{16,24},{24,16},{1,9},{9,1},{17,25},{25,17},{2,10},{10... | collective-permute-start | bytes 1622024 | tf_op jit(solution)/shard_map/ppermute | solution.py:328
  106.4 0.8 copy-start
  107.2 16.8 %collective-permute-start.17 = (s16[528,512]{1,0:T(8,128)(2,1)S(1)}, s16[528,512]{1,0:T(8,128)(2,1)S(1)}, u32[]{:S(2)}, u32[]{:S(2)}) collective-permute-start(s16[528,512]{1,0:T(8,128)(2,1)S(1)} %add.13.own_ref), channel_id=1, source_target_pairs={{8,16},{16,8},{9,17},{17,9},{10,18},{18,10},{11,19},{19,11},{12,20... | collective-permute-start | bytes 1622024 | tf_op jit(solution)/shard_map/ppermute | solution.py:325
  107.9 1.0 copy-start.1
  109.0 10.4 %copy-start.3 = (s16[528,512]{1,0:T(8,128)(2,1)S(1)}, s16[528,512]{1,0:T(8,128)(2,1)}, u32[]{:S(2)}) copy-start(s16[528,512]{1,0:T(8,128)(2,1)} %copy-done.2) | copy-start | bytes 1622020
  114.2 16.4 %collective-permute-start.18 = (s16[528,512]{1,0:T(8,128)(2,1)S(1)}, s16[528,512]{1,0:T(8,128)(2,1)S(1)}, u32[]{:S(2)}, u32[]{:S(2)}) collective-permute-start(s16[528,512]{1,0:T(8,128)(2,1)S(1)} %reply.11), channel_id=1, source_target_pairs={{0,8},{8,0},{16,24},{24,16},{1,9},{9,1},{17,25},{25,17},{2,10},{10... | collective-permute-start | bytes 1622024 | tf_op jit(solution)/shard_map/ppermute | solution.py:328
  118.7 17.8 %collective-permute-start.19 = (s16[528,512]{1,0:T(8,128)(2,1)S(1)}, s16[528,512]{1,0:T(8,128)(2,1)S(1)}, u32[]{:S(2)}, u32[]{:S(2)}) collective-permute-start(s16[528,512]{1,0:T(8,128)(2,1)S(1)} %add.14.own_ref), channel_id=1, source_target_pairs={{8,16},{16,8},{9,17},{17,9},{10,18},{18,10},{11,19},{19,11},{12,20... | collective-permute-start | bytes 1622024 | tf_op jit(solution)/shard_map/ppermute | solution.py:325
  124.6 14.4 %collective-permute-start.20 = (s16[528,512]{1,0:T(8,128)(2,1)S(1)}, s16[528,512]{1,0:T(8,128)(2,1)S(1)}, u32[]{:S(2)}, u32[]{:S(2)}) collective-permute-start(s16[528,512]{1,0:T(8,128)(2,1)S(1)} %reply.12), channel_id=1, source_target_pairs={{0,8},{8,0},{16,24},{24,16},{1,9},{9,1},{17,25},{25,17},{2,10},{10... | collective-permute-start | bytes 1622024 | tf_op jit(solution)/shard_map/ppermute | solution.py:328
  131.2 10.4 %collective-permute-start.21 = (s16[528,512]{1,0:T(8,128)(2,1)S(1)}, s16[528,512]{1,0:T(8,128)(2,1)S(1)}, u32[]{:S(2)}, u32[]{:S(2)}) collective-permute-start(s16[528,512]{1,0:T(8,128)(2,1)S(1)} %add.15.own_ref), channel_id=1, source_target_pairs={{8,16},{16,8},{9,17},{17,9},{10,18},{18,10},{11,19},{19,11},{12,20... | collective-permute-start | bytes 1622024 | tf_op jit(solution)/shard_map/ppermute | solution.py:325
  139.6 8.5 %collective-permute-start.22 = (s16[528,512]{1,0:T(8,128)(2,1)S(1)}, s16[528,512]{1,0:T(8,128)(2,1)S(1)}, u32[]{:S(2)}, u32[]{:S(2)}) collective-permute-start(s16[528,512]{1,0:T(8,128)(2,1)S(1)} %add.16.own_ref), channel_id=1, source_target_pairs={{8,16},{16,8},{9,17},{17,9},{10,18},{18,10},{11,19},{19,11},{12,20... | collective-permute-start | bytes 1622024 | tf_op jit(solution)/shard_map/ppermute | solution.py:325
  140.3 18.2 %collective-permute-start.23 = (s16[528,512]{1,0:T(8,128)(2,1)S(1)}, s16[528,512]{1,0:T(8,128)(2,1)S(1)}, u32[]{:S(2)}, u32[]{:S(2)}) collective-permute-start(s16[528,512]{1,0:T(8,128)(2,1)S(1)} %reply.13), channel_id=1, source_target_pairs={{8,0},{16,24},{9,1},{17,25},{10,2},{18,26},{11,3},{19,27},{12,4},{... | collective-permute-start | bytes 1622024 | tf_op jit(solution)/shard_map/ppermute | solution.py:319
  142.2 27.8 %collective-permute-start.24 = (s16[528,512]{1,0:T(8,128)(2,1)S(1)}, s16[528,512]{1,0:T(8,128)(2,1)S(1)}, u32[]{:S(2)}, u32[]{:S(2)}) collective-permute-start(s16[528,512]{1,0:T(8,128)(2,1)S(1)} %reply.14), channel_id=1, source_target_pairs={{8,0},{16,24},{9,1},{17,25},{10,2},{18,26},{11,3},{19,27},{12,4},{... | collective-permute-start | bytes 1622024 | tf_op jit(solution)/shard_map/ppermute | solution.py:319
  148.9 28.1 %collective-permute-start.25 = (s16[528,512]{1,0:T(8,128)(2,1)S(1)}, s16[528,512]{1,0:T(8,128)(2,1)S(1)}, u32[]{:S(2)}, u32[]{:S(2)}) collective-permute-start(s16[528,512]{1,0:T(8,128)(2,1)S(1)} %reply.15), channel_id=1, source_target_pairs={{8,0},{16,24},{9,1},{17,25},{10,2},{18,26},{11,3},{19,27},{12,4},{... | collective-permute-start | bytes 1622024 | tf_op jit(solution)/shard_map/ppermute | solution.py:319

commit v10 on v8

--- a/solution.py
+++ b/solution.py
@@ -10,7 +10,7 @@
 BLOCK = 128
 GROUPS = 16
 CHUNK = 2
-AHEAD = 5
+AHEAD = 4
 LAG = 3
 EARLY, LATE, TURN = 8000, 1, 1
 ROWS = 512
@@ -327,7 +327,7 @@
     def exchange(value):
         return lax.ppermute(value, "row", [(i, i ^ 1) for i in range(ring)])
 
-    near = [exchange(hidden_grad), swap(hidden_grad)] if short else []
+    near = [exchange(hidden_grad)] if short else []
     gathered = gather_tokens(tokens, devices, near)
     on_left = me < right
     if short:
@@ -372,24 +372,24 @@
         return tuple(outs)
 
     ahead = min(AHEAD, chunks)
-    far = [near[1], swap(near[0])]
-    moved = [outward(near[1], 0)]
     run_forward(0, 1)
     arrived.append(inward(own[0], 0))
-    place = tie(place, far[1], moved[0])
+    far = [swap(hidden_grad), swap(tie(near[0], place))]
     run_forward(1, 2)
     arrived.append(inward(own[1], 0))
-    moved.append(outward(tie(far[1], place), 0))
+    moved = [outward(tie(far[0], place), 0)]
     run_forward(2, ahead)
     turned = ordered(turn, *gathered)
     for s in range(chunks + LAG):
         if s < chunks:
             if s == 0:
-                place = tie(place, moved[1])
+                place = tie(place, far[1], moved[0])
             if s + 2 < min(chunks, LAG):
                 arrived.append(inward(tie(own[s + 2], arrived[s]), 0))
             sums.append(ordered(add, own[s], arrived[s]))
             across.append(swap(sums[s]))
+        if s == 0:
+            moved.append(outward(tie(far[1], place), 0))
         def weights_of(s):
             c = s - LAG
             run_weights(c, (sums[c], across[c], arrived[s]), back)
@@ -402,13 +402,15 @@
             weights_of(s)
         c = s - 1
         if 0 <= c < chunks:
+            if c == 0:
+                place = tie(place, moved[1])
             both_ways = c + LAG < chunks
             message = ordered(reply, own[c], across[c], own[c + LAG] if both_ways else own[c])
             arrived.append(exchange(message) if both_ways else outward(message, 0))
         if s >= max(LAG, chunks - 1):
             weights_of(s)
-        if s + ahead < chunks:
-            run_forward(s + ahead, s + ahead + 1)
+        if len(own) < chunks:
+            run_forward(len(own), len(own) + 1)
     return tuple(outs)
 
 

time: 183 us -> 182 us (level)
  starting transfers between devices: 60.3 us -> 57.9 us
    ppermute x6, starting transfers between devices: 25.9 us -> 21.3 us  [exchange(): return lax.ppermute(value, 'row', [(i, i ^ 1) for i in range(ring)])]
    ppermute x3, starting transfers between devices: 16.4 us -> 19.2 us  [inward(): lax.ppermute(value, 'row', [(left - hop - 1, left - hop), (right + hop +...]
    pallas_call x6 -> x7, Pallas kernels: 27.6 us -> 29.2 us  [forward(): pl.pallas_call(functools.partial(forward_kernel, first=start // BLOCK, sp...]
where the time goes in v10:
time: 182 us; the launch traced here: 181 us
  Pallas kernels  77.5 us (43%)
  starting transfers between devices  57.9 us (32%)
  waiting for transfers between devices  40.3 us (22%)
  other arithmetic  2.35 us (1%)
    pallas_call x8, Pallas kernels, weight_grads(): pl.pallas_call(functools.partial(weights_kernel, first=first, devices=dev...  36.6 us
    pallas_call x7, Pallas kernels, forward(): pl.pallas_call(functools.partial(forward_kernel, first=start // BLOCK, sp...  29.2 us
    ppermute x5, waiting for transfers between devices, outward(): lax.ppermute(value, 'row', [(left - hop, left - hop - 1), (right + hop, r...  23.6 us
    ppermute x6, starting transfers between devices, exchange(): return lax.ppermute(value, 'row', [(i, i ^ 1) for i in range(ring)])  21.3 us
    ppermute x3, starting transfers between devices, inward(): lax.ppermute(value, 'row', [(left - hop - 1, left - hop), (right + hop +...  19.2 us
    ppermute x3, waiting for transfers between devices, gather_tokens(): lax.ppermute(tokens, 'col', [(i, i ^ other) for i in range(devices)])  11.3 us
    ppermute x10, starting transfers between devices, swap(): return lax.ppermute(value, 'row', [(left, right), (right, left)])  7.13 us
    ppermute x5, starting transfers between devices, outward(): lax.ppermute(value, 'row', [(left - hop, left - hop - 1), (right + hop, r...  6.68 us
  transfers between devices with their start and end apart: 28, of which 8 were waited for; matrix products, arithmetic and copies ran while one was open for 1% of the time, Pallas kernels for 40%

profile of v10, /device:TPU:0, one launch (start us, length us, event | category | flops | bytes accessed | tf_op | source)
XLA Modules:
  0.0 180.9 jit_solution(3102935654089990822)
XLA Ops:
  0.6 3.1 %collective-permute-start.3 = (bf16[128,2048]{1,0:T(8,128)(2,1)}, bf16[128,2048]{1,0:T(8,128)(2,1)S(1)}, u32[]{:S(2)}, u32[]{:S(2)}) collective-permute-start(bf16[128,2048]{1,0:T(8,128)(2,1)} %param.9), channel_id=1, source_target_pairs={{0,8},{8,0},{16,24},{24,16},{1,9},{9,1},{17,25},{25,17},{2,10},{10... | collective-permute-start | bytes 1572872 | tf_op jit(solution)/shard_map/ppermute | solution.py:328
  3.7 1.5 collective-permute-start
  5.2 1.5 collective-permute-start.1
  7.2 6.0 %collective-permute-done = bf16[64,2048]{1,0:T(8,128)(2,1)S(1)} collective-permute-done((bf16[64,2048]{1,0:T(8,128)(2,1)}, bf16[64,2048]{1,0:T(8,128)(2,1)S(1)}, u32[]{:S(2)}, u32[]{:S(2)}) %collective-permute-start) | collective-permute-done | bytes 262176 | tf_op jit(solution)/shard_map/ppermute | solution.py:297
  13.2 5.4 %collective-permute-done.1 = bf16[64,2048]{1,0:T(8,128)(2,1)S(1)} collective-permute-done((bf16[64,2048]{1,0:T(8,128)(2,1)}, bf16[64,2048]{1,0:T(8,128)(2,1)S(1)}, u32[]{:S(2)}, u32[]{:S(2)}) %collective-permute-start.1) | collective-permute-done | bytes 262176 | tf_op jit(solution)/shard_map/ppermute | solution.py:297
  18.5 1.0 pad_maximum_fusion.1.low_ref
  20.5 1.8 %collective-permute-done.4.high_ref = bf16[256,2048]{1,0:T(8,128)(2,1)S(1)} collective-permute-done((bf16[256,2048]{1,0:T(8,128)(2,1)S(1)}, bf16[256,2048]{1,0:T(8,128)(2,1)S(1)}, u32[]{:S(2)}, u32[]{:S(2)}) %collective-permute-start.4) | collective-permute-done | bytes 1048608 | tf_op jit(solution)/shard_map/ppermute | solution.py:299
  22.3 0.7 copy-done.4
  23.0 3.9 %forward.7.a_ref = s16[528,512]{1,0:T(8,128)(2,1)S(1)} custom-call(s32[7]{0:T(128)S(1)} %stack.35.place_ref, s32[16,16]{1,0:T(8,128)S(1)} %copy-done.4, bf16[256,2048]{1,0:T(8,128)(2,1)S(1)} %pad_maximum_fusion.1.low_ref, bf16[256,2048]{1,0:T(8,128)(2,1)S(1)} %collective-permute-done.4.high_ref, bf16[2048,2048]{1,0:T(8,128)(2,1)} %gate_ref.13, ...), custom_call_target="tpu_custom_call" | custom-call | flops 8000000000 | bytes 20000000 | tf_op jit(solution)/shard_map/forward/pallas_call | solution.py:98
  26.9 4.5 %collective-permute-start.8 = (s16[528,512]{1,0:T(8,128)(2,1)S(1)}, s16[528,512]{1,0:T(8,128)(2,1)S(1)}, u32[]{:S(2)}, u32[]{:S(2)}) collective-permute-start(s16[528,512]{1,0:T(8,128)(2,1)S(1)} %forward.7.a_ref), channel_id=1, source_target_pairs={{0,8},{24,16},{1,9},{25,17},{2,10},{26,18},{3,11},{27,19},{4,12},{... | collective-permute-start | bytes 1622024 | tf_op jit(solution)/shard_map/ppermute | solution.py:322
  31.4 3.9 %forward.8.a_ref = s16[528,512]{1,0:T(8,128)(2,1)S(1)} custom-call(s32[7]{0:T(128)S(1)} %stack.35.place_ref, s32[16,16]{1,0:T(8,128)S(1)} %copy-done.4, bf16[256,2048]{1,0:T(8,128)(2,1)S(1)} %pad_maximum_fusion.1.low_ref, bf16[256,2048]{1,0:T(8,128)(2,1)S(1)} %collective-permute-done.4.high_ref, bf16[2048,2048]{1,0:T(8,128)(2,1)} %gate_ref.13, ...), custom_call_target="tpu_custom_call" | custom-call | flops 8000000000 | bytes 20000000 | tf_op jit(solution)/shard_map/forward/pallas_call | solution.py:98
  35.3 1.3 collective-permute-start.7
  37.3 7.2 %collective-permute-start.9 = (s16[528,512]{1,0:T(8,128)(2,1)S(1)}, s16[528,512]{1,0:T(8,128)(2,1)S(1)}, u32[]{:S(2)}, u32[]{:S(2)}) collective-permute-start(s16[528,512]{1,0:T(8,128)(2,1)S(1)} %forward.8.a_ref), channel_id=1, source_target_pairs={{0,8},{24,16},{1,9},{25,17},{2,10},{26,18},{3,11},{27,19},{4,12},{... | collective-permute-start | bytes 1622024 | tf_op jit(solution)/shard_map/ppermute | solution.py:322
  44.5 6.1 %forward.9 = (s16[528,512]{1,0:T(8,128)(2,1)S(1)}, s16[528,512]{1,0:T(8,128)(2,1)S(1)}) custom-call(s32[7]{0:T(128)S(1)} %stack.35.place_ref, s32[16,16]{1,0:T(8,128)S(1)} %copy-done.4, bf16[256,2048]{1,0:T(8,128)(2,1)S(1)} %pad_maximum_fusion.1.low_ref, bf16[256,2048]{1,0:T(8,128)(2,1)S(1)} %collective-permute-done.4.high_ref, ...), custom_call_target="tpu_custom_call" | custom-call | flops 1000000 | bytes 2500 | tf_op jit(solution)/shard_map/forward/pallas_call | solution.py:98
  50.6 1.5 turn.1.turned_ref
  52.7 0.7 collective-permute-start.11
  53.4 1.3 collective-permute-start.10
  54.7 7.6 %collective-permute-start.12 = (s16[528,512]{1,0:T(8,128)(2,1)S(1)}, s16[528,512]{1,0:T(8,128)(2,1)S(1)}, u32[]{:S(2)}, u32[]{:S(2)}) collective-permute-start(s16[528,512]{1,0:T(8,128)(2,1)S(1)} %get-tuple-element.85.a_ref), channel_id=1, source_target_pairs={{0,8},{24,16},{1,9},{25,17},{2,10},{26,18},{3,11},{27,19},{4,12},{... | collective-permute-start | bytes 1622024 | tf_op jit(solution)/shard_map/ppermute | solution.py:322
  62.4 3.9 %forward.10.next_ref.a_ref = s16[528,512]{1,0:T(8,128)(2,1)S(1)} custom-call(s32[7]{0:T(128)S(1)} %stack.35.place_ref, s32[16,16]{1,0:T(8,128)S(1)} %copy-done.4, bf16[256,2048]{1,0:T(8,128)(2,1)S(1)} %pad_maximum_fusion.1.low_ref, bf16[256,2048]{1,0:T(8,128)(2,1)S(1)} %collective-permute-done.4.high_ref, bf16[2048,2048]{1,0:T(8,128)(2,1)} %gate_ref.13, ...), custom_call_target="tpu_custom_call" | custom-call | flops 1000000 | bytes 2500 | tf_op jit(solution)/shard_map/forward/pallas_call | solution.py:98
  66.8 0.7 collective-permute-start.13
  67.5 3.5 %collective-permute-done.10 = bf16[128,2048]{1,0:T(8,128)(2,1)S(1)} collective-permute-done((bf16[128,2048]{1,0:T(8,128)(2,1)S(1)}, bf16[128,2048]{1,0:T(8,128)(2,1)S(1)}, u32[]{:S(2)}, u32[]{:S(2)}) %collective-permute-start.10) | collective-permute-done | bytes 524320 | tf_op jit(solution)/shard_map/ppermute | solution.py:319
  71.6 1.0 collective-permute-start.14
  72.5 3.8 %forward.11.next_ref.a_ref = s16[528,512]{1,0:T(8,128)(2,1)S(1)} custom-call(s32[7]{0:T(128)S(1)} %stack.35.place_ref, s32[16,16]{1,0:T(8,128)S(1)} %copy-done.5, bf16[256,2048]{1,0:T(8,128)(2,1)S(1)} %pad_maximum_fusion.1.low_ref, bf16[256,2048]{1,0:T(8,128)(2,1)S(1)} %collective-permute-done.4.high_ref, bf16[2048,2048]{1,0:T(8,128)(2,1)} %gate_ref.13, ...), custom_call_target="tpu_custom_call" | custom-call | flops 1000000 | bytes 2500 | tf_op jit(solution)/shard_map/forward/pallas_call | solution.py:98
  78.3 6.4 %collective-permute-start.16 = (s16[528,512]{1,0:T(8,128)(2,1)S(1)}, s16[528,512]{1,0:T(8,128)(2,1)S(1)}, u32[]{:S(2)}, u32[]{:S(2)}) collective-permute-start(s16[528,512]{1,0:T(8,128)(2,1)S(1)} %reply.9), channel_id=1, source_target_pairs={{0,8},{8,0},{16,24},{24,16},{1,9},{9,1},{17,25},{25,17},{2,10},{10... | collective-permute-start | bytes 1622024 | tf_op jit(solution)/shard_map/ppermute | solution.py:328
  84.7 3.8 %forward.12.next_ref.a_ref = s16[528,512]{1,0:T(8,128)(2,1)S(1)} custom-call(s32[7]{0:T(128)S(1)} %stack.35.place_ref, s32[16,16]{1,0:T(8,128)S(1)} %copy-done.5, bf16[256,2048]{1,0:T(8,128)(2,1)S(1)} %pad_maximum_fusion.1.low_ref, bf16[256,2048]{1,0:T(8,128)(2,1)S(1)} %collective-permute-done.4.high_ref, bf16[2048,2048]{1,0:T(8,128)(2,1)} %gate_ref.13, ...), custom_call_target="tpu_custom_call" | custom-call | flops 1000000 | bytes 2500 | tf_op jit(solution)/shard_map/forward/pallas_call | solution.py:98
  89.2 0.9 collective-permute-start.17
  90.2 1.2 pad_maximum_fusion.back_ref
  91.4 4.6 %weight_grads.8 = (bf16[128,2048]{1,0:T(8,128)(2,1)}, f32[2048,2048]{1,0:T(8,128)}, f32[2048,2048]{1,0:T(8,128)}) custom-call(s32[7]{0:T(128)S(1)} %stack.35.place_ref, s32[16,16]{1,0:T(8,128)S(1)} %copy-done.5, bf16[2048,512]{1,0:T(8,128)(2,1)S(1)} %turn.1.turned_ref, bf16[512,2048]{1,0:T(8,128)(2,1)S(1)} %pad_maximum_fusion.back_ref, ...), custom_call_target="tpu_custom_call" | custom-call | flops 1000000 | bytes 2500 | tf_op jit(solution)/shard_map/weight_grads/pallas_call | solution.py:261
  96.0 1.4 reply.10
  97.4 0.8 copy-done
  98.2 4.1 %collective-permute-start.18 = (s16[528,512]{1,0:T(8,128)(2,1)}, s16[528,512]{1,0:T(8,128)(2,1)S(1)}, u32[]{:S(2)}, u32[]{:S(2)}) collective-permute-start(s16[528,512]{1,0:T(8,128)(2,1)} %reply.10), channel_id=1, source_target_pairs={{0,8},{8,0},{16,24},{24,16},{1,9},{9,1},{17,25},{25,17},{2,10},{10... | collective-permute-start | bytes 1622024 | tf_op jit(solution)/shard_map/ppermute | solution.py:328
  102.3 3.8 %forward.13.next_ref.a_ref = s16[528,512]{1,0:T(8,128)(2,1)S(1)} custom-call(s32[7]{0:T(128)S(1)} %stack.35.place_ref, s32[16,16]{1,0:T(8,128)S(1)} %copy-done.5, bf16[256,2048]{1,0:T(8,128)(2,1)S(1)} %pad_maximum_fusion.1.low_ref, bf16[256,2048]{1,0:T(8,128)(2,1)S(1)} %collective-permute-done.4.high_ref, bf16[2048,2048]{1,0:T(8,128)(2,1)} %gate_ref.13, ...), custom_call_target="tpu_custom_call" | custom-call | flops 1000000 | bytes 2500 | tf_op jit(solution)/shard_map/forward/pallas_call | solution.py:98
  107.5 4.6 %weight_grads.9 = (bf16[128,2048]{1,0:T(8,128)(2,1)}, f32[2048,2048]{1,0:T(8,128)}, f32[2048,2048]{1,0:T(8,128)}) custom-call(s32[7]{0:T(128)S(1)} %stack.35.place_ref, s32[16,16]{1,0:T(8,128)S(1)} %copy-done.5, bf16[2048,512]{1,0:T(8,128)(2,1)S(1)} %turn.1.turned_ref, ...), custom_call_target="tpu_custom_call", output_to_operand_aliasing={{0}: (7, {}), {1}: (8, {}), {2}: (9, {})} | custom-call | flops 1000000 | bytes 2500 | tf_op jit(solution)/shard_map/weight_grads/pallas_call | solution.py:261
  112.7 2.6 %collective-permute-start.20 = (s16[528,512]{1,0:T(8,128)(2,1)S(1)}, s16[528,512]{1,0:T(8,128)(2,1)S(1)}, u32[]{:S(2)}, u32[]{:S(2)}) collective-permute-start(s16[528,512]{1,0:T(8,128)(2,1)S(1)} %reply.11), channel_id=1, source_target_pairs={{0,8},{8,0},{16,24},{24,16},{1,9},{9,1},{17,25},{25,17},{2,10},{10... | collective-permute-start | bytes 1622024 | tf_op jit(solution)/shard_map/ppermute | solution.py:328
  116.6 4.6 %weight_grads.10 = (bf16[128,2048]{1,0:T(8,128)(2,1)}, f32[2048,2048]{1,0:T(8,128)}, f32[2048,2048]{1,0:T(8,128)}) custom-call(s32[7]{0:T(128)S(1)} %stack.35.place_ref, s32[16,16]{1,0:T(8,128)S(1)} %copy-done.5, bf16[2048,512]{1,0:T(8,128)(2,1)S(1)} %turn.1.turned_ref, ...), custom_call_target="tpu_custom_call", output_to_operand_aliasing={{0}: (7, {}), {1}: (8, {}), {2}: (9, {})} | custom-call | flops 1000000 | bytes 2500 | tf_op jit(solution)/shard_map/weight_grads/pallas_call | solution.py:261
  121.8 4.1 %collective-permute-start.22 = (s16[528,512]{1,0:T(8,128)(2,1)S(1)}, s16[528,512]{1,0:T(8,128)(2,1)S(1)}, u32[]{:S(2)}, u32[]{:S(2)}) collective-permute-start(s16[528,512]{1,0:T(8,128)(2,1)S(1)} %reply.12), channel_id=1, source_target_pairs={{0,8},{8,0},{16,24},{24,16},{1,9},{9,1},{17,25},{25,17},{2,10},{10... | collective-permute-start | bytes 1622024 | tf_op jit(solution)/shard_map/ppermute | solution.py:328
  127.2 4.6 %weight_grads.11 = (bf16[128,2048]{1,0:T(8,128)(2,1)}, f32[2048,2048]{1,0:T(8,128)}, f32[2048,2048]{1,0:T(8,128)}) custom-call(s32[7]{0:T(128)S(1)} %stack.35.place_ref, s32[16,16]{1,0:T(8,128)S(1)} %copy-done.5, bf16[2048,512]{1,0:T(8,128)(2,1)S(1)} %turn.1.turned_ref, ...), custom_call_target="tpu_custom_call", output_to_operand_aliasing={{0}: (7, {}), {1}: (8, {}), {2}: (9, {})} | custom-call | flops 1000000 | bytes 2500 | tf_op jit(solution)/shard_map/weight_grads/pallas_call | solution.py:261
  132.4 3.4 %collective-permute-done.22.b_ref.out_ref = s16[528,512]{1,0:T(8,128)(2,1)S(1)} collective-permute-done((s16[528,512]{1,0:T(8,128)(2,1)S(1)}, s16[528,512]{1,0:T(8,128)(2,1)S(1)}, u32[]{:S(2)}, u32[]{:S(2)}) %collective-permute-start.22) | collective-permute-done | bytes 540704 | tf_op jit(solution)/shard_map/ppermute | solution.py:328
  137.1 1.3 collective-permute-start.25
  139.0 1.5 collective-permute-start.26
  140.5 4.6 %weight_grads.12 = (bf16[128,2048]{1,0:T(8,128)(2,1)}, f32[2048,2048]{1,0:T(8,128)}, f32[2048,2048]{1,0:T(8,128)}) custom-call(s32[7]{0:T(128)S(1)} %stack.35.place_ref, s32[16,16]{1,0:T(8,128)S(1)} %copy-done.5, bf16[2048,512]{1,0:T(8,128)(2,1)S(1)} %turn.1.turned_ref, ...), custom_call_target="tpu_custom_call", output_to_operand_aliasing={{0}: (7, {}), {1}: (8, {}), {2}: (9, {})} | custom-call | flops 1000000 | bytes 2500 | tf_op jit(solution)/shard_map/weight_grads/pallas_call | solution.py:261
  145.7 1.3 collective-permute-start.27
  147.0 9.5 %collective-permute-done.25.out_ref = s16[528,512]{1,0:T(8,128)(2,1)S(1)} collective-permute-done((s16[528,512]{1,0:T(8,128)(2,1)S(1)}, s16[528,512]{1,0:T(8,128)(2,1)S(1)}, u32[]{:S(2)}, u32[]{:S(2)}) %collective-permute-start.25) | collective-permute-done | bytes 540704 | tf_op jit(solution)/shard_map/ppermute | solution.py:319
  156.5 4.6 %weight_grads.13 = (bf16[128,2048]{1,0:T(8,128)(2,1)}, f32[2048,2048]{1,0:T(8,128)}, f32[2048,2048]{1,0:T(8,128)}) custom-call(s32[7]{0:T(128)S(1)} %stack.35.place_ref, s32[16,16]{1,0:T(8,128)S(1)} %copy-done.5, bf16[2048,512]{1,0:T(8,128)(2,1)S(1)} %turn.1.turned_ref, ...), custom_call_target="tpu_custom_call", output_to_operand_aliasing={{0}: (7, {}), {1}: (8, {}), {2}: (9, {})} | custom-call | flops 1000000 | bytes 2500 | tf_op jit(solution)/shard_map/weight_grads/pallas_call | solution.py:261
  161.1 7.0 %collective-permute-done.26.out_ref = s16[528,512]{1,0:T(8,128)(2,1)S(1)} collective-permute-done((s16[528,512]{1,0:T(8,128)(2,1)S(1)}, s16[528,512]{1,0:T(8,128)(2,1)S(1)}, u32[]{:S(2)}, u32[]{:S(2)}) %collective-permute-start.26) | collective-permute-done | bytes 540704 | tf_op jit(solution)/shard_map/ppermute | solution.py:319
  168.1 4.6 %weight_grads.14 = (bf16[128,2048]{1,0:T(8,128)(2,1)}, f32[2048,2048]{1,0:T(8,128)}, f32[2048,2048]{1,0:T(8,128)}) custom-call(s32[7]{0:T(128)S(1)} %stack.35.place_ref, s32[16,16]{1,0:T(8,128)S(1)} %copy-done.5, bf16[2048,512]{1,0:T(8,128)(2,1)S(1)} %turn.1.turned_ref, ...), custom_call_target="tpu_custom_call", output_to_operand_aliasing={{0}: (7, {}), {1}: (8, {}), {2}: (9, {})} | custom-call | flops 1000000 | bytes 2500 | tf_op jit(solution)/shard_map/weight_grads/pallas_call | solution.py:261
  172.6 3.7 %collective-permute-done.27.out_ref = s16[528,512]{1,0:T(8,128)(2,1)S(1)} collective-permute-done((s16[528,512]{1,0:T(8,128)(2,1)S(1)}, s16[528,512]{1,0:T(8,128)(2,1)S(1)}, u32[]{:S(2)}, u32[]{:S(2)}) %collective-permute-start.27) | collective-permute-done | bytes 540704 | tf_op jit(solution)/shard_map/ppermute | solution.py:319
  176.3 4.6 %weight_grads.15 = (bf16[128,2048]{1,0:T(8,128)(2,1)}, f32[2048,2048]{1,0:T(8,128)}, f32[2048,2048]{1,0:T(8,128)}) custom-call(s32[7]{0:T(128)S(1)} %stack.35.place_ref, s32[16,16]{1,0:T(8,128)S(1)} %copy-done.5, bf16[2048,512]{1,0:T(8,128)(2,1)S(1)} %turn.1.turned_ref, ...), custom_call_target="tpu_custom_call", output_to_operand_aliasing={{0}: (7, {}), {1}: (8, {}), {2}: (9, {})} | custom-call | flops 1000000 | bytes 2500 | tf_op jit(solution)/shard_map/weight_grads/pallas_call | solution.py:261
  (64 shorter events, 14.5 us)
Async XLA Ops:
  0.6 19.0 %collective-permute-start.3 = (bf16[128,2048]{1,0:T(8,128)(2,1)}, bf16[128,2048]{1,0:T(8,128)(2,1)S(1)}, u32[]{:S(2)}, u32[]{:S(2)}) collective-permute-start(bf16[128,2048]{1,0:T(8,128)(2,1)} %param.9), channel_id=1, source_target_pairs={{0,8},{8,0},{16,24},{24,16},{1,9},{9,1},{17,25},{25,17},{2,10},{10... | collective-permute-start | bytes 1572872 | tf_op jit(solution)/shard_map/ppermute | solution.py:328
  3.7 9.4 %collective-permute-start = (bf16[64,2048]{1,0:T(8,128)(2,1)}, bf16[64,2048]{1,0:T(8,128)(2,1)S(1)}, u32[]{:S(2)}, u32[]{:S(2)}) collective-permute-start(bf16[64,2048]{1,0:T(8,128)(2,1)} %param.5), channel_id=1, source_target_pairs={{0,2},{1,3},{2,0},{3,1},{4,6},{5,7},{6,4},{7,5},{8,10},{9,11},{10,... | collective-permute-start | bytes 786440 | tf_op jit(solution)/shard_map/ppermute | solution.py:297
  5.2 13.3 %collective-permute-start.1 = (bf16[64,2048]{1,0:T(8,128)(2,1)}, bf16[64,2048]{1,0:T(8,128)(2,1)S(1)}, u32[]{:S(2)}, u32[]{:S(2)}) collective-permute-start(bf16[64,2048]{1,0:T(8,128)(2,1)} %param.5), channel_id=1, source_target_pairs={{0,4},{1,5},{2,6},{3,7},{4,0},{5,1},{6,2},{7,3},{8,12},{9,13},{10,... | collective-permute-start | bytes 786440 | tf_op jit(solution)/shard_map/ppermute | solution.py:297
  6.7 11.8 %collective-permute-start.2 = (bf16[64,2048]{1,0:T(8,128)(2,1)}, bf16[64,2048]{1,0:T(8,128)(2,1)S(1)}, u32[]{:S(2)}, u32[]{:S(2)}) collective-permute-start(bf16[64,2048]{1,0:T(8,128)(2,1)} %param.5), channel_id=1, source_target_pairs={{0,6},{1,7},{2,4},{3,5},{4,2},{5,3},{6,0},{7,1},{8,14},{9,15},{10,... | collective-permute-start | bytes 786440 | tf_op jit(solution)/shard_map/ppermute | solution.py:297
  19.6 17.0 %copy-start.9 = (bf16[128,2048]{1,0:T(8,128)(2,1)}, bf16[128,2048]{1,0:T(8,128)(2,1)S(1)}, u32[]{:S(2)}) copy-start(bf16[128,2048]{1,0:T(8,128)(2,1)S(1)} %collective-permute-done.3) | copy-start | bytes 1572868
  19.6 2.7 %collective-permute-start.4 = (bf16[256,2048]{1,0:T(8,128)(2,1)S(1)}, bf16[256,2048]{1,0:T(8,128)(2,1)S(1)}, u32[]{:S(2)}, u32[]{:S(2)}) collective-permute-start(bf16[256,2048]{1,0:T(8,128)(2,1)S(1)} %pad_maximum_fusion.1.low_ref), channel_id=1, source_target_pairs={{0,1},{1,0},{2,3},{3,2},{4,5},{5,4},{6,7},{7,6},{8,9},{9,8},{10,11... | collective-permute-start | bytes 3145736 | tf_op jit(solution)/shard_map/ppermute | solution.py:299
  19.7 15.6 %collective-permute-start.6 = (bf16[128,2048]{1,0:T(8,128)(2,1)}, bf16[128,2048]{1,0:T(8,128)(2,1)S(1)}, u32[]{:S(2)}, u32[]{:S(2)}) collective-permute-start(bf16[128,2048]{1,0:T(8,128)(2,1)} %param.9), channel_id=1, source_target_pairs={{8,16},{16,8},{9,17},{17,9},{10,18},{18,10},{11,19},{19,11},{12,20... | collective-permute-start | bytes 1572872 | tf_op jit(solution)/shard_map/ppermute | solution.py:325
  22.3 0.7 copy-start.4
  26.9 25.2 %collective-permute-start.8 = (s16[528,512]{1,0:T(8,128)(2,1)S(1)}, s16[528,512]{1,0:T(8,128)(2,1)S(1)}, u32[]{:S(2)}, u32[]{:S(2)}) collective-permute-start(s16[528,512]{1,0:T(8,128)(2,1)S(1)} %forward.7.a_ref), channel_id=1, source_target_pairs={{0,8},{24,16},{1,9},{25,17},{2,10},{26,18},{3,11},{27,19},{4,12},{... | collective-permute-start | bytes 1622024 | tf_op jit(solution)/shard_map/ppermute | solution.py:322
  35.3 15.3 %copy-start.6 = (bf16[128,2048]{1,0:T(8,128)(2,1)}, bf16[128,2048]{1,0:T(8,128)(2,1)S(1)}, u32[]{:S(2)}) copy-start(bf16[128,2048]{1,0:T(8,128)(2,1)S(1)} %collective-permute-done.6) | copy-start | bytes 1572868
  35.3 16.8 %collective-permute-start.7 = (bf16[128,2048]{1,0:T(8,128)(2,1)S(1)}, bf16[128,2048]{1,0:T(8,128)(2,1)S(1)}, u32[]{:S(2)}, u32[]{:S(2)}) collective-permute-start(bf16[128,2048]{1,0:T(8,128)(2,1)S(1)} %collective-permute-done.6), channel_id=1, source_target_pairs={{8,0},{16,24},{9,1},{17,25},{10,2},{18,26},{11,3},{19,27},{12,4},{... | collective-permute-start | bytes 1572872 | tf_op jit(solution)/shard_map/ppermute | solution.py:319
  36.6 15.5 %collective-permute-start.5 = (bf16[128,2048]{1,0:T(8,128)(2,1)S(1)}, bf16[128,2048]{1,0:T(8,128)(2,1)S(1)}, u32[]{:S(2)}, u32[]{:S(2)}) collective-permute-start(bf16[128,2048]{1,0:T(8,128)(2,1)S(1)} %collective-permute-done.3), channel_id=1, source_target_pairs={{8,16},{16,8},{9,17},{17,9},{10,18},{18,10},{11,19},{19,11},{12,20... | collective-permute-start | bytes 1572872 | tf_op jit(solution)/shard_map/ppermute | solution.py:325
  37.3 28.9 %collective-permute-start.9 = (s16[528,512]{1,0:T(8,128)(2,1)S(1)}, s16[528,512]{1,0:T(8,128)(2,1)S(1)}, u32[]{:S(2)}, u32[]{:S(2)}) collective-permute-start(s16[528,512]{1,0:T(8,128)(2,1)S(1)} %forward.8.a_ref), channel_id=1, source_target_pairs={{0,8},{24,16},{1,9},{25,17},{2,10},{26,18},{3,11},{27,19},{4,12},{... | collective-permute-start | bytes 1622024 | tf_op jit(solution)/shard_map/ppermute | solution.py:322
  52.7 19.8 %copy-start.5 = (s32[16,16]{1,0:T(8,128)S(1)}, s32[16,16]{1,0:T(8,128)}, u32[]{:S(2)}) copy-start(s32[16,16]{1,0:T(8,128)} %mask_ref.29) | copy-start | bytes 3076
  52.7 18.2 %collective-permute-start.11 = (s16[528,512]{1,0:T(8,128)(2,1)S(1)}, s16[528,512]{1,0:T(8,128)(2,1)S(1)}, u32[]{:S(2)}, u32[]{:S(2)}) collective-permute-start(s16[528,512]{1,0:T(8,128)(2,1)S(1)} %add.9.own_ref), channel_id=1, source_target_pairs={{8,16},{16,8},{9,17},{17,9},{10,18},{18,10},{11,19},{19,11},{12,20... | collective-permute-start | bytes 1622024 | tf_op jit(solution)/shard_map/ppermute | solution.py:325
  53.4 17.5 %collective-permute-start.10 = (bf16[128,2048]{1,0:T(8,128)(2,1)S(1)}, bf16[128,2048]{1,0:T(8,128)(2,1)S(1)}, u32[]{:S(2)}, u32[]{:S(2)}) collective-permute-start(bf16[128,2048]{1,0:T(8,128)(2,1)S(1)} %collective-permute-done.5), channel_id=1, source_target_pairs={{8,0},{16,24},{9,1},{17,25},{10,2},{18,26},{11,3},{19,27},{12,4},{... | collective-permute-start | bytes 1572872 | tf_op jit(solution)/shard_map/ppermute | solution.py:319
  54.7 21.7 %collective-permute-start.12 = (s16[528,512]{1,0:T(8,128)(2,1)S(1)}, s16[528,512]{1,0:T(8,128)(2,1)S(1)}, u32[]{:S(2)}, u32[]{:S(2)}) collective-permute-start(s16[528,512]{1,0:T(8,128)(2,1)S(1)} %get-tuple-element.85.a_ref), channel_id=1, source_target_pairs={{0,8},{24,16},{1,9},{25,17},{2,10},{26,18},{3,11},{27,19},{4,12},{... | collective-permute-start | bytes 1622024 | tf_op jit(solution)/shard_map/ppermute | solution.py:322
  66.8 10.9 %collective-permute-start.13 = (s16[528,512]{1,0:T(8,128)(2,1)S(1)}, s16[528,512]{1,0:T(8,128)(2,1)S(1)}, u32[]{:S(2)}, u32[]{:S(2)}) collective-permute-start(s16[528,512]{1,0:T(8,128)(2,1)S(1)} %add.10.own_ref), channel_id=1, source_target_pairs={{8,16},{16,8},{9,17},{17,9},{10,18},{18,10},{11,19},{19,11},{12,20... | collective-permute-start | bytes 1622024 | tf_op jit(solution)/shard_map/ppermute | solution.py:325
  71.6 17.0 %collective-permute-start.14 = (s16[528,512]{1,0:T(8,128)(2,1)S(1)}, s16[528,512]{1,0:T(8,128)(2,1)S(1)}, u32[]{:S(2)}, u32[]{:S(2)}) collective-permute-start(s16[528,512]{1,0:T(8,128)(2,1)S(1)} %reply.8), channel_id=1, source_target_pairs={{0,8},{8,0},{16,24},{24,16},{1,9},{9,1},{17,25},{25,17},{2,10},{10... | collective-permute-start | bytes 1622024 | tf_op jit(solution)/shard_map/ppermute | solution.py:328
  77.0 19.0 %collective-permute-start.15 = (s16[528,512]{1,0:T(8,128)(2,1)S(1)}, s16[528,512]{1,0:T(8,128)(2,1)S(1)}, u32[]{:S(2)}, u32[]{:S(2)}) collective-permute-start(s16[528,512]{1,0:T(8,128)(2,1)S(1)} %add.11.own_ref), channel_id=1, source_target_pairs={{8,16},{16,8},{9,17},{17,9},{10,18},{18,10},{11,19},{19,11},{12,20... | collective-permute-start | bytes 1622024 | tf_op jit(solution)/shard_map/ppermute | solution.py:325
  77.7 10.8 %copy-start.2 = (s16[528,512]{1,0:T(8,128)(2,1)}, s16[528,512]{1,0:T(8,128)(2,1)S(1)}, u32[]{:S(2)}) copy-start(s16[528,512]{1,0:T(8,128)(2,1)S(1)} %collective-permute-done.13.b_ref.across_ref) | copy-start | bytes 1622020
  78.3 11.7 %copy-start.7 = (bf16[128,2048]{1,0:T(8,128)(2,1)S(1)}, bf16[128,2048]{1,0:T(8,128)(2,1)}, u32[]{:S(2)}) copy-start(bf16[128,2048]{1,0:T(8,128)(2,1)} %copy-done.6) | copy-start | bytes 1572868
  78.3 27.9 %collective-permute-start.16 = (s16[528,512]{1,0:T(8,128)(2,1)S(1)}, s16[528,512]{1,0:T(8,128)(2,1)S(1)}, u32[]{:S(2)}, u32[]{:S(2)}) collective-permute-start(s16[528,512]{1,0:T(8,128)(2,1)S(1)} %reply.9), channel_id=1, source_target_pairs={{0,8},{8,0},{16,24},{24,16},{1,9},{9,1},{17,25},{25,17},{2,10},{10... | collective-permute-start | bytes 1622024 | tf_op jit(solution)/shard_map/ppermute | solution.py:328
  88.6 1.6 copy-start.8
  89.2 22.9 %collective-permute-start.17 = (s16[528,512]{1,0:T(8,128)(2,1)S(1)}, s16[528,512]{1,0:T(8,128)(2,1)S(1)}, u32[]{:S(2)}, u32[]{:S(2)}) collective-permute-start(s16[528,512]{1,0:T(8,128)(2,1)S(1)} %add.12.own_ref), channel_id=1, source_target_pairs={{8,16},{16,8},{9,17},{17,9},{10,18},{18,10},{11,19},{19,11},{12,20... | collective-permute-start | bytes 1622024 | tf_op jit(solution)/shard_map/ppermute | solution.py:325
  97.4 0.8 copy-start
  98.2 9.3 %copy-start.3 = (s16[528,512]{1,0:T(8,128)(2,1)S(1)}, s16[528,512]{1,0:T(8,128)(2,1)}, u32[]{:S(2)}) copy-start(s16[528,512]{1,0:T(8,128)(2,1)} %copy-done.2) | copy-start | bytes 1622020
  98.2 17.1 %collective-permute-start.18 = (s16[528,512]{1,0:T(8,128)(2,1)}, s16[528,512]{1,0:T(8,128)(2,1)S(1)}, u32[]{:S(2)}, u32[]{:S(2)}) collective-permute-start(s16[528,512]{1,0:T(8,128)(2,1)} %reply.10), channel_id=1, source_target_pairs={{0,8},{8,0},{16,24},{24,16},{1,9},{9,1},{17,25},{25,17},{2,10},{10... | collective-permute-start | bytes 1622024 | tf_op jit(solution)/shard_map/ppermute | solution.py:328
  106.8 14.4 %collective-permute-start.19 = (s16[528,512]{1,0:T(8,128)(2,1)S(1)}, s16[528,512]{1,0:T(8,128)(2,1)S(1)}, u32[]{:S(2)}, u32[]{:S(2)}) collective-permute-start(s16[528,512]{1,0:T(8,128)(2,1)S(1)} %add.13.own_ref), channel_id=1, source_target_pairs={{8,16},{16,8},{9,17},{17,9},{10,18},{18,10},{11,19},{19,11},{12,20... | collective-permute-start | bytes 1622024 | tf_op jit(solution)/shard_map/ppermute | solution.py:325
  107.5 9.1 %copy-start.1 = (s16[528,512]{1,0:T(8,128)(2,1)S(1)}, s16[528,512]{1,0:T(8,128)(2,1)}, u32[]{:S(2)}) copy-start(s16[528,512]{1,0:T(8,128)(2,1)} %copy-done) | copy-start | bytes 1622020
  112.7 13.2 %collective-permute-start.20 = (s16[528,512]{1,0:T(8,128)(2,1)S(1)}, s16[528,512]{1,0:T(8,128)(2,1)S(1)}, u32[]{:S(2)}, u32[]{:S(2)}) collective-permute-start(s16[528,512]{1,0:T(8,128)(2,1)S(1)} %reply.11), channel_id=1, source_target_pairs={{0,8},{8,0},{16,24},{24,16},{1,9},{9,1},{17,25},{25,17},{2,10},{10... | collective-permute-start | bytes 1622024 | tf_op jit(solution)/shard_map/ppermute | solution.py:328
  115.9 15.9 %collective-permute-start.21 = (s16[528,512]{1,0:T(8,128)(2,1)S(1)}, s16[528,512]{1,0:T(8,128)(2,1)S(1)}, u32[]{:S(2)}, u32[]{:S(2)}) collective-permute-start(s16[528,512]{1,0:T(8,128)(2,1)S(1)} %add.14.own_ref), channel_id=1, source_target_pairs={{8,16},{16,8},{9,17},{17,9},{10,18},{18,10},{11,19},{19,11},{12,20... | collective-permute-start | bytes 1622024 | tf_op jit(solution)/shard_map/ppermute | solution.py:325
  121.8 14.0 %collective-permute-start.22 = (s16[528,512]{1,0:T(8,128)(2,1)S(1)}, s16[528,512]{1,0:T(8,128)(2,1)S(1)}, u32[]{:S(2)}, u32[]{:S(2)}) collective-permute-start(s16[528,512]{1,0:T(8,128)(2,1)S(1)} %reply.12), channel_id=1, source_target_pairs={{0,8},{8,0},{16,24},{24,16},{1,9},{9,1},{17,25},{25,17},{2,10},{10... | collective-permute-start | bytes 1622024 | tf_op jit(solution)/shard_map/ppermute | solution.py:328
  126.5 11.9 %collective-permute-start.23 = (s16[528,512]{1,0:T(8,128)(2,1)S(1)}, s16[528,512]{1,0:T(8,128)(2,1)S(1)}, u32[]{:S(2)}, u32[]{:S(2)}) collective-permute-start(s16[528,512]{1,0:T(8,128)(2,1)S(1)} %add.15.own_ref), channel_id=1, source_target_pairs={{8,16},{16,8},{9,17},{17,9},{10,18},{18,10},{11,19},{19,11},{12,20... | collective-permute-start | bytes 1622024 | tf_op jit(solution)/shard_map/ppermute | solution.py:325
  136.4 8.7 %collective-permute-start.24 = (s16[528,512]{1,0:T(8,128)(2,1)S(1)}, s16[528,512]{1,0:T(8,128)(2,1)S(1)}, u32[]{:S(2)}, u32[]{:S(2)}) collective-permute-start(s16[528,512]{1,0:T(8,128)(2,1)S(1)} %add.16.own_ref), channel_id=1, source_target_pairs={{8,16},{16,8},{9,17},{17,9},{10,18},{18,10},{11,19},{19,11},{12,20... | collective-permute-start | bytes 1622024 | tf_op jit(solution)/shard_map/ppermute | solution.py:325
  137.1 19.4 %collective-permute-start.25 = (s16[528,512]{1,0:T(8,128)(2,1)S(1)}, s16[528,512]{1,0:T(8,128)(2,1)S(1)}, u32[]{:S(2)}, u32[]{:S(2)}) collective-permute-start(s16[528,512]{1,0:T(8,128)(2,1)S(1)} %reply.13), channel_id=1, source_target_pairs={{8,0},{16,24},{9,1},{17,25},{10,2},{18,26},{11,3},{19,27},{12,4},{... | collective-permute-start | bytes 1622024 | tf_op jit(solution)/shard_map/ppermute | solution.py:319
  139.0 29.1 %collective-permute-start.26 = (s16[528,512]{1,0:T(8,128)(2,1)S(1)}, s16[528,512]{1,0:T(8,128)(2,1)S(1)}, u32[]{:S(2)}, u32[]{:S(2)}) collective-permute-start(s16[528,512]{1,0:T(8,128)(2,1)S(1)} %reply.14), channel_id=1, source_target_pairs={{8,0},{16,24},{9,1},{17,25},{10,2},{18,26},{11,3},{19,27},{12,4},{... | collective-permute-start | bytes 1622024 | tf_op jit(solution)/shard_map/ppermute | solution.py:319
  145.7 30.6 %collective-permute-start.27 = (s16[528,512]{1,0:T(8,128)(2,1)S(1)}, s16[528,512]{1,0:T(8,128)(2,1)S(1)}, u32[]{:S(2)}, u32[]{:S(2)}) collective-permute-start(s16[528,512]{1,0:T(8,128)(2,1)S(1)} %reply.15), channel_id=1, source_target_pairs={{8,0},{16,24},{9,1},{17,25},{10,2},{18,26},{11,3},{19,27},{12,4},{... | collective-permute-start | bytes 1622024 | tf_op jit(solution)/shard_map/ppermute | solution.py:319

commit v11 on v10

--- a/solution.py
+++ b/solution.py
@@ -10,7 +10,7 @@
 BLOCK = 128
 GROUPS = 16
 CHUNK = 2
-AHEAD = 4
+AHEAD = 5
 LAG = 3
 EARLY, LATE, TURN = 8000, 1, 1
 ROWS = 512

time: 182 us -> 178 us (0.978)
  starting transfers between devices: 57.9 us -> 55.5 us
  waiting for transfers between devices: 40.3 us -> 38.1 us
    ppermute x3, starting transfers between devices: 19.2 us -> 17 us  [inward(): lax.ppermute(value, 'row', [(left - hop - 1, left - hop), (right + hop +...]
    pallas_call x7 -> x6, Pallas kernels: 29.2 us -> 27.6 us  [forward(): pl.pallas_call(functools.partial(forward_kernel, first=start // BLOCK, sp...]
  transfers between devices with their start and end apart: 28 -> 28, of which waited for: 8 -> 8; matrix products, arithmetic and copies ran while one was open for 1% -> 1% of each run, Pallas kernels for 40% -> 42%
where the time goes in v11:
time: 178 us; the launch traced here: 177 us
  Pallas kernels  78.2 us (44%)
  starting transfers between devices  55.5 us (31%)
  waiting for transfers between devices  38.1 us (21%)
  local copies, waits for them, and re-layouts  2.68 us (2%)
    pallas_call x8, Pallas kernels, weight_grads(): pl.pallas_call(functools.partial(weights_kernel, first=first, devices=dev...  37.6 us
    pallas_call x6, Pallas kernels, forward(): pl.pallas_call(functools.partial(forward_kernel, first=start // BLOCK, sp...  27.6 us
    ppermute x5, waiting for transfers between devices, outward(): lax.ppermute(value, 'row', [(left - hop, left - hop - 1), (right + hop, r...  21.9 us
    ppermute x6, starting transfers between devices, exchange(): return lax.ppermute(value, 'row', [(i, i ^ 1) for i in range(ring)])  20.6 us
    ppermute x3, starting transfers between devices, inward(): lax.ppermute(value, 'row', [(left - hop - 1, left - hop), (right + hop +...  17 us
    ppermute x3, waiting for transfers between devices, gather_tokens(): lax.ppermute(tokens, 'col', [(i, i ^ other) for i in range(devices)])  11.3 us
    ppermute x10, starting transfers between devices, swap(): return lax.ppermute(value, 'row', [(left, right), (right, left)])  7.9 us
    pallas_call x8, Pallas kernels, reply(): pl.pallas_call(reply_kernel, grid_spec=pltpu.PrefetchScalarGridSpec(num_s...  6.76 us
  transfers between devices with their start and end apart: 28, of which 8 were waited for; matrix products, arithmetic and copies ran while one was open for 1% of the time, Pallas kernels for 42%

profile of v11, /device:TPU:0, one launch (start us, length us, event | category | flops | bytes accessed | tf_op | source)
XLA Modules:
  0.0 176.9 jit_solution(13716721807829956359)
XLA Ops:
  0.6 3.1 %collective-permute-start.3 = (bf16[128,2048]{1,0:T(8,128)(2,1)}, bf16[128,2048]{1,0:T(8,128)(2,1)S(1)}, u32[]{:S(2)}, u32[]{:S(2)}) collective-permute-start(bf16[128,2048]{1,0:T(8,128)(2,1)} %param.9), channel_id=1, source_target_pairs={{0,8},{8,0},{16,24},{24,16},{1,9},{9,1},{17,25},{25,17},{2,10},{10... | collective-permute-start | bytes 1572872 | tf_op jit(solution)/shard_map/ppermute | solution.py:328
  3.7 1.5 collective-permute-start
  5.2 1.5 collective-permute-start.1
  7.2 6.0 %collective-permute-done = bf16[64,2048]{1,0:T(8,128)(2,1)S(1)} collective-permute-done((bf16[64,2048]{1,0:T(8,128)(2,1)}, bf16[64,2048]{1,0:T(8,128)(2,1)S(1)}, u32[]{:S(2)}, u32[]{:S(2)}) %collective-permute-start) | collective-permute-done | bytes 262176 | tf_op jit(solution)/shard_map/ppermute | solution.py:297
  13.2 5.4 %collective-permute-done.1 = bf16[64,2048]{1,0:T(8,128)(2,1)S(1)} collective-permute-done((bf16[64,2048]{1,0:T(8,128)(2,1)}, bf16[64,2048]{1,0:T(8,128)(2,1)S(1)}, u32[]{:S(2)}, u32[]{:S(2)}) %collective-permute-start.1) | collective-permute-done | bytes 262176 | tf_op jit(solution)/shard_map/ppermute | solution.py:297
  18.5 1.0 pad_maximum_fusion.1.low_ref
  20.5 1.8 %collective-permute-done.4.high_ref = bf16[256,2048]{1,0:T(8,128)(2,1)S(1)} collective-permute-done((bf16[256,2048]{1,0:T(8,128)(2,1)S(1)}, bf16[256,2048]{1,0:T(8,128)(2,1)S(1)}, u32[]{:S(2)}, u32[]{:S(2)}) %collective-permute-start.4) | collective-permute-done | bytes 1048608 | tf_op jit(solution)/shard_map/ppermute | solution.py:299
  23.0 3.9 %forward.6.a_ref = s16[528,512]{1,0:T(8,128)(2,1)S(1)} custom-call(s32[7]{0:T(128)S(1)} %stack.35.place_ref, s32[16,16]{1,0:T(8,128)S(1)} %copy-done.4, bf16[256,2048]{1,0:T(8,128)(2,1)S(1)} %pad_maximum_fusion.1.low_ref, bf16[256,2048]{1,0:T(8,128)(2,1)S(1)} %collective-permute-done.4.high_ref, bf16[2048,2048]{1,0:T(8,128)(2,1)} %gate_ref.11, ...), custom_call_target="tpu_custom_call" | custom-call | flops 8000000000 | bytes 20000000 | tf_op jit(solution)/shard_map/forward/pallas_call | solution.py:98
  26.9 4.5 %collective-permute-start.8 = (s16[528,512]{1,0:T(8,128)(2,1)S(1)}, s16[528,512]{1,0:T(8,128)(2,1)S(1)}, u32[]{:S(2)}, u32[]{:S(2)}) collective-permute-start(s16[528,512]{1,0:T(8,128)(2,1)S(1)} %forward.6.a_ref), channel_id=1, source_target_pairs={{0,8},{24,16},{1,9},{25,17},{2,10},{26,18},{3,11},{27,19},{4,12},{... | collective-permute-start | bytes 1622024 | tf_op jit(solution)/shard_map/ppermute | solution.py:322
  31.4 3.9 %forward.7.a_ref = s16[528,512]{1,0:T(8,128)(2,1)S(1)} custom-call(s32[7]{0:T(128)S(1)} %stack.35.place_ref, s32[16,16]{1,0:T(8,128)S(1)} %copy-done.4, bf16[256,2048]{1,0:T(8,128)(2,1)S(1)} %pad_maximum_fusion.1.low_ref, bf16[256,2048]{1,0:T(8,128)(2,1)S(1)} %collective-permute-done.4.high_ref, bf16[2048,2048]{1,0:T(8,128)(2,1)} %gate_ref.11, ...), custom_call_target="tpu_custom_call" | custom-call | flops 8000000000 | bytes 20000000 | tf_op jit(solution)/shard_map/forward/pallas_call | solution.py:98
  35.3 1.3 collective-permute-start.7
  37.3 7.2 %collective-permute-start.9 = (s16[528,512]{1,0:T(8,128)(2,1)S(1)}, s16[528,512]{1,0:T(8,128)(2,1)S(1)}, u32[]{:S(2)}, u32[]{:S(2)}) collective-permute-start(s16[528,512]{1,0:T(8,128)(2,1)S(1)} %forward.7.a_ref), channel_id=1, source_target_pairs={{0,8},{24,16},{1,9},{25,17},{2,10},{26,18},{3,11},{27,19},{4,12},{... | collective-permute-start | bytes 1622024 | tf_op jit(solution)/shard_map/ppermute | solution.py:322
  44.4 8.4 %forward.8 = (s16[528,512]{1,0:T(8,128)(2,1)S(1)}, s16[528,512]{1,0:T(8,128)(2,1)S(1)}, s16[528,512]{1,0:T(8,128)(2,1)S(1)}) custom-call(s32[7]{0:T(128)S(1)} %stack.35.place_ref, s32[16,16]{1,0:T(8,128)S(1)} %copy-done.4, bf16[256,2048]{1,0:T(8,128)(2,1)S(1)} %pad_maximum_fusion.1.low_ref, bf16[256,2048]{1,0:T(8,128)(2,1)S(1)} %collective-permute-done.4.high_ref, ...), custom_call_target="tpu_custom_call" | custom-call | flops 1000000 | bytes 2500 | tf_op jit(solution)/shard_map/forward/pallas_call | solution.py:98
  52.8 1.5 turn.1.turned_ref
  55.7 1.3 collective-permute-start.10
  57.0 5.3 %collective-permute-start.12 = (s16[528,512]{1,0:T(8,128)(2,1)S(1)}, s16[528,512]{1,0:T(8,128)(2,1)S(1)}, u32[]{:S(2)}, u32[]{:S(2)}) collective-permute-start(s16[528,512]{1,0:T(8,128)(2,1)S(1)} %get-tuple-element.85.a_ref), channel_id=1, source_target_pairs={{0,8},{24,16},{1,9},{25,17},{2,10},{26,18},{3,11},{27,19},{4,12},{... | collective-permute-start | bytes 1622024 | tf_op jit(solution)/shard_map/ppermute | solution.py:322
  62.3 3.9 %forward.9.next_ref.a_ref = s16[528,512]{1,0:T(8,128)(2,1)S(1)} custom-call(s32[7]{0:T(128)S(1)} %stack.35.place_ref, s32[16,16]{1,0:T(8,128)S(1)} %copy-done.4, bf16[256,2048]{1,0:T(8,128)(2,1)S(1)} %pad_maximum_fusion.1.low_ref, bf16[256,2048]{1,0:T(8,128)(2,1)S(1)} %collective-permute-done.4.high_ref, bf16[2048,2048]{1,0:T(8,128)(2,1)} %gate_ref.11, ...), custom_call_target="tpu_custom_call" | custom-call | flops 1000000 | bytes 2500 | tf_op jit(solution)/shard_map/forward/pallas_call | solution.py:98
  66.8 0.7 collective-permute-start.13
  67.5 3.5 %collective-permute-done.10 = bf16[128,2048]{1,0:T(8,128)(2,1)S(1)} collective-permute-done((bf16[128,2048]{1,0:T(8,128)(2,1)S(1)}, bf16[128,2048]{1,0:T(8,128)(2,1)S(1)}, u32[]{:S(2)}, u32[]{:S(2)}) %collective-permute-start.10) | collective-permute-done | bytes 524320 | tf_op jit(solution)/shard_map/ppermute | solution.py:319
  71.5 1.0 collective-permute-start.14
  72.5 3.8 %forward.10.next_ref.a_ref = s16[528,512]{1,0:T(8,128)(2,1)S(1)} custom-call(s32[7]{0:T(128)S(1)} %stack.35.place_ref, s32[16,16]{1,0:T(8,128)S(1)} %copy-done.5, bf16[256,2048]{1,0:T(8,128)(2,1)S(1)} %pad_maximum_fusion.1.low_ref, bf16[256,2048]{1,0:T(8,128)(2,1)S(1)} %collective-permute-done.4.high_ref, bf16[2048,2048]{1,0:T(8,128)(2,1)} %gate_ref.11, ...), custom_call_target="tpu_custom_call" | custom-call | flops 1000000 | bytes 2500 | tf_op jit(solution)/shard_map/forward/pallas_call | solution.py:98
  77.0 1.5 collective-permute-start.15
  78.5 1.4 reply.9
  79.9 5.5 %collective-permute-start.16 = (s16[528,512]{1,0:T(8,128)(2,1)}, s16[528,512]{1,0:T(8,128)(2,1)S(1)}, u32[]{:S(2)}, u32[]{:S(2)}) collective-permute-start(s16[528,512]{1,0:T(8,128)(2,1)} %reply.9), channel_id=1, source_target_pairs={{0,8},{8,0},{16,24},{24,16},{1,9},{9,1},{17,25},{25,17},{2,10},{10... | collective-permute-start | bytes 1622024 | tf_op jit(solution)/shard_map/ppermute | solution.py:328
  85.4 3.8 %forward.11.next_ref.a_ref = s16[528,512]{1,0:T(8,128)(2,1)S(1)} custom-call(s32[7]{0:T(128)S(1)} %stack.35.place_ref, s32[16,16]{1,0:T(8,128)S(1)} %copy-done.5, bf16[256,2048]{1,0:T(8,128)(2,1)S(1)} %pad_maximum_fusion.1.low_ref, bf16[256,2048]{1,0:T(8,128)(2,1)S(1)} %collective-permute-done.4.high_ref, bf16[2048,2048]{1,0:T(8,128)(2,1)} %gate_ref.11, ...), custom_call_target="tpu_custom_call" | custom-call | flops 1000000 | bytes 2500 | tf_op jit(solution)/shard_map/forward/pallas_call | solution.py:98
  89.9 0.9 collective-permute-start.17
  91.1 4.6 %weight_grads.8 = (bf16[128,2048]{1,0:T(8,128)(2,1)}, f32[2048,2048]{1,0:T(8,128)}, f32[2048,2048]{1,0:T(8,128)}) custom-call(s32[7]{0:T(128)S(1)} %stack.35.place_ref, s32[16,16]{1,0:T(8,128)S(1)} %copy-done.5, bf16[2048,512]{1,0:T(8,128)(2,1)S(1)} %turn.1.turned_ref, bf16[512,2048]{1,0:T(8,128)(2,1)S(1)} %pad_maximum_fusion.back_ref, ...), custom_call_target="tpu_custom_call" | custom-call | flops 1000000 | bytes 2500 | tf_op jit(solution)/shard_map/weight_grads/pallas_call | solution.py:261
  95.7 1.6 reply.10
  97.3 4.2 %collective-permute-start.18 = (s16[528,512]{1,0:T(8,128)(2,1)S(1)}, s16[528,512]{1,0:T(8,128)(2,1)S(1)}, u32[]{:S(2)}, u32[]{:S(2)}) collective-permute-start(s16[528,512]{1,0:T(8,128)(2,1)S(1)} %reply.10), channel_id=1, source_target_pairs={{0,8},{8,0},{16,24},{24,16},{1,9},{9,1},{17,25},{25,17},{2,10},{10... | collective-permute-start | bytes 1622024 | tf_op jit(solution)/shard_map/ppermute | solution.py:328
  102.1 0.8 copy-done
  103.6 1.0 copy-done.1
  104.7 4.6 %weight_grads.9 = (bf16[128,2048]{1,0:T(8,128)(2,1)}, f32[2048,2048]{1,0:T(8,128)}, f32[2048,2048]{1,0:T(8,128)}) custom-call(s32[7]{0:T(128)S(1)} %stack.35.place_ref, s32[16,16]{1,0:T(8,128)S(1)} %copy-done.5, bf16[2048,512]{1,0:T(8,128)(2,1)S(1)} %turn.1.turned_ref, ...), custom_call_target="tpu_custom_call", output_to_operand_aliasing={{0}: (7, {}), {1}: (8, {}), {2}: (9, {})} | custom-call | flops 1000000 | bytes 2500 | tf_op jit(solution)/shard_map/weight_grads/pallas_call | solution.py:261
  109.8 2.6 %collective-permute-start.20 = (s16[528,512]{1,0:T(8,128)(2,1)S(1)}, s16[528,512]{1,0:T(8,128)(2,1)S(1)}, u32[]{:S(2)}, u32[]{:S(2)}) collective-permute-start(s16[528,512]{1,0:T(8,128)(2,1)S(1)} %reply.11), channel_id=1, source_target_pairs={{0,8},{8,0},{16,24},{24,16},{1,9},{9,1},{17,25},{25,17},{2,10},{10... | collective-permute-start | bytes 1622024 | tf_op jit(solution)/shard_map/ppermute | solution.py:328
  113.7 5.6 %weight_grads.10 = (bf16[128,2048]{1,0:T(8,128)(2,1)}, f32[2048,2048]{1,0:T(8,128)}, f32[2048,2048]{1,0:T(8,128)}) custom-call(s32[7]{0:T(128)S(1)} %stack.35.place_ref, s32[16,16]{1,0:T(8,128)S(1)} %copy-done.5, bf16[2048,512]{1,0:T(8,128)(2,1)S(1)} %turn.1.turned_ref, ...), custom_call_target="tpu_custom_call", output_to_operand_aliasing={{0}: (7, {}), {1}: (8, {}), {2}: (9, {})} | custom-call | flops 1000000 | bytes 2500 | tf_op jit(solution)/shard_map/weight_grads/pallas_call | solution.py:261
  119.9 4.2 %collective-permute-start.22 = (s16[528,512]{1,0:T(8,128)(2,1)S(1)}, s16[528,512]{1,0:T(8,128)(2,1)S(1)}, u32[]{:S(2)}, u32[]{:S(2)}) collective-permute-start(s16[528,512]{1,0:T(8,128)(2,1)S(1)} %reply.12), channel_id=1, source_target_pairs={{0,8},{8,0},{16,24},{24,16},{1,9},{9,1},{17,25},{25,17},{2,10},{10... | collective-permute-start | bytes 1622024 | tf_op jit(solution)/shard_map/ppermute | solution.py:328
  125.4 4.6 %weight_grads.11 = (bf16[128,2048]{1,0:T(8,128)(2,1)}, f32[2048,2048]{1,0:T(8,128)}, f32[2048,2048]{1,0:T(8,128)}) custom-call(s32[7]{0:T(128)S(1)} %stack.35.place_ref, s32[16,16]{1,0:T(8,128)S(1)} %copy-done.5, bf16[2048,512]{1,0:T(8,128)(2,1)S(1)} %turn.1.turned_ref, ...), custom_call_target="tpu_custom_call", output_to_operand_aliasing={{0}: (7, {}), {1}: (8, {}), {2}: (9, {})} | custom-call | flops 1000000 | bytes 2500 | tf_op jit(solution)/shard_map/weight_grads/pallas_call | solution.py:261
  130.6 2.9 %collective-permute-done.22.b_ref.out_ref = s16[528,512]{1,0:T(8,128)(2,1)S(1)} collective-permute-done((s16[528,512]{1,0:T(8,128)(2,1)S(1)}, s16[528,512]{1,0:T(8,128)(2,1)S(1)}, u32[]{:S(2)}, u32[]{:S(2)}) %collective-permute-start.22) | collective-permute-done | bytes 540704 | tf_op jit(solution)/shard_map/ppermute | solution.py:328
  134.8 1.3 collective-permute-start.25
  136.7 1.3 collective-permute-start.26
  138.0 4.6 %weight_grads.12 = (bf16[128,2048]{1,0:T(8,128)(2,1)}, f32[2048,2048]{1,0:T(8,128)}, f32[2048,2048]{1,0:T(8,128)}) custom-call(s32[7]{0:T(128)S(1)} %stack.35.place_ref, s32[16,16]{1,0:T(8,128)S(1)} %copy-done.5, bf16[2048,512]{1,0:T(8,128)(2,1)S(1)} %turn.1.turned_ref, ...), custom_call_target="tpu_custom_call", output_to_operand_aliasing={{0}: (7, {}), {1}: (8, {}), {2}: (9, {})} | custom-call | flops 1000000 | bytes 2500 | tf_op jit(solution)/shard_map/weight_grads/pallas_call | solution.py:261
  142.6 0.8 reply.15
  143.4 1.3 collective-permute-start.27
  144.7 8.9 %collective-permute-done.25.out_ref = s16[528,512]{1,0:T(8,128)(2,1)S(1)} collective-permute-done((s16[528,512]{1,0:T(8,128)(2,1)S(1)}, s16[528,512]{1,0:T(8,128)(2,1)S(1)}, u32[]{:S(2)}, u32[]{:S(2)}) %collective-permute-start.25) | collective-permute-done | bytes 540704 | tf_op jit(solution)/shard_map/ppermute | solution.py:319
  153.6 4.6 %weight_grads.13 = (bf16[128,2048]{1,0:T(8,128)(2,1)}, f32[2048,2048]{1,0:T(8,128)}, f32[2048,2048]{1,0:T(8,128)}) custom-call(s32[7]{0:T(128)S(1)} %stack.35.place_ref, s32[16,16]{1,0:T(8,128)S(1)} %copy-done.5, bf16[2048,512]{1,0:T(8,128)(2,1)S(1)} %turn.1.turned_ref, ...), custom_call_target="tpu_custom_call", output_to_operand_aliasing={{0}: (7, {}), {1}: (8, {}), {2}: (9, {})} | custom-call | flops 1000000 | bytes 2500 | tf_op jit(solution)/shard_map/weight_grads/pallas_call | solution.py:261
  158.2 7.0 %collective-permute-done.26.out_ref = s16[528,512]{1,0:T(8,128)(2,1)S(1)} collective-permute-done((s16[528,512]{1,0:T(8,128)(2,1)S(1)}, s16[528,512]{1,0:T(8,128)(2,1)S(1)}, u32[]{:S(2)}, u32[]{:S(2)}) %collective-permute-start.26) | collective-permute-done | bytes 540704 | tf_op jit(solution)/shard_map/ppermute | solution.py:319
  165.2 4.6 %weight_grads.14 = (bf16[128,2048]{1,0:T(8,128)(2,1)}, f32[2048,2048]{1,0:T(8,128)}, f32[2048,2048]{1,0:T(8,128)}) custom-call(s32[7]{0:T(128)S(1)} %stack.35.place_ref, s32[16,16]{1,0:T(8,128)S(1)} %copy-done.5, bf16[2048,512]{1,0:T(8,128)(2,1)S(1)} %turn.1.turned_ref, ...), custom_call_target="tpu_custom_call", output_to_operand_aliasing={{0}: (7, {}), {1}: (8, {}), {2}: (9, {})} | custom-call | flops 1000000 | bytes 2500 | tf_op jit(solution)/shard_map/weight_grads/pallas_call | solution.py:261
  169.8 2.5 %collective-permute-done.27.out_ref = s16[528,512]{1,0:T(8,128)(2,1)S(1)} collective-permute-done((s16[528,512]{1,0:T(8,128)(2,1)S(1)}, s16[528,512]{1,0:T(8,128)(2,1)S(1)}, u32[]{:S(2)}, u32[]{:S(2)}) %collective-permute-start.27) | collective-permute-done | bytes 540704 | tf_op jit(solution)/shard_map/ppermute | solution.py:319
  172.3 4.6 %weight_grads.15 = (bf16[128,2048]{1,0:T(8,128)(2,1)}, f32[2048,2048]{1,0:T(8,128)}, f32[2048,2048]{1,0:T(8,128)}) custom-call(s32[7]{0:T(128)S(1)} %stack.35.place_ref, s32[16,16]{1,0:T(8,128)S(1)} %copy-done.5, bf16[2048,512]{1,0:T(8,128)(2,1)S(1)} %turn.1.turned_ref, ...), custom_call_target="tpu_custom_call", output_to_operand_aliasing={{0}: (7, {}), {1}: (8, {}), {2}: (9, {})} | custom-call | flops 1000000 | bytes 2500 | tf_op jit(solution)/shard_map/weight_grads/pallas_call | solution.py:261
  (61 shorter events, 14.1 us)
Async XLA Ops:
  0.6 19.0 %collective-permute-start.3 = (bf16[128,2048]{1,0:T(8,128)(2,1)}, bf16[128,2048]{1,0:T(8,128)(2,1)S(1)}, u32[]{:S(2)}, u32[]{:S(2)}) collective-permute-start(bf16[128,2048]{1,0:T(8,128)(2,1)} %param.9), channel_id=1, source_target_pairs={{0,8},{8,0},{16,24},{24,16},{1,9},{9,1},{17,25},{25,17},{2,10},{10... | collective-permute-start | bytes 1572872 | tf_op jit(solution)/shard_map/ppermute | solution.py:328
  3.7 9.4 %collective-permute-start = (bf16[64,2048]{1,0:T(8,128)(2,1)}, bf16[64,2048]{1,0:T(8,128)(2,1)S(1)}, u32[]{:S(2)}, u32[]{:S(2)}) collective-permute-start(bf16[64,2048]{1,0:T(8,128)(2,1)} %param.5), channel_id=1, source_target_pairs={{0,2},{1,3},{2,0},{3,1},{4,6},{5,7},{6,4},{7,5},{8,10},{9,11},{10,... | collective-permute-start | bytes 786440 | tf_op jit(solution)/shard_map/ppermute | solution.py:297
  5.2 13.3 %collective-permute-start.1 = (bf16[64,2048]{1,0:T(8,128)(2,1)}, bf16[64,2048]{1,0:T(8,128)(2,1)S(1)}, u32[]{:S(2)}, u32[]{:S(2)}) collective-permute-start(bf16[64,2048]{1,0:T(8,128)(2,1)} %param.5), channel_id=1, source_target_pairs={{0,4},{1,5},{2,6},{3,7},{4,0},{5,1},{6,2},{7,3},{8,12},{9,13},{10,... | collective-permute-start | bytes 786440 | tf_op jit(solution)/shard_map/ppermute | solution.py:297
  6.7 11.8 %collective-permute-start.2 = (bf16[64,2048]{1,0:T(8,128)(2,1)}, bf16[64,2048]{1,0:T(8,128)(2,1)S(1)}, u32[]{:S(2)}, u32[]{:S(2)}) collective-permute-start(bf16[64,2048]{1,0:T(8,128)(2,1)} %param.5), channel_id=1, source_target_pairs={{0,6},{1,7},{2,4},{3,5},{4,2},{5,3},{6,0},{7,1},{8,14},{9,15},{10,... | collective-permute-start | bytes 786440 | tf_op jit(solution)/shard_map/ppermute | solution.py:297
  19.6 2.7 %collective-permute-start.4 = (bf16[256,2048]{1,0:T(8,128)(2,1)S(1)}, bf16[256,2048]{1,0:T(8,128)(2,1)S(1)}, u32[]{:S(2)}, u32[]{:S(2)}) collective-permute-start(bf16[256,2048]{1,0:T(8,128)(2,1)S(1)} %pad_maximum_fusion.1.low_ref), channel_id=1, source_target_pairs={{0,1},{1,0},{2,3},{3,2},{4,5},{5,4},{6,7},{7,6},{8,9},{9,8},{10,11... | collective-permute-start | bytes 3145736 | tf_op jit(solution)/shard_map/ppermute | solution.py:299
  19.7 15.6 %collective-permute-start.6 = (bf16[128,2048]{1,0:T(8,128)(2,1)}, bf16[128,2048]{1,0:T(8,128)(2,1)S(1)}, u32[]{:S(2)}, u32[]{:S(2)}) collective-permute-start(bf16[128,2048]{1,0:T(8,128)(2,1)} %param.9), channel_id=1, source_target_pairs={{8,16},{16,8},{9,17},{17,9},{10,18},{18,10},{11,19},{19,11},{12,20... | collective-permute-start | bytes 1572872 | tf_op jit(solution)/shard_map/ppermute | solution.py:325
  22.3 0.7 copy-start.4
  26.9 27.5 %collective-permute-start.8 = (s16[528,512]{1,0:T(8,128)(2,1)S(1)}, s16[528,512]{1,0:T(8,128)(2,1)S(1)}, u32[]{:S(2)}, u32[]{:S(2)}) collective-permute-start(s16[528,512]{1,0:T(8,128)(2,1)S(1)} %forward.6.a_ref), channel_id=1, source_target_pairs={{0,8},{24,16},{1,9},{25,17},{2,10},{26,18},{3,11},{27,19},{4,12},{... | collective-permute-start | bytes 1622024 | tf_op jit(solution)/shard_map/ppermute | solution.py:322
  35.2 17.6 %copy-start.6 = (bf16[128,2048]{1,0:T(8,128)(2,1)}, bf16[128,2048]{1,0:T(8,128)(2,1)S(1)}, u32[]{:S(2)}) copy-start(bf16[128,2048]{1,0:T(8,128)(2,1)S(1)} %collective-permute-done.6) | copy-start | bytes 1572868
  35.3 19.1 %collective-permute-start.7 = (bf16[128,2048]{1,0:T(8,128)(2,1)S(1)}, bf16[128,2048]{1,0:T(8,128)(2,1)S(1)}, u32[]{:S(2)}, u32[]{:S(2)}) collective-permute-start(bf16[128,2048]{1,0:T(8,128)(2,1)S(1)} %collective-permute-done.6), channel_id=1, source_target_pairs={{8,0},{16,24},{9,1},{17,25},{10,2},{18,26},{11,3},{19,27},{12,4},{... | collective-permute-start | bytes 1572872 | tf_op jit(solution)/shard_map/ppermute | solution.py:319
  36.6 17.8 %collective-permute-start.5 = (bf16[128,2048]{1,0:T(8,128)(2,1)S(1)}, bf16[128,2048]{1,0:T(8,128)(2,1)S(1)}, u32[]{:S(2)}, u32[]{:S(2)}) collective-permute-start(bf16[128,2048]{1,0:T(8,128)(2,1)S(1)} %collective-permute-done.3), channel_id=1, source_target_pairs={{8,16},{16,8},{9,17},{17,9},{10,18},{18,10},{11,19},{19,11},{12,20... | collective-permute-start | bytes 1572872 | tf_op jit(solution)/shard_map/ppermute | solution.py:325
  37.3 28.9 %collective-permute-start.9 = (s16[528,512]{1,0:T(8,128)(2,1)S(1)}, s16[528,512]{1,0:T(8,128)(2,1)S(1)}, u32[]{:S(2)}, u32[]{:S(2)}) collective-permute-start(s16[528,512]{1,0:T(8,128)(2,1)S(1)} %forward.7.a_ref), channel_id=1, source_target_pairs={{0,8},{24,16},{1,9},{25,17},{2,10},{26,18},{3,11},{27,19},{4,12},{... | collective-permute-start | bytes 1622024 | tf_op jit(solution)/shard_map/ppermute | solution.py:322
  55.0 17.5 %copy-start.5 = (s32[16,16]{1,0:T(8,128)S(1)}, s32[16,16]{1,0:T(8,128)}, u32[]{:S(2)}) copy-start(s32[16,16]{1,0:T(8,128)} %mask_ref.27) | copy-start | bytes 3076
  55.0 16.0 %collective-permute-start.11 = (s16[528,512]{1,0:T(8,128)(2,1)S(1)}, s16[528,512]{1,0:T(8,128)(2,1)S(1)}, u32[]{:S(2)}, u32[]{:S(2)}) collective-permute-start(s16[528,512]{1,0:T(8,128)(2,1)S(1)} %add.9.own_ref), channel_id=1, source_target_pairs={{8,16},{16,8},{9,17},{17,9},{10,18},{18,10},{11,19},{19,11},{12,20... | collective-permute-start | bytes 1622024 | tf_op jit(solution)/shard_map/ppermute | solution.py:325
  55.7 15.3 %collective-permute-start.10 = (bf16[128,2048]{1,0:T(8,128)(2,1)S(1)}, bf16[128,2048]{1,0:T(8,128)(2,1)S(1)}, u32[]{:S(2)}, u32[]{:S(2)}) collective-permute-start(bf16[128,2048]{1,0:T(8,128)(2,1)S(1)} %collective-permute-done.5), channel_id=1, source_target_pairs={{8,0},{16,24},{9,1},{17,25},{10,2},{18,26},{11,3},{19,27},{12,4},{... | collective-permute-start | bytes 1572872 | tf_op jit(solution)/shard_map/ppermute | solution.py:319
  57.0 19.4 %collective-permute-start.12 = (s16[528,512]{1,0:T(8,128)(2,1)S(1)}, s16[528,512]{1,0:T(8,128)(2,1)S(1)}, u32[]{:S(2)}, u32[]{:S(2)}) collective-permute-start(s16[528,512]{1,0:T(8,128)(2,1)S(1)} %get-tuple-element.85.a_ref), channel_id=1, source_target_pairs={{0,8},{24,16},{1,9},{25,17},{2,10},{26,18},{3,11},{27,19},{4,12},{... | collective-permute-start | bytes 1622024 | tf_op jit(solution)/shard_map/ppermute | solution.py:322
  66.8 11.7 %collective-permute-start.13 = (s16[528,512]{1,0:T(8,128)(2,1)S(1)}, s16[528,512]{1,0:T(8,128)(2,1)S(1)}, u32[]{:S(2)}, u32[]{:S(2)}) collective-permute-start(s16[528,512]{1,0:T(8,128)(2,1)S(1)} %add.10.own_ref), channel_id=1, source_target_pairs={{8,16},{16,8},{9,17},{17,9},{10,18},{18,10},{11,19},{19,11},{12,20... | collective-permute-start | bytes 1622024 | tf_op jit(solution)/shard_map/ppermute | solution.py:325
  71.5 17.8 %collective-permute-start.14 = (s16[528,512]{1,0:T(8,128)(2,1)S(1)}, s16[528,512]{1,0:T(8,128)(2,1)S(1)}, u32[]{:S(2)}, u32[]{:S(2)}) collective-permute-start(s16[528,512]{1,0:T(8,128)(2,1)S(1)} %reply.8), channel_id=1, source_target_pairs={{0,8},{8,0},{16,24},{24,16},{1,9},{9,1},{17,25},{25,17},{2,10},{10... | collective-permute-start | bytes 1622024 | tf_op jit(solution)/shard_map/ppermute | solution.py:328
  77.0 18.7 %collective-permute-start.15 = (s16[528,512]{1,0:T(8,128)(2,1)S(1)}, s16[528,512]{1,0:T(8,128)(2,1)}, u32[]{:S(2)}, u32[]{:S(2)}) collective-permute-start(s16[528,512]{1,0:T(8,128)(2,1)S(1)} %add.11.own_ref), channel_id=1, source_target_pairs={{8,16},{16,8},{9,17},{17,9},{10,18},{18,10},{11,19},{19,11},{12,20... | collective-permute-start | bytes 1622024 | tf_op jit(solution)/shard_map/ppermute | solution.py:325
  78.5 10.8 %copy-start.2 = (s16[528,512]{1,0:T(8,128)(2,1)}, s16[528,512]{1,0:T(8,128)(2,1)S(1)}, u32[]{:S(2)}) copy-start(s16[528,512]{1,0:T(8,128)(2,1)S(1)} %collective-permute-done.13.b_ref.across_ref) | copy-start | bytes 1622020
  79.9 10.9 %copy-start.7 = (bf16[128,2048]{1,0:T(8,128)(2,1)S(1)}, bf16[128,2048]{1,0:T(8,128)(2,1)}, u32[]{:S(2)}) copy-start(bf16[128,2048]{1,0:T(8,128)(2,1)} %copy-done.6) | copy-start | bytes 1572868
  79.9 21.6 %collective-permute-start.16 = (s16[528,512]{1,0:T(8,128)(2,1)}, s16[528,512]{1,0:T(8,128)(2,1)S(1)}, u32[]{:S(2)}, u32[]{:S(2)}) collective-permute-start(s16[528,512]{1,0:T(8,128)(2,1)} %reply.9), channel_id=1, source_target_pairs={{0,8},{8,0},{16,24},{24,16},{1,9},{9,1},{17,25},{25,17},{2,10},{10... | collective-permute-start | bytes 1622024 | tf_op jit(solution)/shard_map/ppermute | solution.py:328
  89.3 1.6 copy-start.8
  89.9 19.3 %collective-permute-start.17 = (s16[528,512]{1,0:T(8,128)(2,1)S(1)}, s16[528,512]{1,0:T(8,128)(2,1)S(1)}, u32[]{:S(2)}, u32[]{:S(2)}) collective-permute-start(s16[528,512]{1,0:T(8,128)(2,1)S(1)} %add.12.own_ref), channel_id=1, source_target_pairs={{8,16},{16,8},{9,17},{17,9},{10,18},{18,10},{11,19},{19,11},{12,20... | collective-permute-start | bytes 1622024 | tf_op jit(solution)/shard_map/ppermute | solution.py:325
  91.1 12.5 %copy-start.3 = (s16[528,512]{1,0:T(8,128)(2,1)S(1)}, s16[528,512]{1,0:T(8,128)(2,1)}, u32[]{:S(2)}) copy-start(s16[528,512]{1,0:T(8,128)(2,1)} %copy-done.2) | copy-start | bytes 1622020
  97.3 15.1 %collective-permute-start.18 = (s16[528,512]{1,0:T(8,128)(2,1)S(1)}, s16[528,512]{1,0:T(8,128)(2,1)S(1)}, u32[]{:S(2)}, u32[]{:S(2)}) collective-permute-start(s16[528,512]{1,0:T(8,128)(2,1)S(1)} %reply.10), channel_id=1, source_target_pairs={{0,8},{8,0},{16,24},{24,16},{1,9},{9,1},{17,25},{25,17},{2,10},{10... | collective-permute-start | bytes 1622024 | tf_op jit(solution)/shard_map/ppermute | solution.py:328
  102.1 0.8 copy-start
  102.9 16.4 %collective-permute-start.19 = (s16[528,512]{1,0:T(8,128)(2,1)S(1)}, s16[528,512]{1,0:T(8,128)(2,1)S(1)}, u32[]{:S(2)}, u32[]{:S(2)}) collective-permute-start(s16[528,512]{1,0:T(8,128)(2,1)S(1)} %add.13.own_ref), channel_id=1, source_target_pairs={{8,16},{16,8},{9,17},{17,9},{10,18},{18,10},{11,19},{19,11},{12,20... | collective-permute-start | bytes 1622024 | tf_op jit(solution)/shard_map/ppermute | solution.py:325
  103.6 1.0 copy-start.1
  109.8 14.3 %collective-permute-start.20 = (s16[528,512]{1,0:T(8,128)(2,1)S(1)}, s16[528,512]{1,0:T(8,128)(2,1)S(1)}, u32[]{:S(2)}, u32[]{:S(2)}) collective-permute-start(s16[528,512]{1,0:T(8,128)(2,1)S(1)} %reply.11), channel_id=1, source_target_pairs={{0,8},{8,0},{16,24},{24,16},{1,9},{9,1},{17,25},{25,17},{2,10},{10... | collective-permute-start | bytes 1622024 | tf_op jit(solution)/shard_map/ppermute | solution.py:328
  113.0 17.0 %collective-permute-start.21 = (s16[528,512]{1,0:T(8,128)(2,1)S(1)}, s16[528,512]{1,0:T(8,128)(2,1)S(1)}, u32[]{:S(2)}, u32[]{:S(2)}) collective-permute-start(s16[528,512]{1,0:T(8,128)(2,1)S(1)} %add.14.own_ref), channel_id=1, source_target_pairs={{8,16},{16,8},{9,17},{17,9},{10,18},{18,10},{11,19},{19,11},{12,20... | collective-permute-start | bytes 1622024 | tf_op jit(solution)/shard_map/ppermute | solution.py:325
  119.9 13.6 %collective-permute-start.22 = (s16[528,512]{1,0:T(8,128)(2,1)S(1)}, s16[528,512]{1,0:T(8,128)(2,1)S(1)}, u32[]{:S(2)}, u32[]{:S(2)}) collective-permute-start(s16[528,512]{1,0:T(8,128)(2,1)S(1)} %reply.12), channel_id=1, source_target_pairs={{0,8},{8,0},{16,24},{24,16},{1,9},{9,1},{17,25},{25,17},{2,10},{10... | collective-permute-start | bytes 1622024 | tf_op jit(solution)/shard_map/ppermute | solution.py:328
  124.7 11.4 %collective-permute-start.23 = (s16[528,512]{1,0:T(8,128)(2,1)S(1)}, s16[528,512]{1,0:T(8,128)(2,1)S(1)}, u32[]{:S(2)}, u32[]{:S(2)}) collective-permute-start(s16[528,512]{1,0:T(8,128)(2,1)S(1)} %add.15.own_ref), channel_id=1, source_target_pairs={{8,16},{16,8},{9,17},{17,9},{10,18},{18,10},{11,19},{19,11},{12,20... | collective-permute-start | bytes 1622024 | tf_op jit(solution)/shard_map/ppermute | solution.py:325
  134.1 8.5 %collective-permute-start.24 = (s16[528,512]{1,0:T(8,128)(2,1)S(1)}, s16[528,512]{1,0:T(8,128)(2,1)S(1)}, u32[]{:S(2)}, u32[]{:S(2)}) collective-permute-start(s16[528,512]{1,0:T(8,128)(2,1)S(1)} %add.16.own_ref), channel_id=1, source_target_pairs={{8,16},{16,8},{9,17},{17,9},{10,18},{18,10},{11,19},{19,11},{12,20... | collective-permute-start | bytes 1622024 | tf_op jit(solution)/shard_map/ppermute | solution.py:325
  134.8 18.8 %collective-permute-start.25 = (s16[528,512]{1,0:T(8,128)(2,1)S(1)}, s16[528,512]{1,0:T(8,128)(2,1)S(1)}, u32[]{:S(2)}, u32[]{:S(2)}) collective-permute-start(s16[528,512]{1,0:T(8,128)(2,1)S(1)} %reply.13), channel_id=1, source_target_pairs={{8,0},{16,24},{9,1},{17,25},{10,2},{18,26},{11,3},{19,27},{12,4},{... | collective-permute-start | bytes 1622024 | tf_op jit(solution)/shard_map/ppermute | solution.py:319
  136.7 28.5 %collective-permute-start.26 = (s16[528,512]{1,0:T(8,128)(2,1)S(1)}, s16[528,512]{1,0:T(8,128)(2,1)S(1)}, u32[]{:S(2)}, u32[]{:S(2)}) collective-permute-start(s16[528,512]{1,0:T(8,128)(2,1)S(1)} %reply.14), channel_id=1, source_target_pairs={{8,0},{16,24},{9,1},{17,25},{10,2},{18,26},{11,3},{19,27},{12,4},{... | collective-permute-start | bytes 1622024 | tf_op jit(solution)/shard_map/ppermute | solution.py:319
  143.4 28.9 %collective-permute-start.27 = (s16[528,512]{1,0:T(8,128)(2,1)S(1)}, s16[528,512]{1,0:T(8,128)(2,1)S(1)}, u32[]{:S(2)}, u32[]{:S(2)}) collective-permute-start(s16[528,512]{1,0:T(8,128)(2,1)S(1)} %reply.15), channel_id=1, source_target_pairs={{8,0},{16,24},{9,1},{17,25},{10,2},{18,26},{11,3},{19,27},{12,4},{... | collective-permute-start | bytes 1622024 | tf_op jit(solution)/shard_map/ppermute | solution.py:319

commit v12 on v10

--- a/solution.py
+++ b/solution.py
@@ -379,16 +379,14 @@
     arrived.append(inward(own[1], 0))
     moved = [outward(tie(far[0], place), 0)]
     run_forward(2, ahead)
-    turned = ordered(turn, *gathered)
     for s in range(chunks + LAG):
         if s < chunks:
-            if s == 0:
-                place = tie(place, far[1], moved[0])
             if s + 2 < min(chunks, LAG):
                 arrived.append(inward(tie(own[s + 2], arrived[s]), 0))
             sums.append(ordered(add, own[s], arrived[s]))
             across.append(swap(sums[s]))
         if s == 0:
+            place = tie(place, far[1], moved[0])
             moved.append(outward(tie(far[1], place), 0))
         def weights_of(s):
             c = s - LAG
@@ -410,7 +408,9 @@
         if s >= max(LAG, chunks - 1):
             weights_of(s)
         if len(own) < chunks:
-            run_forward(len(own), len(own) + 1)
+            run_forward(len(own), min(len(own) + (2 if s == 0 else 1), chunks))
+        if s == 2:
+            turned = ordered(turn, *gathered)
     return tuple(outs)
 
 

time: 182 us -> 176 us (0.967)
  waiting for transfers between devices: 40.3 us -> 34.1 us
    ppermute x5, waiting for transfers between devices: 23.6 us -> 19.6 us  [outward(): lax.ppermute(value, 'row', [(left - hop, left - hop - 1), (right + hop, r...]
    ppermute x3, starting transfers between devices: 19.2 us -> 16.3 us  [inward(): lax.ppermute(value, 'row', [(left - hop - 1, left - hop), (right + hop +...]
    ppermute x6, waiting for transfers between devices: 3.46 us -> 1.38 us  [exchange(): return lax.ppermute(value, 'row', [(i, i ^ 1) for i in range(ring)])]
    pallas_call x7 -> x6, Pallas kernels: 29.2 us -> 27.6 us  [forward(): pl.pallas_call(functools.partial(forward_kernel, first=start // BLOCK, sp...]
  transfers between devices with their start and end apart: 28 -> 28, of which waited for: 8 -> 8; matrix products, arithmetic and copies ran while one was open for 1% -> 1% of each run, Pallas kernels for 40% -> 42%
where the time goes in v12:
time: 176 us; the launch traced here: 175 us
  Pallas kernels  78.3 us (44%)
  starting transfers between devices  57 us (32%)
  waiting for transfers between devices  34.1 us (19%)
  local copies, waits for them, and re-layouts  2.69 us (2%)
    pallas_call x8, Pallas kernels, weight_grads(): pl.pallas_call(functools.partial(weights_kernel, first=first, devices=dev...  37.7 us
    pallas_call x6, Pallas kernels, forward(): pl.pallas_call(functools.partial(forward_kernel, first=start // BLOCK, sp...  27.6 us
    ppermute x6, starting transfers between devices, exchange(): return lax.ppermute(value, 'row', [(i, i ^ 1) for i in range(ring)])  22.7 us
    ppermute x5, waiting for transfers between devices, outward(): lax.ppermute(value, 'row', [(left - hop, left - hop - 1), (right + hop, r...  19.6 us
    ppermute x3, starting transfers between devices, inward(): lax.ppermute(value, 'row', [(left - hop - 1, left - hop), (right + hop +...  16.3 us
    ppermute x3, waiting for transfers between devices, gather_tokens(): lax.ppermute(tokens, 'col', [(i, i ^ other) for i in range(devices)])  11.3 us
    ppermute x10, starting transfers between devices, swap(): return lax.ppermute(value, 'row', [(left, right), (right, left)])  7.91 us
    pallas_call x8, Pallas kernels, reply(): pl.pallas_call(reply_kernel, grid_spec=pltpu.PrefetchScalarGridSpec(num_s...  6.76 us
  transfers between devices with their start and end apart: 28, of which 8 were waited for; matrix products, arithmetic and copies ran while one was open for 1% of the time, Pallas kernels for 42%

profile of v12, /device:TPU:0, one launch (start us, length us, event | category | flops | bytes accessed | tf_op | source)
XLA Modules:
  0.0 174.6 jit_solution(14926619560362457604)
XLA Ops:
  0.6 3.1 %collective-permute-start.3 = (bf16[128,2048]{1,0:T(8,128)(2,1)}, bf16[128,2048]{1,0:T(8,128)(2,1)S(1)}, u32[]{:S(2)}, u32[]{:S(2)}) collective-permute-start(bf16[128,2048]{1,0:T(8,128)(2,1)} %param.9), channel_id=1, source_target_pairs={{0,8},{8,0},{16,24},{24,16},{1,9},{9,1},{17,25},{25,17},{2,10},{10... | collective-permute-start | bytes 1572872 | tf_op jit(solution)/shard_map/ppermute | solution.py:328
  3.7 1.5 collective-permute-start
  5.2 1.5 collective-permute-start.1
  7.2 6.0 %collective-permute-done = bf16[64,2048]{1,0:T(8,128)(2,1)S(1)} collective-permute-done((bf16[64,2048]{1,0:T(8,128)(2,1)}, bf16[64,2048]{1,0:T(8,128)(2,1)S(1)}, u32[]{:S(2)}, u32[]{:S(2)}) %collective-permute-start) | collective-permute-done | bytes 262176 | tf_op jit(solution)/shard_map/ppermute | solution.py:297
  13.2 5.4 %collective-permute-done.1 = bf16[64,2048]{1,0:T(8,128)(2,1)S(1)} collective-permute-done((bf16[64,2048]{1,0:T(8,128)(2,1)}, bf16[64,2048]{1,0:T(8,128)(2,1)S(1)}, u32[]{:S(2)}, u32[]{:S(2)}) %collective-permute-start.1) | collective-permute-done | bytes 262176 | tf_op jit(solution)/shard_map/ppermute | solution.py:297
  18.5 1.0 pad_maximum_fusion.1.low_ref
  20.5 1.8 %collective-permute-done.4.high_ref = bf16[256,2048]{1,0:T(8,128)(2,1)S(1)} collective-permute-done((bf16[256,2048]{1,0:T(8,128)(2,1)S(1)}, bf16[256,2048]{1,0:T(8,128)(2,1)S(1)}, u32[]{:S(2)}, u32[]{:S(2)}) %collective-permute-start.4) | collective-permute-done | bytes 1048608 | tf_op jit(solution)/shard_map/ppermute | solution.py:299
  23.0 3.9 %forward.6.a_ref = s16[528,512]{1,0:T(8,128)(2,1)S(1)} custom-call(s32[7]{0:T(128)S(1)} %stack.35.place_ref, s32[16,16]{1,0:T(8,128)S(1)} %copy-done.4, bf16[256,2048]{1,0:T(8,128)(2,1)S(1)} %pad_maximum_fusion.1.low_ref, bf16[256,2048]{1,0:T(8,128)(2,1)S(1)} %collective-permute-done.4.high_ref, bf16[2048,2048]{1,0:T(8,128)(2,1)} %gate_ref.11, ...), custom_call_target="tpu_custom_call" | custom-call | flops 8000000000 | bytes 20000000 | tf_op jit(solution)/shard_map/forward/pallas_call | solution.py:98
  26.9 4.5 %collective-permute-start.5 = (s16[528,512]{1,0:T(8,128)(2,1)S(1)}, s16[528,512]{1,0:T(8,128)(2,1)S(1)}, u32[]{:S(2)}, u32[]{:S(2)}) collective-permute-start(s16[528,512]{1,0:T(8,128)(2,1)S(1)} %forward.6.a_ref), channel_id=1, source_target_pairs={{0,8},{24,16},{1,9},{25,17},{2,10},{26,18},{3,11},{27,19},{4,12},{... | collective-permute-start | bytes 1622024 | tf_op jit(solution)/shard_map/ppermute | solution.py:322
  31.4 3.9 %forward.7.a_ref = s16[528,512]{1,0:T(8,128)(2,1)S(1)} custom-call(s32[7]{0:T(128)S(1)} %stack.35.place_ref, s32[16,16]{1,0:T(8,128)S(1)} %copy-done.4, bf16[256,2048]{1,0:T(8,128)(2,1)S(1)} %pad_maximum_fusion.1.low_ref, bf16[256,2048]{1,0:T(8,128)(2,1)S(1)} %collective-permute-done.4.high_ref, bf16[2048,2048]{1,0:T(8,128)(2,1)} %gate_ref.11, ...), custom_call_target="tpu_custom_call" | custom-call | flops 8000000000 | bytes 20000000 | tf_op jit(solution)/shard_map/forward/pallas_call | solution.py:98
  35.3 1.3 collective-permute-start.8
  37.3 7.2 %collective-permute-start.9 = (s16[528,512]{1,0:T(8,128)(2,1)S(1)}, s16[528,512]{1,0:T(8,128)(2,1)S(1)}, u32[]{:S(2)}, u32[]{:S(2)}) collective-permute-start(s16[528,512]{1,0:T(8,128)(2,1)S(1)} %forward.7.a_ref), channel_id=1, source_target_pairs={{0,8},{24,16},{1,9},{25,17},{2,10},{26,18},{3,11},{27,19},{4,12},{... | collective-permute-start | bytes 1622024 | tf_op jit(solution)/shard_map/ppermute | solution.py:322
  44.5 6.1 %forward.8 = (s16[528,512]{1,0:T(8,128)(2,1)S(1)}, s16[528,512]{1,0:T(8,128)(2,1)S(1)}) custom-call(s32[7]{0:T(128)S(1)} %stack.35.place_ref, s32[16,16]{1,0:T(8,128)S(1)} %copy-done.4, bf16[256,2048]{1,0:T(8,128)(2,1)S(1)} %pad_maximum_fusion.1.low_ref, bf16[256,2048]{1,0:T(8,128)(2,1)S(1)} %collective-permute-done.4.high_ref, ...), custom_call_target="tpu_custom_call" | custom-call | flops 1000000 | bytes 2500 | tf_op jit(solution)/shard_map/forward/pallas_call | solution.py:98
  51.9 1.3 collective-permute-start.10
  53.2 4.6 %collective-permute-start.12 = (s16[528,512]{1,0:T(8,128)(2,1)S(1)}, s16[528,512]{1,0:T(8,128)(2,1)S(1)}, u32[]{:S(2)}, u32[]{:S(2)}) collective-permute-start(s16[528,512]{1,0:T(8,128)(2,1)S(1)} %get-tuple-element.86.a_ref), channel_id=1, source_target_pairs={{0,8},{24,16},{1,9},{25,17},{2,10},{26,18},{3,11},{27,19},{4,12},{... | collective-permute-start | bytes 1622024 | tf_op jit(solution)/shard_map/ppermute | solution.py:322
  57.9 6.1 %forward.9 = (s16[528,512]{1,0:T(8,128)(2,1)S(1)}, s16[528,512]{1,0:T(8,128)(2,1)S(1)}) custom-call(s32[7]{0:T(128)S(1)} %stack.35.place_ref, s32[16,16]{1,0:T(8,128)S(1)} %copy-done.4, bf16[256,2048]{1,0:T(8,128)(2,1)S(1)} %pad_maximum_fusion.1.low_ref, bf16[256,2048]{1,0:T(8,128)(2,1)S(1)} %collective-permute-done.4.high_ref, ...), custom_call_target="tpu_custom_call" | custom-call | flops 1000000 | bytes 2500 | tf_op jit(solution)/shard_map/forward/pallas_call | solution.py:98
  64.6 0.7 collective-permute-start.13
  65.3 1.5 collective-permute-done.10
  67.4 1.9 %collective-permute-start.14 = (s16[528,512]{1,0:T(8,128)(2,1)S(1)}, s16[528,512]{1,0:T(8,128)(2,1)S(1)}, u32[]{:S(2)}, u32[]{:S(2)}) collective-permute-start(s16[528,512]{1,0:T(8,128)(2,1)S(1)} %reply.8), channel_id=1, source_target_pairs={{0,8},{8,0},{16,24},{24,16},{1,9},{9,1},{17,25},{25,17},{2,10},{10... | collective-permute-start | bytes 1622024 | tf_op jit(solution)/shard_map/ppermute | solution.py:328
  69.3 3.8 %forward.10.next_ref.a_ref = s16[528,512]{1,0:T(8,128)(2,1)S(1)} custom-call(s32[7]{0:T(128)S(1)} %stack.35.place_ref, s32[16,16]{1,0:T(8,128)S(1)} %copy-done.5, bf16[256,2048]{1,0:T(8,128)(2,1)S(1)} %pad_maximum_fusion.1.low_ref, bf16[256,2048]{1,0:T(8,128)(2,1)S(1)} %collective-permute-done.4.high_ref, bf16[2048,2048]{1,0:T(8,128)(2,1)} %gate_ref.11, ...), custom_call_target="tpu_custom_call" | custom-call | flops 1000000 | bytes 2500 | tf_op jit(solution)/shard_map/forward/pallas_call | solution.py:98
  73.8 1.5 collective-permute-start.15
  75.3 1.4 reply.9
  76.7 6.9 %collective-permute-start.16 = (s16[528,512]{1,0:T(8,128)(2,1)}, s16[528,512]{1,0:T(8,128)(2,1)S(1)}, u32[]{:S(2)}, u32[]{:S(2)}) collective-permute-start(s16[528,512]{1,0:T(8,128)(2,1)} %reply.9), channel_id=1, source_target_pairs={{0,8},{8,0},{16,24},{24,16},{1,9},{9,1},{17,25},{25,17},{2,10},{10... | collective-permute-start | bytes 1622024 | tf_op jit(solution)/shard_map/ppermute | solution.py:328
  83.6 3.8 %forward.11.next_ref.a_ref = s16[528,512]{1,0:T(8,128)(2,1)S(1)} custom-call(s32[7]{0:T(128)S(1)} %stack.35.place_ref, s32[16,16]{1,0:T(8,128)S(1)} %copy-done.5, bf16[256,2048]{1,0:T(8,128)(2,1)S(1)} %pad_maximum_fusion.1.low_ref, bf16[256,2048]{1,0:T(8,128)(2,1)S(1)} %collective-permute-done.4.high_ref, bf16[2048,2048]{1,0:T(8,128)(2,1)} %gate_ref.11, ...), custom_call_target="tpu_custom_call" | custom-call | flops 1000000 | bytes 2500 | tf_op jit(solution)/shard_map/forward/pallas_call | solution.py:98
  87.4 1.5 turn.1.turned_ref
  89.6 0.9 collective-permute-start.17
  90.8 4.6 %weight_grads.8 = (bf16[128,2048]{1,0:T(8,128)(2,1)}, f32[2048,2048]{1,0:T(8,128)}, f32[2048,2048]{1,0:T(8,128)}) custom-call(s32[7]{0:T(128)S(1)} %stack.35.place_ref, s32[16,16]{1,0:T(8,128)S(1)} %copy-done.5, bf16[2048,512]{1,0:T(8,128)(2,1)S(1)} %turn.1.turned_ref, bf16[512,2048]{1,0:T(8,128)(2,1)S(1)} %pad_maximum_fusion.back_ref, ...), custom_call_target="tpu_custom_call" | custom-call | flops 1000000 | bytes 2500 | tf_op jit(solution)/shard_map/weight_grads/pallas_call | solution.py:261
  95.4 1.6 reply.10
  97.0 4.1 %collective-permute-start.18 = (s16[528,512]{1,0:T(8,128)(2,1)S(1)}, s16[528,512]{1,0:T(8,128)(2,1)S(1)}, u32[]{:S(2)}, u32[]{:S(2)}) collective-permute-start(s16[528,512]{1,0:T(8,128)(2,1)S(1)} %reply.10), channel_id=1, source_target_pairs={{0,8},{8,0},{16,24},{24,16},{1,9},{9,1},{17,25},{25,17},{2,10},{10... | collective-permute-start | bytes 1622024 | tf_op jit(solution)/shard_map/ppermute | solution.py:328
  101.7 0.8 copy-done
  103.2 1.0 copy-done.1
  104.2 4.6 %weight_grads.9 = (bf16[128,2048]{1,0:T(8,128)(2,1)}, f32[2048,2048]{1,0:T(8,128)}, f32[2048,2048]{1,0:T(8,128)}) custom-call(s32[7]{0:T(128)S(1)} %stack.35.place_ref, s32[16,16]{1,0:T(8,128)S(1)} %copy-done.5, bf16[2048,512]{1,0:T(8,128)(2,1)S(1)} %turn.1.turned_ref, ...), custom_call_target="tpu_custom_call", output_to_operand_aliasing={{0}: (7, {}), {1}: (8, {}), {2}: (9, {})} | custom-call | flops 1000000 | bytes 2500 | tf_op jit(solution)/shard_map/weight_grads/pallas_call | solution.py:261
  109.4 2.7 %collective-permute-start.20 = (s16[528,512]{1,0:T(8,128)(2,1)S(1)}, s16[528,512]{1,0:T(8,128)(2,1)S(1)}, u32[]{:S(2)}, u32[]{:S(2)}) collective-permute-start(s16[528,512]{1,0:T(8,128)(2,1)S(1)} %reply.11), channel_id=1, source_target_pairs={{0,8},{8,0},{16,24},{24,16},{1,9},{9,1},{17,25},{25,17},{2,10},{10... | collective-permute-start | bytes 1622024 | tf_op jit(solution)/shard_map/ppermute | solution.py:328
  113.4 5.6 %weight_grads.10 = (bf16[128,2048]{1,0:T(8,128)(2,1)}, f32[2048,2048]{1,0:T(8,128)}, f32[2048,2048]{1,0:T(8,128)}) custom-call(s32[7]{0:T(128)S(1)} %stack.35.place_ref, s32[16,16]{1,0:T(8,128)S(1)} %copy-done.5, bf16[2048,512]{1,0:T(8,128)(2,1)S(1)} %turn.1.turned_ref, ...), custom_call_target="tpu_custom_call", output_to_operand_aliasing={{0}: (7, {}), {1}: (8, {}), {2}: (9, {})} | custom-call | flops 1000000 | bytes 2500 | tf_op jit(solution)/shard_map/weight_grads/pallas_call | solution.py:261
  119.6 4.1 %collective-permute-start.22 = (s16[528,512]{1,0:T(8,128)(2,1)S(1)}, s16[528,512]{1,0:T(8,128)(2,1)S(1)}, u32[]{:S(2)}, u32[]{:S(2)}) collective-permute-start(s16[528,512]{1,0:T(8,128)(2,1)S(1)} %reply.12), channel_id=1, source_target_pairs={{0,8},{8,0},{16,24},{24,16},{1,9},{9,1},{17,25},{25,17},{2,10},{10... | collective-permute-start | bytes 1622024 | tf_op jit(solution)/shard_map/ppermute | solution.py:328
  125.0 4.6 %weight_grads.11 = (bf16[128,2048]{1,0:T(8,128)(2,1)}, f32[2048,2048]{1,0:T(8,128)}, f32[2048,2048]{1,0:T(8,128)}) custom-call(s32[7]{0:T(128)S(1)} %stack.35.place_ref, s32[16,16]{1,0:T(8,128)S(1)} %copy-done.5, bf16[2048,512]{1,0:T(8,128)(2,1)S(1)} %turn.1.turned_ref, ...), custom_call_target="tpu_custom_call", output_to_operand_aliasing={{0}: (7, {}), {1}: (8, {}), {2}: (9, {})} | custom-call | flops 1000000 | bytes 2500 | tf_op jit(solution)/shard_map/weight_grads/pallas_call | solution.py:261
  130.2 1.4 collective-permute-done.22.b_ref.out_ref
  132.9 1.3 collective-permute-start.25
  134.8 1.3 collective-permute-start.26
  136.1 4.6 %weight_grads.12 = (bf16[128,2048]{1,0:T(8,128)(2,1)}, f32[2048,2048]{1,0:T(8,128)}, f32[2048,2048]{1,0:T(8,128)}) custom-call(s32[7]{0:T(128)S(1)} %stack.35.place_ref, s32[16,16]{1,0:T(8,128)S(1)} %copy-done.5, bf16[2048,512]{1,0:T(8,128)(2,1)S(1)} %turn.1.turned_ref, ...), custom_call_target="tpu_custom_call", output_to_operand_aliasing={{0}: (7, {}), {1}: (8, {}), {2}: (9, {})} | custom-call | flops 1000000 | bytes 2500 | tf_op jit(solution)/shard_map/weight_grads/pallas_call | solution.py:261
  140.6 0.8 reply.15
  141.5 1.3 collective-permute-start.27
  142.8 9.5 %collective-permute-done.25.out_ref = s16[528,512]{1,0:T(8,128)(2,1)S(1)} collective-permute-done((s16[528,512]{1,0:T(8,128)(2,1)S(1)}, s16[528,512]{1,0:T(8,128)(2,1)S(1)}, u32[]{:S(2)}, u32[]{:S(2)}) %collective-permute-start.25) | collective-permute-done | bytes 540704 | tf_op jit(solution)/shard_map/ppermute | solution.py:319
  152.3 4.6 %weight_grads.13 = (bf16[128,2048]{1,0:T(8,128)(2,1)}, f32[2048,2048]{1,0:T(8,128)}, f32[2048,2048]{1,0:T(8,128)}) custom-call(s32[7]{0:T(128)S(1)} %stack.35.place_ref, s32[16,16]{1,0:T(8,128)S(1)} %copy-done.5, bf16[2048,512]{1,0:T(8,128)(2,1)S(1)} %turn.1.turned_ref, ...), custom_call_target="tpu_custom_call", output_to_operand_aliasing={{0}: (7, {}), {1}: (8, {}), {2}: (9, {})} | custom-call | flops 1000000 | bytes 2500 | tf_op jit(solution)/shard_map/weight_grads/pallas_call | solution.py:261
  156.8 7.0 %collective-permute-done.26.out_ref = s16[528,512]{1,0:T(8,128)(2,1)S(1)} collective-permute-done((s16[528,512]{1,0:T(8,128)(2,1)S(1)}, s16[528,512]{1,0:T(8,128)(2,1)S(1)}, u32[]{:S(2)}, u32[]{:S(2)}) %collective-permute-start.26) | collective-permute-done | bytes 540704 | tf_op jit(solution)/shard_map/ppermute | solution.py:319
  163.8 4.6 %weight_grads.14 = (bf16[128,2048]{1,0:T(8,128)(2,1)}, f32[2048,2048]{1,0:T(8,128)}, f32[2048,2048]{1,0:T(8,128)}) custom-call(s32[7]{0:T(128)S(1)} %stack.35.place_ref, s32[16,16]{1,0:T(8,128)S(1)} %copy-done.5, bf16[2048,512]{1,0:T(8,128)(2,1)S(1)} %turn.1.turned_ref, ...), custom_call_target="tpu_custom_call", output_to_operand_aliasing={{0}: (7, {}), {1}: (8, {}), {2}: (9, {})} | custom-call | flops 1000000 | bytes 2500 | tf_op jit(solution)/shard_map/weight_grads/pallas_call | solution.py:261
  168.4 1.6 collective-permute-done.27.out_ref
  170.0 4.6 %weight_grads.15 = (bf16[128,2048]{1,0:T(8,128)(2,1)}, f32[2048,2048]{1,0:T(8,128)}, f32[2048,2048]{1,0:T(8,128)}) custom-call(s32[7]{0:T(128)S(1)} %stack.35.place_ref, s32[16,16]{1,0:T(8,128)S(1)} %copy-done.5, bf16[2048,512]{1,0:T(8,128)(2,1)S(1)} %turn.1.turned_ref, ...), custom_call_target="tpu_custom_call", output_to_operand_aliasing={{0}: (7, {}), {1}: (8, {}), {2}: (9, {})} | custom-call | flops 1000000 | bytes 2500 | tf_op jit(solution)/shard_map/weight_grads/pallas_call | solution.py:261
  (65 shorter events, 14.1 us)
Async XLA Ops:
  0.6 19.0 %collective-permute-start.3 = (bf16[128,2048]{1,0:T(8,128)(2,1)}, bf16[128,2048]{1,0:T(8,128)(2,1)S(1)}, u32[]{:S(2)}, u32[]{:S(2)}) collective-permute-start(bf16[128,2048]{1,0:T(8,128)(2,1)} %param.9), channel_id=1, source_target_pairs={{0,8},{8,0},{16,24},{24,16},{1,9},{9,1},{17,25},{25,17},{2,10},{10... | collective-permute-start | bytes 1572872 | tf_op jit(solution)/shard_map/ppermute | solution.py:328
  3.7 9.4 %collective-permute-start = (bf16[64,2048]{1,0:T(8,128)(2,1)}, bf16[64,2048]{1,0:T(8,128)(2,1)S(1)}, u32[]{:S(2)}, u32[]{:S(2)}) collective-permute-start(bf16[64,2048]{1,0:T(8,128)(2,1)} %param.5), channel_id=1, source_target_pairs={{0,2},{1,3},{2,0},{3,1},{4,6},{5,7},{6,4},{7,5},{8,10},{9,11},{10,... | collective-permute-start | bytes 786440 | tf_op jit(solution)/shard_map/ppermute | solution.py:297
  5.2 13.3 %collective-permute-start.1 = (bf16[64,2048]{1,0:T(8,128)(2,1)}, bf16[64,2048]{1,0:T(8,128)(2,1)S(1)}, u32[]{:S(2)}, u32[]{:S(2)}) collective-permute-start(bf16[64,2048]{1,0:T(8,128)(2,1)} %param.5), channel_id=1, source_target_pairs={{0,4},{1,5},{2,6},{3,7},{4,0},{5,1},{6,2},{7,3},{8,12},{9,13},{10,... | collective-permute-start | bytes 786440 | tf_op jit(solution)/shard_map/ppermute | solution.py:297
  6.7 11.8 %collective-permute-start.2 = (bf16[64,2048]{1,0:T(8,128)(2,1)}, bf16[64,2048]{1,0:T(8,128)(2,1)S(1)}, u32[]{:S(2)}, u32[]{:S(2)}) collective-permute-start(bf16[64,2048]{1,0:T(8,128)(2,1)} %param.5), channel_id=1, source_target_pairs={{0,6},{1,7},{2,4},{3,5},{4,2},{5,3},{6,0},{7,1},{8,14},{9,15},{10,... | collective-permute-start | bytes 786440 | tf_op jit(solution)/shard_map/ppermute | solution.py:297
  19.6 17.0 %copy-start.9 = (bf16[128,2048]{1,0:T(8,128)(2,1)}, bf16[128,2048]{1,0:T(8,128)(2,1)S(1)}, u32[]{:S(2)}) copy-start(bf16[128,2048]{1,0:T(8,128)(2,1)S(1)} %collective-permute-done.3) | copy-start | bytes 1572868
  19.6 2.7 %collective-permute-start.4 = (bf16[256,2048]{1,0:T(8,128)(2,1)S(1)}, bf16[256,2048]{1,0:T(8,128)(2,1)S(1)}, u32[]{:S(2)}, u32[]{:S(2)}) collective-permute-start(bf16[256,2048]{1,0:T(8,128)(2,1)S(1)} %pad_maximum_fusion.1.low_ref), channel_id=1, source_target_pairs={{0,1},{1,0},{2,3},{3,2},{4,5},{5,4},{6,7},{7,6},{8,9},{9,8},{10,11... | collective-permute-start | bytes 3145736 | tf_op jit(solution)/shard_map/ppermute | solution.py:299
  19.7 15.6 %collective-permute-start.7 = (bf16[128,2048]{1,0:T(8,128)(2,1)}, bf16[128,2048]{1,0:T(8,128)(2,1)S(1)}, u32[]{:S(2)}, u32[]{:S(2)}) collective-permute-start(bf16[128,2048]{1,0:T(8,128)(2,1)} %param.9), channel_id=1, source_target_pairs={{8,16},{16,8},{9,17},{17,9},{10,18},{18,10},{11,19},{19,11},{12,20... | collective-permute-start | bytes 1572872 | tf_op jit(solution)/shard_map/ppermute | solution.py:325
  22.3 0.7 copy-start.4
  26.9 23.7 %collective-permute-start.5 = (s16[528,512]{1,0:T(8,128)(2,1)S(1)}, s16[528,512]{1,0:T(8,128)(2,1)S(1)}, u32[]{:S(2)}, u32[]{:S(2)}) collective-permute-start(s16[528,512]{1,0:T(8,128)(2,1)S(1)} %forward.6.a_ref), channel_id=1, source_target_pairs={{0,8},{24,16},{1,9},{25,17},{2,10},{26,18},{3,11},{27,19},{4,12},{... | collective-permute-start | bytes 1622024 | tf_op jit(solution)/shard_map/ppermute | solution.py:322
  35.3 15.3 %copy-start.6 = (bf16[128,2048]{1,0:T(8,128)(2,1)}, bf16[128,2048]{1,0:T(8,128)(2,1)S(1)}, u32[]{:S(2)}) copy-start(bf16[128,2048]{1,0:T(8,128)(2,1)S(1)} %collective-permute-done.7) | copy-start | bytes 1572868
  35.3 16.6 %collective-permute-start.8 = (bf16[128,2048]{1,0:T(8,128)(2,1)S(1)}, bf16[128,2048]{1,0:T(8,128)(2,1)S(1)}, u32[]{:S(2)}, u32[]{:S(2)}) collective-permute-start(bf16[128,2048]{1,0:T(8,128)(2,1)S(1)} %collective-permute-done.7), channel_id=1, source_target_pairs={{8,0},{16,24},{9,1},{17,25},{10,2},{18,26},{11,3},{19,27},{12,4},{... | collective-permute-start | bytes 1572872 | tf_op jit(solution)/shard_map/ppermute | solution.py:319
  36.6 15.3 %collective-permute-start.6 = (bf16[128,2048]{1,0:T(8,128)(2,1)S(1)}, bf16[128,2048]{1,0:T(8,128)(2,1)S(1)}, u32[]{:S(2)}, u32[]{:S(2)}) collective-permute-start(bf16[128,2048]{1,0:T(8,128)(2,1)S(1)} %collective-permute-done.3), channel_id=1, source_target_pairs={{8,16},{16,8},{9,17},{17,9},{10,18},{18,10},{11,19},{19,11},{12,20... | collective-permute-start | bytes 1572872 | tf_op jit(solution)/shard_map/ppermute | solution.py:325
  37.3 26.7 %collective-permute-start.9 = (s16[528,512]{1,0:T(8,128)(2,1)S(1)}, s16[528,512]{1,0:T(8,128)(2,1)S(1)}, u32[]{:S(2)}, u32[]{:S(2)}) collective-permute-start(s16[528,512]{1,0:T(8,128)(2,1)S(1)} %forward.7.a_ref), channel_id=1, source_target_pairs={{0,8},{24,16},{1,9},{25,17},{2,10},{26,18},{3,11},{27,19},{4,12},{... | collective-permute-start | bytes 1622024 | tf_op jit(solution)/shard_map/ppermute | solution.py:322
  51.2 18.1 %copy-start.5 = (s32[16,16]{1,0:T(8,128)S(1)}, s32[16,16]{1,0:T(8,128)}, u32[]{:S(2)}) copy-start(s32[16,16]{1,0:T(8,128)} %mask_ref.27) | copy-start | bytes 3076
  51.2 15.6 %collective-permute-start.11 = (s16[528,512]{1,0:T(8,128)(2,1)S(1)}, s16[528,512]{1,0:T(8,128)(2,1)S(1)}, u32[]{:S(2)}, u32[]{:S(2)}) collective-permute-start(s16[528,512]{1,0:T(8,128)(2,1)S(1)} %add.9.own_ref), channel_id=1, source_target_pairs={{8,16},{16,8},{9,17},{17,9},{10,18},{18,10},{11,19},{19,11},{12,20... | collective-permute-start | bytes 1622024 | tf_op jit(solution)/shard_map/ppermute | solution.py:325
  51.9 14.9 %collective-permute-start.10 = (bf16[128,2048]{1,0:T(8,128)(2,1)S(1)}, bf16[128,2048]{1,0:T(8,128)(2,1)S(1)}, u32[]{:S(2)}, u32[]{:S(2)}) collective-permute-start(bf16[128,2048]{1,0:T(8,128)(2,1)S(1)} %collective-permute-done.6), channel_id=1, source_target_pairs={{8,0},{16,24},{9,1},{17,25},{10,2},{18,26},{11,3},{19,27},{12,4},{... | collective-permute-start | bytes 1572872 | tf_op jit(solution)/shard_map/ppermute | solution.py:319
  53.2 20.0 %collective-permute-start.12 = (s16[528,512]{1,0:T(8,128)(2,1)S(1)}, s16[528,512]{1,0:T(8,128)(2,1)S(1)}, u32[]{:S(2)}, u32[]{:S(2)}) collective-permute-start(s16[528,512]{1,0:T(8,128)(2,1)S(1)} %get-tuple-element.86.a_ref), channel_id=1, source_target_pairs={{0,8},{24,16},{1,9},{25,17},{2,10},{26,18},{3,11},{27,19},{4,12},{... | collective-permute-start | bytes 1622024 | tf_op jit(solution)/shard_map/ppermute | solution.py:322
  64.6 10.7 %collective-permute-start.13 = (s16[528,512]{1,0:T(8,128)(2,1)S(1)}, s16[528,512]{1,0:T(8,128)(2,1)S(1)}, u32[]{:S(2)}, u32[]{:S(2)}) collective-permute-start(s16[528,512]{1,0:T(8,128)(2,1)S(1)} %add.10.own_ref), channel_id=1, source_target_pairs={{8,16},{16,8},{9,17},{17,9},{10,18},{18,10},{11,19},{19,11},{12,20... | collective-permute-start | bytes 1622024 | tf_op jit(solution)/shard_map/ppermute | solution.py:325
  67.4 21.6 %collective-permute-start.14 = (s16[528,512]{1,0:T(8,128)(2,1)S(1)}, s16[528,512]{1,0:T(8,128)(2,1)S(1)}, u32[]{:S(2)}, u32[]{:S(2)}) collective-permute-start(s16[528,512]{1,0:T(8,128)(2,1)S(1)} %reply.8), channel_id=1, source_target_pairs={{0,8},{8,0},{16,24},{24,16},{1,9},{9,1},{17,25},{25,17},{2,10},{10... | collective-permute-start | bytes 1622024 | tf_op jit(solution)/shard_map/ppermute | solution.py:328
  73.8 21.6 %collective-permute-start.15 = (s16[528,512]{1,0:T(8,128)(2,1)S(1)}, s16[528,512]{1,0:T(8,128)(2,1)}, u32[]{:S(2)}, u32[]{:S(2)}) collective-permute-start(s16[528,512]{1,0:T(8,128)(2,1)S(1)} %add.11.own_ref), channel_id=1, source_target_pairs={{8,16},{16,8},{9,17},{17,9},{10,18},{18,10},{11,19},{19,11},{12,20... | collective-permute-start | bytes 1622024 | tf_op jit(solution)/shard_map/ppermute | solution.py:325
  75.3 12.1 %copy-start.2 = (s16[528,512]{1,0:T(8,128)(2,1)}, s16[528,512]{1,0:T(8,128)(2,1)S(1)}, u32[]{:S(2)}) copy-start(s16[528,512]{1,0:T(8,128)(2,1)S(1)} %collective-permute-done.13.b_ref.across_ref) | copy-start | bytes 1622020
  76.7 24.3 %collective-permute-start.16 = (s16[528,512]{1,0:T(8,128)(2,1)}, s16[528,512]{1,0:T(8,128)(2,1)S(1)}, u32[]{:S(2)}, u32[]{:S(2)}) collective-permute-start(s16[528,512]{1,0:T(8,128)(2,1)} %reply.9), channel_id=1, source_target_pairs={{0,8},{8,0},{16,24},{24,16},{1,9},{9,1},{17,25},{25,17},{2,10},{10... | collective-permute-start | bytes 1622024 | tf_op jit(solution)/shard_map/ppermute | solution.py:328
  87.4 3.0 %copy-start.7 = (bf16[128,2048]{1,0:T(8,128)(2,1)S(1)}, bf16[128,2048]{1,0:T(8,128)(2,1)}, u32[]{:S(2)}) copy-start(bf16[128,2048]{1,0:T(8,128)(2,1)} %copy-done.6) | copy-start | bytes 1572868
  89.0 1.6 copy-start.8
  89.0 1.6 copy-start.10
  89.6 19.2 %collective-permute-start.17 = (s16[528,512]{1,0:T(8,128)(2,1)S(1)}, s16[528,512]{1,0:T(8,128)(2,1)S(1)}, u32[]{:S(2)}, u32[]{:S(2)}) collective-permute-start(s16[528,512]{1,0:T(8,128)(2,1)S(1)} %add.12.own_ref), channel_id=1, source_target_pairs={{8,16},{16,8},{9,17},{17,9},{10,18},{18,10},{11,19},{19,11},{12,20... | collective-permute-start | bytes 1622024 | tf_op jit(solution)/shard_map/ppermute | solution.py:325
  90.8 12.4 %copy-start.3 = (s16[528,512]{1,0:T(8,128)(2,1)S(1)}, s16[528,512]{1,0:T(8,128)(2,1)}, u32[]{:S(2)}) copy-start(s16[528,512]{1,0:T(8,128)(2,1)} %copy-done.2) | copy-start | bytes 1622020
  97.0 15.1 %collective-permute-start.18 = (s16[528,512]{1,0:T(8,128)(2,1)S(1)}, s16[528,512]{1,0:T(8,128)(2,1)S(1)}, u32[]{:S(2)}, u32[]{:S(2)}) collective-permute-start(s16[528,512]{1,0:T(8,128)(2,1)S(1)} %reply.10), channel_id=1, source_target_pairs={{0,8},{8,0},{16,24},{24,16},{1,9},{9,1},{17,25},{25,17},{2,10},{10... | collective-permute-start | bytes 1622024 | tf_op jit(solution)/shard_map/ppermute | solution.py:328
  101.6 0.8 copy-start
  102.5 16.6 %collective-permute-start.19 = (s16[528,512]{1,0:T(8,128)(2,1)S(1)}, s16[528,512]{1,0:T(8,128)(2,1)S(1)}, u32[]{:S(2)}, u32[]{:S(2)}) collective-permute-start(s16[528,512]{1,0:T(8,128)(2,1)S(1)} %add.13.own_ref), channel_id=1, source_target_pairs={{8,16},{16,8},{9,17},{17,9},{10,18},{18,10},{11,19},{19,11},{12,20... | collective-permute-start | bytes 1622024 | tf_op jit(solution)/shard_map/ppermute | solution.py:325
  103.2 1.0 copy-start.1
  109.4 14.3 %collective-permute-start.20 = (s16[528,512]{1,0:T(8,128)(2,1)S(1)}, s16[528,512]{1,0:T(8,128)(2,1)S(1)}, u32[]{:S(2)}, u32[]{:S(2)}) collective-permute-start(s16[528,512]{1,0:T(8,128)(2,1)S(1)} %reply.11), channel_id=1, source_target_pairs={{0,8},{8,0},{16,24},{24,16},{1,9},{9,1},{17,25},{25,17},{2,10},{10... | collective-permute-start | bytes 1622024 | tf_op jit(solution)/shard_map/ppermute | solution.py:328
  112.7 16.9 %collective-permute-start.21 = (s16[528,512]{1,0:T(8,128)(2,1)S(1)}, s16[528,512]{1,0:T(8,128)(2,1)S(1)}, u32[]{:S(2)}, u32[]{:S(2)}) collective-permute-start(s16[528,512]{1,0:T(8,128)(2,1)S(1)} %add.14.own_ref), channel_id=1, source_target_pairs={{8,16},{16,8},{9,17},{17,9},{10,18},{18,10},{11,19},{19,11},{12,20... | collective-permute-start | bytes 1622024 | tf_op jit(solution)/shard_map/ppermute | solution.py:325
  119.6 11.9 %collective-permute-start.22 = (s16[528,512]{1,0:T(8,128)(2,1)S(1)}, s16[528,512]{1,0:T(8,128)(2,1)S(1)}, u32[]{:S(2)}, u32[]{:S(2)}) collective-permute-start(s16[528,512]{1,0:T(8,128)(2,1)S(1)} %reply.12), channel_id=1, source_target_pairs={{0,8},{8,0},{16,24},{24,16},{1,9},{9,1},{17,25},{25,17},{2,10},{10... | collective-permute-start | bytes 1622024 | tf_op jit(solution)/shard_map/ppermute | solution.py:328
  124.3 9.9 %collective-permute-start.23 = (s16[528,512]{1,0:T(8,128)(2,1)S(1)}, s16[528,512]{1,0:T(8,128)(2,1)S(1)}, u32[]{:S(2)}, u32[]{:S(2)}) collective-permute-start(s16[528,512]{1,0:T(8,128)(2,1)S(1)} %add.15.own_ref), channel_id=1, source_target_pairs={{8,16},{16,8},{9,17},{17,9},{10,18},{18,10},{11,19},{19,11},{12,20... | collective-permute-start | bytes 1622024 | tf_op jit(solution)/shard_map/ppermute | solution.py:325
  132.1 8.5 %collective-permute-start.24 = (s16[528,512]{1,0:T(8,128)(2,1)S(1)}, s16[528,512]{1,0:T(8,128)(2,1)S(1)}, u32[]{:S(2)}, u32[]{:S(2)}) collective-permute-start(s16[528,512]{1,0:T(8,128)(2,1)S(1)} %add.16.own_ref), channel_id=1, source_target_pairs={{8,16},{16,8},{9,17},{17,9},{10,18},{18,10},{11,19},{19,11},{12,20... | collective-permute-start | bytes 1622024 | tf_op jit(solution)/shard_map/ppermute | solution.py:325
  132.9 19.4 %collective-permute-start.25 = (s16[528,512]{1,0:T(8,128)(2,1)S(1)}, s16[528,512]{1,0:T(8,128)(2,1)S(1)}, u32[]{:S(2)}, u32[]{:S(2)}) collective-permute-start(s16[528,512]{1,0:T(8,128)(2,1)S(1)} %reply.13), channel_id=1, source_target_pairs={{8,0},{16,24},{9,1},{17,25},{10,2},{18,26},{11,3},{19,27},{12,4},{... | collective-permute-start | bytes 1622024 | tf_op jit(solution)/shard_map/ppermute | solution.py:319
  134.8 29.1 %collective-permute-start.26 = (s16[528,512]{1,0:T(8,128)(2,1)S(1)}, s16[528,512]{1,0:T(8,128)(2,1)S(1)}, u32[]{:S(2)}, u32[]{:S(2)}) collective-permute-start(s16[528,512]{1,0:T(8,128)(2,1)S(1)} %reply.14), channel_id=1, source_target_pairs={{8,0},{16,24},{9,1},{17,25},{10,2},{18,26},{11,3},{19,27},{12,4},{... | collective-permute-start | bytes 1622024 | tf_op jit(solution)/shard_map/ppermute | solution.py:319
  141.5 28.6 %collective-permute-start.27 = (s16[528,512]{1,0:T(8,128)(2,1)S(1)}, s16[528,512]{1,0:T(8,128)(2,1)S(1)}, u32[]{:S(2)}, u32[]{:S(2)}) collective-permute-start(s16[528,512]{1,0:T(8,128)(2,1)S(1)} %reply.15), channel_id=1, source_target_pairs={{8,0},{16,24},{9,1},{17,25},{10,2},{18,26},{11,3},{19,27},{12,4},{... | collective-permute-start | bytes 1622024 | tf_op jit(solution)/shard_map/ppermute | solution.py:319

commit v13 on v12

--- a/solution.py
+++ b/solution.py
@@ -396,7 +396,7 @@
             *late, _ = lax.optimization_barrier((*far, *moved, place))
             others = [pick(distance == 0, a, b) for a, b in zip(late[:2], late[2:])]
             back = jnp.concatenate([hidden_grad, near[0], *others], axis=0)
-        if LAG <= s < chunks - 1:
+        if LAG <= s < chunks - 2:
             weights_of(s)
         c = s - 1
         if 0 <= c < chunks:
@@ -405,7 +405,7 @@
             both_ways = c + LAG < chunks
             message = ordered(reply, own[c], across[c], own[c + LAG] if both_ways else own[c])
             arrived.append(exchange(message) if both_ways else outward(message, 0))
-        if s >= max(LAG, chunks - 1):
+        if s >= max(LAG, chunks - 2):
             weights_of(s)
         if len(own) < chunks:
             run_forward(len(own), min(len(own) + (2 if s == 0 else 1), chunks))

time: 176 us -> 176 us (level)
  Pallas kernels: 78.3 us -> 76.2 us
  waiting for transfers between devices: 34.1 us -> 36 us
  transfers between devices with their start and end apart: 28 -> 28, of which waited for: 8 -> 8; matrix products, arithmetic and copies ran while one was open for 1% -> 1% of each run, Pallas kernels for 42% -> 41%
where the time goes in v13:
time: 176 us; the launch traced here: 175 us
  Pallas kernels  76.2 us (43%)
  starting transfers between devices  56.8 us (32%)
  waiting for transfers between devices  36 us (20%)
  local copies, waits for them, and re-layouts  3.47 us (2%)
    pallas_call x8, Pallas kernels, weight_grads(): pl.pallas_call(functools.partial(weights_kernel, first=first, devices=dev...  36.6 us
    pallas_call x6, Pallas kernels, forward(): pl.pallas_call(functools.partial(forward_kernel, first=start // BLOCK, sp...  27.6 us
    ppermute x6, starting transfers between devices, exchange(): return lax.ppermute(value, 'row', [(i, i ^ 1) for i in range(ring)])  23.3 us
    ppermute x5, waiting for transfers between devices, outward(): lax.ppermute(value, 'row', [(left - hop, left - hop - 1), (right + hop, r...  20.2 us
    ppermute x3, starting transfers between devices, inward(): lax.ppermute(value, 'row', [(left - hop - 1, left - hop), (right + hop +...  16.4 us
    ppermute x3, waiting for transfers between devices, gather_tokens(): lax.ppermute(tokens, 'col', [(i, i ^ other) for i in range(devices)])  11.3 us
    ppermute x10, starting transfers between devices, swap(): return lax.ppermute(value, 'row', [(left, right), (right, left)])  7.11 us
    ppermute x5, starting transfers between devices, outward(): lax.ppermute(value, 'row', [(left - hop, left - hop - 1), (right + hop, r...  6.46 us
  transfers between devices with their start and end apart: 28, of which 8 were waited for; matrix products, arithmetic and copies ran while one was open for 1% of the time, Pallas kernels for 41%

profile of v13, /device:TPU:0, one launch (start us, length us, event | category | flops | bytes accessed | tf_op | source)
XLA Modules:
  0.0 175.1 jit_solution(5510484621282020868)
XLA Ops:
  0.6 3.1 %collective-permute-start.3 = (bf16[128,2048]{1,0:T(8,128)(2,1)}, bf16[128,2048]{1,0:T(8,128)(2,1)S(1)}, u32[]{:S(2)}, u32[]{:S(2)}) collective-permute-start(bf16[128,2048]{1,0:T(8,128)(2,1)} %param.9), channel_id=1, source_target_pairs={{0,8},{8,0},{16,24},{24,16},{1,9},{9,1},{17,25},{25,17},{2,10},{10... | collective-permute-start | bytes 1572872 | tf_op jit(solution)/shard_map/ppermute | solution.py:328
  3.7 1.5 collective-permute-start
  5.2 1.5 collective-permute-start.1
  7.2 6.0 %collective-permute-done = bf16[64,2048]{1,0:T(8,128)(2,1)S(1)} collective-permute-done((bf16[64,2048]{1,0:T(8,128)(2,1)}, bf16[64,2048]{1,0:T(8,128)(2,1)S(1)}, u32[]{:S(2)}, u32[]{:S(2)}) %collective-permute-start) | collective-permute-done | bytes 262176 | tf_op jit(solution)/shard_map/ppermute | solution.py:297
  13.2 5.4 %collective-permute-done.1 = bf16[64,2048]{1,0:T(8,128)(2,1)S(1)} collective-permute-done((bf16[64,2048]{1,0:T(8,128)(2,1)}, bf16[64,2048]{1,0:T(8,128)(2,1)S(1)}, u32[]{:S(2)}, u32[]{:S(2)}) %collective-permute-start.1) | collective-permute-done | bytes 262176 | tf_op jit(solution)/shard_map/ppermute | solution.py:297
  18.5 1.1 pad_maximum_fusion.1.low_ref
  19.6 0.8 copy-done.9
  21.2 1.9 %collective-permute-done.4.high_ref = bf16[256,2048]{1,0:T(8,128)(2,1)S(1)} collective-permute-done((bf16[256,2048]{1,0:T(8,128)(2,1)S(1)}, bf16[256,2048]{1,0:T(8,128)(2,1)S(1)}, u32[]{:S(2)}, u32[]{:S(2)}) %collective-permute-start.4) | collective-permute-done | bytes 1048608 | tf_op jit(solution)/shard_map/ppermute | solution.py:299
  23.1 0.7 copy-done.4
  23.8 3.9 %forward.6.a_ref = s16[528,512]{1,0:T(8,128)(2,1)S(1)} custom-call(s32[7]{0:T(128)S(1)} %stack.35.place_ref, s32[16,16]{1,0:T(8,128)S(1)} %copy-done.4, bf16[256,2048]{1,0:T(8,128)(2,1)S(1)} %pad_maximum_fusion.1.low_ref, bf16[256,2048]{1,0:T(8,128)(2,1)S(1)} %collective-permute-done.4.high_ref, bf16[2048,2048]{1,0:T(8,128)(2,1)} %gate_ref.11, ...), custom_call_target="tpu_custom_call" | custom-call | flops 8000000000 | bytes 20000000 | tf_op jit(solution)/shard_map/forward/pallas_call | solution.py:98
  27.7 4.6 %collective-permute-start.5 = (s16[528,512]{1,0:T(8,128)(2,1)S(1)}, s16[528,512]{1,0:T(8,128)(2,1)S(1)}, u32[]{:S(2)}, u32[]{:S(2)}) collective-permute-start(s16[528,512]{1,0:T(8,128)(2,1)S(1)} %forward.6.a_ref), channel_id=1, source_target_pairs={{0,8},{24,16},{1,9},{25,17},{2,10},{26,18},{3,11},{27,19},{4,12},{... | collective-permute-start | bytes 1622024 | tf_op jit(solution)/shard_map/ppermute | solution.py:322
  32.3 3.9 %forward.7.a_ref = s16[528,512]{1,0:T(8,128)(2,1)S(1)} custom-call(s32[7]{0:T(128)S(1)} %stack.35.place_ref, s32[16,16]{1,0:T(8,128)S(1)} %copy-done.4, bf16[256,2048]{1,0:T(8,128)(2,1)S(1)} %pad_maximum_fusion.1.low_ref, bf16[256,2048]{1,0:T(8,128)(2,1)S(1)} %collective-permute-done.4.high_ref, bf16[2048,2048]{1,0:T(8,128)(2,1)} %gate_ref.11, ...), custom_call_target="tpu_custom_call" | custom-call | flops 8000000000 | bytes 20000000 | tf_op jit(solution)/shard_map/forward/pallas_call | solution.py:98
  36.1 1.3 collective-permute-start.8
  38.1 7.0 %collective-permute-start.9 = (s16[528,512]{1,0:T(8,128)(2,1)S(1)}, s16[528,512]{1,0:T(8,128)(2,1)S(1)}, u32[]{:S(2)}, u32[]{:S(2)}) collective-permute-start(s16[528,512]{1,0:T(8,128)(2,1)S(1)} %forward.7.a_ref), channel_id=1, source_target_pairs={{0,8},{24,16},{1,9},{25,17},{2,10},{26,18},{3,11},{27,19},{4,12},{... | collective-permute-start | bytes 1622024 | tf_op jit(solution)/shard_map/ppermute | solution.py:322
  45.2 6.1 %forward.8 = (s16[528,512]{1,0:T(8,128)(2,1)S(1)}, s16[528,512]{1,0:T(8,128)(2,1)S(1)}) custom-call(s32[7]{0:T(128)S(1)} %stack.35.place_ref, s32[16,16]{1,0:T(8,128)S(1)} %copy-done.4, bf16[256,2048]{1,0:T(8,128)(2,1)S(1)} %pad_maximum_fusion.1.low_ref, bf16[256,2048]{1,0:T(8,128)(2,1)S(1)} %collective-permute-done.4.high_ref, ...), custom_call_target="tpu_custom_call" | custom-call | flops 1000000 | bytes 2500 | tf_op jit(solution)/shard_map/forward/pallas_call | solution.py:98
  52.7 1.3 collective-permute-start.10
  54.0 4.8 %collective-permute-start.12 = (s16[528,512]{1,0:T(8,128)(2,1)S(1)}, s16[528,512]{1,0:T(8,128)(2,1)S(1)}, u32[]{:S(2)}, u32[]{:S(2)}) collective-permute-start(s16[528,512]{1,0:T(8,128)(2,1)S(1)} %get-tuple-element.86.a_ref), channel_id=1, source_target_pairs={{0,8},{24,16},{1,9},{25,17},{2,10},{26,18},{3,11},{27,19},{4,12},{... | collective-permute-start | bytes 1622024 | tf_op jit(solution)/shard_map/ppermute | solution.py:322
  58.8 6.1 %forward.9 = (s16[528,512]{1,0:T(8,128)(2,1)S(1)}, s16[528,512]{1,0:T(8,128)(2,1)S(1)}) custom-call(s32[7]{0:T(128)S(1)} %stack.35.place_ref, s32[16,16]{1,0:T(8,128)S(1)} %copy-done.4, bf16[256,2048]{1,0:T(8,128)(2,1)S(1)} %pad_maximum_fusion.1.low_ref, bf16[256,2048]{1,0:T(8,128)(2,1)S(1)} %collective-permute-done.4.high_ref, ...), custom_call_target="tpu_custom_call" | custom-call | flops 1000000 | bytes 2500 | tf_op jit(solution)/shard_map/forward/pallas_call | solution.py:98
  66.2 1.4 collective-permute-done.10
  68.2 1.8 %collective-permute-start.14 = (s16[528,512]{1,0:T(8,128)(2,1)S(1)}, s16[528,512]{1,0:T(8,128)(2,1)S(1)}, u32[]{:S(2)}, u32[]{:S(2)}) collective-permute-start(s16[528,512]{1,0:T(8,128)(2,1)S(1)} %reply.8), channel_id=1, source_target_pairs={{0,8},{8,0},{16,24},{24,16},{1,9},{9,1},{17,25},{25,17},{2,10},{10... | collective-permute-start | bytes 1622024 | tf_op jit(solution)/shard_map/ppermute | solution.py:328
  70.0 3.8 %forward.10.next_ref.a_ref = s16[528,512]{1,0:T(8,128)(2,1)S(1)} custom-call(s32[7]{0:T(128)S(1)} %stack.35.place_ref, s32[16,16]{1,0:T(8,128)S(1)} %copy-done.5, bf16[256,2048]{1,0:T(8,128)(2,1)S(1)} %pad_maximum_fusion.1.low_ref, bf16[256,2048]{1,0:T(8,128)(2,1)S(1)} %collective-permute-done.4.high_ref, bf16[2048,2048]{1,0:T(8,128)(2,1)} %gate_ref.11, ...), custom_call_target="tpu_custom_call" | custom-call | flops 1000000 | bytes 2500 | tf_op jit(solution)/shard_map/forward/pallas_call | solution.py:98
  75.2 1.4 reply.9
  76.6 7.9 %collective-permute-start.16 = (s16[528,512]{1,0:T(8,128)(2,1)}, s16[528,512]{1,0:T(8,128)(2,1)S(1)}, u32[]{:S(2)}, u32[]{:S(2)}) collective-permute-start(s16[528,512]{1,0:T(8,128)(2,1)} %reply.9), channel_id=1, source_target_pairs={{0,8},{8,0},{16,24},{24,16},{1,9},{9,1},{17,25},{25,17},{2,10},{10... | collective-permute-start | bytes 1622024 | tf_op jit(solution)/shard_map/ppermute | solution.py:328
  84.4 3.8 %forward.11.next_ref.a_ref = s16[528,512]{1,0:T(8,128)(2,1)S(1)} custom-call(s32[7]{0:T(128)S(1)} %stack.35.place_ref, s32[16,16]{1,0:T(8,128)S(1)} %copy-done.5, bf16[256,2048]{1,0:T(8,128)(2,1)S(1)} %pad_maximum_fusion.1.low_ref, bf16[256,2048]{1,0:T(8,128)(2,1)S(1)} %collective-permute-done.4.high_ref, bf16[2048,2048]{1,0:T(8,128)(2,1)} %gate_ref.11, ...), custom_call_target="tpu_custom_call" | custom-call | flops 1000000 | bytes 2500 | tf_op jit(solution)/shard_map/forward/pallas_call | solution.py:98
  88.3 1.5 turn.1.turned_ref
  90.5 0.9 collective-permute-start.17
  91.7 4.6 %weight_grads.8 = (bf16[128,2048]{1,0:T(8,128)(2,1)}, f32[2048,2048]{1,0:T(8,128)}, f32[2048,2048]{1,0:T(8,128)}) custom-call(s32[7]{0:T(128)S(1)} %stack.35.place_ref, s32[16,16]{1,0:T(8,128)S(1)} %copy-done.5, bf16[2048,512]{1,0:T(8,128)(2,1)S(1)} %turn.1.turned_ref, bf16[512,2048]{1,0:T(8,128)(2,1)S(1)} %pad_maximum_fusion.back_ref, ...), custom_call_target="tpu_custom_call" | custom-call | flops 1000000 | bytes 2500 | tf_op jit(solution)/shard_map/weight_grads/pallas_call | solution.py:261
  96.9 3.8 %collective-permute-start.18 = (s16[528,512]{1,0:T(8,128)(2,1)S(1)}, s16[528,512]{1,0:T(8,128)(2,1)S(1)}, u32[]{:S(2)}, u32[]{:S(2)}) collective-permute-start(s16[528,512]{1,0:T(8,128)(2,1)S(1)} %reply.10), channel_id=1, source_target_pairs={{0,8},{8,0},{16,24},{24,16},{1,9},{9,1},{17,25},{25,17},{2,10},{10... | collective-permute-start | bytes 1622024 | tf_op jit(solution)/shard_map/ppermute | solution.py:328
  101.3 0.8 copy-done
  102.9 1.0 copy-done.1
  103.9 4.6 %weight_grads.9 = (bf16[128,2048]{1,0:T(8,128)(2,1)}, f32[2048,2048]{1,0:T(8,128)}, f32[2048,2048]{1,0:T(8,128)}) custom-call(s32[7]{0:T(128)S(1)} %stack.35.place_ref, s32[16,16]{1,0:T(8,128)S(1)} %copy-done.5, bf16[2048,512]{1,0:T(8,128)(2,1)S(1)} %turn.1.turned_ref, ...), custom_call_target="tpu_custom_call", output_to_operand_aliasing={{0}: (7, {}), {1}: (8, {}), {2}: (9, {})} | custom-call | flops 1000000 | bytes 2500 | tf_op jit(solution)/shard_map/weight_grads/pallas_call | solution.py:261
  109.1 2.9 %collective-permute-start.20 = (s16[528,512]{1,0:T(8,128)(2,1)S(1)}, s16[528,512]{1,0:T(8,128)(2,1)S(1)}, u32[]{:S(2)}, u32[]{:S(2)}) collective-permute-start(s16[528,512]{1,0:T(8,128)(2,1)S(1)} %reply.11), channel_id=1, source_target_pairs={{0,8},{8,0},{16,24},{24,16},{1,9},{9,1},{17,25},{25,17},{2,10},{10... | collective-permute-start | bytes 1622024 | tf_op jit(solution)/shard_map/ppermute | solution.py:328
  113.3 4.6 %weight_grads.10 = (bf16[128,2048]{1,0:T(8,128)(2,1)}, f32[2048,2048]{1,0:T(8,128)}, f32[2048,2048]{1,0:T(8,128)}) custom-call(s32[7]{0:T(128)S(1)} %stack.35.place_ref, s32[16,16]{1,0:T(8,128)S(1)} %copy-done.5, bf16[2048,512]{1,0:T(8,128)(2,1)S(1)} %turn.1.turned_ref, ...), custom_call_target="tpu_custom_call", output_to_operand_aliasing={{0}: (7, {}), {1}: (8, {}), {2}: (9, {})} | custom-call | flops 1000000 | bytes 2500 | tf_op jit(solution)/shard_map/weight_grads/pallas_call | solution.py:261
  118.5 3.8 %collective-permute-start.22 = (s16[528,512]{1,0:T(8,128)(2,1)S(1)}, s16[528,512]{1,0:T(8,128)(2,1)S(1)}, u32[]{:S(2)}, u32[]{:S(2)}) collective-permute-start(s16[528,512]{1,0:T(8,128)(2,1)S(1)} %reply.12), channel_id=1, source_target_pairs={{0,8},{8,0},{16,24},{24,16},{1,9},{9,1},{17,25},{25,17},{2,10},{10... | collective-permute-start | bytes 1622024 | tf_op jit(solution)/shard_map/ppermute | solution.py:328
  122.9 0.7 collective-permute-start.23
  124.2 4.6 %weight_grads.11 = (bf16[128,2048]{1,0:T(8,128)(2,1)}, f32[2048,2048]{1,0:T(8,128)}, f32[2048,2048]{1,0:T(8,128)}) custom-call(s32[7]{0:T(128)S(1)} %stack.35.place_ref, s32[16,16]{1,0:T(8,128)S(1)} %copy-done.5, bf16[2048,512]{1,0:T(8,128)(2,1)S(1)} %turn.1.turned_ref, ...), custom_call_target="tpu_custom_call", output_to_operand_aliasing={{0}: (7, {}), {1}: (8, {}), {2}: (9, {})} | custom-call | flops 1000000 | bytes 2500 | tf_op jit(solution)/shard_map/weight_grads/pallas_call | solution.py:261
  128.8 2.6 %collective-permute-done.22.b_ref.out_ref = s16[528,512]{1,0:T(8,128)(2,1)S(1)} collective-permute-done((s16[528,512]{1,0:T(8,128)(2,1)S(1)}, s16[528,512]{1,0:T(8,128)(2,1)S(1)}, u32[]{:S(2)}, u32[]{:S(2)}) %collective-permute-start.22) | collective-permute-done | bytes 540704 | tf_op jit(solution)/shard_map/ppermute | solution.py:328
  132.7 1.3 collective-permute-start.25
  134.6 1.3 collective-permute-start.26
  135.9 4.6 %weight_grads.12 = (bf16[128,2048]{1,0:T(8,128)(2,1)}, f32[2048,2048]{1,0:T(8,128)}, f32[2048,2048]{1,0:T(8,128)}) custom-call(s32[7]{0:T(128)S(1)} %stack.35.place_ref, s32[16,16]{1,0:T(8,128)S(1)} %copy-done.5, bf16[2048,512]{1,0:T(8,128)(2,1)S(1)} %turn.1.turned_ref, ...), custom_call_target="tpu_custom_call", output_to_operand_aliasing={{0}: (7, {}), {1}: (8, {}), {2}: (9, {})} | custom-call | flops 1000000 | bytes 2500 | tf_op jit(solution)/shard_map/weight_grads/pallas_call | solution.py:261
  140.5 0.8 reply.15
  141.3 1.3 collective-permute-start.27
  142.6 12.3 %collective-permute-done.25.out_ref = s16[528,512]{1,0:T(8,128)(2,1)S(1)} collective-permute-done((s16[528,512]{1,0:T(8,128)(2,1)S(1)}, s16[528,512]{1,0:T(8,128)(2,1)S(1)}, u32[]{:S(2)}, u32[]{:S(2)}) %collective-permute-start.25) | collective-permute-done | bytes 540704 | tf_op jit(solution)/shard_map/ppermute | solution.py:319
  154.9 4.6 %weight_grads.13 = (bf16[128,2048]{1,0:T(8,128)(2,1)}, f32[2048,2048]{1,0:T(8,128)}, f32[2048,2048]{1,0:T(8,128)}) custom-call(s32[7]{0:T(128)S(1)} %stack.35.place_ref, s32[16,16]{1,0:T(8,128)S(1)} %copy-done.5, bf16[2048,512]{1,0:T(8,128)(2,1)S(1)} %turn.1.turned_ref, ...), custom_call_target="tpu_custom_call", output_to_operand_aliasing={{0}: (7, {}), {1}: (8, {}), {2}: (9, {})} | custom-call | flops 1000000 | bytes 2500 | tf_op jit(solution)/shard_map/weight_grads/pallas_call | solution.py:261
  159.5 5.2 %collective-permute-done.26.out_ref = s16[528,512]{1,0:T(8,128)(2,1)S(1)} collective-permute-done((s16[528,512]{1,0:T(8,128)(2,1)S(1)}, s16[528,512]{1,0:T(8,128)(2,1)S(1)}, u32[]{:S(2)}, u32[]{:S(2)}) %collective-permute-start.26) | collective-permute-done | bytes 540704 | tf_op jit(solution)/shard_map/ppermute | solution.py:319
  164.7 4.6 %weight_grads.14 = (bf16[128,2048]{1,0:T(8,128)(2,1)}, f32[2048,2048]{1,0:T(8,128)}, f32[2048,2048]{1,0:T(8,128)}) custom-call(s32[7]{0:T(128)S(1)} %stack.35.place_ref, s32[16,16]{1,0:T(8,128)S(1)} %copy-done.5, bf16[2048,512]{1,0:T(8,128)(2,1)S(1)} %turn.1.turned_ref, ...), custom_call_target="tpu_custom_call", output_to_operand_aliasing={{0}: (7, {}), {1}: (8, {}), {2}: (9, {})} | custom-call | flops 1000000 | bytes 2500 | tf_op jit(solution)/shard_map/weight_grads/pallas_call | solution.py:261
  169.3 1.2 collective-permute-done.27.out_ref
  170.5 4.6 %weight_grads.15 = (bf16[128,2048]{1,0:T(8,128)(2,1)}, f32[2048,2048]{1,0:T(8,128)}, f32[2048,2048]{1,0:T(8,128)}) custom-call(s32[7]{0:T(128)S(1)} %stack.35.place_ref, s32[16,16]{1,0:T(8,128)S(1)} %copy-done.5, bf16[2048,512]{1,0:T(8,128)(2,1)S(1)} %turn.1.turned_ref, ...), custom_call_target="tpu_custom_call", output_to_operand_aliasing={{0}: (7, {}), {1}: (8, {}), {2}: (9, {})} | custom-call | flops 1000000 | bytes 2500 | tf_op jit(solution)/shard_map/weight_grads/pallas_call | solution.py:261
  (67 shorter events, 14.7 us)
Async XLA Ops:
  0.6 19.0 %collective-permute-start.3 = (bf16[128,2048]{1,0:T(8,128)(2,1)}, bf16[128,2048]{1,0:T(8,128)(2,1)S(1)}, u32[]{:S(2)}, u32[]{:S(2)}) collective-permute-start(bf16[128,2048]{1,0:T(8,128)(2,1)} %param.9), channel_id=1, source_target_pairs={{0,8},{8,0},{16,24},{24,16},{1,9},{9,1},{17,25},{25,17},{2,10},{10... | collective-permute-start | bytes 1572872 | tf_op jit(solution)/shard_map/ppermute | solution.py:328
  3.7 9.4 %collective-permute-start = (bf16[64,2048]{1,0:T(8,128)(2,1)}, bf16[64,2048]{1,0:T(8,128)(2,1)S(1)}, u32[]{:S(2)}, u32[]{:S(2)}) collective-permute-start(bf16[64,2048]{1,0:T(8,128)(2,1)} %param.5), channel_id=1, source_target_pairs={{0,2},{1,3},{2,0},{3,1},{4,6},{5,7},{6,4},{7,5},{8,10},{9,11},{10,... | collective-permute-start | bytes 786440 | tf_op jit(solution)/shard_map/ppermute | solution.py:297
  5.2 13.3 %collective-permute-start.1 = (bf16[64,2048]{1,0:T(8,128)(2,1)}, bf16[64,2048]{1,0:T(8,128)(2,1)S(1)}, u32[]{:S(2)}, u32[]{:S(2)}) collective-permute-start(bf16[64,2048]{1,0:T(8,128)(2,1)} %param.5), channel_id=1, source_target_pairs={{0,4},{1,5},{2,6},{3,7},{4,0},{5,1},{6,2},{7,3},{8,12},{9,13},{10,... | collective-permute-start | bytes 786440 | tf_op jit(solution)/shard_map/ppermute | solution.py:297
  6.7 11.8 %collective-permute-start.2 = (bf16[64,2048]{1,0:T(8,128)(2,1)}, bf16[64,2048]{1,0:T(8,128)(2,1)S(1)}, u32[]{:S(2)}, u32[]{:S(2)}) collective-permute-start(bf16[64,2048]{1,0:T(8,128)(2,1)} %param.5), channel_id=1, source_target_pairs={{0,6},{1,7},{2,4},{3,5},{4,2},{5,3},{6,0},{7,1},{8,14},{9,15},{10,... | collective-permute-start | bytes 786440 | tf_op jit(solution)/shard_map/ppermute | solution.py:297
  19.6 0.8 copy-start.9
  20.4 2.7 %collective-permute-start.4 = (bf16[256,2048]{1,0:T(8,128)(2,1)S(1)}, bf16[256,2048]{1,0:T(8,128)(2,1)S(1)}, u32[]{:S(2)}, u32[]{:S(2)}) collective-permute-start(bf16[256,2048]{1,0:T(8,128)(2,1)S(1)} %pad_maximum_fusion.1.low_ref), channel_id=1, source_target_pairs={{0,1},{1,0},{2,3},{3,2},{4,5},{5,4},{6,7},{7,6},{8,9},{9,8},{10,11... | collective-permute-start | bytes 3145736 | tf_op jit(solution)/shard_map/ppermute | solution.py:299
  20.4 15.7 %collective-permute-start.7 = (bf16[128,2048]{1,0:T(8,128)(2,1)}, bf16[128,2048]{1,0:T(8,128)(2,1)S(1)}, u32[]{:S(2)}, u32[]{:S(2)}) collective-permute-start(bf16[128,2048]{1,0:T(8,128)(2,1)} %param.9), channel_id=1, source_target_pairs={{8,16},{16,8},{9,17},{17,9},{10,18},{18,10},{11,19},{19,11},{12,20... | collective-permute-start | bytes 1572872 | tf_op jit(solution)/shard_map/ppermute | solution.py:325
  23.1 0.7 copy-start.4
  27.6 9.8 %copy-start.10 = (bf16[128,2048]{1,0:T(8,128)(2,1)S(1)}, bf16[128,2048]{1,0:T(8,128)(2,1)}, u32[]{:S(2)}) copy-start(bf16[128,2048]{1,0:T(8,128)(2,1)} %copy-done.9) | copy-start | bytes 1572868
  27.7 23.7 %collective-permute-start.5 = (s16[528,512]{1,0:T(8,128)(2,1)S(1)}, s16[528,512]{1,0:T(8,128)(2,1)S(1)}, u32[]{:S(2)}, u32[]{:S(2)}) collective-permute-start(s16[528,512]{1,0:T(8,128)(2,1)S(1)} %forward.6.a_ref), channel_id=1, source_target_pairs={{0,8},{24,16},{1,9},{25,17},{2,10},{26,18},{3,11},{27,19},{4,12},{... | collective-permute-start | bytes 1622024 | tf_op jit(solution)/shard_map/ppermute | solution.py:322
  36.1 15.2 %copy-start.6 = (bf16[128,2048]{1,0:T(8,128)(2,1)}, bf16[128,2048]{1,0:T(8,128)(2,1)S(1)}, u32[]{:S(2)}) copy-start(bf16[128,2048]{1,0:T(8,128)(2,1)S(1)} %collective-permute-done.7) | copy-start | bytes 1572868
  36.1 16.5 %collective-permute-start.8 = (bf16[128,2048]{1,0:T(8,128)(2,1)S(1)}, bf16[128,2048]{1,0:T(8,128)(2,1)S(1)}, u32[]{:S(2)}, u32[]{:S(2)}) collective-permute-start(bf16[128,2048]{1,0:T(8,128)(2,1)S(1)} %collective-permute-done.7), channel_id=1, source_target_pairs={{8,0},{16,24},{9,1},{17,25},{10,2},{18,26},{11,3},{19,27},{12,4},{... | collective-permute-start | bytes 1572872 | tf_op jit(solution)/shard_map/ppermute | solution.py:319
  37.4 15.2 %collective-permute-start.6 = (bf16[128,2048]{1,0:T(8,128)(2,1)S(1)}, bf16[128,2048]{1,0:T(8,128)(2,1)S(1)}, u32[]{:S(2)}, u32[]{:S(2)}) collective-permute-start(bf16[128,2048]{1,0:T(8,128)(2,1)S(1)} %copy-done.10), channel_id=1, source_target_pairs={{8,16},{16,8},{9,17},{17,9},{10,18},{18,10},{11,19},{19,11},{12,20... | collective-permute-start | bytes 1572872 | tf_op jit(solution)/shard_map/ppermute | solution.py:325
  38.1 26.8 %collective-permute-start.9 = (s16[528,512]{1,0:T(8,128)(2,1)S(1)}, s16[528,512]{1,0:T(8,128)(2,1)S(1)}, u32[]{:S(2)}, u32[]{:S(2)}) collective-permute-start(s16[528,512]{1,0:T(8,128)(2,1)S(1)} %forward.7.a_ref), channel_id=1, source_target_pairs={{0,8},{24,16},{1,9},{25,17},{2,10},{26,18},{3,11},{27,19},{4,12},{... | collective-permute-start | bytes 1622024 | tf_op jit(solution)/shard_map/ppermute | solution.py:322
  51.9 18.1 %copy-start.5 = (s32[16,16]{1,0:T(8,128)S(1)}, s32[16,16]{1,0:T(8,128)}, u32[]{:S(2)}) copy-start(s32[16,16]{1,0:T(8,128)} %mask_ref.27) | copy-start | bytes 3076
  51.9 15.7 %collective-permute-start.11 = (s16[528,512]{1,0:T(8,128)(2,1)S(1)}, s16[528,512]{1,0:T(8,128)(2,1)S(1)}, u32[]{:S(2)}, u32[]{:S(2)}) collective-permute-start(s16[528,512]{1,0:T(8,128)(2,1)S(1)} %add.9.own_ref), channel_id=1, source_target_pairs={{8,16},{16,8},{9,17},{17,9},{10,18},{18,10},{11,19},{19,11},{12,20... | collective-permute-start | bytes 1622024 | tf_op jit(solution)/shard_map/ppermute | solution.py:325
  52.7 15.0 %collective-permute-start.10 = (bf16[128,2048]{1,0:T(8,128)(2,1)S(1)}, bf16[128,2048]{1,0:T(8,128)(2,1)S(1)}, u32[]{:S(2)}, u32[]{:S(2)}) collective-permute-start(bf16[128,2048]{1,0:T(8,128)(2,1)S(1)} %collective-permute-done.6), channel_id=1, source_target_pairs={{8,0},{16,24},{9,1},{17,25},{10,2},{18,26},{11,3},{19,27},{12,4},{... | collective-permute-start | bytes 1572872 | tf_op jit(solution)/shard_map/ppermute | solution.py:319
  54.0 19.9 %collective-permute-start.12 = (s16[528,512]{1,0:T(8,128)(2,1)S(1)}, s16[528,512]{1,0:T(8,128)(2,1)S(1)}, u32[]{:S(2)}, u32[]{:S(2)}) collective-permute-start(s16[528,512]{1,0:T(8,128)(2,1)S(1)} %get-tuple-element.86.a_ref), channel_id=1, source_target_pairs={{0,8},{24,16},{1,9},{25,17},{2,10},{26,18},{3,11},{27,19},{4,12},{... | collective-permute-start | bytes 1622024 | tf_op jit(solution)/shard_map/ppermute | solution.py:322
  65.5 9.6 %collective-permute-start.13 = (s16[528,512]{1,0:T(8,128)(2,1)S(1)}, s16[528,512]{1,0:T(8,128)(2,1)S(1)}, u32[]{:S(2)}, u32[]{:S(2)}) collective-permute-start(s16[528,512]{1,0:T(8,128)(2,1)S(1)} %add.10.own_ref), channel_id=1, source_target_pairs={{8,16},{16,8},{9,17},{17,9},{10,18},{18,10},{11,19},{19,11},{12,20... | collective-permute-start | bytes 1622024 | tf_op jit(solution)/shard_map/ppermute | solution.py:325
  68.2 21.6 %collective-permute-start.14 = (s16[528,512]{1,0:T(8,128)(2,1)S(1)}, s16[528,512]{1,0:T(8,128)(2,1)S(1)}, u32[]{:S(2)}, u32[]{:S(2)}) collective-permute-start(s16[528,512]{1,0:T(8,128)(2,1)S(1)} %reply.8), channel_id=1, source_target_pairs={{0,8},{8,0},{16,24},{24,16},{1,9},{9,1},{17,25},{25,17},{2,10},{10... | collective-permute-start | bytes 1622024 | tf_op jit(solution)/shard_map/ppermute | solution.py:328
  74.4 21.9 %collective-permute-start.15 = (s16[528,512]{1,0:T(8,128)(2,1)S(1)}, s16[528,512]{1,0:T(8,128)(2,1)S(1)}, u32[]{:S(2)}, u32[]{:S(2)}) collective-permute-start(s16[528,512]{1,0:T(8,128)(2,1)S(1)} %add.11.own_ref), channel_id=1, source_target_pairs={{8,16},{16,8},{9,17},{17,9},{10,18},{18,10},{11,19},{19,11},{12,20... | collective-permute-start | bytes 1622024 | tf_op jit(solution)/shard_map/ppermute | solution.py:325
  75.2 13.1 %copy-start.2 = (s16[528,512]{1,0:T(8,128)(2,1)}, s16[528,512]{1,0:T(8,128)(2,1)S(1)}, u32[]{:S(2)}) copy-start(s16[528,512]{1,0:T(8,128)(2,1)S(1)} %collective-permute-done.13.b_ref.across_ref) | copy-start | bytes 1622020
  76.6 24.2 %collective-permute-start.16 = (s16[528,512]{1,0:T(8,128)(2,1)}, s16[528,512]{1,0:T(8,128)(2,1)S(1)}, u32[]{:S(2)}, u32[]{:S(2)}) collective-permute-start(s16[528,512]{1,0:T(8,128)(2,1)} %reply.9), channel_id=1, source_target_pairs={{0,8},{8,0},{16,24},{24,16},{1,9},{9,1},{17,25},{25,17},{2,10},{10... | collective-permute-start | bytes 1622024 | tf_op jit(solution)/shard_map/ppermute | solution.py:328
  88.3 3.0 %copy-start.7 = (bf16[128,2048]{1,0:T(8,128)(2,1)S(1)}, bf16[128,2048]{1,0:T(8,128)(2,1)}, u32[]{:S(2)}) copy-start(bf16[128,2048]{1,0:T(8,128)(2,1)} %copy-done.6) | copy-start | bytes 1572868
  89.8 1.6 copy-start.8
  89.8 1.6 copy-start.11
  90.5 18.0 %collective-permute-start.17 = (s16[528,512]{1,0:T(8,128)(2,1)S(1)}, s16[528,512]{1,0:T(8,128)(2,1)S(1)}, u32[]{:S(2)}, u32[]{:S(2)}) collective-permute-start(s16[528,512]{1,0:T(8,128)(2,1)S(1)} %add.12.own_ref), channel_id=1, source_target_pairs={{8,16},{16,8},{9,17},{17,9},{10,18},{18,10},{11,19},{19,11},{12,20... | collective-permute-start | bytes 1622024 | tf_op jit(solution)/shard_map/ppermute | solution.py:325
  91.7 11.1 %copy-start.3 = (s16[528,512]{1,0:T(8,128)(2,1)S(1)}, s16[528,512]{1,0:T(8,128)(2,1)}, u32[]{:S(2)}) copy-start(s16[528,512]{1,0:T(8,128)(2,1)} %copy-done.2) | copy-start | bytes 1622020
  96.9 15.1 %collective-permute-start.18 = (s16[528,512]{1,0:T(8,128)(2,1)S(1)}, s16[528,512]{1,0:T(8,128)(2,1)S(1)}, u32[]{:S(2)}, u32[]{:S(2)}) collective-permute-start(s16[528,512]{1,0:T(8,128)(2,1)S(1)} %reply.10), channel_id=1, source_target_pairs={{0,8},{8,0},{16,24},{24,16},{1,9},{9,1},{17,25},{25,17},{2,10},{10... | collective-permute-start | bytes 1622024 | tf_op jit(solution)/shard_map/ppermute | solution.py:328
  101.3 0.8 copy-start
  102.1 15.7 %collective-permute-start.19 = (s16[528,512]{1,0:T(8,128)(2,1)S(1)}, s16[528,512]{1,0:T(8,128)(2,1)S(1)}, u32[]{:S(2)}, u32[]{:S(2)}) collective-permute-start(s16[528,512]{1,0:T(8,128)(2,1)S(1)} %add.13.own_ref), channel_id=1, source_target_pairs={{8,16},{16,8},{9,17},{17,9},{10,18},{18,10},{11,19},{19,11},{12,20... | collective-permute-start | bytes 1622024 | tf_op jit(solution)/shard_map/ppermute | solution.py:325
  102.8 1.0 copy-start.1
  109.1 13.2 %collective-permute-start.20 = (s16[528,512]{1,0:T(8,128)(2,1)S(1)}, s16[528,512]{1,0:T(8,128)(2,1)S(1)}, u32[]{:S(2)}, u32[]{:S(2)}) collective-permute-start(s16[528,512]{1,0:T(8,128)(2,1)S(1)} %reply.11), channel_id=1, source_target_pairs={{0,8},{8,0},{16,24},{24,16},{1,9},{9,1},{17,25},{25,17},{2,10},{10... | collective-permute-start | bytes 1622024 | tf_op jit(solution)/shard_map/ppermute | solution.py:328
  112.6 11.0 %collective-permute-start.21 = (s16[528,512]{1,0:T(8,128)(2,1)S(1)}, s16[528,512]{1,0:T(8,128)(2,1)S(1)}, u32[]{:S(2)}, u32[]{:S(2)}) collective-permute-start(s16[528,512]{1,0:T(8,128)(2,1)S(1)} %add.14.own_ref), channel_id=1, source_target_pairs={{8,16},{16,8},{9,17},{17,9},{10,18},{18,10},{11,19},{19,11},{12,20... | collective-permute-start | bytes 1622024 | tf_op jit(solution)/shard_map/ppermute | solution.py:325
  118.5 12.9 %collective-permute-start.22 = (s16[528,512]{1,0:T(8,128)(2,1)S(1)}, s16[528,512]{1,0:T(8,128)(2,1)S(1)}, u32[]{:S(2)}, u32[]{:S(2)}) collective-permute-start(s16[528,512]{1,0:T(8,128)(2,1)S(1)} %reply.12), channel_id=1, source_target_pairs={{0,8},{8,0},{16,24},{24,16},{1,9},{9,1},{17,25},{25,17},{2,10},{10... | collective-permute-start | bytes 1622024 | tf_op jit(solution)/shard_map/ppermute | solution.py:328
  122.9 11.1 %collective-permute-start.23 = (s16[528,512]{1,0:T(8,128)(2,1)S(1)}, s16[528,512]{1,0:T(8,128)(2,1)S(1)}, u32[]{:S(2)}, u32[]{:S(2)}) collective-permute-start(s16[528,512]{1,0:T(8,128)(2,1)S(1)} %add.15.own_ref), channel_id=1, source_target_pairs={{8,16},{16,8},{9,17},{17,9},{10,18},{18,10},{11,19},{19,11},{12,20... | collective-permute-start | bytes 1622024 | tf_op jit(solution)/shard_map/ppermute | solution.py:325
  132.0 8.5 %collective-permute-start.24 = (s16[528,512]{1,0:T(8,128)(2,1)S(1)}, s16[528,512]{1,0:T(8,128)(2,1)S(1)}, u32[]{:S(2)}, u32[]{:S(2)}) collective-permute-start(s16[528,512]{1,0:T(8,128)(2,1)S(1)} %add.16.own_ref), channel_id=1, source_target_pairs={{8,16},{16,8},{9,17},{17,9},{10,18},{18,10},{11,19},{19,11},{12,20... | collective-permute-start | bytes 1622024 | tf_op jit(solution)/shard_map/ppermute | solution.py:325
  132.7 22.2 %collective-permute-start.25 = (s16[528,512]{1,0:T(8,128)(2,1)S(1)}, s16[528,512]{1,0:T(8,128)(2,1)S(1)}, u32[]{:S(2)}, u32[]{:S(2)}) collective-permute-start(s16[528,512]{1,0:T(8,128)(2,1)S(1)} %reply.13), channel_id=1, source_target_pairs={{8,0},{16,24},{9,1},{17,25},{10,2},{18,26},{11,3},{19,27},{12,4},{... | collective-permute-start | bytes 1622024 | tf_op jit(solution)/shard_map/ppermute | solution.py:319
  134.6 30.1 %collective-permute-start.26 = (s16[528,512]{1,0:T(8,128)(2,1)S(1)}, s16[528,512]{1,0:T(8,128)(2,1)S(1)}, u32[]{:S(2)}, u32[]{:S(2)}) collective-permute-start(s16[528,512]{1,0:T(8,128)(2,1)S(1)} %reply.14), channel_id=1, source_target_pairs={{8,0},{16,24},{9,1},{17,25},{10,2},{18,26},{11,3},{19,27},{12,4},{... | collective-permute-start | bytes 1622024 | tf_op jit(solution)/shard_map/ppermute | solution.py:319
  141.3 29.2 %collective-permute-start.27 = (s16[528,512]{1,0:T(8,128)(2,1)S(1)}, s16[528,512]{1,0:T(8,128)(2,1)S(1)}, u32[]{:S(2)}, u32[]{:S(2)}) collective-permute-start(s16[528,512]{1,0:T(8,128)(2,1)S(1)} %reply.15), channel_id=1, source_target_pairs={{8,0},{16,24},{9,1},{17,25},{10,2},{18,26},{11,3},{19,27},{12,4},{... | collective-permute-start | bytes 1622024 | tf_op jit(solution)/shard_map/ppermute | solution.py:319
